TPU v7x, 32 devices: a whole 2x2x4 slice. The times are simulated.
32 devices in a mesh: row: 4 (over y, core), col: 8 (over z, x).
Axes of the slice: x: 2, y: 2, z: 4, core: 2. Of those that a mesh axis runs over, the one named last changes fastest.
Arguments:
- velocity: float32 [3, 64, 32, 128], P(None, 'row', 'col'), may hold values from -6 to 6
- wall_counts: int32 [4], replicated, may hold values from 1 to 16, 32 in all
- x_first: float32 [128], replicated, may hold values from -0.5 to 0.5
- x_second: float32 [128], replicated, may hold values from -0.5 to 0.5
- y_first: float32 [32, 32], replicated, may hold values from -1 to 1
- y_second: float32 [32, 32], replicated, may hold values from -1 to 1
- z_first: float32 [32], replicated, may hold values from -1 to 1
- z_second: float32 [32], replicated, may hold values from -1 to 1
- metric_table: float32 [64], replicated, may hold values from 0.5 to 4
- metric_index: int32 [32], replicated, may hold values from 0 to 63
Outputs:
- tendency: float32 [3, 64, 32, 128], P(None, 'row', 'col')
Inputs may be any that keep to these rules, and one draw needn't show every extreme that they name: Index r of row holds wall_counts[r] consecutive wall-normal planes, from the lower wall in order of r; they sum to 32. `metric_index`: entry of metric_table that scales the wall-normal derivative at each cell.
All inputs are finite; a program needn't handle non-finite values.
Results may differ from a plain program's by a relative error of at most 0.00012.
Values sent between devices are 32-bit elements; how exact they have to be, the bound alone decides.
No kernel may reach another device: no remote copies, remote signals or barrier semaphores. Data moves between devices by JAX's collectives and lax.ppermute only.
A program may use at most 64 MiB of HBM per device.

v0:
```python
import jax
import jax.numpy as jnp
from jax import lax
from jax.sharding import PartitionSpec as P

viscosity = 0.4
exact = lax.Precision.HIGHEST


def circulant(row):
    length = row.shape[0]
    mirror = jnp.roll(row[::-1], 1)
    hankel = jnp.tile(mirror, length + 1).reshape(length, length + 1)[:, :length]
    return jnp.concatenate([hankel[:1], hankel[:0:-1]], axis=0)


def tendency(field, leading, first, second):
    carried = field[leading][None] * field
    return viscosity * jnp.dot(field, second, precision=exact) - jnp.dot(
        carried, first, precision=exact
    )


def plane_table(wall_counts, slots, cells):
    splits = wall_counts.shape[0]
    offsets = jnp.cumsum(wall_counts) - wall_counts
    slot = jnp.arange(splits * slots, dtype=jnp.int32)
    owner = slot // slots
    within = slot - owner * slots
    pick = owner[:, None] == jnp.arange(splits, dtype=jnp.int32)[None, :]
    start = jnp.sum(jnp.where(pick, offsets[None, :], 0), axis=1)
    count = jnp.sum(jnp.where(pick, wall_counts[None, :], 0), axis=1)
    live = within < count
    target = start + within
    return (
        live[:, None] & (target[:, None] == jnp.arange(cells, dtype=jnp.int32)[None, :])
    ).astype(jnp.float32)


def pack_span(normal, cols):
    _, zloc, xloc, depth = normal.shape
    block = depth // cols
    return (
        normal.reshape(3, zloc, xloc, cols, block)
        .transpose(3, 0, 2, 4, 1)
        .reshape(cols, 3, xloc * block * zloc)
    )


def open_span(received, cols, xloc, zloc):
    block = received.shape[2] // (xloc * zloc)
    return (
        received.reshape(cols, 3, xloc, block, zloc)
        .transpose(1, 2, 3, 0, 4)
        .reshape(3, xloc, block, cols * zloc)
    )


def pack_normal(span, cols):
    _, xloc, block, length_z = span.shape
    zloc = length_z // cols
    return (
        span.reshape(3, xloc, block, cols, zloc)
        .transpose(3, 0, 4, 1, 2)
        .reshape(cols, 3, zloc * xloc * block)
    )


def open_normal(received, cols, xloc, zloc):
    block = received.shape[2] // (xloc * zloc)
    return (
        received.reshape(cols, 3, zloc, xloc, block)
        .transpose(1, 2, 3, 0, 4)
        .reshape(3, zloc, xloc, cols * block)
    )


def local(
    velocity,
    wall_counts,
    x_first,
    x_second,
    y_first,
    y_second,
    z_first,
    z_second,
    metric_table,
    metric_index,
):
    rows = lax.axis_size("row")
    cols = lax.axis_size("col")
    slots = velocity.shape[1]
    zloc = velocity.shape[2]
    length_x = velocity.shape[3]
    cells_y = metric_index.shape[0]
    xloc = length_x // rows
    padded = rows * slots
    myself = lax.axis_index("row")
    holding = jnp.sum(jnp.where(jnp.arange(rows, dtype=jnp.int32) == myself, wall_counts, 0))
    live = (jnp.arange(slots, dtype=jnp.int32) < holding).astype(jnp.float32)
    stream = velocity * live[None, :, None, None]
    x_part = tendency(stream, 0, circulant(x_first), circulant(x_second))
    outgoing = (
        stream.reshape(3, slots, zloc, rows, xloc)
        .transpose(3, 0, 1, 2, 4)
        .reshape(rows, 3, slots * zloc * xloc)
    )
    incoming = lax.all_to_all(outgoing, "row", split_axis=0, concat_axis=1, tiled=True)
    normal = (
        incoming.reshape(rows, 3, slots, zloc, xloc)
        .transpose(1, 3, 4, 0, 2)
        .reshape(3, zloc, xloc, padded)
    )
    placing = plane_table(wall_counts, slots, cells_y)
    levels = metric_table.shape[0]
    metric = jnp.sum(
        jnp.where(
            metric_index[:, None] == jnp.arange(levels, dtype=jnp.int32)[None, :],
            metric_table[None, :],
            0.0,
        ),
        axis=1,
    )
    first_live = jnp.dot(placing, y_first.T * metric[None, :], precision=exact)
    second_live = jnp.dot(placing, y_second.T, precision=exact)
    span_first = circulant(z_first)
    span_second = circulant(z_second)
    first_pad = jnp.dot(first_live, placing.T, precision=exact)
    second_pad = jnp.dot(second_live, placing.T, precision=exact)
    y_part = tendency(normal, 1, first_pad, second_pad)
    sent = lax.all_to_all(pack_span(normal, cols), "col", split_axis=0, concat_axis=1, tiled=True)
    span = open_span(sent, cols, xloc, zloc)
    z_part = tendency(span, 2, span_first, span_second)
    returned = lax.all_to_all(
        pack_normal(z_part, cols), "col", split_axis=0, concat_axis=1, tiled=True
    )
    total = y_part + open_normal(returned, cols, xloc, zloc)
    leaving = (
        total.reshape(3, zloc, xloc, rows, slots)
        .transpose(3, 0, 4, 1, 2)
        .reshape(rows, 3, slots * zloc * xloc)
    )
    arriving = lax.all_to_all(leaving, "row", split_axis=0, concat_axis=1, tiled=True)
    gathered = (
        arriving.reshape(rows, 3, slots, zloc, xloc)
        .transpose(1, 2, 3, 0, 4)
        .reshape(3, slots, zloc, length_x)
    )
    return gathered + x_part


def solution(mesh):
    in_specs = (P(None, "row", "col", None), P(), P(), P(), P(), P(), P(), P(), P(), P())
    out_specs = P(None, "row", "col", None)
    return jax.shard_map(local, mesh=mesh, in_specs=in_specs, out_specs=out_specs, check_vma=False)
```

profile of v0, /device:TPU:0, one launch (start us, length us, event | category | flops | bytes accessed | tf_op | source)
XLA Modules:
  0.0 62.8 jit_solution(3126271743242354570)
XLA Ops:
  0.0 0.9 %reduce-window.9 = s32[4,1]{0,1:T(1,128)S(1)} reduce-window(s32[4,1]{0,1:T(1,128)} %bitcast.99, s32[]{:T(128)} %constant.31.clone.1), window={size=4x1 pad=3_0x0_0}, to_apply=%region_2.3 | reduce-window | flops 12 | bytes 36 | tf_op jit(solution)/shard_map/reduce-window.4
  0.9 1.3 %bitcast_subtract_fusion = (s32[4]{0:T(128)S(1)}, s32[]{:T(128)}) fusion(s32[4]{0:T(128)} %param.11, s32[4,1]{0,1:T(1,128)S(1)} %reduce-window.9, s32[]{:T(128)S(6)} %axis_index.15), kind=kLoop, calls=%fused_computation.64 | loop fusion | flops 15 | bytes 56 | tf_op jit(solution)/shard_map/sub | solution.py:26
  2.9 1.0 %broadcast_multiply_fusion.2 = f32[3,16,4,128]{3,2,1,0:T(4,128)S(1)} fusion(f32[3,16,4,128]{3,2,1,0:T(4,128)} %param.10, f32[16]{0:T(128)S(1)} %compare_convert_fusion), kind=kLoop, calls=%fused_computation.25 | loop fusion | flops 24576 | bytes 196672 | tf_op jit(solution)/shard_map/mul | solution.py:101
  4.5 0.7 %copy.65 = f32[4,3,2048]{2,1,0:T(4,128)} copy(f32[4,3,2048]{2,0,1:T(4,128)S(1)} %reshape.132) | data formatting | bytes 196608 | tf_op jit(solution)/shard_map/reshape | solution.py:106
  5.2 4.2 %all-to-all-start = ((f32[4,3,2048]{2,1,0:T(4,128)}), f32[4,3,2048]{2,1,0:T(4,128)S(1)}, u32[]{:S(2)}, u32[]{:S(2)}) async-start(f32[4,3,2048]{2,1,0:T(4,128)} %copy.65), calls=%async_computation | async-start | bytes 262144 | tf_op jit(solution)/shard_map/all_to_all | solution.py:108
  12.0 2.1 %all-to-all-done = f32[4,3,2048]{2,1,0:T(4,128)S(1)} async-done(((f32[4,3,2048]{2,1,0:T(4,128)}), f32[4,3,2048]{2,1,0:T(4,128)S(1)}, u32[]{:S(2)}, u32[]{:S(2)}) %all-to-all-start) | async-done | bytes 98336 | tf_op jit(solution)/shard_map/all_to_all | solution.py:108
  14.5 2.2 %copy.72 = f32[8,3,32,8,4]{0,4,3,2,1:T(4,128)S(1)} copy(f32[8,3,32,8,4]{2,3,0,4,1:T(8,128)S(1)} %bitcast.86) | data formatting | bytes 196608 | tf_op jit(solution)/shard_map/transpose | solution.py:45
  16.7 1.2 %copy.73 = f32[8,3,1024]{2,1,0:T(4,128)} copy(f32[8,3,1024]{0,2,1:T(8,128)S(1)} %bitcast.85) | data formatting | bytes 196608 | tf_op jit(solution)/shard_map/reshape | solution.py:46
  17.9 6.3 %all-to-all-start.1 = ((f32[8,3,1024]{2,1,0:T(4,128)}), f32[8,3,1024]{2,1,0:T(4,128)S(1)}, u32[]{:S(2)}, u32[]{:S(2)}) async-start(f32[8,3,1024]{2,1,0:T(4,128)} %copy.73), calls=%async_computation.1 | async-start | bytes 262144 | tf_op jit(solution)/shard_map/all_to_all | solution.py:131
  25.1 6.4 %all-to-all-done.1 = f32[8,3,1024]{2,1,0:T(4,128)S(1)} async-done(((f32[8,3,1024]{2,1,0:T(4,128)}), f32[8,3,1024]{2,1,0:T(4,128)S(1)}, u32[]{:S(2)}, u32[]{:S(2)}) %all-to-all-start.1) | async-done | bytes 98336 | tf_op jit(solution)/shard_map/all_to_all | solution.py:131
  32.0 1.7 %copy.75 = f32[3,32,8,8,4]{1,2,4,3,0:T(8,128)S(1)} copy(f32[3,32,8,8,4]{3,4,2,1,0:T(4,128)S(1)} %bitcast.81) | data formatting | bytes 196608 | tf_op jit(solution)/shard_map/transpose | solution.py:54
  34.2 0.8 %convolution_multiply_fusion = f32[3,32,8,32]{3,1,2,0:T(8,128)S(1)} fusion(f32[3,32,8,32]{1,2,3,0:T(8,128)S(1)} %bitcast.90, f32[31,32]{1,0:T(8,128)S(1)} %rev.16, f32[1,32]{1,0:T(1,128)S(1)} %slice.115), kind=kOutput, calls=%fused_computation.1 | convolution fusion | flops 9462784 | bytes 200704 | tf_op jit(solution)/shard_map/dot_general | solution.py:19
  35.0 0.8 %convolution_subtract_fusion = f32[3,32,8,32]{3,1,2,0:T(8,128)S(1)} fusion(f32[3,32,8,32]{3,1,2,0:T(8,128)S(1)} %convolution_multiply_fusion, f32[3,32,8,32]{1,2,3,0:T(8,128)S(1)} %broadcast_multiply_fusion, f32[31,32]{1,0:T(8,128)S(1)} %rev.17, f32[1,32]{1,0:T(1,128)S(1)} %slice.118), kind=kOutput, calls=%fused_computation | convolution fusion | flops 9462784 | bytes 299008 | tf_op jit(solution)/shard_map/dot_general | solution.py:19
  35.8 1.3 %copy.101 = f32[3,32,8,32]{2,1,3,0:T(8,128)S(1)} copy(f32[3,32,8,32]{3,1,2,0:T(8,128)S(1)} %convolution_subtract_fusion) | data formatting | bytes 196608 | tf_op jit(solution)/shard_map/transpose | solution.py:64
  37.2 0.8 %reshape.141 = f32[8,3,1024]{2,0,1:T(8,128)S(1)} reshape(f32[8,3,4,32,8]{4,3,2,0,1:T(8,128)S(1)} %bitcast.83) | data formatting | bytes 196608 | tf_op jit(solution)/shard_map/reshape | solution.py:65
  38.0 0.7 %copy.81 = f32[8,3,1024]{2,1,0:T(4,128)} copy(f32[8,3,1024]{2,0,1:T(8,128)S(1)} %reshape.141) | data formatting | bytes 196608 | tf_op jit(solution)/shard_map/reshape | solution.py:65
  38.7 3.5 %all-to-all-start.2 = ((f32[8,3,1024]{2,1,0:T(4,128)}), f32[8,3,1024]{2,1,0:T(4,128)S(1)}, u32[]{:S(2)}, u32[]{:S(2)}) async-start(f32[8,3,1024]{2,1,0:T(4,128)} %copy.81), calls=%async_computation.2 | async-start | bytes 262144 | tf_op jit(solution)/shard_map/all_to_all | solution.py:134
  42.3 0.8 %convolution_multiply_fusion.1 = f32[3,4,32,64]{3,2,1,0:T(8,128)S(1)} fusion(f32[3,4,32,64]{2,3,1,0:T(8,128)S(1)} %bitcast.87, f32[64,64,1,1]{1,0,3,2:T(8,128)S(1)} %convolution_bitcast_fusion.1), kind=kOutput, calls=%fused_computation.4 | convolution fusion | flops 18898944 | bytes 212992 | tf_op jit(solution)/shard_map/dot_general | solution.py:19
  43.1 6.3 %all-to-all-done.2 = f32[8,3,1024]{2,1,0:T(4,128)S(1)} async-done(((f32[8,3,1024]{2,1,0:T(4,128)}), f32[8,3,1024]{2,1,0:T(4,128)S(1)}, u32[]{:S(2)}, u32[]{:S(2)}) %all-to-all-start.2) | async-done | bytes 98336 | tf_op jit(solution)/shard_map/all_to_all | solution.py:134
  49.4 0.9 %reshape.142 = f32[8,3,4,32,8]{4,3,2,0,1:T(8,128)S(1)} reshape(f32[8,3,1024]{2,0,1:T(8,128)S(1)} %copy.82) | data formatting | bytes 196608 | tf_op jit(solution)/shard_map/reshape | solution.py:72
  50.9 0.8 %fusion = f32[3,4,32,64]{3,2,1,0:T(8,128)S(1)} fusion(f32[3,4,32,64]{3,2,1,0:T(8,128)S(1)} %copy.84, f32[3,4,32,64]{3,2,1,0:T(8,128)S(1)} %convolution_multiply_fusion.1, f32[64,64,1,1]{1,0,3,2:T(8,128)S(1)} %convolution_bitcast_fusion, f32[3,4,32,64]{2,3,1,0:T(8,128)S(1)} %bitcast.88, f32[4,32,64]{1,2,0:T(8,128)S(1)} %bitcast.98), kind=kOutput, calls=%fused_computation.3 | convolution fusion | flops 18948096 | bytes 442368 | tf_op jit(solution)/shard_map/dot_general | solution.py:19
  52.2 1.0 %reshape.154 = f32[4,3,2048]{2,1,0:T(4,128)} reshape(f32[4,3,16,4,32]{4,3,2,1,0:T(4,128)S(1)} %copy.102) | data formatting | bytes 196608 | tf_op jit(solution)/shard_map/reshape | solution.py:141
  53.1 3.3 %all-to-all-start.3 = ((f32[4,3,2048]{2,1,0:T(4,128)}), f32[4,3,2048]{2,1,0:T(4,128)S(1)}, u32[]{:S(2)}, u32[]{:S(2)}) async-start(f32[4,3,2048]{2,1,0:T(4,128)} %reshape.154), calls=%async_computation.3 | async-start | bytes 262144 | tf_op jit(solution)/shard_map/all_to_all | solution.py:143
  57.0 4.1 %all-to-all-done.3 = f32[4,3,2048]{2,1,0:T(4,128)S(1)} async-done(((f32[4,3,2048]{2,1,0:T(4,128)}), f32[4,3,2048]{2,1,0:T(4,128)S(1)}, u32[]{:S(2)}, u32[]{:S(2)}) %all-to-all-start.3) | async-done | bytes 98336 | tf_op jit(solution)/shard_map/all_to_all | solution.py:143
  (88 shorter events, 9.1 us)
Async XLA Ops:
  0.0 10.6 %copy-start = (f32[32,32]{1,0:T(8,128)S(1)}, f32[32,32]{1,0:T(8,128)}, u32[]{:S(2)}) copy-start(f32[32,32]{1,0:T(8,128)} %param.15) | copy-start | bytes 12292
  0.0 10.5 %copy-start.2 = (s32[4]{0:T(128)S(1)}, s32[4]{0:T(128)}, u32[]{:S(2)}) copy-start(s32[4]{0:T(128)} %param.11) | copy-start | bytes 52
  0.0 9.5 %copy-start.4 = (f32[128]{0:T(128)S(1)}, f32[128]{0:T(128)}, u32[]{:S(2)}) copy-start(f32[128]{0:T(128)} %param.13) | copy-start | bytes 1540
  0.0 10.1 %copy-start.7 = (f32[32]{0:T(128)S(1)}, f32[32]{0:T(128)}, u32[]{:S(2)}) copy-start(f32[32]{0:T(128)} %param.17) | copy-start | bytes 388
  0.0 10.3 %copy-start.8 = (f32[32]{0:T(128)S(1)}, f32[32]{0:T(128)}, u32[]{:S(2)}) copy-start(f32[32]{0:T(128)} %param.16) | copy-start | bytes 388
  3.8 7.3 %copy-start.1 = (f32[3,16,4,128]{3,2,1,0:T(4,128)S(1)}, f32[3,16,4,128]{3,2,1,0:T(4,128)}, u32[]{:S(2)}) copy-start(f32[3,16,4,128]{3,2,1,0:T(4,128)} %param.10) | copy-start | bytes 294916
  3.8 7.4 %copy-start.5 = (f32[64]{0:T(128)S(1)}, f32[64]{0:T(128)}, u32[]{:S(2)}) copy-start(f32[64]{0:T(128)} %param.18) | copy-start | bytes 772
  3.9 7.4 %copy-start.6 = (s32[32]{0:T(128)S(1)}, s32[32]{0:T(128)}, u32[]{:S(2)}) copy-start(s32[32]{0:T(128)} %param.19) | copy-start | bytes 388
  3.9 7.6 %copy-start.3 = (f32[32,32]{1,0:T(8,128)S(1)}, f32[32,32]{1,0:T(8,128)}, u32[]{:S(2)}) copy-start(f32[32,32]{1,0:T(8,128)} %param.14) | copy-start | bytes 12292
  5.2 8.9 %all-to-all-start = ((f32[4,3,2048]{2,1,0:T(4,128)}), f32[4,3,2048]{2,1,0:T(4,128)S(1)}, u32[]{:S(2)}, u32[]{:S(2)}) async-start(f32[4,3,2048]{2,1,0:T(4,128)} %copy.65), calls=%async_computation | async-start | bytes 262144 | tf_op jit(solution)/shard_map/all_to_all | solution.py:108
  16.7 8.0 %copy-start.9 = (f32[128]{0:T(128)S(1)}, f32[128]{0:T(128)}, u32[]{:S(2)}) copy-start(f32[128]{0:T(128)} %param.12) | copy-start | bytes 1540
  17.9 13.7 %all-to-all-start.1 = ((f32[8,3,1024]{2,1,0:T(4,128)}), f32[8,3,1024]{2,1,0:T(4,128)S(1)}, u32[]{:S(2)}, u32[]{:S(2)}) async-start(f32[8,3,1024]{2,1,0:T(4,128)} %copy.73), calls=%async_computation.1 | async-start | bytes 262144 | tf_op jit(solution)/shard_map/all_to_all | solution.py:131
  38.7 10.7 %all-to-all-start.2 = ((f32[8,3,1024]{2,1,0:T(4,128)}), f32[8,3,1024]{2,1,0:T(4,128)S(1)}, u32[]{:S(2)}, u32[]{:S(2)}) async-start(f32[8,3,1024]{2,1,0:T(4,128)} %copy.81), calls=%async_computation.2 | async-start | bytes 262144 | tf_op jit(solution)/shard_map/all_to_all | solution.py:134
  53.1 7.9 %all-to-all-start.3 = ((f32[4,3,2048]{2,1,0:T(4,128)}), f32[4,3,2048]{2,1,0:T(4,128)S(1)}, u32[]{:S(2)}, u32[]{:S(2)}) async-start(f32[4,3,2048]{2,1,0:T(4,128)} %reshape.154), calls=%async_computation.3 | async-start | bytes 262144 | tf_op jit(solution)/shard_map/all_to_all | solution.py:143
where the time goes:
time: 63.4 us; the launch traced here: 62.8 us
  waiting for transfers between devices  18.9 us (30%)
  starting transfers between devices  17.4 us (27%)
  local copies, waits for them, and re-layouts  16.7 us (26%)
  other arithmetic  4.63 us (7%)
  matrix products  4.59 us (7%)
    all_to_all x1, waiting for transfers between devices, local(): lax.all_to_all(pack_span(normal, cols), 'col', split_axis=0, concat_axis=...  6.4 us
    all_to_all x1, starting transfers between devices, local(): lax.all_to_all(pack_span(normal, cols), 'col', split_axis=0, concat_axis=...  6.31 us
    all_to_all x1, waiting for transfers between devices, local(): lax.all_to_all(pack_normal(z_part, cols), 'col', split_axis=0, concat_axi...  6.31 us
    all_to_all x1, starting transfers between devices, local(): lax.all_to_all(outgoing, 'row', split_axis=0, concat_axis=1, tiled=True)  4.24 us
    all_to_all x1, waiting for transfers between devices, local(): lax.all_to_all(leaving, 'row', split_axis=0, concat_axis=1, tiled=True)  4.08 us
    all_to_all x1, starting transfers between devices, local(): lax.all_to_all(pack_normal(z_part, cols), 'col', split_axis=0, concat_axi...  3.55 us
    all_to_all x1, starting transfers between devices, local(): lax.all_to_all(leaving, 'row', split_axis=0, concat_axis=1, tiled=True)  3.32 us
    transpose x1, local copies, waits for them, and re-layouts, pack_span(): return normal.reshape(3, zloc, xloc, cols, block).transpose(3, 0, 2, 4, 1...  2.19 us
  transfers between devices with their start and end apart: 4, of which 4 were waited for; matrix products, arithmetic and copies ran while one was open for 7% of the time, Pallas kernels for 0%

commit v1 on v0

v1 whole, which is shorter than its diff:
```python
import functools

import jax
import jax.numpy as jnp
from jax import lax
from jax.experimental import pallas as pl
from jax.experimental.pallas import tpu as pltpu
from jax.sharding import PartitionSpec as P

viscosity = 0.4
lanes = 128

VMEM = pltpu.VMEM
SMEM = pltpu.SMEM


def spec(space):
    return pl.BlockSpec(memory_space=space)


def halves(value):
    high = value.astype(jnp.bfloat16)
    low = (value - high.astype(jnp.float32)).astype(jnp.bfloat16)
    return high, low


def dot_split(left, right, transposed=False):
    dims = (((1,), (1 if transposed else 0,)), ((), ()))
    mul = functools.partial(lax.dot_general, dimension_numbers=dims, preferred_element_type=jnp.float32)
    lh, ll = halves(left)
    rh, rl = halves(right)
    return mul(lh, rh) + (mul(lh, rl) + mul(ll, rh))


def swap_blocks(parts, block):
    parts = list(parts)
    count = len(parts)
    lane = lax.broadcasted_iota(jnp.int32, parts[0].shape, 1) // block
    step = count // 2
    while step:
        low = (lane & step) == 0
        for i in range(count):
            if i & step:
                continue
            a, b = parts[i], parts[i | step]
            parts[i] = jnp.where(low, a, pltpu.roll(b, step * block, 1))
            parts[i | step] = jnp.where(low, pltpu.roll(a, lanes - step * block, 1), b)
        step //= 2
    return parts


def pack_kernel(cols, comps, field, *refs):
    outs, scratch = refs[:cols], refs[cols]
    block = field.shape[1] // cols
    per = lanes // block
    depth = field.shape[0] // comps
    rows = depth // per
    me = lax.axis_index("col")
    for tile in range(cols // per):
        for comp in range(comps):
            parts = [
                field[comp * depth + q * rows : comp * depth + (q + 1) * rows, tile * lanes : (tile + 1) * lanes]
                for q in range(per)
            ]
            for p, part in enumerate(swap_blocks(parts, block)):
                scratch[lax.rem(tile * per + p + cols - me, cols), comp * rows : (comp + 1) * rows] = part
    for s in range(cols):
        outs[s][...] = scratch[s]


def span_kernel(cols, comps, matrix, *refs):
    chunks, outs = refs[:cols], refs[cols:]
    rows = chunks[0].shape[0] // comps
    pick = lambda comp: jnp.concatenate(
        [chunks[(cols - s) % cols][comp * rows : (comp + 1) * rows] for s in range(cols)], axis=0
    )
    values = [pick(comp) for comp in range(comps)]
    right = jnp.concatenate(
        [jnp.concatenate([value, values[2] * value], axis=0) for value in values], axis=1
    )
    result = dot_split(matrix[...], right)
    for t in range(cols):
        for comp in range(comps):
            outs[t][comp * rows : (comp + 1) * rows] = result[
                t * rows : (t + 1) * rows, comp * lanes : (comp + 1) * lanes
            ]


def circulant_rows(row, length):
    return pltpu.roll(jnp.broadcast_to(row, (length, length)), 0, 1, stride=1, stride_axis=0)


def stream_kernel(
    rows,
    cols,
    comps,
    slots,
    zloc,
    wall_counts,
    z_first,
    z_second,
    metric_table,
    metric_index,
    field,
    x_first,
    x_second,
    y_first,
    y_second,
    x_part,
    z_matrix,
    y_matrix,
    scaled,
):
    depth = slots * zloc
    length = field.shape[1]
    cells_z = cols * zloc
    cells_y = y_first.shape[0]
    group = z_matrix.shape[0] // cols
    shape = z_matrix.shape
    half = shape[1] // 2
    r = lax.broadcasted_iota(jnp.int32, shape, 0)
    q = lax.broadcasted_iota(jnp.int32, shape, 1)
    second = q < half
    q = jnp.where(second, q, q - half)
    out_cell = (r // group) * zloc + r % zloc
    in_cell = (q // group) * zloc + q % zloc
    same = (r % group) // zloc == (q % group) // zloc
    gap = jnp.where(same, (in_cell - out_cell + cells_z) % cells_z, -1)
    line = lax.broadcasted_iota(jnp.int32, (1, shape[1]), 1) < half

    def fill(k, total):
        value = jnp.where(line, viscosity * z_second[k], -z_first[k])
        return jnp.where(gap == k, value, total)

    z_matrix[...] = lax.fori_loop(0, cells_z, fill, jnp.zeros(shape, jnp.float32), unroll=8)

    u = field[...]
    lead = u[:depth]
    left = jnp.concatenate(
        [u, jnp.concatenate([lead * u[c * depth : (c + 1) * depth] for c in range(comps)], axis=0)], axis=1
    )
    right = jnp.concatenate(
        [viscosity * circulant_rows(x_second[...], length), -circulant_rows(x_first[...], length)], axis=1
    )
    x_part[...] = dot_split(left, right, transposed=True)

    def scale(j, carry):
        scaled[pl.ds(j, 1), :] = y_first[pl.ds(j, 1), :] * -metric_table[metric_index[j]]
        return carry

    lax.fori_loop(0, cells_y, scale, 0, unroll=8)
    me = lax.axis_index("row")

    def start_of(index):
        return lax.fori_loop(0, rows, lambda i, acc: acc + jnp.where(i < index, wall_counts[i], 0), 0, unroll=True)

    own = lax.broadcasted_iota(jnp.int32, (depth, cells_y), 0) // zloc
    cell = lax.broadcasted_iota(jnp.int32, (depth, cells_y), 1)
    mine = ((own < wall_counts[me]) & (own + start_of(me) == cell)).astype(jnp.float32)
    exact = functools.partial(
        lax.dot_general, precision=lax.Precision.HIGHEST, preferred_element_type=jnp.float32
    )
    plain = (((1,), (0,)), ((), ()))
    turned = (((1,), (1,)), ((), ()))
    pair = [exact(mine, viscosity * y_second[...], plain), exact(mine, scaled[...], plain)]
    r = lax.broadcasted_iota(jnp.int32, (depth, depth), 0) % zloc
    q = lax.broadcasted_iota(jnp.int32, (depth, depth), 1) % zloc
    match = r == q
    for s in range(rows):
        other = lax.rem(me + rows - s, rows)
        theirs = ((own < wall_counts[other]) & (own + start_of(other) == cell)).astype(jnp.float32)
        for k in range(2):
            block = jnp.where(match, exact(pair[k], theirs, turned), 0.0)
            y_matrix[:, (2 * s + k) * depth : (2 * s + k + 1) * depth] = block


def wall_kernel(rows, comps, matrix, x_part, *refs):
    fields, out = refs[:rows], refs[rows]
    depth = x_part.shape[0] // comps
    pieces = []
    for comp in range(comps):
        stack = []
        for field in fields:
            value = field[comp * depth : (comp + 1) * depth]
            stack += [value, field[depth : 2 * depth] * value]
        pieces.append(jnp.concatenate(stack, axis=0))
    for comp in range(comps):
        out[comp * depth : (comp + 1) * depth] = x_part[comp * depth : (comp + 1) * depth] + dot_split(
            matrix[...], pieces[comp]
        )


def finish_kernel(cols, comps, zloc, wall_counts, total, *refs):
    chunks, out, scratch = refs[:cols], refs[cols], refs[cols + 1]
    block = out.shape[1] // cols
    per = lanes // block
    depth = out.shape[0] // comps
    rows = depth // per
    me = lax.axis_index("col")
    count = wall_counts[lax.axis_index("row")]
    for t in range(cols):
        scratch[lax.rem(me + cols - t, cols)] = chunks[t][...]
    for tile in range(cols // per):
        for comp in range(comps):
            parts = [scratch[tile * per + p, comp * rows : (comp + 1) * rows] for p in range(per)]
            for q, part in enumerate(swap_blocks(parts, block)):
                at = slice(comp * depth + q * rows, comp * depth + (q + 1) * rows)
                across = slice(tile * lanes, (tile + 1) * lanes)
                plane = (lax.broadcasted_iota(jnp.int32, part.shape, 0) + q * rows) // zloc
                out[at, across] = jnp.where(plane < count, total[at, across] + part, 0.0)


def local(
    velocity,
    wall_counts,
    x_first,
    x_second,
    y_first,
    y_second,
    z_first,
    z_second,
    metric_table,
    metric_index,
):
    rows = lax.axis_size("row")
    cols = lax.axis_size("col")
    comps, slots, zloc, length = velocity.shape
    depth = slots * zloc
    field = velocity.reshape(comps * depth, length)
    block = length // cols
    group = depth // (lanes // block)
    chunk = jax.ShapeDtypeStruct((comps * group, lanes), jnp.float32)
    scratch = pltpu.VMEM((cols,) + chunk.shape, jnp.float32)
    whole = jax.ShapeDtypeStruct(field.shape, jnp.float32)

    def shift(value, axis, size, step):
        return lax.ppermute(value, axis, [(i, (i + step) % size) for i in range(size)])

    chunks = pl.pallas_call(
        functools.partial(pack_kernel, cols, comps),
        out_shape=[chunk] * cols,
        in_specs=[spec(VMEM)],
        out_specs=[spec(VMEM)] * cols,
        scratch_shapes=[scratch],
        name="pack",
    )(field)
    received = [chunks[0]] + [shift(chunks[s], "col", cols, s) for s in range(1, cols)]
    fields = [field] + [shift(field, "row", rows, s) for s in range(1, rows)]
    x_part, z_matrix, y_matrix = pl.pallas_call(
        functools.partial(stream_kernel, rows, cols, comps, slots, zloc),
        out_shape=[
            whole,
            jax.ShapeDtypeStruct((cols * group, 2 * cols * group), jnp.float32),
            jax.ShapeDtypeStruct((depth, 2 * rows * depth), jnp.float32),
        ],
        in_specs=[spec(SMEM)] * 5 + [spec(VMEM)] * 5,
        out_specs=[spec(VMEM)] * 3,
        scratch_shapes=[pltpu.VMEM(y_first.shape, jnp.float32)],
        name="stream",
    )(
        wall_counts,
        z_first,
        z_second,
        metric_table,
        metric_index,
        field,
        x_first.reshape(1, length),
        x_second.reshape(1, length),
        y_first,
        y_second,
    )
    parts = pl.pallas_call(
        functools.partial(span_kernel, cols, comps),
        out_shape=[chunk] * cols,
        in_specs=[spec(VMEM)] * (cols + 1),
        out_specs=[spec(VMEM)] * cols,
        name="span",
    )(z_matrix, *received)
    returned = [parts[0]] + [shift(parts[t], "col", cols, t) for t in range(1, cols)]
    total = pl.pallas_call(
        functools.partial(wall_kernel, rows, comps),
        out_shape=whole,
        in_specs=[spec(VMEM)] * (rows + 2),
        out_specs=spec(VMEM),
        name="wall",
    )(y_matrix, x_part, *fields)
    result = pl.pallas_call(
        functools.partial(finish_kernel, cols, comps, zloc),
        out_shape=whole,
        in_specs=[spec(SMEM)] + [spec(VMEM)] * (cols + 1),
        out_specs=spec(VMEM),
        scratch_shapes=[scratch],
        name="finish",
    )(wall_counts, total, *returned)
    return result.reshape(velocity.shape)


def solution(mesh):
    in_specs = (P(None, "row", "col", None), P(), P(), P(), P(), P(), P(), P(), P(), P())
    out_specs = P(None, "row", "col", None)
    return jax.shard_map(local, mesh=mesh, in_specs=in_specs, out_specs=out_specs, check_vma=False)
```

time: 63.4 us -> 48.8 us (0.77)
  local copies, waits for them, and re-layouts: 16.7 us -> 1.23 us
  Pallas kernels: 0 us -> 10.4 us
  other arithmetic: 4.63 us -> 0 us
  matrix products: 4.59 us -> 0 us
  starting transfers between devices: 17.4 us -> 19.5 us
  waiting for transfers between devices: 18.9 us -> 17.2 us
    ppermute x0 -> x17, starting transfers between devices: none -> 19.5 us  [shift(): lax.ppermute(value, axis, [(i, (i + step) % size) for i in range(size)])]
    all_to_all x4 -> x0, waiting for transfers between devices: 18.9 us -> none  [the longest x1 6.4 us: local(): lax.all_to_all(pack_span(normal, cols), 'col', split_axis=0, concat_axis=...]
    all_to_all x4 -> x0, starting transfers between devices: 17.4 us -> none  [the longest x1 6.31 us: local(): lax.all_to_all(pack_span(normal, cols), 'col', split_axis=0, concat_axis=...]
    ppermute x0 -> x17, waiting for transfers between devices: none -> 17.2 us  [shift(): lax.ppermute(value, axis, [(i, (i + step) % size) for i in range(size)])]
    pallas_call x0 -> x5, Pallas kernels: none -> 10.4 us  [the longest x1 2.94 us: local(): pl.pallas_call(functools.partial(stream_kernel, rows, cols, comps, slots,...]
    reshape x14 -> x0, local copies, waits for them, and re-layouts: 7 us -> none  [the longest x2 1.55 us: pack_normal(): return span.reshape(3, xloc, block, cols, zloc).transpose(3, 0, 4, 1, 2)....]
    transpose x6 -> x0, local copies, waits for them, and re-layouts: 5.98 us -> none  [the longest x1 2.19 us: pack_span(): return normal.reshape(3, zloc, xloc, cols, block).transpose(3, 0, 2, 4, 1...]
    dot_general x10 -> x0, matrix products: 4.59 us -> none  [the longest x3 1.85 us: tendency(): jnp.dot(field, second, precision=exact)]
  transfers between devices with their start and end apart: 4 -> 17, of which waited for: 4 -> 6; matrix products, arithmetic and copies ran while one was open for 7% -> 0% of each run, Pallas kernels for 0% -> 18%
where the time goes in v1:
time: 48.8 us; the launch traced here: 48.5 us
  starting transfers between devices  19.5 us (40%)
  waiting for transfers between devices  17.2 us (35%)
  Pallas kernels  10.4 us (21%)
  local copies, waits for them, and re-layouts  1.23 us (3%)
    ppermute x17, starting transfers between devices, shift(): lax.ppermute(value, axis, [(i, (i + step) % size) for i in range(size)])  19.5 us
    ppermute x17, waiting for transfers between devices, shift(): lax.ppermute(value, axis, [(i, (i + step) % size) for i in range(size)])  17.2 us
    pallas_call x1, Pallas kernels, local(): pl.pallas_call(functools.partial(stream_kernel, rows, cols, comps, slots,...  2.94 us
    pallas_call x1, Pallas kernels, local(): pl.pallas_call(functools.partial(wall_kernel, rows, comps), out_shape=who...  2.13 us
    pallas_call x1, Pallas kernels, local(): pl.pallas_call(functools.partial(finish_kernel, cols, comps, zloc), out_s...  1.88 us
    pallas_call x1, Pallas kernels, local(): pl.pallas_call(functools.partial(pack_kernel, cols, comps), out_shape=[ch...  1.78 us
    pallas_call x1, Pallas kernels, local(): pl.pallas_call(functools.partial(span_kernel, cols, comps), out_shape=[ch...  1.7 us
    unnamed x38, local copies, waits for them, and re-layouts  1.23 us
  transfers between devices with their start and end apart: 17, of which 6 were waited for; matrix products, arithmetic and copies ran while one was open for 0% of the time, Pallas kernels for 18%

profile of v1, /device:TPU:0, one launch (start us, length us, event | category | flops | bytes accessed | tf_op | source)
XLA Modules:
  0.0 48.5 jit_solution(8758229037662826644)
XLA Ops:
  0.5 2.5 %collective-permute-start.1 = (f32[192,128]{1,0:T(8,128)}, f32[192,128]{1,0:T(8,128)S(1)}, u32[]{:S(2)}, u32[]{:S(2)}) collective-permute-start(f32[192,128]{1,0:T(8,128)} %bitcast.5), channel_id=1, source_target_pairs={{0,16},{8,24},{16,0},{24,8},{1,17},{9,25},{17,1},{25,9},{2,18},{10... | collective-permute-start | bytes 294920 | tf_op jit(solution)/shard_map/ppermute | solution.py:237
  3.0 1.4 %collective-permute-start.2 = (f32[192,128]{1,0:T(8,128)}, f32[192,128]{1,0:T(8,128)S(1)}, u32[]{:S(2)}, u32[]{:S(2)}) collective-permute-start(f32[192,128]{1,0:T(8,128)} %bitcast.6), channel_id=1, source_target_pairs={{0,24},{8,0},{16,8},{24,16},{1,25},{9,1},{17,9},{25,17},{2,26},{10... | collective-permute-start | bytes 294920 | tf_op jit(solution)/shard_map/ppermute | solution.py:237
  4.4 1.8 %pack.1 = (f32[24,128]{1,0:T(8,128)}, f32[24,128]{1,0:T(8,128)}, f32[24,128]{1,0:T(8,128)}, f32[24,128]{1,0:T(8,128)}, f32[24,128]{1,0:T(8,128)}, /*index=5*/f32...) custom-call(f32[192,128]{1,0:T(8,128)} %bitcast.7), custom_call_target="tpu_custom_call" | custom-call | tf_op jit(solution)/shard_map/pack/pallas_call | solution.py:239
  6.2 1.5 %collective-permute-start.3 = (f32[24,128]{1,0:T(8,128)}, f32[24,128]{1,0:T(8,128)S(1)}, u32[]{:S(2)}, u32[]{:S(2)}) collective-permute-start(f32[24,128]{1,0:T(8,128)} %get-tuple-element.28), channel_id=1, source_target_pairs={{0,1},{1,2},{2,3},{3,4},{4,5},{5,6},{6,7},{7,0},{8,9},{9,10},{10,1... | collective-permute-start | bytes 36872 | tf_op jit(solution)/shard_map/ppermute | solution.py:237
  7.8 1.6 %collective-permute-start.4 = (f32[24,128]{1,0:T(8,128)}, f32[24,128]{1,0:T(8,128)S(1)}, u32[]{:S(2)}, u32[]{:S(2)}) collective-permute-start(f32[24,128]{1,0:T(8,128)} %get-tuple-element.29), channel_id=1, source_target_pairs={{0,2},{1,3},{2,4},{3,5},{4,6},{5,7},{6,0},{7,1},{8,10},{9,11},{10,... | collective-permute-start | bytes 36872 | tf_op jit(solution)/shard_map/ppermute | solution.py:237
  9.3 3.5 %collective-permute-done.3.refs_1_ = f32[24,128]{1,0:T(8,128)S(1)} collective-permute-done((f32[24,128]{1,0:T(8,128)}, f32[24,128]{1,0:T(8,128)S(1)}, u32[]{:S(2)}, u32[]{:S(2)}) %collective-permute-start.3) | collective-permute-done | bytes 12320 | tf_op jit(solution)/shard_map/ppermute | solution.py:237
  12.9 0.6 %collective-permute-done.4.refs_2_ = f32[24,128]{1,0:T(8,128)S(1)} collective-permute-done((f32[24,128]{1,0:T(8,128)}, f32[24,128]{1,0:T(8,128)S(1)}, u32[]{:S(2)}, u32[]{:S(2)}) %collective-permute-start.4) | collective-permute-done | bytes 12320 | tf_op jit(solution)/shard_map/ppermute | solution.py:237
  13.5 1.8 %collective-permute-start.6 = (f32[24,128]{1,0:T(8,128)}, f32[24,128]{1,0:T(8,128)S(1)}, u32[]{:S(2)}, u32[]{:S(2)}) collective-permute-start(f32[24,128]{1,0:T(8,128)} %get-tuple-element.31), channel_id=1, source_target_pairs={{0,4},{1,5},{2,6},{3,7},{4,0},{5,1},{6,2},{7,3},{8,12},{9,13},{10,... | collective-permute-start | bytes 36872 | tf_op jit(solution)/shard_map/ppermute | solution.py:237
  15.3 3.3 %collective-permute-done.5.refs_3_ = f32[24,128]{1,0:T(8,128)S(1)} collective-permute-done((f32[24,128]{1,0:T(8,128)}, f32[24,128]{1,0:T(8,128)S(1)}, u32[]{:S(2)}, u32[]{:S(2)}) %collective-permute-start.5) | collective-permute-done | bytes 12320 | tf_op jit(solution)/shard_map/ppermute | solution.py:237
  18.6 1.9 %collective-permute-start.8 = (f32[24,128]{1,0:T(8,128)}, f32[24,128]{1,0:T(8,128)S(1)}, u32[]{:S(2)}, u32[]{:S(2)}) collective-permute-start(f32[24,128]{1,0:T(8,128)} %get-tuple-element.33), channel_id=1, source_target_pairs={{0,6},{1,7},{2,0},{3,1},{4,2},{5,3},{6,4},{7,5},{8,14},{9,15},{10,... | collective-permute-start | bytes 36872 | tf_op jit(solution)/shard_map/ppermute | solution.py:237
  20.5 2.9 %collective-permute-done.7.refs_5_ = f32[24,128]{1,0:T(8,128)S(1)} collective-permute-done((f32[24,128]{1,0:T(8,128)}, f32[24,128]{1,0:T(8,128)S(1)}, u32[]{:S(2)}, u32[]{:S(2)}) %collective-permute-start.7) | collective-permute-done | bytes 12320 | tf_op jit(solution)/shard_map/ppermute | solution.py:237
  23.4 1.9 %collective-permute-start.9 = (f32[24,128]{1,0:T(8,128)S(1)}, f32[24,128]{1,0:T(8,128)S(1)}, u32[]{:S(2)}, u32[]{:S(2)}) collective-permute-start(f32[24,128]{1,0:T(8,128)S(1)} %copy-done.18), channel_id=1, source_target_pairs={{0,7},{1,0},{2,1},{3,2},{4,3},{5,4},{6,5},{7,6},{8,15},{9,8},{10,9... | collective-permute-start | bytes 36872 | tf_op jit(solution)/shard_map/ppermute | solution.py:237
  25.3 2.9 %stream.1 = (f32[192,128]{1,0:T(8,128)}, f32[64,128]{1,0:T(8,128)}, f32[64,512]{1,0:T(8,128)}) custom-call(s32[4]{0:T(128)} %wall_counts.3, f32[32]{0:T(128)} %z_first.1, f32[32]{0:T(128)} %z_second.1, f32[64]{0:T(128)} %metric_table.1, s32[32]{0:T(128)} %metric_index.1, f32[192,128]{1,0:T(8,128)} %bitcast.8, f32[1,128]{1,0:T(1,128)} %bitcast.10, ...), custom_call_target="tpu_custom_call" | custom-call | tf_op jit(solution)/shard_map/stream/pallas_call | solution.py:249
  28.3 0.6 %copy-done.15 = f32[24,128]{1,0:T(8,128)} copy-done((f32[24,128]{1,0:T(8,128)}, f32[24,128]{1,0:T(8,128)S(1)}, u32[]{:S(2)}) %copy-start.15) | copy-done | bytes 12312
  28.9 1.7 %span.1 = (f32[24,128]{1,0:T(8,128)}, f32[24,128]{1,0:T(8,128)}, f32[24,128]{1,0:T(8,128)}, f32[24,128]{1,0:T(8,128)}, f32[24,128]{1,0:T(8,128)}, /*index=5*/f32...) custom-call(f32[64,128]{1,0:T(8,128)} %get-tuple-element.26.matrix, f32[24,128]{1,0:T(8,128)} %get-tuple-element.27.refs_0_, ...), custom_call_target="tpu_custom_call" | custom-call | tf_op jit(solution)/shard_map/span/pallas_call | solution.py:272
  31.3 6.0 %collective-permute-done.10.refs_1_ = f32[24,128]{1,0:T(8,128)S(1)} collective-permute-done((f32[24,128]{1,0:T(8,128)}, f32[24,128]{1,0:T(8,128)S(1)}, u32[]{:S(2)}, u32[]{:S(2)}) %collective-permute-start.10) | collective-permute-done | bytes 12320 | tf_op jit(solution)/shard_map/ppermute | solution.py:237
  37.3 1.2 %collective-permute-start.13 = (f32[24,128]{1,0:T(8,128)}, f32[24,128]{1,0:T(8,128)S(1)}, u32[]{:S(2)}, u32[]{:S(2)}) collective-permute-start(f32[24,128]{1,0:T(8,128)} %get-tuple-element.39), channel_id=1, source_target_pairs={{0,4},{1,5},{2,6},{3,7},{4,0},{5,1},{6,2},{7,3},{8,12},{9,13},{10,... | collective-permute-start | bytes 36872 | tf_op jit(solution)/shard_map/ppermute | solution.py:237
  38.5 2.6 %collective-permute-start.14 = (f32[24,128]{1,0:T(8,128)}, f32[24,128]{1,0:T(8,128)S(1)}, u32[]{:S(2)}, u32[]{:S(2)}) collective-permute-start(f32[24,128]{1,0:T(8,128)} %get-tuple-element.40), channel_id=1, source_target_pairs={{0,5},{1,6},{2,7},{3,0},{4,1},{5,2},{6,3},{7,4},{8,13},{9,14},{10,... | collective-permute-start | bytes 36872 | tf_op jit(solution)/shard_map/ppermute | solution.py:237
  41.2 1.0 %collective-permute-start.15 = (f32[24,128]{1,0:T(8,128)}, f32[24,128]{1,0:T(8,128)S(1)}, u32[]{:S(2)}, u32[]{:S(2)}) collective-permute-start(f32[24,128]{1,0:T(8,128)} %get-tuple-element.41), channel_id=1, source_target_pairs={{0,6},{1,7},{2,0},{3,1},{4,2},{5,3},{6,4},{7,5},{8,14},{9,15},{10,... | collective-permute-start | bytes 36872 | tf_op jit(solution)/shard_map/ppermute | solution.py:237
  42.2 0.7 %collective-permute-start.16 = (f32[24,128]{1,0:T(8,128)S(1)}, f32[24,128]{1,0:T(8,128)S(1)}, u32[]{:S(2)}, u32[]{:S(2)}) collective-permute-start(f32[24,128]{1,0:T(8,128)S(1)} %copy-done.17), channel_id=1, source_target_pairs={{0,7},{1,0},{2,1},{3,2},{4,3},{5,4},{6,5},{7,6},{8,15},{9,8},{10,9... | collective-permute-start | bytes 36872 | tf_op jit(solution)/shard_map/ppermute | solution.py:237
  43.0 2.1 %wall.1.total = f32[192,128]{1,0:T(8,128)} custom-call(f32[64,512]{1,0:T(8,128)} %get-tuple-element.24.matrix, f32[192,128]{1,0:T(8,128)} %get-tuple-element.25.x_part, f32[192,128]{1,0:T(8,128)} %bitcast.9, f32[192,128]{1,0:T(8,128)} %copy-done, f32[192,128]{1,0:T(8,128)} %copy-done.1, f32[192,128]{1,0:T(8,128)} %copy-done.2), custom_call_target="tpu_custom_call" | custom-call | tf_op jit(solution)/shard_map/wall/pallas_call | solution.py:280
  45.2 0.8 %collective-permute-done.16.refs_7_ = f32[24,128]{1,0:T(8,128)S(1)} collective-permute-done((f32[24,128]{1,0:T(8,128)S(1)}, f32[24,128]{1,0:T(8,128)S(1)}, u32[]{:S(2)}, u32[]{:S(2)}) %collective-permute-start.16) | collective-permute-done | bytes 12320 | tf_op jit(solution)/shard_map/ppermute | solution.py:237
  46.0 0.6 %copy-done.9 = f32[24,128]{1,0:T(8,128)} copy-done((f32[24,128]{1,0:T(8,128)}, f32[24,128]{1,0:T(8,128)S(1)}, u32[]{:S(2)}) %copy-start.9) | copy-done | bytes 12312
  46.6 1.9 %finish.1 = f32[192,128]{1,0:T(8,128)} custom-call(s32[4]{0:T(128)} %wall_counts.3, f32[192,128]{1,0:T(8,128)} %wall.1.total, f32[24,128]{1,0:T(8,128)} %get-tuple-element.35.refs_0_, f32[24,128]{1,0:T(8,128)} %copy-done.3, f32[24,128]{1,0:T(8,128)} %copy-done.4, f32[24,128]{1,0:T(8,128)} %copy-done.5, f32[24,128]{1,0:T(8,128)} %copy-done.6, ...), custom_call_target="tpu_custom_call" | custom-call | tf_op jit(solution)/shard_map/finish/pallas_call | solution.py:287
  (53 shorter events, 1.2 us)
Async XLA Ops:
  0.0 38.5 %collective-permute-start = (f32[192,128]{1,0:T(8,128)}, f32[192,128]{1,0:T(8,128)S(1)}, u32[]{:S(2)}, u32[]{:S(2)}) collective-permute-start(f32[192,128]{1,0:T(8,128)} %bitcast.4), channel_id=1, source_target_pairs={{0,8},{8,16},{16,24},{24,0},{1,9},{9,17},{17,25},{25,1},{2,10},{10... | collective-permute-start | bytes 294920 | tf_op jit(solution)/shard_map/ppermute | solution.py:237
  0.5 40.7 %collective-permute-start.1 = (f32[192,128]{1,0:T(8,128)}, f32[192,128]{1,0:T(8,128)S(1)}, u32[]{:S(2)}, u32[]{:S(2)}) collective-permute-start(f32[192,128]{1,0:T(8,128)} %bitcast.5), channel_id=1, source_target_pairs={{0,16},{8,24},{16,0},{24,8},{1,17},{9,25},{17,1},{25,9},{2,18},{10... | collective-permute-start | bytes 294920 | tf_op jit(solution)/shard_map/ppermute | solution.py:237
  3.0 39.2 %collective-permute-start.2 = (f32[192,128]{1,0:T(8,128)}, f32[192,128]{1,0:T(8,128)S(1)}, u32[]{:S(2)}, u32[]{:S(2)}) collective-permute-start(f32[192,128]{1,0:T(8,128)} %bitcast.6), channel_id=1, source_target_pairs={{0,24},{8,0},{16,8},{24,16},{1,25},{9,1},{17,9},{25,17},{2,26},{10... | collective-permute-start | bytes 294920 | tf_op jit(solution)/shard_map/ppermute | solution.py:237
  6.2 17.2 %copy-start.18 = (f32[24,128]{1,0:T(8,128)S(1)}, f32[24,128]{1,0:T(8,128)}, u32[]{:S(2)}) copy-start(f32[24,128]{1,0:T(8,128)} %get-tuple-element.34) | copy-start | bytes 36868
  6.2 6.6 %collective-permute-start.3 = (f32[24,128]{1,0:T(8,128)}, f32[24,128]{1,0:T(8,128)S(1)}, u32[]{:S(2)}, u32[]{:S(2)}) collective-permute-start(f32[24,128]{1,0:T(8,128)} %get-tuple-element.28), channel_id=1, source_target_pairs={{0,1},{1,2},{2,3},{3,4},{4,5},{5,6},{6,7},{7,0},{8,9},{9,10},{10,1... | collective-permute-start | bytes 36872 | tf_op jit(solution)/shard_map/ppermute | solution.py:237
  7.8 5.7 %collective-permute-start.4 = (f32[24,128]{1,0:T(8,128)}, f32[24,128]{1,0:T(8,128)S(1)}, u32[]{:S(2)}, u32[]{:S(2)}) collective-permute-start(f32[24,128]{1,0:T(8,128)} %get-tuple-element.29), channel_id=1, source_target_pairs={{0,2},{1,3},{2,4},{3,5},{4,6},{5,7},{6,0},{7,1},{8,10},{9,11},{10,... | collective-permute-start | bytes 36872 | tf_op jit(solution)/shard_map/ppermute | solution.py:237
  12.9 15.4 %copy-start.10 = (f32[24,128]{1,0:T(8,128)}, f32[24,128]{1,0:T(8,128)S(1)}, u32[]{:S(2)}) copy-start(f32[24,128]{1,0:T(8,128)S(1)} %collective-permute-done.3.refs_1_) | copy-start | bytes 36868
  12.9 5.7 %collective-permute-start.5 = (f32[24,128]{1,0:T(8,128)}, f32[24,128]{1,0:T(8,128)S(1)}, u32[]{:S(2)}, u32[]{:S(2)}) collective-permute-start(f32[24,128]{1,0:T(8,128)} %get-tuple-element.30), channel_id=1, source_target_pairs={{0,3},{1,4},{2,5},{3,6},{4,7},{5,0},{6,1},{7,2},{8,11},{9,12},{10,... | collective-permute-start | bytes 36872 | tf_op jit(solution)/shard_map/ppermute | solution.py:237
  13.5 14.8 %copy-start.11 = (f32[24,128]{1,0:T(8,128)}, f32[24,128]{1,0:T(8,128)S(1)}, u32[]{:S(2)}) copy-start(f32[24,128]{1,0:T(8,128)S(1)} %collective-permute-done.4.refs_2_) | copy-start | bytes 36868
  13.5 5.1 %collective-permute-start.6 = (f32[24,128]{1,0:T(8,128)}, f32[24,128]{1,0:T(8,128)S(1)}, u32[]{:S(2)}, u32[]{:S(2)}) collective-permute-start(f32[24,128]{1,0:T(8,128)} %get-tuple-element.31), channel_id=1, source_target_pairs={{0,4},{1,5},{2,6},{3,7},{4,0},{5,1},{6,2},{7,3},{8,12},{9,13},{10,... | collective-permute-start | bytes 36872 | tf_op jit(solution)/shard_map/ppermute | solution.py:237
  18.6 9.7 %copy-start.12 = (f32[24,128]{1,0:T(8,128)}, f32[24,128]{1,0:T(8,128)S(1)}, u32[]{:S(2)}) copy-start(f32[24,128]{1,0:T(8,128)S(1)} %collective-permute-done.5.refs_3_) | copy-start | bytes 36868
  18.6 4.8 %collective-permute-start.7 = (f32[24,128]{1,0:T(8,128)}, f32[24,128]{1,0:T(8,128)S(1)}, u32[]{:S(2)}, u32[]{:S(2)}) collective-permute-start(f32[24,128]{1,0:T(8,128)} %get-tuple-element.32), channel_id=1, source_target_pairs={{0,5},{1,6},{2,7},{3,0},{4,1},{5,2},{6,3},{7,4},{8,13},{9,14},{10,... | collective-permute-start | bytes 36872 | tf_op jit(solution)/shard_map/ppermute | solution.py:237
  18.6 9.7 %copy-start.13 = (f32[24,128]{1,0:T(8,128)}, f32[24,128]{1,0:T(8,128)S(1)}, u32[]{:S(2)}) copy-start(f32[24,128]{1,0:T(8,128)S(1)} %collective-permute-done.6.refs_4_) | copy-start | bytes 36868
  18.6 9.7 %collective-permute-start.8 = (f32[24,128]{1,0:T(8,128)}, f32[24,128]{1,0:T(8,128)S(1)}, u32[]{:S(2)}, u32[]{:S(2)}) collective-permute-start(f32[24,128]{1,0:T(8,128)} %get-tuple-element.33), channel_id=1, source_target_pairs={{0,6},{1,7},{2,0},{3,1},{4,2},{5,3},{6,4},{7,5},{8,14},{9,15},{10,... | collective-permute-start | bytes 36872 | tf_op jit(solution)/shard_map/ppermute | solution.py:237
  23.4 4.9 %collective-permute-start.9 = (f32[24,128]{1,0:T(8,128)S(1)}, f32[24,128]{1,0:T(8,128)S(1)}, u32[]{:S(2)}, u32[]{:S(2)}) collective-permute-start(f32[24,128]{1,0:T(8,128)S(1)} %copy-done.18), channel_id=1, source_target_pairs={{0,7},{1,0},{2,1},{3,2},{4,3},{5,4},{6,5},{7,6},{8,15},{9,8},{10,9... | collective-permute-start | bytes 36872 | tf_op jit(solution)/shard_map/ppermute | solution.py:237
  30.6 11.6 %copy-start.17 = (f32[24,128]{1,0:T(8,128)S(1)}, f32[24,128]{1,0:T(8,128)}, u32[]{:S(2)}) copy-start(f32[24,128]{1,0:T(8,128)} %get-tuple-element.42) | copy-start | bytes 36868
  30.6 6.6 %collective-permute-start.10 = (f32[24,128]{1,0:T(8,128)}, f32[24,128]{1,0:T(8,128)S(1)}, u32[]{:S(2)}, u32[]{:S(2)}) collective-permute-start(f32[24,128]{1,0:T(8,128)} %get-tuple-element.36), channel_id=1, source_target_pairs={{0,1},{1,2},{2,3},{3,4},{4,5},{5,6},{6,7},{7,0},{8,9},{9,10},{10,1... | collective-permute-start | bytes 36872 | tf_op jit(solution)/shard_map/ppermute | solution.py:237
  30.9 6.4 %collective-permute-start.11 = (f32[24,128]{1,0:T(8,128)}, f32[24,128]{1,0:T(8,128)S(1)}, u32[]{:S(2)}, u32[]{:S(2)}) collective-permute-start(f32[24,128]{1,0:T(8,128)} %get-tuple-element.37), channel_id=1, source_target_pairs={{0,2},{1,3},{2,4},{3,5},{4,6},{5,7},{6,0},{7,1},{8,10},{9,11},{10,... | collective-permute-start | bytes 36872 | tf_op jit(solution)/shard_map/ppermute | solution.py:237
  37.3 7.9 %copy-start.3 = (f32[24,128]{1,0:T(8,128)}, f32[24,128]{1,0:T(8,128)S(1)}, u32[]{:S(2)}) copy-start(f32[24,128]{1,0:T(8,128)S(1)} %collective-permute-done.10.refs_1_) | copy-start | bytes 36868
  37.3 7.9 %collective-permute-start.12 = (f32[24,128]{1,0:T(8,128)}, f32[24,128]{1,0:T(8,128)S(1)}, u32[]{:S(2)}, u32[]{:S(2)}) collective-permute-start(f32[24,128]{1,0:T(8,128)} %get-tuple-element.38), channel_id=1, source_target_pairs={{0,3},{1,4},{2,5},{3,6},{4,7},{5,0},{6,1},{7,2},{8,11},{9,12},{10,... | collective-permute-start | bytes 36872 | tf_op jit(solution)/shard_map/ppermute | solution.py:237
  37.3 7.9 %collective-permute-start.13 = (f32[24,128]{1,0:T(8,128)}, f32[24,128]{1,0:T(8,128)S(1)}, u32[]{:S(2)}, u32[]{:S(2)}) collective-permute-start(f32[24,128]{1,0:T(8,128)} %get-tuple-element.39), channel_id=1, source_target_pairs={{0,4},{1,5},{2,6},{3,7},{4,0},{5,1},{6,2},{7,3},{8,12},{9,13},{10,... | collective-permute-start | bytes 36872 | tf_op jit(solution)/shard_map/ppermute | solution.py:237
  38.5 6.6 %collective-permute-start.14 = (f32[24,128]{1,0:T(8,128)}, f32[24,128]{1,0:T(8,128)S(1)}, u32[]{:S(2)}, u32[]{:S(2)}) collective-permute-start(f32[24,128]{1,0:T(8,128)} %get-tuple-element.40), channel_id=1, source_target_pairs={{0,5},{1,6},{2,7},{3,0},{4,1},{5,2},{6,3},{7,4},{8,13},{9,14},{10,... | collective-permute-start | bytes 36872 | tf_op jit(solution)/shard_map/ppermute | solution.py:237
  41.2 4.0 %collective-permute-start.15 = (f32[24,128]{1,0:T(8,128)}, f32[24,128]{1,0:T(8,128)S(1)}, u32[]{:S(2)}, u32[]{:S(2)}) collective-permute-start(f32[24,128]{1,0:T(8,128)} %get-tuple-element.41), channel_id=1, source_target_pairs={{0,6},{1,7},{2,0},{3,1},{4,2},{5,3},{6,4},{7,5},{8,14},{9,15},{10,... | collective-permute-start | bytes 36872 | tf_op jit(solution)/shard_map/ppermute | solution.py:237
  42.2 3.7 %collective-permute-start.16 = (f32[24,128]{1,0:T(8,128)S(1)}, f32[24,128]{1,0:T(8,128)S(1)}, u32[]{:S(2)}, u32[]{:S(2)}) collective-permute-start(f32[24,128]{1,0:T(8,128)S(1)} %copy-done.17), channel_id=1, source_target_pairs={{0,7},{1,0},{2,1},{3,2},{4,3},{5,4},{6,5},{7,6},{8,15},{9,8},{10,9... | collective-permute-start | bytes 36872 | tf_op jit(solution)/shard_map/ppermute | solution.py:237
  (12 other events, 24.9 us)

commit v2 on v1

v2 whole, which is shorter than its diff:
```python
import functools

import jax
import jax.numpy as jnp
from jax import lax
from jax.experimental import pallas as pl
from jax.experimental.pallas import tpu as pltpu
from jax.sharding import PartitionSpec as P

viscosity = 0.4
lanes = 128

VMEM = pltpu.VMEM
SMEM = pltpu.SMEM


def spec(space):
    return pl.BlockSpec(memory_space=space)


def halves(value):
    high = value.astype(jnp.bfloat16)
    low = (value - high.astype(jnp.float32)).astype(jnp.bfloat16)
    return high, low


def dot_split(left, right, transposed=False):
    dims = (((1,), (1 if transposed else 0,)), ((), ()))
    mul = functools.partial(lax.dot_general, dimension_numbers=dims, preferred_element_type=jnp.float32)
    lh, ll = halves(left)
    rh, rl = halves(right)
    return mul(lh, rh) + (mul(lh, rl) + mul(ll, rh))


def circulant_rows(row, length):
    return pltpu.roll(jnp.broadcast_to(row, (length, length)), 0, 1, stride=1, stride_axis=0)


def stream_kernel(
    rows,
    cols,
    comps,
    slots,
    zloc,
    wall_counts,
    z_first,
    z_second,
    metric_table,
    metric_index,
    field,
    x_first,
    x_second,
    y_first,
    y_second,
    x_part,
    z_matrix,
    y_matrix,
    scaled,
):
    depth = slots * zloc
    length = field.shape[1]
    cells_z = cols * zloc
    cells_y = y_first.shape[0]
    group = z_matrix.shape[0]
    first_cell = lax.axis_index("col") * zloc
    shape = z_matrix.shape
    half = shape[1] // 2
    r = lax.broadcasted_iota(jnp.int32, shape, 0)
    q = lax.broadcasted_iota(jnp.int32, shape, 1)
    second = q < half
    q = jnp.where(second, q, q - half)
    out_cell = first_cell + r % zloc
    in_cell = (q // group) * zloc + q % zloc
    same = r // zloc == (q % group) // zloc
    gap = jnp.where(same, (in_cell - out_cell + cells_z) % cells_z, -1)
    line = lax.broadcasted_iota(jnp.int32, (1, shape[1]), 1) < half

    def fill(k, total):
        value = jnp.where(line, viscosity * z_second[k], -z_first[k])
        return jnp.where(gap == k, value, total)

    z_matrix[...] = lax.fori_loop(0, cells_z, fill, jnp.zeros(shape, jnp.float32), unroll=8)

    u = field[...]
    lead = u[:depth]
    left = jnp.concatenate(
        [u, jnp.concatenate([lead * u[c * depth : (c + 1) * depth] for c in range(comps)], axis=0)], axis=1
    )
    right = jnp.concatenate(
        [viscosity * circulant_rows(x_second[...], length), -circulant_rows(x_first[...], length)], axis=1
    )
    x_part[...] = dot_split(left, right, transposed=True)

    def scale(j, carry):
        scaled[pl.ds(j, 1), :] = y_first[pl.ds(j, 1), :] * -metric_table[metric_index[j]]
        return carry

    lax.fori_loop(0, cells_y, scale, 0, unroll=8)
    me = lax.axis_index("row")

    def start_of(index):
        return lax.fori_loop(0, rows, lambda i, acc: acc + jnp.where(i < index, wall_counts[i], 0), 0, unroll=True)

    own = lax.broadcasted_iota(jnp.int32, (depth, cells_y), 0) // zloc
    cell = lax.broadcasted_iota(jnp.int32, (depth, cells_y), 1)
    mine = ((own < wall_counts[me]) & (own + start_of(me) == cell)).astype(jnp.float32)
    exact = functools.partial(
        lax.dot_general, precision=lax.Precision.HIGHEST, preferred_element_type=jnp.float32
    )
    plain = (((1,), (0,)), ((), ()))
    turned = (((1,), (1,)), ((), ()))
    pair = [exact(mine, viscosity * y_second[...], plain), exact(mine, scaled[...], plain)]
    r = lax.broadcasted_iota(jnp.int32, (depth, depth), 0) % zloc
    q = lax.broadcasted_iota(jnp.int32, (depth, depth), 1) % zloc
    match = r == q
    for s in range(rows):
        theirs = ((own < wall_counts[s]) & (own + start_of(s) == cell)).astype(jnp.float32)
        for k in range(2):
            block = jnp.where(match, exact(pair[k], theirs, turned), 0.0)
            y_matrix[:, (2 * s + k) * depth : (2 * s + k + 1) * depth] = block


def join_kernel(comps, zloc, counts, z_matrix, y_matrix, x_part, row_fields, col_fields, out):
    rows, cols = row_fields.shape[0], col_fields.shape[0]
    depth = x_part.shape[0] // comps
    group = z_matrix.shape[0]
    count = counts[lax.axis_index("row")]
    length = x_part.shape[1]
    groups = depth // group
    for comp in range(comps):
        stack = []
        for r in range(rows):
            value = row_fields[r, comp * depth : (comp + 1) * depth]
            stack += [value, row_fields[r, depth : 2 * depth] * value]
        part = dot_split(y_matrix[...], jnp.concatenate(stack, axis=0))
        right = []
        for g in range(groups):
            at = comp * depth + g * group
            carry = (comps - 1) * depth + g * group
            value = jnp.concatenate([col_fields[p, at : at + group] for p in range(cols)], axis=0)
            lead = jnp.concatenate([col_fields[p, carry : carry + group] for p in range(cols)], axis=0)
            right.append(jnp.concatenate([value, lead * value], axis=0))
        wide = dot_split(z_matrix[...], jnp.concatenate(right, axis=1))
        span = jnp.concatenate([wide[:, g * length : (g + 1) * length] for g in range(groups)], axis=0)
        total = x_part[comp * depth : (comp + 1) * depth] + part + span
        plane = lax.broadcasted_iota(jnp.int32, total.shape, 0) // zloc
        out[comp * depth : (comp + 1) * depth] = jnp.where(plane < count, total, 0.0)


def local(
    velocity,
    wall_counts,
    x_first,
    x_second,
    y_first,
    y_second,
    z_first,
    z_second,
    metric_table,
    metric_index,
):
    rows = lax.axis_size("row")
    cols = lax.axis_size("col")
    comps, slots, zloc, length = velocity.shape
    depth = slots * zloc
    field = velocity.reshape(comps * depth, length)
    group = 8
    whole = jax.ShapeDtypeStruct(field.shape, jnp.float32)
    col_fields = lax.all_gather(field, "col")
    row_fields = lax.all_gather(field, "row")
    x_part, z_matrix, y_matrix = pl.pallas_call(
        functools.partial(stream_kernel, rows, cols, comps, slots, zloc),
        out_shape=[
            whole,
            jax.ShapeDtypeStruct((group, 2 * cols * group), jnp.float32),
            jax.ShapeDtypeStruct((depth, 2 * rows * depth), jnp.float32),
        ],
        in_specs=[spec(SMEM)] * 5 + [spec(VMEM)] * 5,
        out_specs=[spec(VMEM)] * 3,
        scratch_shapes=[pltpu.VMEM(y_first.shape, jnp.float32)],
        name="stream",
    )(
        wall_counts,
        z_first,
        z_second,
        metric_table,
        metric_index,
        field,
        x_first.reshape(1, length),
        x_second.reshape(1, length),
        y_first,
        y_second,
    )
    result = pl.pallas_call(
        functools.partial(join_kernel, comps, zloc),
        out_shape=whole,
        in_specs=[spec(SMEM)] + [spec(VMEM)] * 5,
        out_specs=spec(VMEM),
        name="join",
    )(wall_counts, z_matrix, y_matrix, x_part, row_fields, col_fields)
    return result.reshape(velocity.shape)


def solution(mesh):
    in_specs = (P(None, "row", "col", None), P(), P(), P(), P(), P(), P(), P(), P(), P())
    out_specs = P(None, "row", "col", None)
    return jax.shard_map(local, mesh=mesh, in_specs=in_specs, out_specs=out_specs, check_vma=False)
```

time: 48.8 us -> 48.4 us (level)
  blocking collectives: 0 us -> 42.5 us
  starting transfers between devices: 19.5 us -> 0 us
  waiting for transfers between devices: 17.2 us -> 0 us
  Pallas kernels: 10.4 us -> 5.67 us
  local copies, waits for them, and re-layouts: 1.23 us -> 0.01 us
    all_gather x0 -> x2, blocking collectives: none -> 42.5 us  [the longest x1 34.1 us: local(): col_fields = lax.all_gather(field, 'col')]
    ppermute x17 -> x0, starting transfers between devices: 19.5 us -> none  [shift(): lax.ppermute(value, axis, [(i, (i + step) % size) for i in range(size)])]
    ppermute x17 -> x0, waiting for transfers between devices: 17.2 us -> none  [shift(): lax.ppermute(value, axis, [(i, (i + step) % size) for i in range(size)])]
    pallas_call x4 -> x1, Pallas kernels: 7.5 us -> 2.74 us  [local(): pl.pallas_call(functools.partial(join_kernel, comps, zloc), out_shape=who...]
    unnamed x38 -> x2, local copies, waits for them, and re-layouts: 1.23 us -> 0.01 us
  transfers between devices with their start and end apart: 17 -> 0, of which waited for: 6 -> 0; matrix products, arithmetic and copies ran while one was open for 0% -> 0% of each run, Pallas kernels for 18% -> 0%
where the time goes in v2:
time: 48.4 us; the launch traced here: 48.2 us
  blocking collectives  42.5 us (88%)
  Pallas kernels  5.67 us (12%)
    all_gather x1, blocking collectives, local(): col_fields = lax.all_gather(field, 'col')  34.1 us
    all_gather x1, blocking collectives, local(): row_fields = lax.all_gather(field, 'row')  8.37 us
    pallas_call x1, Pallas kernels, local(): pl.pallas_call(functools.partial(stream_kernel, rows, cols, comps, slots,...  2.93 us
    pallas_call x1, Pallas kernels, local(): pl.pallas_call(functools.partial(join_kernel, comps, zloc), out_shape=who...  2.74 us

profile of v2, /device:TPU:0, one launch (start us, length us, event | category | flops | bytes accessed | tf_op | source)
XLA Modules:
  0.0 48.2 jit_solution(1464474594568819326)
XLA Ops:
  0.0 0.0 copy-start
  0.0 2.9 %stream.1 = (f32[192,128]{1,0:T(8,128)}, f32[8,128]{1,0:T(8,128)}, f32[64,512]{1,0:T(8,128)}) custom-call(s32[4]{0:T(128)} %counts.1, f32[32]{0:T(128)} %z_first.1, f32[32]{0:T(128)} %z_second.1, f32[64]{0:T(128)} %metric_table.1, s32[32]{0:T(128)} %metric_index.1, f32[192,128]{1,0:T(8,128)} %bitcast.5, f32[1,128]{1,0:T(1,128)} %bitcast.8, ...), custom_call_target="tpu_custom_call" | custom-call | tf_op jit(solution)/shard_map/stream/pallas_call | solution.py:171
  2.9 0.0 copy-done
  2.9 8.4 %all_gather.6.row_fields = f32[4,192,128]{2,1,0:T(8,128)} all-gather(f32[1,192,128]{2,1,0:T(8,128)S(1)} %bitcast.6), channel_id=1, replica_groups=mesh['row'=4,'col'=8] {'row'}, dimensions={0}, use_global_device_ids=true | all-gather | bytes 491520 | tf_op jit(solution)/shard_map/all_gather | solution.py:170
  11.3 34.1 %all_gather.7.col_fields = f32[8,192,128]{2,1,0:T(8,128)} all-gather(f32[1,192,128]{2,1,0:T(8,128)S(1)} %bitcast.7), channel_id=1, replica_groups=mesh['row'=4,'col'=8] {'col'}, dimensions={0}, use_global_device_ids=true | all-gather | bytes 884736 | tf_op jit(solution)/shard_map/all_gather | solution.py:169
  45.4 2.7 %join.1 = f32[192,128]{1,0:T(8,128)} custom-call(s32[4]{0:T(128)} %counts.1, f32[8,128]{1,0:T(8,128)} %get-tuple-element.8.z_matrix, f32[64,512]{1,0:T(8,128)} %get-tuple-element.9.y_matrix, f32[192,128]{1,0:T(8,128)} %get-tuple-element.10.x_part, f32[4,192,128]{2,1,0:T(8,128)} %all_gather.6.row_fields, f32[8,192,128]{2,1,0:T(8,128)} %all_gather.7.col_fields), custom_call_target="tpu_custom_call" | custom-call | tf_op jit(solution)/shard_map/join/pallas_call | solution.py:194
Async XLA Ops:
  0.0 2.9 %copy-start = (f32[3,16,4,128]{3,2,1,0:T(4,128)S(1)}, f32[3,16,4,128]{3,2,1,0:T(4,128)}, u32[]{:S(2)}) copy-start(f32[3,16,4,128]{3,2,1,0:T(4,128)} %param.10) | copy-start | bytes 294916

commit v3 on v1

--- a/solution.py
+++ b/solution.py
@@ -49,13 +49,12 @@
     return parts
 
 
-def pack_kernel(cols, comps, field, *refs):
-    outs, scratch = refs[:cols], refs[cols]
+def pack_kernel(comps, field, out):
+    cols = out.shape[0]
     block = field.shape[1] // cols
     per = lanes // block
     depth = field.shape[0] // comps
     rows = depth // per
-    me = lax.axis_index("col")
     for tile in range(cols // per):
         for comp in range(comps):
             parts = [
@@ -63,26 +62,24 @@
                 for q in range(per)
             ]
             for p, part in enumerate(swap_blocks(parts, block)):
-                scratch[lax.rem(tile * per + p + cols - me, cols), comp * rows : (comp + 1) * rows] = part
-    for s in range(cols):
-        outs[s][...] = scratch[s]
-
-
-def span_kernel(cols, comps, matrix, *refs):
-    chunks, outs = refs[:cols], refs[cols:]
-    rows = chunks[0].shape[0] // comps
-    pick = lambda comp: jnp.concatenate(
-        [chunks[(cols - s) % cols][comp * rows : (comp + 1) * rows] for s in range(cols)], axis=0
-    )
-    values = [pick(comp) for comp in range(comps)]
+                out[tile * per + p, comp * rows : (comp + 1) * rows] = part
+
+
+def span_kernel(comps, matrix, chunks, out):
+    cols = out.shape[0]
+    rows = out.shape[1] // comps
+    values = [
+        jnp.concatenate([chunks[p, comp * rows : (comp + 1) * rows] for p in range(cols)], axis=0)
+        for comp in range(comps)
+    ]
     right = jnp.concatenate(
         [jnp.concatenate([value, values[2] * value], axis=0) for value in values], axis=1
     )
     result = dot_split(matrix[...], right)
-    for t in range(cols):
+    for p in range(cols):
         for comp in range(comps):
-            outs[t][comp * rows : (comp + 1) * rows] = result[
-                t * rows : (t + 1) * rows, comp * lanes : (comp + 1) * lanes
+            out[p, comp * rows : (comp + 1) * rows] = result[
+                p * rows : (p + 1) * rows, comp * lanes : (comp + 1) * lanes
             ]
 
 
@@ -167,7 +164,7 @@
     q = lax.broadcasted_iota(jnp.int32, (depth, depth), 1) % zloc
     match = r == q
     for s in range(rows):
-        other = lax.rem(me + rows - s, rows)
+        other = me ^ s
         theirs = ((own < wall_counts[other]) & (own + start_of(other) == cell)).astype(jnp.float32)
         for k in range(2):
             block = jnp.where(match, exact(pair[k], theirs, turned), 0.0)
@@ -190,19 +187,16 @@
         )
 
 
-def finish_kernel(cols, comps, zloc, wall_counts, total, *refs):
-    chunks, out, scratch = refs[:cols], refs[cols], refs[cols + 1]
+def finish_kernel(comps, zloc, wall_counts, total, chunks, out):
+    cols = chunks.shape[0]
     block = out.shape[1] // cols
     per = lanes // block
     depth = out.shape[0] // comps
     rows = depth // per
-    me = lax.axis_index("col")
     count = wall_counts[lax.axis_index("row")]
-    for t in range(cols):
-        scratch[lax.rem(me + cols - t, cols)] = chunks[t][...]
     for tile in range(cols // per):
         for comp in range(comps):
-            parts = [scratch[tile * per + p, comp * rows : (comp + 1) * rows] for p in range(per)]
+            parts = [chunks[tile * per + p, comp * rows : (comp + 1) * rows] for p in range(per)]
             for q, part in enumerate(swap_blocks(parts, block)):
                 at = slice(comp * depth + q * rows, comp * depth + (q + 1) * rows)
                 across = slice(tile * lanes, (tile + 1) * lanes)
@@ -229,23 +223,24 @@
     field = velocity.reshape(comps * depth, length)
     block = length // cols
     group = depth // (lanes // block)
-    chunk = jax.ShapeDtypeStruct((comps * group, lanes), jnp.float32)
-    scratch = pltpu.VMEM((cols,) + chunk.shape, jnp.float32)
+    chunks = jax.ShapeDtypeStruct((cols, comps * group, lanes), jnp.float32)
     whole = jax.ShapeDtypeStruct(field.shape, jnp.float32)
 
-    def shift(value, axis, size, step):
-        return lax.ppermute(value, axis, [(i, (i + step) % size) for i in range(size)])
-
-    chunks = pl.pallas_call(
-        functools.partial(pack_kernel, cols, comps),
-        out_shape=[chunk] * cols,
+    def swap(value, step):
+        return lax.ppermute(value, "row", [(i, i ^ step) for i in range(rows)])
+
+    def turn(value):
+        return lax.all_to_all(value, "col", split_axis=0, concat_axis=0, tiled=True)
+
+    packed = pl.pallas_call(
+        functools.partial(pack_kernel, comps),
+        out_shape=chunks,
         in_specs=[spec(VMEM)],
-        out_specs=[spec(VMEM)] * cols,
-        scratch_shapes=[scratch],
+        out_specs=spec(VMEM),
         name="pack",
     )(field)
-    received = [chunks[0]] + [shift(chunks[s], "col", cols, s) for s in range(1, cols)]
-    fields = [field] + [shift(field, "row", rows, s) for s in range(1, rows)]
+    received = turn(packed)
+    fields = [field] + [swap(field, s) for s in range(1, rows)]
     x_part, z_matrix, y_matrix = pl.pallas_call(
         functools.partial(stream_kernel, rows, cols, comps, slots, zloc),
         out_shape=[
@@ -270,13 +265,13 @@
         y_second,
     )
     parts = pl.pallas_call(
-        functools.partial(span_kernel, cols, comps),
-        out_shape=[chunk] * cols,
-        in_specs=[spec(VMEM)] * (cols + 1),
-        out_specs=[spec(VMEM)] * cols,
+        functools.partial(span_kernel, comps),
+        out_shape=chunks,
+        in_specs=[spec(VMEM)] * 2,
+        out_specs=spec(VMEM),
         name="span",
-    )(z_matrix, *received)
-    returned = [parts[0]] + [shift(parts[t], "col", cols, t) for t in range(1, cols)]
+    )(z_matrix, received)
+    returned = turn(parts)
     total = pl.pallas_call(
         functools.partial(wall_kernel, rows, comps),
         out_shape=whole,
@@ -285,13 +280,12 @@
         name="wall",
     )(y_matrix, x_part, *fields)
     result = pl.pallas_call(
-        functools.partial(finish_kernel, cols, comps, zloc),
+        functools.partial(finish_kernel, comps, zloc),
         out_shape=whole,
-        in_specs=[spec(SMEM)] + [spec(VMEM)] * (cols + 1),
-        out_specs=spec(VMEM),
-        scratch_shapes=[scratch],
+        in_specs=[spec(SMEM)] + [spec(VMEM)] * 2,
+        out_specs=spec(VMEM),
         name="finish",
-    )(wall_counts, total, *returned)
+    )(wall_counts, total, returned)
     return result.reshape(velocity.shape)
 
 

time: 48.8 us -> 34.6 us (0.71)
  waiting for transfers between devices: 17.2 us -> 9.17 us
  starting transfers between devices: 19.5 us -> 12.7 us
  local copies, waits for them, and re-layouts: 1.23 us -> 1.89 us
    ppermute x17 -> x3, starting transfers between devices: 19.5 us -> 1.93 us  [swap(): return lax.ppermute(value, 'row', [(i, i ^ step) for i in range(rows)])]
    ppermute x17 -> x3, waiting for transfers between devices: 17.2 us -> 4.99 us  [swap(): return lax.ppermute(value, 'row', [(i, i ^ step) for i in range(rows)])]
    all_to_all x0 -> x2, starting transfers between devices: none -> 10.7 us  [turn(): return lax.all_to_all(value, 'col', split_axis=0, concat_axis=0, tiled=True)]
    all_to_all x0 -> x2, waiting for transfers between devices: none -> 4.18 us  [turn(): return lax.all_to_all(value, 'col', split_axis=0, concat_axis=0, tiled=True)]
    unnamed x38 -> x12, local copies, waits for them, and re-layouts: 1.23 us -> 1.89 us
  transfers between devices with their start and end apart: 17 -> 5, of which waited for: 6 -> 3; matrix products, arithmetic and copies ran while one was open for 0% -> 0% of each run, Pallas kernels for 18% -> 15%
where the time goes in v3:
time: 34.6 us; the launch traced here: 34.2 us
  starting transfers between devices  12.7 us (37%)
  Pallas kernels  10.4 us (30%)
  waiting for transfers between devices  9.17 us (27%)
  local copies, waits for them, and re-layouts  1.89 us (5%)
    all_to_all x2, starting transfers between devices, turn(): return lax.all_to_all(value, 'col', split_axis=0, concat_axis=0, tiled=True)  10.7 us
    ppermute x3, waiting for transfers between devices, swap(): return lax.ppermute(value, 'row', [(i, i ^ step) for i in range(rows)])  4.99 us
    all_to_all x2, waiting for transfers between devices, turn(): return lax.all_to_all(value, 'col', split_axis=0, concat_axis=0, tiled=True)  4.18 us
    pallas_call x1, Pallas kernels, local(): pl.pallas_call(functools.partial(stream_kernel, rows, cols, comps, slots,...  2.95 us
    pallas_call x1, Pallas kernels, local(): pl.pallas_call(functools.partial(wall_kernel, rows, comps), out_shape=who...  2.12 us
    ppermute x3, starting transfers between devices, swap(): return lax.ppermute(value, 'row', [(i, i ^ step) for i in range(rows)])  1.93 us
    unnamed x12, local copies, waits for them, and re-layouts  1.89 us
    pallas_call x1, Pallas kernels, local(): pl.pallas_call(functools.partial(finish_kernel, comps, zloc), out_shape=w...  1.82 us
  transfers between devices with their start and end apart: 5, of which 3 were waited for; matrix products, arithmetic and copies ran while one was open for 0% of the time, Pallas kernels for 15%

profile of v3, /device:TPU:0, one launch (start us, length us, event | category | flops | bytes accessed | tf_op | source)
XLA Modules:
  0.0 34.2 jit_solution(8020010870580414947)
XLA Ops:
  0.0 1.8 %pack.1 = f32[8,24,128]{2,1,0:T(8,128)} custom-call(f32[192,128]{1,0:T(8,128)} %bitcast.4), custom_call_target="tpu_custom_call" | custom-call | tf_op jit(solution)/shard_map/pack/pallas_call | solution.py:235
  1.8 7.3 %all-to-all-start = ((f32[8,24,128]{2,1,0:T(8,128)}), f32[8,24,128]{2,1,0:T(8,128)S(1)}, u32[]{:S(2)}, u32[]{:S(2)}) async-start(f32[8,24,128]{2,1,0:T(8,128)} %pack.1), calls=%async_computation | async-start | bytes 196608 | tf_op jit(solution)/shard_map/all_to_all | solution.py:233
  9.0 2.9 %stream.1 = (f32[192,128]{1,0:T(8,128)}, f32[64,128]{1,0:T(8,128)}, f32[64,512]{1,0:T(8,128)}) custom-call(s32[4]{0:T(128)} %wall_counts.3, f32[32]{0:T(128)} %z_first.1, f32[32]{0:T(128)} %z_second.1, f32[64]{0:T(128)} %metric_table.1, s32[32]{0:T(128)} %metric_index.1, f32[192,128]{1,0:T(8,128)} %bitcast.5, f32[1,128]{1,0:T(1,128)} %bitcast.10, ...), custom_call_target="tpu_custom_call" | custom-call | tf_op jit(solution)/shard_map/stream/pallas_call | solution.py:244
  12.0 4.2 %all-to-all-done.chunks = f32[8,24,128]{2,1,0:T(8,128)S(1)} async-done(((f32[8,24,128]{2,1,0:T(8,128)}), f32[8,24,128]{2,1,0:T(8,128)S(1)}, u32[]{:S(2)}, u32[]{:S(2)}) %all-to-all-start) | async-done | bytes 98336 | tf_op jit(solution)/shard_map/all_to_all | solution.py:233
  16.1 0.0 copy-start.1
  16.1 0.6 %copy-done.1 = f32[8,24,128]{2,1,0:T(8,128)} copy-done((f32[8,24,128]{2,1,0:T(8,128)}, f32[8,24,128]{2,1,0:T(8,128)S(1)}, u32[]{:S(2)}) %copy-start.1) | copy-done | bytes 98328
  16.8 1.7 %span.1 = f32[8,24,128]{2,1,0:T(8,128)} custom-call(f32[64,128]{1,0:T(8,128)} %get-tuple-element.10.matrix, f32[8,24,128]{2,1,0:T(8,128)} %copy-done.1), custom_call_target="tpu_custom_call" | custom-call | tf_op jit(solution)/shard_map/span/pallas_call | solution.py:267
  18.5 0.0 copy-start
  18.5 3.5 %all-to-all-start.1 = ((f32[8,24,128]{2,1,0:T(8,128)}), f32[8,24,128]{2,1,0:T(8,128)S(1)}, u32[]{:S(2)}, u32[]{:S(2)}) async-start(f32[8,24,128]{2,1,0:T(8,128)} %span.1), calls=%async_computation.1 | async-start | bytes 196608 | tf_op jit(solution)/shard_map/all_to_all | solution.py:233
  22.0 0.0 copy-done
  22.0 0.1 collective-permute-start
  22.1 1.6 %collective-permute-start.1 = (f32[192,128]{1,0:T(8,128)S(1)}, f32[192,128]{1,0:T(8,128)S(1)}, u32[]{:S(2)}, u32[]{:S(2)}) collective-permute-start(f32[192,128]{1,0:T(8,128)S(1)} %bitcast.8), channel_id=1, source_target_pairs={{0,16},{8,24},{16,0},{24,8},{1,17},{9,25},{17,1},{25,9},{2,18},{10... | collective-permute-start | bytes 294920 | tf_op jit(solution)/shard_map/ppermute | solution.py:230
  23.7 0.3 collective-permute-start.2
  24.0 0.0 collective-permute-done.refs_1_
  24.0 0.0 copy-start.3
  24.0 3.8 %collective-permute-done.1.refs_2_ = f32[192,128]{1,0:T(8,128)S(1)} collective-permute-done((f32[192,128]{1,0:T(8,128)S(1)}, f32[192,128]{1,0:T(8,128)S(1)}, u32[]{:S(2)}, u32[]{:S(2)}) %collective-permute-start.1) | collective-permute-done | bytes 98336 | tf_op jit(solution)/shard_map/ppermute | solution.py:230
  27.8 1.2 %collective-permute-done.2.refs_3_ = f32[192,128]{1,0:T(8,128)S(1)} collective-permute-done((f32[192,128]{1,0:T(8,128)S(1)}, f32[192,128]{1,0:T(8,128)S(1)}, u32[]{:S(2)}, u32[]{:S(2)}) %collective-permute-start.2) | collective-permute-done | bytes 98336 | tf_op jit(solution)/shard_map/ppermute | solution.py:230
  29.0 0.0 copy-done.3
  29.0 0.0 copy-done.4
  29.0 0.6 %copy-done.5 = f32[192,128]{1,0:T(8,128)} copy-done((f32[192,128]{1,0:T(8,128)}, f32[192,128]{1,0:T(8,128)S(1)}, u32[]{:S(2)}) %copy-start.5) | copy-done | bytes 98328
  29.6 2.1 %wall.1.total = f32[192,128]{1,0:T(8,128)} custom-call(f32[64,512]{1,0:T(8,128)} %get-tuple-element.8.matrix, f32[192,128]{1,0:T(8,128)} %get-tuple-element.9.x_part, f32[192,128]{1,0:T(8,128)} %bitcast.6, f32[192,128]{1,0:T(8,128)} %copy-done.3, f32[192,128]{1,0:T(8,128)} %copy-done.4, f32[192,128]{1,0:T(8,128)} %copy-done.5), custom_call_target="tpu_custom_call" | custom-call | tf_op jit(solution)/shard_map/wall/pallas_call | solution.py:275
  31.7 0.0 all-to-all-done.1.chunks
  31.7 0.6 %copy-done.2 = f32[8,24,128]{2,1,0:T(8,128)} copy-done((f32[8,24,128]{2,1,0:T(8,128)}, f32[8,24,128]{2,1,0:T(8,128)S(1)}, u32[]{:S(2)}) %copy-start.2) | copy-done | bytes 98328
  32.4 1.8 %finish.1 = f32[192,128]{1,0:T(8,128)} custom-call(s32[4]{0:T(128)} %wall_counts.3, f32[192,128]{1,0:T(8,128)} %wall.1.total, f32[8,24,128]{2,1,0:T(8,128)} %copy-done.2), custom_call_target="tpu_custom_call" | custom-call | tf_op jit(solution)/shard_map/finish/pallas_call | solution.py:282
  (3 shorter events, 0.0 us)
Async XLA Ops:
  1.8 14.4 %all-to-all-start = ((f32[8,24,128]{2,1,0:T(8,128)}), f32[8,24,128]{2,1,0:T(8,128)S(1)}, u32[]{:S(2)}, u32[]{:S(2)}) async-start(f32[8,24,128]{2,1,0:T(8,128)} %pack.1), calls=%async_computation | async-start | bytes 196608 | tf_op jit(solution)/shard_map/all_to_all | solution.py:233
  16.1 0.6 %copy-start.1 = (f32[8,24,128]{2,1,0:T(8,128)}, f32[8,24,128]{2,1,0:T(8,128)S(1)}, u32[]{:S(2)}) copy-start(f32[8,24,128]{2,1,0:T(8,128)S(1)} %all-to-all-done.chunks) | copy-start | bytes 294916
  18.5 3.5 %copy-start = (f32[3,16,4,128]{3,2,1,0:T(4,128)S(1)}, f32[3,16,4,128]{3,2,1,0:T(4,128)}, u32[]{:S(2)}) copy-start(f32[3,16,4,128]{3,2,1,0:T(4,128)} %param.10) | copy-start | bytes 294916
  18.5 13.2 %all-to-all-start.1 = ((f32[8,24,128]{2,1,0:T(8,128)}), f32[8,24,128]{2,1,0:T(8,128)S(1)}, u32[]{:S(2)}, u32[]{:S(2)}) async-start(f32[8,24,128]{2,1,0:T(8,128)} %span.1), calls=%async_computation.1 | async-start | bytes 196608 | tf_op jit(solution)/shard_map/all_to_all | solution.py:233
  22.0 1.9 %collective-permute-start = (f32[192,128]{1,0:T(8,128)S(1)}, f32[192,128]{1,0:T(8,128)S(1)}, u32[]{:S(2)}, u32[]{:S(2)}) collective-permute-start(f32[192,128]{1,0:T(8,128)S(1)} %bitcast.7), channel_id=1, source_target_pairs={{0,8},{8,0},{16,24},{24,16},{1,9},{9,1},{17,25},{25,17},{2,10},{10... | collective-permute-start | bytes 294920 | tf_op jit(solution)/shard_map/ppermute | solution.py:230
  22.1 5.7 %collective-permute-start.1 = (f32[192,128]{1,0:T(8,128)S(1)}, f32[192,128]{1,0:T(8,128)S(1)}, u32[]{:S(2)}, u32[]{:S(2)}) collective-permute-start(f32[192,128]{1,0:T(8,128)S(1)} %bitcast.8), channel_id=1, source_target_pairs={{0,16},{8,24},{16,0},{24,8},{1,17},{9,25},{17,1},{25,9},{2,18},{10... | collective-permute-start | bytes 294920 | tf_op jit(solution)/shard_map/ppermute | solution.py:230
  23.7 5.3 %collective-permute-start.2 = (f32[192,128]{1,0:T(8,128)S(1)}, f32[192,128]{1,0:T(8,128)S(1)}, u32[]{:S(2)}, u32[]{:S(2)}) collective-permute-start(f32[192,128]{1,0:T(8,128)S(1)} %bitcast.9), channel_id=1, source_target_pairs={{0,24},{8,16},{16,8},{24,0},{1,25},{9,17},{17,9},{25,1},{2,26},{10... | collective-permute-start | bytes 294920 | tf_op jit(solution)/shard_map/ppermute | solution.py:230
  24.0 5.0 %copy-start.3 = (f32[192,128]{1,0:T(8,128)}, f32[192,128]{1,0:T(8,128)S(1)}, u32[]{:S(2)}) copy-start(f32[192,128]{1,0:T(8,128)S(1)} %collective-permute-done.refs_1_) | copy-start | bytes 294916
  27.8 1.2 %copy-start.4 = (f32[192,128]{1,0:T(8,128)}, f32[192,128]{1,0:T(8,128)S(1)}, u32[]{:S(2)}) copy-start(f32[192,128]{1,0:T(8,128)S(1)} %collective-permute-done.1.refs_2_) | copy-start | bytes 294916
  29.0 0.6 %copy-start.5 = (f32[192,128]{1,0:T(8,128)}, f32[192,128]{1,0:T(8,128)S(1)}, u32[]{:S(2)}) copy-start(f32[192,128]{1,0:T(8,128)S(1)} %collective-permute-done.2.refs_3_) | copy-start | bytes 294916
  31.7 0.6 %copy-start.2 = (f32[8,24,128]{2,1,0:T(8,128)}, f32[8,24,128]{2,1,0:T(8,128)S(1)}, u32[]{:S(2)}) copy-start(f32[8,24,128]{2,1,0:T(8,128)S(1)} %all-to-all-done.1.chunks) | copy-start | bytes 294916

commit v4 on v3

v4 whole, which is shorter than its diff:
```python
import functools
import math

import jax
import jax.numpy as jnp
from jax import lax
from jax.experimental import pallas as pl
from jax.experimental.pallas import tpu as pltpu
from jax.sharding import PartitionSpec as P

viscosity = 0.4
lanes = 128

VMEM = pltpu.VMEM
SMEM = pltpu.SMEM


def halves(value):
    high = value.astype(jnp.bfloat16)
    low = (value - high.astype(jnp.float32)).astype(jnp.bfloat16)
    return high, low


def dot_split(left, right, transposed=False):
    dims = (((1,), (1 if transposed else 0,)), ((), ()))
    mul = functools.partial(lax.dot_general, dimension_numbers=dims, preferred_element_type=jnp.float32)
    lh, ll = halves(left)
    rh, rl = halves(right)
    return mul(lh, rh) + (mul(lh, rl) + mul(ll, rh))


def swap_blocks(parts, block):
    parts = list(parts)
    count = len(parts)
    lane = lax.broadcasted_iota(jnp.int32, parts[0].shape, 1) // block
    step = count // 2
    while step:
        low = (lane & step) == 0
        for i in range(count):
            if i & step:
                continue
            a, b = parts[i], parts[i | step]
            parts[i] = jnp.where(low, a, pltpu.roll(b, step * block, 1))
            parts[i | step] = jnp.where(low, pltpu.roll(a, lanes - step * block, 1), b)
        step //= 2
    return parts


def pack_kernel(comps, field, out):
    cols = out.shape[0]
    block = field.shape[1] // cols
    per = lanes // block
    depth = field.shape[0] // comps
    rows = depth // per
    for tile in range(cols // per):
        for comp in range(comps):
            parts = [
                field[comp * depth + q * rows : comp * depth + (q + 1) * rows, tile * lanes : (tile + 1) * lanes]
                for q in range(per)
            ]
            for p, part in enumerate(swap_blocks(parts, block)):
                out[tile * per + p, comp * rows : (comp + 1) * rows] = part


def span_kernel(comps, matrix, chunks, *refs):
    out = refs[-1]
    cols = out.shape[0]
    rows = out.shape[1] // comps
    values = [
        jnp.concatenate([chunks[p, comp * rows : (comp + 1) * rows] for p in range(cols)], axis=0)
        for comp in range(comps)
    ]
    right = jnp.concatenate(
        [jnp.concatenate([value, values[2] * value], axis=0) for value in values], axis=1
    )
    result = dot_split(matrix[...], right)
    for p in range(cols):
        for comp in range(comps):
            out[p, comp * rows : (comp + 1) * rows] = result[
                p * rows : (p + 1) * rows, comp * lanes : (comp + 1) * lanes
            ]


def circulant_rows(row, length):
    return pltpu.roll(jnp.broadcast_to(row, (length, length)), 0, 1, stride=1, stride_axis=0)


def span_matrix_kernel(zloc, z_first, z_second, field, packed, z_matrix, copied):
    cols = packed.shape[0]
    cells = cols * zloc
    group = z_matrix.shape[0] // cols
    shape = z_matrix.shape
    half = shape[1] // 2
    copied[...] = field[...]
    r = lax.broadcasted_iota(jnp.int32, shape, 0)
    q = lax.broadcasted_iota(jnp.int32, shape, 1)
    q = jnp.where(q < half, q, q - half)
    out_cell = (r // group) * zloc + r % zloc
    in_cell = (q // group) * zloc + q % zloc
    same = (r % group) // zloc == (q % group) // zloc
    gap = jnp.where(same, (in_cell - out_cell + cells) % cells, -1)
    line = lax.broadcasted_iota(jnp.int32, (1, shape[1]), 1) < half

    def fill(k, total):
        value = jnp.where(line, viscosity * z_second[k], -z_first[k])
        return jnp.where(gap == k, value, total)

    z_matrix[...] = lax.fori_loop(0, cells, fill, jnp.zeros(shape, jnp.float32), unroll=8)


def stream_kernel(
    rows,
    comps,
    slots,
    zloc,
    wall_counts,
    metric_table,
    metric_index,
    field,
    x_first,
    x_second,
    y_first,
    y_second,
    *refs,
):
    across = refs[: rows // 2 - 1]
    x_part, y_matrix, pair, scaled = refs[rows // 2 :]
    depth = slots * zloc
    length = field.shape[1]
    cells = y_first.shape[0]
    pair[0] = field[...]
    for i, other in enumerate(across):
        pair[i + 1] = other[...]

    u = field[...]
    lead = u[:depth]
    left = jnp.concatenate(
        [u, jnp.concatenate([lead * u[c * depth : (c + 1) * depth] for c in range(comps)], axis=0)], axis=1
    )
    right = jnp.concatenate(
        [viscosity * circulant_rows(x_second[...], length), -circulant_rows(x_first[...], length)], axis=1
    )
    x_part[...] = dot_split(left, right, transposed=True)

    def scale(j, carry):
        scaled[pl.ds(j, 1), :] = y_first[pl.ds(j, 1), :] * -metric_table[metric_index[j]]
        return carry

    lax.fori_loop(0, cells, scale, 0, unroll=8)
    me = lax.axis_index("row")

    def start_of(index):
        return lax.fori_loop(0, rows, lambda i, acc: acc + jnp.where(i < index, wall_counts[i], 0), 0, unroll=True)

    own = lax.broadcasted_iota(jnp.int32, (depth, cells), 0) // zloc
    cell = lax.broadcasted_iota(jnp.int32, (depth, cells), 1)
    mine = ((own < wall_counts[me]) & (own + start_of(me) == cell)).astype(jnp.float32)
    exact = functools.partial(
        lax.dot_general, precision=lax.Precision.HIGHEST, preferred_element_type=jnp.float32
    )
    plain = (((1,), (0,)), ((), ()))
    turned = (((1,), (1,)), ((), ()))
    both = [exact(mine, viscosity * y_second[...], plain), exact(mine, scaled[...], plain)]
    r = lax.broadcasted_iota(jnp.int32, (depth, depth), 0) % zloc
    q = lax.broadcasted_iota(jnp.int32, (depth, depth), 1) % zloc
    match = r == q
    for b in range(rows):
        other = me ^ (2 * b if b < rows // 2 else 2 * b + 1 - rows)
        theirs = ((own < wall_counts[other]) & (own + start_of(other) == cell)).astype(jnp.float32)
        for k in range(2):
            block = jnp.where(match, exact(both[k], theirs, turned), 0.0)
            y_matrix[:, (2 * b + k) * depth : (2 * b + k + 1) * depth] = block


def wall_kernel(comps, matrix, x_part, ours, theirs, out):
    depth = x_part.shape[0] // comps
    for comp in range(comps):
        at = slice(comp * depth, (comp + 1) * depth)
        stack = []
        for fields in (ours, theirs):
            for i in range(fields.shape[0]):
                value = fields[i, at]
                stack += [value, fields[i, depth : 2 * depth] * value]
        out[at] = x_part[at] + dot_split(matrix[...], jnp.concatenate(stack, axis=0))


def finish_kernel(comps, zloc, wall_counts, total, chunks, out):
    cols = chunks.shape[0]
    block = out.shape[1] // cols
    per = lanes // block
    depth = out.shape[0] // comps
    rows = depth // per
    count = wall_counts[lax.axis_index("row")]
    for tile in range(cols // per):
        for comp in range(comps):
            parts = [chunks[tile * per + p, comp * rows : (comp + 1) * rows] for p in range(per)]
            for q, part in enumerate(swap_blocks(parts, block)):
                at = slice(comp * depth + q * rows, comp * depth + (q + 1) * rows)
                across = slice(tile * lanes, (tile + 1) * lanes)
                plane = (lax.broadcasted_iota(jnp.int32, part.shape, 0) + q * rows) // zloc
                out[at, across] = jnp.where(plane < count, total[at, across] + part, 0.0)


def call(kernel, operands, spaces, results, name, scratch=()):
    results = [jax.ShapeDtypeStruct(shape, jnp.float32) for shape in results]
    held = sum(4 * math.prod(array.shape) for array in list(operands) + results)
    return pl.pallas_call(
        kernel,
        out_shape=results,
        in_specs=[pl.BlockSpec(memory_space=space) for space in spaces],
        out_specs=[pl.BlockSpec(memory_space=VMEM)] * len(results),
        scratch_shapes=[pltpu.VMEM(shape, jnp.float32) for shape in scratch],
        compiler_params=pltpu.CompilerParams(vmem_limit_bytes=(4 << 20) + 3 * held),
        name=name,
    )(*operands)


def local(
    velocity,
    wall_counts,
    x_first,
    x_second,
    y_first,
    y_second,
    z_first,
    z_second,
    metric_table,
    metric_index,
):
    rows = lax.axis_size("row")
    cols = lax.axis_size("col")
    comps, slots, zloc, length = velocity.shape
    depth = slots * zloc
    field = velocity.reshape(comps * depth, length)
    block = length // cols
    group = depth // (lanes // block)
    chunks = (cols, comps * group, lanes)

    def swap(value, step):
        return lax.ppermute(value, "row", [(i, i ^ step) for i in range(rows)])

    def turn(value):
        return lax.all_to_all(value, "col", split_axis=0, concat_axis=0, tiled=True)

    (packed,) = call(functools.partial(pack_kernel, comps), [field], [VMEM], [chunks], "pack")
    received = turn(packed)
    z_matrix, copied = call(
        functools.partial(span_matrix_kernel, zloc),
        [z_first, z_second, field, packed],
        [SMEM] * 2 + [VMEM, pl.ANY],
        [(cols * group, 2 * cols * group), field.shape],
        "span_matrix",
    )
    across = [swap(copied, step) for step in range(2, rows, 2)]
    (parts,) = call(
        functools.partial(span_kernel, comps),
        [z_matrix, received] + across,
        [VMEM] * 2 + [pl.ANY] * len(across),
        [chunks],
        "span",
    )
    returned = turn(parts)
    x_part, y_matrix, pair = call(
        functools.partial(stream_kernel, rows, comps, slots, zloc),
        [
            wall_counts,
            metric_table,
            metric_index,
            field,
            x_first.reshape(1, length),
            x_second.reshape(1, length),
            y_first,
            y_second,
        ]
        + across
        + [parts],
        [SMEM] * 3 + [VMEM] * (5 + len(across)) + [pl.ANY],
        [field.shape, (depth, 2 * rows * depth), (rows // 2,) + field.shape],
        "stream",
        [y_first.shape],
    )
    other = swap(pair, 1)
    (total,) = call(
        functools.partial(wall_kernel, comps), [y_matrix, x_part, pair, other], [VMEM] * 4, [field.shape], "wall"
    )
    (result,) = call(
        functools.partial(finish_kernel, comps, zloc),
        [wall_counts, total, returned],
        [SMEM] + [VMEM] * 2,
        [field.shape],
        "finish",
    )
    return result.reshape(velocity.shape)


def solution(mesh):
    in_specs = (P(None, "row", "col", None), P(), P(), P(), P(), P(), P(), P(), P(), P())
    out_specs = P(None, "row", "col", None)
    return jax.shard_map(local, mesh=mesh, in_specs=in_specs, out_specs=out_specs, check_vma=False)
```

time: 34.6 us -> 32.8 us (0.948)
  Pallas kernels: 10.4 us -> 5.93 us
  waiting for transfers between devices: 9.17 us -> 11.6 us
  starting transfers between devices: 12.7 us -> 13.3 us
    pallas_call x5 -> x6, Pallas kernels: 10.4 us -> 5.93 us  [call(): pl.pallas_call(kernel, out_shape=results, in_specs=[pl.BlockSpec(memory_s...]
    all_to_all x2, waiting for transfers between devices: 4.18 us -> 8.51 us  [turn(): return lax.all_to_all(value, 'col', split_axis=0, concat_axis=0, tiled=True)]
    ppermute x3 -> x2, waiting for transfers between devices: 4.99 us -> 3.1 us  [swap(): return lax.ppermute(value, 'row', [(i, i ^ step) for i in range(rows)])]
    all_to_all x2, starting transfers between devices: 10.7 us -> 11.7 us  [turn(): return lax.all_to_all(value, 'col', split_axis=0, concat_axis=0, tiled=True)]
    ppermute x3 -> x2, starting transfers between devices: 1.93 us -> 1.6 us  [swap(): return lax.ppermute(value, 'row', [(i, i ^ step) for i in range(rows)])]
    unnamed x12 -> x22, local copies, waits for them, and re-layouts: 1.89 us -> 1.57 us
  transfers between devices with their start and end apart: 5 -> 4, of which waited for: 3 -> 3; matrix products, arithmetic and copies ran while one was open for 0% -> 0% of each run, Pallas kernels for 15% -> 3%
where the time goes in v4:
time: 32.8 us; the launch traced here: 32.5 us
  starting transfers between devices  13.3 us (41%)
  waiting for transfers between devices  11.6 us (35%)
  Pallas kernels  5.93 us (18%)
  local copies, waits for them, and re-layouts  1.57 us (5%)
    all_to_all x2, starting transfers between devices, turn(): return lax.all_to_all(value, 'col', split_axis=0, concat_axis=0, tiled=True)  11.7 us
    all_to_all x2, waiting for transfers between devices, turn(): return lax.all_to_all(value, 'col', split_axis=0, concat_axis=0, tiled=True)  8.51 us
    pallas_call x6, Pallas kernels, call(): pl.pallas_call(kernel, out_shape=results, in_specs=[pl.BlockSpec(memory_s...  5.93 us
    ppermute x2, waiting for transfers between devices, swap(): return lax.ppermute(value, 'row', [(i, i ^ step) for i in range(rows)])  3.1 us
    ppermute x2, starting transfers between devices, swap(): return lax.ppermute(value, 'row', [(i, i ^ step) for i in range(rows)])  1.6 us
    unnamed x22, local copies, waits for them, and re-layouts  1.57 us
  transfers between devices with their start and end apart: 4, of which 3 were waited for; matrix products, arithmetic and copies ran while one was open for 0% of the time, Pallas kernels for 3%

profile of v4, /device:TPU:0, one launch (start us, length us, event | category | flops | bytes accessed | tf_op | source)
XLA Modules:
  0.0 32.5 jit_solution(16191531817715495186)
XLA Ops:
  0.0 0.9 %copy-done = f32[3,16,4,128]{3,2,1,0:T(4,128)S(1)} copy-done((f32[3,16,4,128]{3,2,1,0:T(4,128)S(1)}, f32[3,16,4,128]{3,2,1,0:T(4,128)}, u32[]{:S(2)}) %copy-start) | copy-done | bytes 98328
  0.9 0.9 %pack.1.packed = f32[8,24,128]{2,1,0:T(8,128)} custom-call(f32[192,128]{1,0:T(8,128)S(1)} %bitcast.4), custom_call_target="tpu_custom_call" | custom-call | tf_op jit(solution)/shard_map/pack/pallas_call | solution.py:207
  1.8 7.4 %all-to-all-start = ((f32[8,24,128]{2,1,0:T(8,128)}), f32[8,24,128]{2,1,0:T(8,128)S(1)}, u32[]{:S(2)}, u32[]{:S(2)}) async-start(f32[8,24,128]{2,1,0:T(8,128)} %pack.1.packed), calls=%async_computation | async-start | bytes 196608 | tf_op jit(solution)/shard_map/all_to_all | solution.py:243
  9.2 0.0 copy-done.1
  9.2 0.0 copy-done.5
  9.2 0.0 copy-done.6
  9.2 0.7 %span_matrix.1 = (f32[64,128]{1,0:T(8,128)S(1)}, f32[192,128]{1,0:T(8,128)S(1)}) custom-call(f32[32]{0:T(128)S(1)} %copy-done.5, f32[32]{0:T(128)S(1)} %copy-done.6, f32[192,128]{1,0:T(8,128)S(1)} %bitcast.5, f32[8,24,128]{2,1,0:T(8,128)} %pack.1.packed), custom_call_target="tpu_custom_call" | custom-call | tf_op jit(solution)/shard_map/span_matrix/pallas_call | solution.py:207
  9.9 1.6 %collective-permute-start = (f32[192,128]{1,0:T(8,128)S(1)}, f32[192,128]{1,0:T(8,128)S(1)}, u32[]{:S(2)}, u32[]{:S(2)}) collective-permute-start(f32[192,128]{1,0:T(8,128)S(1)} %get-tuple-element.10), channel_id=1, source_target_pairs={{0,16},{8,24},{16,0},{24,8},{1,17},{9,25},{17,1},{25,9},{2,18},{10... | collective-permute-start | bytes 294920 | tf_op jit(solution)/shard_map/ppermute | solution.py:240
  11.5 3.1 %collective-permute-done.refs_0_ = f32[192,128]{1,0:T(8,128)S(1)} collective-permute-done((f32[192,128]{1,0:T(8,128)S(1)}, f32[192,128]{1,0:T(8,128)S(1)}, u32[]{:S(2)}, u32[]{:S(2)}) %collective-permute-start) | collective-permute-done | bytes 98336 | tf_op jit(solution)/shard_map/ppermute | solution.py:240
  14.6 1.7 %all-to-all-done.chunks = f32[8,24,128]{2,1,0:T(8,128)S(1)} async-done(((f32[8,24,128]{2,1,0:T(8,128)}), f32[8,24,128]{2,1,0:T(8,128)S(1)}, u32[]{:S(2)}, u32[]{:S(2)}) %all-to-all-start) | async-done | bytes 98336 | tf_op jit(solution)/shard_map/all_to_all | solution.py:243
  16.3 0.8 %span.1.refs_1_ = f32[8,24,128]{2,1,0:T(8,128)} custom-call(f32[64,128]{1,0:T(8,128)S(1)} %get-tuple-element.11.matrix, f32[8,24,128]{2,1,0:T(8,128)S(1)} %all-to-all-done.chunks, f32[192,128]{1,0:T(8,128)S(1)} %collective-permute-done.refs_0_), custom_call_target="tpu_custom_call" | custom-call | tf_op jit(solution)/shard_map/span/pallas_call | solution.py:207
  17.1 0.0 copy-done.2
  17.1 0.0 copy-done.3
  17.1 0.0 copy-done.9
  17.2 0.6 %copy-done.4 = s32[4]{0:T(128)S(1)} copy-done((s32[4]{0:T(128)S(1)}, s32[4]{0:T(128)}, u32[]{:S(2)}) %copy-start.4) | copy-done | bytes 40
  17.8 0.0 copy-done.7
  17.8 0.0 copy-done.8
  17.8 1.8 %stream.1 = (f32[192,128]{1,0:T(8,128)S(1)}, f32[64,512]{1,0:T(8,128)S(1)}, f32[2,192,128]{2,1,0:T(8,128)S(1)}) custom-call(s32[4]{0:T(128)S(1)} %copy-done.4, f32[64]{0:T(128)S(1)} %copy-done.7, s32[32]{0:T(128)S(1)} %copy-done.8, f32[192,128]{1,0:T(8,128)S(1)} %bitcast.6, f32[1,128]{1,0:T(1,128)S(1)} %bitcast.7, f32[1,128]{1,0:T(1,128)S(1)} %bitcast.8, ...), custom_call_target="tpu_custom_call" | custom-call | tf_op jit(solution)/shard_map/stream/pallas_call | solution.py:207
  19.6 0.0 collective-permute-start.1
  19.6 4.3 %all-to-all-start.1 = ((f32[8,24,128]{2,1,0:T(8,128)}), f32[8,24,128]{2,1,0:T(8,128)S(1)}, u32[]{:S(2)}, u32[]{:S(2)}) async-start(f32[8,24,128]{2,1,0:T(8,128)} %span.1.refs_1_), calls=%async_computation.1 | async-start | bytes 196608 | tf_op jit(solution)/shard_map/all_to_all | solution.py:243
  23.9 0.0 collective-permute-done.1.theirs
  23.9 0.4 %wall.1.total = f32[192,128]{1,0:T(8,128)S(1)} custom-call(f32[64,512]{1,0:T(8,128)S(1)} %get-tuple-element.12.matrix, f32[192,128]{1,0:T(8,128)S(1)} %get-tuple-element.13.x_part, f32[2,192,128]{2,1,0:T(8,128)S(1)} %get-tuple-element.14.ours, f32[2,192,128]{2,1,0:T(8,128)S(1)} %collective-permute-done.1.theirs), custom_call_target="tpu_custom_call" | custom-call | tf_op jit(solution)/shard_map/wall/pallas_call | solution.py:207
  24.3 6.8 %all-to-all-done.1.chunks = f32[8,24,128]{2,1,0:T(8,128)S(1)} async-done(((f32[8,24,128]{2,1,0:T(8,128)}), f32[8,24,128]{2,1,0:T(8,128)S(1)}, u32[]{:S(2)}, u32[]{:S(2)}) %all-to-all-start.1) | async-done | bytes 98336 | tf_op jit(solution)/shard_map/all_to_all | solution.py:243
  31.1 1.4 %finish.1 = f32[192,128]{1,0:T(8,128)} custom-call(s32[4]{0:T(128)S(1)} %copy-done.4, f32[192,128]{1,0:T(8,128)S(1)} %wall.1.total, f32[8,24,128]{2,1,0:T(8,128)S(1)} %all-to-all-done.1.chunks), custom_call_target="tpu_custom_call" | custom-call | tf_op jit(solution)/shard_map/finish/pallas_call | solution.py:207
  (12 shorter events, 0.0 us)
Async XLA Ops:
  0.0 0.9 %copy-start = (f32[3,16,4,128]{3,2,1,0:T(4,128)S(1)}, f32[3,16,4,128]{3,2,1,0:T(4,128)}, u32[]{:S(2)}) copy-start(f32[3,16,4,128]{3,2,1,0:T(4,128)} %param.10) | copy-start | bytes 294916
  1.8 7.4 %copy-start.1 = (f32[3,16,4,128]{3,2,1,0:T(4,128)S(1)}, f32[3,16,4,128]{3,2,1,0:T(4,128)}, u32[]{:S(2)}) copy-start(f32[3,16,4,128]{3,2,1,0:T(4,128)} %param.10) | copy-start | bytes 294916
  1.8 7.4 %copy-start.5 = (f32[32]{0:T(128)S(1)}, f32[32]{0:T(128)}, u32[]{:S(2)}) copy-start(f32[32]{0:T(128)} %z_first.1) | copy-start | bytes 388
  1.8 7.4 %copy-start.6 = (f32[32]{0:T(128)S(1)}, f32[32]{0:T(128)}, u32[]{:S(2)}) copy-start(f32[32]{0:T(128)} %z_second.1) | copy-start | bytes 388
  1.8 14.5 %all-to-all-start = ((f32[8,24,128]{2,1,0:T(8,128)}), f32[8,24,128]{2,1,0:T(8,128)S(1)}, u32[]{:S(2)}, u32[]{:S(2)}) async-start(f32[8,24,128]{2,1,0:T(8,128)} %pack.1.packed), calls=%async_computation | async-start | bytes 196608 | tf_op jit(solution)/shard_map/all_to_all | solution.py:243
  9.9 4.7 %collective-permute-start = (f32[192,128]{1,0:T(8,128)S(1)}, f32[192,128]{1,0:T(8,128)S(1)}, u32[]{:S(2)}, u32[]{:S(2)}) collective-permute-start(f32[192,128]{1,0:T(8,128)S(1)} %get-tuple-element.10), channel_id=1, source_target_pairs={{0,16},{8,24},{16,0},{24,8},{1,17},{9,25},{17,1},{25,9},{2,18},{10... | collective-permute-start | bytes 294920 | tf_op jit(solution)/shard_map/ppermute | solution.py:240
  16.3 0.9 %copy-start.2 = (f32[32,32]{1,0:T(8,128)S(1)}, f32[32,32]{1,0:T(8,128)}, u32[]{:S(2)}) copy-start(f32[32,32]{1,0:T(8,128)} %y_first.1) | copy-start | bytes 12292
  16.3 0.9 %copy-start.3 = (f32[32,32]{1,0:T(8,128)S(1)}, f32[32,32]{1,0:T(8,128)}, u32[]{:S(2)}) copy-start(f32[32,32]{1,0:T(8,128)} %y_second.1) | copy-start | bytes 12292
  16.3 0.9 %copy-start.9 = (f32[128]{0:T(128)S(1)}, f32[128]{0:T(128)}, u32[]{:S(2)}) copy-start(f32[128]{0:T(128)} %param.12) | copy-start | bytes 1540
  16.3 0.9 %copy-start.10 = (f32[128]{0:T(128)S(1)}, f32[128]{0:T(128)}, u32[]{:S(2)}) copy-start(f32[128]{0:T(128)} %param.13) | copy-start | bytes 1540
  17.1 0.7 %copy-start.4 = (s32[4]{0:T(128)S(1)}, s32[4]{0:T(128)}, u32[]{:S(2)}) copy-start(s32[4]{0:T(128)} %wall_counts.3) | copy-start | bytes 52
  17.1 0.7 %copy-start.7 = (f32[64]{0:T(128)S(1)}, f32[64]{0:T(128)}, u32[]{:S(2)}) copy-start(f32[64]{0:T(128)} %metric_table.1) | copy-start | bytes 772
  17.1 0.7 %copy-start.8 = (s32[32]{0:T(128)S(1)}, s32[32]{0:T(128)}, u32[]{:S(2)}) copy-start(s32[32]{0:T(128)} %metric_index.1) | copy-start | bytes 388
  19.6 4.3 %collective-permute-start.1 = (f32[2,192,128]{2,1,0:T(8,128)S(1)}, f32[2,192,128]{2,1,0:T(8,128)S(1)}, u32[]{:S(2)}, u32[]{:S(2)}) collective-permute-start(f32[2,192,128]{2,1,0:T(8,128)S(1)} %get-tuple-element.14.ours), channel_id=1, source_target_pairs={{0,8},{8,0},{16,24},{24,16},{1,9},{9,1},{17,25},{25,17},{2,10},{10... | collective-permute-start | bytes 589832 | tf_op jit(solution)/shard_map/ppermute | solution.py:240
  19.6 11.4 %all-to-all-start.1 = ((f32[8,24,128]{2,1,0:T(8,128)}), f32[8,24,128]{2,1,0:T(8,128)S(1)}, u32[]{:S(2)}, u32[]{:S(2)}) async-start(f32[8,24,128]{2,1,0:T(8,128)} %span.1.refs_1_), calls=%async_computation.1 | async-start | bytes 196608 | tf_op jit(solution)/shard_map/all_to_all | solution.py:243

commit v5 on v4

v5 whole, which is shorter than its diff:
```python
import functools
import math

import jax
import jax.numpy as jnp
from jax import lax
from jax.experimental import pallas as pl
from jax.experimental.pallas import tpu as pltpu
from jax.sharding import PartitionSpec as P

viscosity = 0.4
lanes = 128

VMEM = pltpu.VMEM
SMEM = pltpu.SMEM


def halves(value):
    high = value.astype(jnp.bfloat16)
    low = (value - high.astype(jnp.float32)).astype(jnp.bfloat16)
    return high, low


def dot_split(left, right, transposed=False):
    dims = (((1,), (1 if transposed else 0,)), ((), ()))
    mul = functools.partial(lax.dot_general, dimension_numbers=dims, preferred_element_type=jnp.float32)
    lh, ll = halves(left)
    rh, rl = halves(right)
    return mul(lh, rh) + (mul(lh, rl) + mul(ll, rh))


def swap_blocks(parts, block):
    parts = list(parts)
    count = len(parts)
    lane = lax.broadcasted_iota(jnp.int32, parts[0].shape, 1) // block
    step = count // 2
    while step:
        low = (lane & step) == 0
        for i in range(count):
            if i & step:
                continue
            a, b = parts[i], parts[i | step]
            parts[i] = jnp.where(low, a, pltpu.roll(b, step * block, 1))
            parts[i | step] = jnp.where(low, pltpu.roll(a, lanes - step * block, 1), b)
        step //= 2
    return parts


def pack_kernel(comps, line, field, partner, *refs):
    outs, scratch = refs[:line], refs[line]
    block = field.shape[1] // line
    per = lanes // block
    depth = field.shape[0] // comps
    rows = depth // per
    my = lax.axis_index("col") // 2
    for i, source in enumerate((field, partner)):
        for comp in range(comps):
            at = (i * comps + comp) * rows
            for tile in range(line // per):
                across = slice(tile * lanes, (tile + 1) * lanes)
                parts = [source[comp * depth + q * rows : comp * depth + (q + 1) * rows, across] for q in range(per)]
                for p, part in enumerate(swap_blocks(parts, block)):
                    scratch[tile * per + p, at : at + rows] = part
    for s in range(line):
        outs[s][...] = scratch[my ^ s]


def span_kernel(comps, line, matrix, *refs):
    chunks, outs = refs[:line], refs[-line:]
    rows = outs[0].shape[0] // comps
    values = [
        jnp.concatenate(
            [chunk[(i * comps + comp) * rows : (i * comps + comp + 1) * rows] for chunk in chunks for i in range(2)],
            axis=0,
        )
        for comp in range(comps)
    ]
    right = jnp.concatenate(
        [jnp.concatenate([value, values[2] * value], axis=0) for value in values], axis=1
    )
    result = dot_split(matrix[...], right)
    for t in range(line):
        for comp in range(comps):
            outs[t][comp * rows : (comp + 1) * rows] = result[
                t * rows : (t + 1) * rows, comp * lanes : (comp + 1) * lanes
            ]


def circulant_rows(row, length):
    return pltpu.roll(jnp.broadcast_to(row, (length, length)), 0, 1, stride=1, stride_axis=0)


def stream_kernel(
    rows,
    cols,
    comps,
    slots,
    zloc,
    wall_counts,
    z_first,
    z_second,
    metric_table,
    metric_index,
    field,
    x_first,
    x_second,
    y_first,
    y_second,
    x_part,
    y_matrix,
    z_matrix,
    scaled,
):
    depth = slots * zloc
    length = field.shape[1]
    cells = y_first.shape[0]

    cells_z = cols * zloc
    shape = z_matrix.shape
    half = shape[1] // 2
    group = shape[0] // (cols // 2)
    my = lax.axis_index("col") // 2
    low = lax.axis_index("col") % 2
    r = lax.broadcasted_iota(jnp.int32, shape, 0)
    q = lax.broadcasted_iota(jnp.int32, shape, 1)
    q = jnp.where(q < half, q, q - half)
    out_cell = (2 * ((r // group) ^ my) + low) * zloc + r % zloc
    in_cell = (2 * ((q // (2 * group)) ^ my) + (((q // group) % 2) ^ low)) * zloc + q % zloc
    same = (r % group) // zloc == (q % group) // zloc
    gap = jnp.where(same, (in_cell - out_cell + cells_z) % cells_z, -1)
    side = lax.broadcasted_iota(jnp.int32, (1, shape[1]), 1) < half

    def fill(k, total):
        value = jnp.where(side, viscosity * z_second[k], -z_first[k])
        return jnp.where(gap == k, value, total)

    z_matrix[...] = lax.fori_loop(0, cells_z, fill, jnp.zeros(shape, jnp.float32), unroll=8)

    u = field[...]
    lead = u[:depth]
    left = jnp.concatenate(
        [u, jnp.concatenate([lead * u[c * depth : (c + 1) * depth] for c in range(comps)], axis=0)], axis=1
    )
    right = jnp.concatenate(
        [viscosity * circulant_rows(x_second[...], length), -circulant_rows(x_first[...], length)], axis=1
    )
    x_part[...] = dot_split(left, right, transposed=True)

    def scale(j, carry):
        scaled[pl.ds(j, 1), :] = y_first[pl.ds(j, 1), :] * -metric_table[metric_index[j]]
        return carry

    lax.fori_loop(0, cells, scale, 0, unroll=8)
    me = lax.axis_index("row")

    def start_of(index):
        return lax.fori_loop(0, rows, lambda i, acc: acc + jnp.where(i < index, wall_counts[i], 0), 0, unroll=True)

    own = lax.broadcasted_iota(jnp.int32, (depth, cells), 0) // zloc
    cell = lax.broadcasted_iota(jnp.int32, (depth, cells), 1)
    mine = ((own < wall_counts[me]) & (own + start_of(me) == cell)).astype(jnp.float32)
    exact = functools.partial(
        lax.dot_general, precision=lax.Precision.HIGHEST, preferred_element_type=jnp.float32
    )
    plain = (((1,), (0,)), ((), ()))
    turned = (((1,), (1,)), ((), ()))
    both = [exact(mine, viscosity * y_second[...], plain), exact(mine, scaled[...], plain)]
    r = lax.broadcasted_iota(jnp.int32, (depth, depth), 0) % zloc
    q = lax.broadcasted_iota(jnp.int32, (depth, depth), 1) % zloc
    match = r == q
    for b in range(rows):
        other = me ^ (2 * b if b < rows // 2 else 2 * b + 1 - rows)
        theirs = ((own < wall_counts[other]) & (own + start_of(other) == cell)).astype(jnp.float32)
        for k in range(2):
            block = jnp.where(match, exact(both[k], theirs, turned), 0.0)
            y_matrix[:, (2 * b + k) * depth : (2 * b + k + 1) * depth] = block


def wall_kernel(comps, matrix, x_part, *refs):
    fields, out = refs[:-1], refs[-1]
    depth = x_part.shape[0] // comps
    for comp in range(comps):
        at = slice(comp * depth, (comp + 1) * depth)
        stack = []
        for field in fields:
            value = field[at]
            stack += [value, field[depth : 2 * depth] * value]
        out[at] = x_part[at] + dot_split(matrix[...], jnp.concatenate(stack, axis=0))


def finish_kernel(comps, line, zloc, wall_counts, total, *refs):
    chunks, out, scratch = refs[:line], refs[line], refs[line + 1]
    block = out.shape[1] // line
    per = lanes // block
    depth = out.shape[0] // comps
    rows = depth // per
    my = lax.axis_index("col") // 2
    count = wall_counts[lax.axis_index("row")]
    for t in range(line):
        scratch[my ^ t] = chunks[t][...]
    for tile in range(line // per):
        across = slice(tile * lanes, (tile + 1) * lanes)
        for comp in range(comps):
            parts = [scratch[tile * per + p, comp * rows : (comp + 1) * rows] for p in range(per)]
            for q, part in enumerate(swap_blocks(parts, block)):
                at = slice(comp * depth + q * rows, comp * depth + (q + 1) * rows)
                plane = (lax.broadcasted_iota(jnp.int32, part.shape, 0) + q * rows) // zloc
                out[at, across] = jnp.where(plane < count, total[at, across] + part, 0.0)


def call(kernel, operands, spaces, results, name, scratch=()):
    results = [jax.ShapeDtypeStruct(shape, jnp.float32) for shape in results]
    held = sum(4 * math.prod(array.shape) for array in list(operands) + results)
    return pl.pallas_call(
        kernel,
        out_shape=results,
        in_specs=[pl.BlockSpec(memory_space=space) for space in spaces],
        out_specs=[pl.BlockSpec(memory_space=VMEM)] * len(results),
        scratch_shapes=[pltpu.VMEM(shape, jnp.float32) for shape in scratch],
        compiler_params=pltpu.CompilerParams(vmem_limit_bytes=(4 << 20) + 3 * held),
        name=name,
    )(*operands)


def local(
    velocity,
    wall_counts,
    x_first,
    x_second,
    y_first,
    y_second,
    z_first,
    z_second,
    metric_table,
    metric_index,
):
    rows = lax.axis_size("row")
    cols = lax.axis_size("col")
    comps, slots, zloc, length = velocity.shape
    depth = slots * zloc
    field = velocity.reshape(comps * depth, length)
    line = cols // 2
    group = depth // (lanes // (length // line))
    chunk = (comps * group, lanes)

    def along(value, step):
        return lax.ppermute(value, "col", [(i, i ^ step) for i in range(cols)])

    def across(value, step):
        return lax.ppermute(value, "row", [(i, i ^ step) for i in range(rows)])

    partner = along(field, 1)
    far = [across(field, step) for step in range(2, rows, 2)]
    near = across(field, 1)
    x_part, y_matrix, z_matrix = call(
        functools.partial(stream_kernel, rows, cols, comps, slots, zloc),
        [
            wall_counts,
            z_first,
            z_second,
            metric_table,
            metric_index,
            field,
            x_first.reshape(1, length),
            x_second.reshape(1, length),
            y_first,
            y_second,
        ],
        [SMEM] * 5 + [VMEM] * 5,
        [field.shape, (depth, 2 * rows * depth), (line * group, 4 * line * group)],
        "stream",
        [y_first.shape],
    )
    chunks = call(
        functools.partial(pack_kernel, comps, line),
        [field, partner],
        [VMEM] * 2,
        [(2 * comps * group, lanes)] * line,
        "pack",
        [(line, 2 * comps * group, lanes)],
    )
    received = [chunks[0]] + [along(chunks[s], 2 * s) for s in range(1, line)]
    parts = call(
        functools.partial(span_kernel, comps, line),
        [z_matrix] + received + far + [near],
        [VMEM] * (line + 1) + [pl.ANY] * (rows // 2),
        [chunk] * line,
        "span",
    )
    returned = [parts[0]] + [along(parts[t], 2 * t) for t in range(1, line)]
    (total,) = call(
        functools.partial(wall_kernel, comps),
        [y_matrix, x_part, field] + far + [near] + [across(value, 1) for value in far],
        [VMEM] * (rows + 2),
        [field.shape],
        "wall",
    )
    (result,) = call(
        functools.partial(finish_kernel, comps, line, zloc),
        [wall_counts, total] + returned,
        [SMEM] + [VMEM] * (line + 1),
        [field.shape],
        "finish",
        [(line,) + chunk],
    )
    return result.reshape(velocity.shape)


def solution(mesh):
    in_specs = (P(None, "row", "col", None), P(), P(), P(), P(), P(), P(), P(), P(), P())
    out_specs = P(None, "row", "col", None)
    return jax.shard_map(local, mesh=mesh, in_specs=in_specs, out_specs=out_specs, check_vma=False)
```

time: 32.8 us -> 27.7 us (0.84)
  waiting for transfers between devices: 11.6 us -> 8.4 us
  Pallas kernels: 5.93 us -> 4.11 us
    ppermute x2 -> x10, starting transfers between devices: 1.6 us -> 13.4 us  [the longest x7 10.5 us: along(): return lax.ppermute(value, 'col', [(i, i ^ step) for i in range(cols)])]
    all_to_all x2 -> x0, starting transfers between devices: 11.7 us -> none  [turn(): return lax.all_to_all(value, 'col', split_axis=0, concat_axis=0, tiled=True)]
    all_to_all x2 -> x0, waiting for transfers between devices: 8.51 us -> none  [turn(): return lax.all_to_all(value, 'col', split_axis=0, concat_axis=0, tiled=True)]
    ppermute x2 -> x10, waiting for transfers between devices: 3.1 us -> 8.4 us  [the longest x7 6.88 us: along(): return lax.ppermute(value, 'col', [(i, i ^ step) for i in range(cols)])]
    pallas_call x6 -> x5, Pallas kernels: 5.93 us -> 4.11 us  [call(): pl.pallas_call(kernel, out_shape=results, in_specs=[pl.BlockSpec(memory_s...]
  transfers between devices with their start and end apart: 4 -> 10, of which waited for: 3 -> 5; matrix products, arithmetic and copies ran while one was open for 0% -> 0% of each run, Pallas kernels for 3% -> 10%
where the time goes in v5:
time: 27.7 us; the launch traced here: 27.6 us
  starting transfers between devices  13.4 us (48%)
  waiting for transfers between devices  8.4 us (30%)
  Pallas kernels  4.11 us (15%)
  local copies, waits for them, and re-layouts  1.57 us (6%)
    ppermute x7, starting transfers between devices, along(): return lax.ppermute(value, 'col', [(i, i ^ step) for i in range(cols)])  10.5 us
    ppermute x7, waiting for transfers between devices, along(): return lax.ppermute(value, 'col', [(i, i ^ step) for i in range(cols)])  6.88 us
    pallas_call x5, Pallas kernels, call(): pl.pallas_call(kernel, out_shape=results, in_specs=[pl.BlockSpec(memory_s...  4.11 us
    ppermute x3, starting transfers between devices, across(): return lax.ppermute(value, 'row', [(i, i ^ step) for i in range(rows)])  2.97 us
    unnamed x22, local copies, waits for them, and re-layouts  1.57 us
    ppermute x3, waiting for transfers between devices, across(): return lax.ppermute(value, 'row', [(i, i ^ step) for i in range(rows)])  1.51 us
  transfers between devices with their start and end apart: 10, of which 5 were waited for; matrix products, arithmetic and copies ran while one was open for 0% of the time, Pallas kernels for 10%

profile of v5, /device:TPU:0, one launch (start us, length us, event | category | flops | bytes accessed | tf_op | source)
XLA Modules:
  0.0 27.6 jit_solution(17685807317407268452)
XLA Ops:
  0.0 3.0 %collective-permute-start = (f32[192,128]{1,0:T(8,128)}, f32[192,128]{1,0:T(8,128)S(1)}, u32[]{:S(2)}, u32[]{:S(2)}) collective-permute-start(f32[192,128]{1,0:T(8,128)} %bitcast.4), channel_id=1, source_target_pairs={{0,16},{8,24},{16,0},{24,8},{1,17},{9,25},{17,1},{25,9},{2,18},{10... | collective-permute-start | bytes 294920 | tf_op jit(solution)/shard_map/ppermute | solution.py:250
  3.0 1.5 %collective-permute-start.3 = (f32[192,128]{1,0:T(8,128)}, f32[192,128]{1,0:T(8,128)S(1)}, u32[]{:S(2)}, u32[]{:S(2)}) collective-permute-start(f32[192,128]{1,0:T(8,128)} %bitcast.5), channel_id=1, source_target_pairs={{0,1},{1,0},{2,3},{3,2},{4,5},{5,4},{6,7},{7,6},{8,9},{9,8},{10,11... | collective-permute-start | bytes 294920 | tf_op jit(solution)/shard_map/ppermute | solution.py:247
  4.5 1.5 %collective-permute-done.refs_1_.refs_4_ = f32[192,128]{1,0:T(8,128)S(1)} collective-permute-done((f32[192,128]{1,0:T(8,128)}, f32[192,128]{1,0:T(8,128)S(1)}, u32[]{:S(2)}, u32[]{:S(2)}) %collective-permute-start) | collective-permute-done | bytes 98336 | tf_op jit(solution)/shard_map/ppermute | solution.py:250
  6.0 1.8 %collective-permute-done.3.partner = f32[192,128]{1,0:T(8,128)S(1)} collective-permute-done((f32[192,128]{1,0:T(8,128)}, f32[192,128]{1,0:T(8,128)S(1)}, u32[]{:S(2)}, u32[]{:S(2)}) %collective-permute-start.3) | collective-permute-done | bytes 98336 | tf_op jit(solution)/shard_map/ppermute | solution.py:247
  7.8 0.9 %copy-done = f32[3,16,4,128]{3,2,1,0:T(4,128)S(1)} copy-done((f32[3,16,4,128]{3,2,1,0:T(4,128)S(1)}, f32[3,16,4,128]{3,2,1,0:T(4,128)}, u32[]{:S(2)}) %copy-start) | copy-done | bytes 98328
  8.7 0.2 pack.1
  8.9 1.6 %collective-permute-start.4 = (f32[96,128]{1,0:T(8,128)S(1)}, f32[96,128]{1,0:T(8,128)S(1)}, u32[]{:S(2)}, u32[]{:S(2)}) collective-permute-start(f32[96,128]{1,0:T(8,128)S(1)} %get-tuple-element.20), channel_id=1, source_target_pairs={{0,2},{1,3},{2,0},{3,1},{4,6},{5,7},{6,4},{7,5},{8,10},{9,11},{10,... | collective-permute-start | bytes 147464 | tf_op jit(solution)/shard_map/ppermute | solution.py:247
  10.5 2.6 %collective-permute-start.5 = (f32[96,128]{1,0:T(8,128)S(1)}, f32[96,128]{1,0:T(8,128)S(1)}, u32[]{:S(2)}, u32[]{:S(2)}) collective-permute-start(f32[96,128]{1,0:T(8,128)S(1)} %get-tuple-element.21), channel_id=1, source_target_pairs={{0,4},{1,5},{2,6},{3,7},{4,0},{5,1},{6,2},{7,3},{8,12},{9,13},{10,... | collective-permute-start | bytes 147464 | tf_op jit(solution)/shard_map/ppermute | solution.py:247
  13.1 0.3 %collective-permute-start.6 = (f32[96,128]{1,0:T(8,128)S(1)}, f32[96,128]{1,0:T(8,128)S(1)}, u32[]{:S(2)}, u32[]{:S(2)}) collective-permute-start(f32[96,128]{1,0:T(8,128)S(1)} %get-tuple-element.22), channel_id=1, source_target_pairs={{0,6},{1,7},{2,4},{3,5},{4,2},{5,3},{6,0},{7,1},{8,14},{9,15},{10,... | collective-permute-start | bytes 147464 | tf_op jit(solution)/shard_map/ppermute | solution.py:247
  13.5 0.3 %copy-done.7 = f32[64]{0:T(128)S(1)} copy-done((f32[64]{0:T(128)S(1)}, f32[64]{0:T(128)}, u32[]{:S(2)}) %copy-start.7) | copy-done | bytes 280
  13.8 0.0 copy-done.8
  13.8 0.0 copy-done.9
  13.8 0.2 copy-done.4
  14.1 2.0 %stream.1 = (f32[192,128]{1,0:T(8,128)S(1)}, f32[64,512]{1,0:T(8,128)S(1)}, f32[64,256]{1,0:T(8,128)S(1)}) custom-call(s32[4]{0:T(128)S(1)} %copy-done.4, f32[32]{0:T(128)S(1)} %copy-done.5, f32[32]{0:T(128)S(1)} %copy-done.6, f32[64]{0:T(128)S(1)} %copy-done.7, s32[32]{0:T(128)S(1)} %copy-done.8, f32[192,128]{1,0:T(8,128)S(1)} %bitcast.8, ...), custom_call_target="tpu_custom_call" | custom-call | tf_op jit(solution)/shard_map/stream/pallas_call | solution.py:214
  16.1 0.5 %collective-permute-done.5.refs_2_ = f32[96,128]{1,0:T(8,128)S(1)} collective-permute-done((f32[96,128]{1,0:T(8,128)S(1)}, f32[96,128]{1,0:T(8,128)S(1)}, u32[]{:S(2)}, u32[]{:S(2)}) %collective-permute-start.5) | collective-permute-done | bytes 49184 | tf_op jit(solution)/shard_map/ppermute | solution.py:247
  16.6 2.7 %collective-permute-done.6.refs_3_ = f32[96,128]{1,0:T(8,128)S(1)} collective-permute-done((f32[96,128]{1,0:T(8,128)S(1)}, f32[96,128]{1,0:T(8,128)S(1)}, u32[]{:S(2)}, u32[]{:S(2)}) %collective-permute-start.6) | collective-permute-done | bytes 49184 | tf_op jit(solution)/shard_map/ppermute | solution.py:247
  19.2 0.2 span.1
  19.5 0.1 collective-permute-start.7
  19.5 1.0 %collective-permute-start.8 = (f32[48,128]{1,0:T(8,128)S(1)}, f32[48,128]{1,0:T(8,128)S(1)}, u32[]{:S(2)}, u32[]{:S(2)}) collective-permute-start(f32[48,128]{1,0:T(8,128)S(1)} %get-tuple-element.25), channel_id=1, source_target_pairs={{0,4},{1,5},{2,6},{3,7},{4,0},{5,1},{6,2},{7,3},{8,12},{9,13},{10,... | collective-permute-start | bytes 73736 | tf_op jit(solution)/shard_map/ppermute | solution.py:247
  20.6 3.3 %collective-permute-start.9 = (f32[48,128]{1,0:T(8,128)S(1)}, f32[48,128]{1,0:T(8,128)S(1)}, u32[]{:S(2)}, u32[]{:S(2)}) collective-permute-start(f32[48,128]{1,0:T(8,128)S(1)} %get-tuple-element.26), channel_id=1, source_target_pairs={{0,6},{1,7},{2,4},{3,5},{4,2},{5,3},{6,0},{7,1},{8,14},{9,15},{10,... | collective-permute-start | bytes 73736 | tf_op jit(solution)/shard_map/ppermute | solution.py:247
  23.9 0.4 %wall.1.total = f32[192,128]{1,0:T(8,128)S(1)} custom-call(f32[64,512]{1,0:T(8,128)S(1)} %get-tuple-element.16.matrix, f32[192,128]{1,0:T(8,128)S(1)} %get-tuple-element.17.x_part, f32[192,128]{1,0:T(8,128)S(1)} %bitcast.9, f32[192,128]{1,0:T(8,128)S(1)} %collective-permute-done.refs_1_.refs_4_, f32[192,128]{1,0:T(8,128)S(1)} %collective-permute-done.1.refs_2_.refs_5_, ...), custom_call_target="tpu_custom_call" | custom-call | tf_op jit(solution)/shard_map/wall/pallas_call | solution.py:214
  24.3 0.0 collective-permute-done.8.refs_2_
  24.3 1.9 %collective-permute-done.9.refs_3_ = f32[48,128]{1,0:T(8,128)S(1)} collective-permute-done((f32[48,128]{1,0:T(8,128)S(1)}, f32[48,128]{1,0:T(8,128)S(1)}, u32[]{:S(2)}, u32[]{:S(2)}) %collective-permute-start.9) | collective-permute-done | bytes 24608 | tf_op jit(solution)/shard_map/ppermute | solution.py:247
  26.2 1.4 %finish.1 = f32[192,128]{1,0:T(8,128)} custom-call(s32[4]{0:T(128)S(1)} %copy-done.4, f32[192,128]{1,0:T(8,128)S(1)} %wall.1.total, f32[48,128]{1,0:T(8,128)S(1)} %get-tuple-element.23.refs_0_, f32[48,128]{1,0:T(8,128)S(1)} %collective-permute-done.7.refs_1_, f32[48,128]{1,0:T(8,128)S(1)} %collective-permute-done.8.refs_2_, ...), custom_call_target="tpu_custom_call" | custom-call | tf_op jit(solution)/shard_map/finish/pallas_call | solution.py:214
  (23 shorter events, 0.1 us)
Async XLA Ops:
  0.0 6.0 %collective-permute-start = (f32[192,128]{1,0:T(8,128)}, f32[192,128]{1,0:T(8,128)S(1)}, u32[]{:S(2)}, u32[]{:S(2)}) collective-permute-start(f32[192,128]{1,0:T(8,128)} %bitcast.4), channel_id=1, source_target_pairs={{0,16},{8,24},{16,0},{24,8},{1,17},{9,25},{17,1},{25,9},{2,18},{10... | collective-permute-start | bytes 294920 | tf_op jit(solution)/shard_map/ppermute | solution.py:250
  3.0 4.8 %collective-permute-start.3 = (f32[192,128]{1,0:T(8,128)}, f32[192,128]{1,0:T(8,128)S(1)}, u32[]{:S(2)}, u32[]{:S(2)}) collective-permute-start(f32[192,128]{1,0:T(8,128)} %bitcast.5), channel_id=1, source_target_pairs={{0,1},{1,0},{2,3},{3,2},{4,5},{5,4},{6,7},{7,6},{8,9},{9,8},{10,11... | collective-permute-start | bytes 294920 | tf_op jit(solution)/shard_map/ppermute | solution.py:247
  4.5 11.6 %collective-permute-start.1 = (f32[192,128]{1,0:T(8,128)}, f32[192,128]{1,0:T(8,128)S(1)}, u32[]{:S(2)}, u32[]{:S(2)}) collective-permute-start(f32[192,128]{1,0:T(8,128)} %bitcast.6), channel_id=1, source_target_pairs={{0,8},{8,0},{16,24},{24,16},{1,9},{9,1},{17,25},{25,17},{2,10},{10... | collective-permute-start | bytes 294920 | tf_op jit(solution)/shard_map/ppermute | solution.py:250
  6.0 18.0 %collective-permute-start.2 = (f32[192,128]{1,0:T(8,128)S(1)}, f32[192,128]{1,0:T(8,128)S(1)}, u32[]{:S(2)}, u32[]{:S(2)}) collective-permute-start(f32[192,128]{1,0:T(8,128)S(1)} %collective-permute-done.refs_1_.refs_4_), channel_id=1, source_target_pairs={{0,8},{8,0},{16,24},{24,16},{1,9},{9,1},{17,25},{25,17},{2,10},{10... | collective-permute-start | bytes 294920 | tf_op jit(solution)/shard_map/ppermute | solution.py:250
  7.8 0.9 %copy-start = (f32[3,16,4,128]{3,2,1,0:T(4,128)S(1)}, f32[3,16,4,128]{3,2,1,0:T(4,128)}, u32[]{:S(2)}) copy-start(f32[3,16,4,128]{3,2,1,0:T(4,128)} %param.10) | copy-start | bytes 294916
  8.7 4.8 %copy-start.1 = (f32[3,16,4,128]{3,2,1,0:T(4,128)S(1)}, f32[3,16,4,128]{3,2,1,0:T(4,128)}, u32[]{:S(2)}) copy-start(f32[3,16,4,128]{3,2,1,0:T(4,128)} %param.10) | copy-start | bytes 294916
  8.7 4.8 %copy-start.2 = (f32[32,32]{1,0:T(8,128)S(1)}, f32[32,32]{1,0:T(8,128)}, u32[]{:S(2)}) copy-start(f32[32,32]{1,0:T(8,128)} %y_first.1) | copy-start | bytes 12292
  8.7 4.8 %copy-start.3 = (f32[32,32]{1,0:T(8,128)S(1)}, f32[32,32]{1,0:T(8,128)}, u32[]{:S(2)}) copy-start(f32[32,32]{1,0:T(8,128)} %y_second.1) | copy-start | bytes 12292
  8.9 7.2 %collective-permute-start.4 = (f32[96,128]{1,0:T(8,128)S(1)}, f32[96,128]{1,0:T(8,128)S(1)}, u32[]{:S(2)}, u32[]{:S(2)}) collective-permute-start(f32[96,128]{1,0:T(8,128)S(1)} %get-tuple-element.20), channel_id=1, source_target_pairs={{0,2},{1,3},{2,0},{3,1},{4,6},{5,7},{6,4},{7,5},{8,10},{9,11},{10,... | collective-permute-start | bytes 147464 | tf_op jit(solution)/shard_map/ppermute | solution.py:247
  10.5 6.0 %collective-permute-start.5 = (f32[96,128]{1,0:T(8,128)S(1)}, f32[96,128]{1,0:T(8,128)S(1)}, u32[]{:S(2)}, u32[]{:S(2)}) collective-permute-start(f32[96,128]{1,0:T(8,128)S(1)} %get-tuple-element.21), channel_id=1, source_target_pairs={{0,4},{1,5},{2,6},{3,7},{4,0},{5,1},{6,2},{7,3},{8,12},{9,13},{10,... | collective-permute-start | bytes 147464 | tf_op jit(solution)/shard_map/ppermute | solution.py:247
  13.1 0.7 %copy-start.7 = (f32[64]{0:T(128)S(1)}, f32[64]{0:T(128)}, u32[]{:S(2)}) copy-start(f32[64]{0:T(128)} %metric_table.1) | copy-start | bytes 772
  13.1 0.7 %copy-start.8 = (s32[32]{0:T(128)S(1)}, s32[32]{0:T(128)}, u32[]{:S(2)}) copy-start(s32[32]{0:T(128)} %metric_index.1) | copy-start | bytes 388
  13.1 0.7 %copy-start.9 = (f32[128]{0:T(128)S(1)}, f32[128]{0:T(128)}, u32[]{:S(2)}) copy-start(f32[128]{0:T(128)} %param.12) | copy-start | bytes 1540
  13.1 0.7 %copy-start.10 = (f32[128]{0:T(128)S(1)}, f32[128]{0:T(128)}, u32[]{:S(2)}) copy-start(f32[128]{0:T(128)} %param.13) | copy-start | bytes 1540
  13.1 6.1 %collective-permute-start.6 = (f32[96,128]{1,0:T(8,128)S(1)}, f32[96,128]{1,0:T(8,128)S(1)}, u32[]{:S(2)}, u32[]{:S(2)}) collective-permute-start(f32[96,128]{1,0:T(8,128)S(1)} %get-tuple-element.22), channel_id=1, source_target_pairs={{0,6},{1,7},{2,4},{3,5},{4,2},{5,3},{6,0},{7,1},{8,14},{9,15},{10,... | collective-permute-start | bytes 147464 | tf_op jit(solution)/shard_map/ppermute | solution.py:247
  13.4 0.7 %copy-start.4 = (s32[4]{0:T(128)S(1)}, s32[4]{0:T(128)}, u32[]{:S(2)}) copy-start(s32[4]{0:T(128)} %wall_counts.3) | copy-start | bytes 52
  13.4 0.7 %copy-start.5 = (f32[32]{0:T(128)S(1)}, f32[32]{0:T(128)}, u32[]{:S(2)}) copy-start(f32[32]{0:T(128)} %z_first.1) | copy-start | bytes 388
  13.4 0.7 %copy-start.6 = (f32[32]{0:T(128)S(1)}, f32[32]{0:T(128)}, u32[]{:S(2)}) copy-start(f32[32]{0:T(128)} %z_second.1) | copy-start | bytes 388
  19.5 4.8 %collective-permute-start.7 = (f32[48,128]{1,0:T(8,128)S(1)}, f32[48,128]{1,0:T(8,128)S(1)}, u32[]{:S(2)}, u32[]{:S(2)}) collective-permute-start(f32[48,128]{1,0:T(8,128)S(1)} %get-tuple-element.24), channel_id=1, source_target_pairs={{0,2},{1,3},{2,0},{3,1},{4,6},{5,7},{6,4},{7,5},{8,10},{9,11},{10,... | collective-permute-start | bytes 73736 | tf_op jit(solution)/shard_map/ppermute | solution.py:247
  19.5 4.8 %collective-permute-start.8 = (f32[48,128]{1,0:T(8,128)S(1)}, f32[48,128]{1,0:T(8,128)S(1)}, u32[]{:S(2)}, u32[]{:S(2)}) collective-permute-start(f32[48,128]{1,0:T(8,128)S(1)} %get-tuple-element.25), channel_id=1, source_target_pairs={{0,4},{1,5},{2,6},{3,7},{4,0},{5,1},{6,2},{7,3},{8,12},{9,13},{10,... | collective-permute-start | bytes 73736 | tf_op jit(solution)/shard_map/ppermute | solution.py:247
  20.6 5.6 %collective-permute-start.9 = (f32[48,128]{1,0:T(8,128)S(1)}, f32[48,128]{1,0:T(8,128)S(1)}, u32[]{:S(2)}, u32[]{:S(2)}) collective-permute-start(f32[48,128]{1,0:T(8,128)S(1)} %get-tuple-element.26), channel_id=1, source_target_pairs={{0,6},{1,7},{2,4},{3,5},{4,2},{5,3},{6,0},{7,1},{8,14},{9,15},{10,... | collective-permute-start | bytes 73736 | tf_op jit(solution)/shard_map/ppermute | solution.py:247

commit v6 on v5

--- a/solution.py
+++ b/solution.py
@@ -46,44 +46,50 @@
     return parts
 
 
-def pack_kernel(comps, line, field, partner, *refs):
+def pack_kernel(comps, line, field, *refs):
     outs, scratch = refs[:line], refs[line]
     block = field.shape[1] // line
     per = lanes // block
     depth = field.shape[0] // comps
     rows = depth // per
     my = lax.axis_index("col") // 2
-    for i, source in enumerate((field, partner)):
-        for comp in range(comps):
-            at = (i * comps + comp) * rows
-            for tile in range(line // per):
-                across = slice(tile * lanes, (tile + 1) * lanes)
-                parts = [source[comp * depth + q * rows : comp * depth + (q + 1) * rows, across] for q in range(per)]
-                for p, part in enumerate(swap_blocks(parts, block)):
-                    scratch[tile * per + p, at : at + rows] = part
+    for comp in range(comps):
+        for tile in range(line // per):
+            across = slice(tile * lanes, (tile + 1) * lanes)
+            parts = [field[comp * depth + q * rows : comp * depth + (q + 1) * rows, across] for q in range(per)]
+            for p, part in enumerate(swap_blocks(parts, block)):
+                scratch[tile * per + p, comp * rows : (comp + 1) * rows] = part
     for s in range(line):
         outs[s][...] = scratch[my ^ s]
 
 
-def span_kernel(comps, line, matrix, *refs):
-    chunks, outs = refs[:line], refs[-line:]
-    rows = outs[0].shape[0] // comps
+def span_kernel(comps, line, matrix, mask, *refs):
+    chunks, (ours, theirs, pair) = refs[:line], refs[-3:]
+    for i in range(pair.shape[0]):
+        pair[i] = refs[line + i][...]
+    group = mask.shape[0]
     values = [
-        jnp.concatenate(
-            [chunk[(i * comps + comp) * rows : (i * comps + comp + 1) * rows] for chunk in chunks for i in range(2)],
-            axis=0,
-        )
+        jnp.concatenate([chunk[comp * group : (comp + 1) * group] for chunk in chunks], axis=0)
         for comp in range(comps)
     ]
     right = jnp.concatenate(
         [jnp.concatenate([value, values[2] * value], axis=0) for value in values], axis=1
     )
     result = dot_split(matrix[...], right)
+    live = jnp.concatenate([mask[...]] * line, axis=0)
+    side = line * group
+    for comp in range(comps):
+        across = slice(comp * lanes, (comp + 1) * lanes)
+        ours[comp] = live * result[:side, across]
+        theirs[comp] = live * result[side:, across]
+
+
+def add_kernel(comps, line, ours, met, after, *outs):
+    group = ours.shape[1] // line
     for t in range(line):
         for comp in range(comps):
-            outs[t][comp * rows : (comp + 1) * rows] = result[
-                t * rows : (t + 1) * rows, comp * lanes : (comp + 1) * lanes
-            ]
+            at = slice(t * group, (t + 1) * group)
+            outs[t][comp * group : (comp + 1) * group] = ours[comp, at] + met[comp, at]
 
 
 def circulant_rows(row, length):
@@ -106,35 +112,45 @@
     x_second,
     y_first,
     y_second,
+    after,
     x_part,
     y_matrix,
     z_matrix,
+    mask,
     scaled,
 ):
     depth = slots * zloc
     length = field.shape[1]
     cells = y_first.shape[0]
+    me = lax.axis_index("row")
 
     cells_z = cols * zloc
+    group = mask.shape[0]
     shape = z_matrix.shape
     half = shape[1] // 2
-    group = shape[0] // (cols // 2)
+    side = shape[0] // 2
     my = lax.axis_index("col") // 2
     low = lax.axis_index("col") % 2
     r = lax.broadcasted_iota(jnp.int32, shape, 0)
     q = lax.broadcasted_iota(jnp.int32, shape, 1)
+    other = jnp.where(r < side, low, 1 - low)
+    r = jnp.where(r < side, r, r - side)
     q = jnp.where(q < half, q, q - half)
-    out_cell = (2 * ((r // group) ^ my) + low) * zloc + r % zloc
-    in_cell = (2 * ((q // (2 * group)) ^ my) + (((q // group) % 2) ^ low)) * zloc + q % zloc
+    out_cell = (2 * ((r // group) ^ my) + other) * zloc + r % zloc
+    in_cell = (2 * ((q // group) ^ my) + low) * zloc + q % zloc
     same = (r % group) // zloc == (q % group) // zloc
     gap = jnp.where(same, (in_cell - out_cell + cells_z) % cells_z, -1)
-    side = lax.broadcasted_iota(jnp.int32, (1, shape[1]), 1) < half
+    kind = lax.broadcasted_iota(jnp.int32, (1, shape[1]), 1) < half
 
     def fill(k, total):
-        value = jnp.where(side, viscosity * z_second[k], -z_first[k])
+        value = jnp.where(kind, viscosity * z_second[k], -z_first[k])
         return jnp.where(gap == k, value, total)
 
     z_matrix[...] = lax.fori_loop(0, cells_z, fill, jnp.zeros(shape, jnp.float32), unroll=8)
+    per = depth // group
+    plane = lax.broadcasted_iota(jnp.int32, mask.shape, 0) // zloc
+    plane += lax.broadcasted_iota(jnp.int32, mask.shape, 1) // (lanes // per) * (group // zloc)
+    mask[...] = (plane < wall_counts[me]).astype(jnp.float32)
 
     u = field[...]
     lead = u[:depth]
@@ -144,14 +160,14 @@
     right = jnp.concatenate(
         [viscosity * circulant_rows(x_second[...], length), -circulant_rows(x_first[...], length)], axis=1
     )
-    x_part[...] = dot_split(left, right, transposed=True)
+    plane = lax.broadcasted_iota(jnp.int32, field.shape, 0) % depth // zloc
+    x_part[...] = jnp.where(plane < wall_counts[me], dot_split(left, right, transposed=True), 0.0)
 
     def scale(j, carry):
         scaled[pl.ds(j, 1), :] = y_first[pl.ds(j, 1), :] * -metric_table[metric_index[j]]
         return carry
 
     lax.fori_loop(0, cells, scale, 0, unroll=8)
-    me = lax.axis_index("row")
 
     def start_of(index):
         return lax.fori_loop(0, rows, lambda i, acc: acc + jnp.where(i < index, wall_counts[i], 0), 0, unroll=True)
@@ -176,26 +192,25 @@
             y_matrix[:, (2 * b + k) * depth : (2 * b + k + 1) * depth] = block
 
 
-def wall_kernel(comps, matrix, x_part, *refs):
-    fields, out = refs[:-1], refs[-1]
+def wall_kernel(comps, matrix, x_part, ours, theirs, out):
     depth = x_part.shape[0] // comps
     for comp in range(comps):
         at = slice(comp * depth, (comp + 1) * depth)
         stack = []
-        for field in fields:
-            value = field[at]
-            stack += [value, field[depth : 2 * depth] * value]
+        for fields in (ours, theirs):
+            for i in range(fields.shape[0]):
+                value = fields[i, at]
+                stack += [value, fields[i, depth : 2 * depth] * value]
         out[at] = x_part[at] + dot_split(matrix[...], jnp.concatenate(stack, axis=0))
 
 
-def finish_kernel(comps, line, zloc, wall_counts, total, *refs):
+def finish_kernel(comps, line, total, *refs):
     chunks, out, scratch = refs[:line], refs[line], refs[line + 1]
     block = out.shape[1] // line
     per = lanes // block
     depth = out.shape[0] // comps
     rows = depth // per
     my = lax.axis_index("col") // 2
-    count = wall_counts[lax.axis_index("row")]
     for t in range(line):
         scratch[my ^ t] = chunks[t][...]
     for tile in range(line // per):
@@ -204,8 +219,7 @@
             parts = [scratch[tile * per + p, comp * rows : (comp + 1) * rows] for p in range(per)]
             for q, part in enumerate(swap_blocks(parts, block)):
                 at = slice(comp * depth + q * rows, comp * depth + (q + 1) * rows)
-                plane = (lax.broadcasted_iota(jnp.int32, part.shape, 0) + q * rows) // zloc
-                out[at, across] = jnp.where(plane < count, total[at, across] + part, 0.0)
+                out[at, across] = total[at, across] + part
 
 
 def call(kernel, operands, spaces, results, name, scratch=()):
@@ -249,10 +263,12 @@
     def across(value, step):
         return lax.ppermute(value, "row", [(i, i ^ step) for i in range(rows)])
 
-    partner = along(field, 1)
     far = [across(field, step) for step in range(2, rows, 2)]
-    near = across(field, 1)
-    x_part, y_matrix, z_matrix = call(
+    chunks = call(functools.partial(pack_kernel, comps, line), [field], [VMEM], [chunk] * line, "pack", [(line,) + chunk])
+    received = [chunks[0]] + [None] * (line - 1)
+    for s in reversed(range(1, line)):
+        received[s] = along(chunks[s], 2 * s)
+    x_part, y_matrix, z_matrix, mask = call(
         functools.partial(stream_kernel, rows, cols, comps, slots, zloc),
         [
             wall_counts,
@@ -265,40 +281,39 @@
             x_second.reshape(1, length),
             y_first,
             y_second,
+            chunks[0],
         ],
-        [SMEM] * 5 + [VMEM] * 5,
-        [field.shape, (depth, 2 * rows * depth), (line * group, 4 * line * group)],
+        [SMEM] * 5 + [VMEM] * 5 + [pl.ANY],
+        [field.shape, (depth, 2 * rows * depth), (2 * line * group, 2 * line * group), (group, lanes)],
         "stream",
         [y_first.shape],
     )
-    chunks = call(
-        functools.partial(pack_kernel, comps, line),
-        [field, partner],
-        [VMEM] * 2,
-        [(2 * comps * group, lanes)] * line,
-        "pack",
-        [(line, 2 * comps * group, lanes)],
-    )
-    received = [chunks[0]] + [along(chunks[s], 2 * s) for s in range(1, line)]
+    ours, theirs, pair = call(
+        functools.partial(span_kernel, comps, line),
+        [z_matrix, mask] + received + [field] + far,
+        [VMEM] * (line + 2 + rows // 2),
+        [(comps, line * group, lanes)] * 2 + [(rows // 2,) + field.shape],
+        "span",
+    )
+    met = along(theirs, 1)
+    other = across(pair, 1)
+    (total,) = call(
+        functools.partial(wall_kernel, comps), [y_matrix, x_part, pair, other], [VMEM] * 4, [field.shape], "wall"
+    )
     parts = call(
-        functools.partial(span_kernel, comps, line),
-        [z_matrix] + received + far + [near],
-        [VMEM] * (line + 1) + [pl.ANY] * (rows // 2),
+        functools.partial(add_kernel, comps, line),
+        [ours, met, total],
+        [VMEM] * 2 + [pl.ANY],
         [chunk] * line,
-        "span",
-    )
-    returned = [parts[0]] + [along(parts[t], 2 * t) for t in range(1, line)]
-    (total,) = call(
-        functools.partial(wall_kernel, comps),
-        [y_matrix, x_part, field] + far + [near] + [across(value, 1) for value in far],
-        [VMEM] * (rows + 2),
-        [field.shape],
-        "wall",
-    )
+        "add",
+    )
+    returned = [parts[0]] + [None] * (line - 1)
+    for t in reversed(range(1, line)):
+        returned[t] = along(parts[t], 2 * t)
     (result,) = call(
-        functools.partial(finish_kernel, comps, line, zloc),
-        [wall_counts, total] + returned,
-        [SMEM] + [VMEM] * (line + 1),
+        functools.partial(finish_kernel, comps, line),
+        [total] + returned,
+        [VMEM] * (line + 1),
         [field.shape],
         "finish",
         [(line,) + chunk],

time: 27.7 us -> 29.4 us (1.061)
  local copies, waits for them, and re-layouts: 1.57 us -> 3.07 us
  Pallas kernels: 4.11 us -> 3.63 us
  waiting for transfers between devices: 8.4 us -> 8.72 us
    ppermute x7, waiting for transfers between devices: 6.88 us -> 8.72 us  [along(): return lax.ppermute(value, 'col', [(i, i ^ step) for i in range(cols)])]
    ppermute x3 -> x2, waiting for transfers between devices: 1.51 us -> 0.01 us  [across(): return lax.ppermute(value, 'row', [(i, i ^ step) for i in range(rows)])]
    unnamed x22, local copies, waits for them, and re-layouts: 1.57 us -> 3.07 us
    pallas_call x5 -> x6, Pallas kernels: 4.11 us -> 3.63 us  [call(): pl.pallas_call(kernel, out_shape=results, in_specs=[pl.BlockSpec(memory_s...]
    ppermute x3 -> x2, starting transfers between devices: 2.97 us -> 3.04 us  [across(): return lax.ppermute(value, 'row', [(i, i ^ step) for i in range(rows)])]
  transfers between devices with their start and end apart: 10 -> 9, of which waited for: 5 -> 4; matrix products, arithmetic and copies ran while one was open for 0% -> 0% of each run, Pallas kernels for 10% -> 9%
where the time goes in v6:
time: 29.4 us; the launch traced here: 29 us
  starting transfers between devices  13.5 us (46%)
  waiting for transfers between devices  8.72 us (30%)
  Pallas kernels  3.63 us (12%)
  local copies, waits for them, and re-layouts  3.07 us (10%)
    ppermute x7, starting transfers between devices, along(): return lax.ppermute(value, 'col', [(i, i ^ step) for i in range(cols)])  10.5 us
    ppermute x7, waiting for transfers between devices, along(): return lax.ppermute(value, 'col', [(i, i ^ step) for i in range(cols)])  8.72 us
    pallas_call x6, Pallas kernels, call(): pl.pallas_call(kernel, out_shape=results, in_specs=[pl.BlockSpec(memory_s...  3.63 us
    unnamed x22, local copies, waits for them, and re-layouts  3.07 us
    ppermute x2, starting transfers between devices, across(): return lax.ppermute(value, 'row', [(i, i ^ step) for i in range(rows)])  3.04 us
  transfers between devices with their start and end apart: 9, of which 4 were waited for; matrix products, arithmetic and copies ran while one was open for 0% of the time, Pallas kernels for 9%

profile of v6, /device:TPU:0, one launch (start us, length us, event | category | flops | bytes accessed | tf_op | source)
XLA Modules:
  0.0 29.0 jit_solution(3149781250742324345)
XLA Ops:
  0.0 3.0 %collective-permute-start.3 = (f32[192,128]{1,0:T(8,128)}, f32[192,128]{1,0:T(8,128)S(1)}, u32[]{:S(2)}, u32[]{:S(2)}) collective-permute-start(f32[192,128]{1,0:T(8,128)} %bitcast.4), channel_id=1, source_target_pairs={{0,16},{8,24},{16,0},{24,8},{1,17},{9,25},{17,1},{25,9},{2,18},{10... | collective-permute-start | bytes 294920 | tf_op jit(solution)/shard_map/ppermute | solution.py:264
  3.0 0.9 %copy-done = f32[3,16,4,128]{3,2,1,0:T(4,128)S(1)} copy-done((f32[3,16,4,128]{3,2,1,0:T(4,128)S(1)}, f32[3,16,4,128]{3,2,1,0:T(4,128)}, u32[]{:S(2)}) %copy-start) | copy-done | bytes 98328
  3.9 0.2 pack.1
  4.1 1.6 %collective-permute-start = (f32[48,128]{1,0:T(8,128)S(1)}, f32[48,128]{1,0:T(8,128)S(1)}, u32[]{:S(2)}, u32[]{:S(2)}) collective-permute-start(f32[48,128]{1,0:T(8,128)S(1)} %get-tuple-element.25), channel_id=1, source_target_pairs={{0,2},{1,3},{2,0},{3,1},{4,6},{5,7},{6,4},{7,5},{8,10},{9,11},{10,... | collective-permute-start | bytes 73736 | tf_op jit(solution)/shard_map/ppermute | solution.py:261
  5.7 2.6 %collective-permute-start.1 = (f32[48,128]{1,0:T(8,128)S(1)}, f32[48,128]{1,0:T(8,128)S(1)}, u32[]{:S(2)}, u32[]{:S(2)}) collective-permute-start(f32[48,128]{1,0:T(8,128)S(1)} %get-tuple-element.26), channel_id=1, source_target_pairs={{0,4},{1,5},{2,6},{3,7},{4,0},{5,1},{6,2},{7,3},{8,12},{9,13},{10,... | collective-permute-start | bytes 73736 | tf_op jit(solution)/shard_map/ppermute | solution.py:261
  8.3 0.2 collective-permute-start.2
  8.6 0.6 %copy-done.7 = f32[64]{0:T(128)S(1)} copy-done((f32[64]{0:T(128)S(1)}, f32[64]{0:T(128)}, u32[]{:S(2)}) %copy-start.7) | copy-done | bytes 280
  9.2 0.0 copy-done.8
  9.2 0.0 copy-done.9
  9.3 0.7 %copy-done.2 = f32[32,32]{1,0:T(8,128)S(1)} copy-done((f32[32,32]{1,0:T(8,128)S(1)}, f32[32,32]{1,0:T(8,128)}, u32[]{:S(2)}) %copy-start.2) | copy-done | bytes 4120
  10.0 0.7 %copy-done.3 = f32[32,32]{1,0:T(8,128)S(1)} copy-done((f32[32,32]{1,0:T(8,128)S(1)}, f32[32,32]{1,0:T(8,128)}, u32[]{:S(2)}) %copy-start.3) | copy-done | bytes 4120
  10.7 2.0 %stream.1 = (f32[192,128]{1,0:T(8,128)S(1)}, f32[64,512]{1,0:T(8,128)S(1)}, f32[128,128]{1,0:T(8,128)S(1)}, f32[16,128]{1,0:T(8,128)S(1)}) custom-call(s32[4]{0:T(128)S(1)} %copy-done.4, f32[32]{0:T(128)S(1)} %copy-done.5, f32[32]{0:T(128)S(1)} %copy-done.6, f32[64]{0:T(128)S(1)} %copy-done.7, s32[32]{0:T(128)S(1)} %copy-done.8, f32[192,128]{1,0:T(8,128)S(1)} %bitcast.6, ...), custom_call_target="tpu_custom_call" | custom-call | tf_op jit(solution)/shard_map/stream/pallas_call | solution.py:228
  12.8 1.2 %collective-permute-done.2.refs_3_ = f32[48,128]{1,0:T(8,128)S(1)} collective-permute-done((f32[48,128]{1,0:T(8,128)S(1)}, f32[48,128]{1,0:T(8,128)S(1)}, u32[]{:S(2)}, u32[]{:S(2)}) %collective-permute-start.2) | collective-permute-done | bytes 24608 | tf_op jit(solution)/shard_map/ppermute | solution.py:261
  13.9 0.2 span.1
  14.2 0.1 collective-permute-start.4
  14.3 1.6 %collective-permute-start.5 = (f32[3,64,128]{2,1,0:T(8,128)S(1)}, f32[3,64,128]{2,1,0:T(8,128)S(1)}, u32[]{:S(2)}, u32[]{:S(2)}) collective-permute-start(f32[3,64,128]{2,1,0:T(8,128)S(1)} %get-tuple-element.30), channel_id=1, source_target_pairs={{0,1},{1,0},{2,3},{3,2},{4,5},{5,4},{6,7},{7,6},{8,9},{9,8},{10,11... | collective-permute-start | bytes 294920 | tf_op jit(solution)/shard_map/ppermute | solution.py:261
  15.8 0.4 %wall.1.after.total = f32[192,128]{1,0:T(8,128)S(1)} custom-call(f32[64,512]{1,0:T(8,128)S(1)} %get-tuple-element.21.matrix, f32[192,128]{1,0:T(8,128)S(1)} %get-tuple-element.22.x_part, f32[2,192,128]{2,1,0:T(8,128)S(1)} %get-tuple-element.28.ours, f32[2,192,128]{2,1,0:T(8,128)S(1)} %collective-permute-done.4.theirs), custom_call_target="tpu_custom_call" | custom-call | tf_op jit(solution)/shard_map/wall/pallas_call | solution.py:228
  16.2 3.3 %collective-permute-done.5.met = f32[3,64,128]{2,1,0:T(8,128)S(1)} collective-permute-done((f32[3,64,128]{2,1,0:T(8,128)S(1)}, f32[3,64,128]{2,1,0:T(8,128)S(1)}, u32[]{:S(2)}, u32[]{:S(2)}) %collective-permute-start.5) | collective-permute-done | bytes 98336 | tf_op jit(solution)/shard_map/ppermute | solution.py:261
  19.5 0.1 collective-permute-start.6
  19.6 3.0 %collective-permute-start.7 = (f32[48,128]{1,0:T(8,128)S(1)}, f32[48,128]{1,0:T(8,128)S(1)}, u32[]{:S(2)}, u32[]{:S(2)}) collective-permute-start(f32[48,128]{1,0:T(8,128)S(1)} %get-tuple-element.33), channel_id=1, source_target_pairs={{0,4},{1,5},{2,6},{3,7},{4,0},{5,1},{6,2},{7,3},{8,12},{9,13},{10,... | collective-permute-start | bytes 73736 | tf_op jit(solution)/shard_map/ppermute | solution.py:261
  22.6 1.4 %collective-permute-start.8 = (f32[48,128]{1,0:T(8,128)S(1)}, f32[48,128]{1,0:T(8,128)S(1)}, u32[]{:S(2)}, u32[]{:S(2)}) collective-permute-start(f32[48,128]{1,0:T(8,128)S(1)} %get-tuple-element.34), channel_id=1, source_target_pairs={{0,6},{1,7},{2,4},{3,5},{4,2},{5,3},{6,0},{7,1},{8,14},{9,15},{10,... | collective-permute-start | bytes 73736 | tf_op jit(solution)/shard_map/ppermute | solution.py:261
  23.9 0.7 %collective-permute-done.7.refs_2_ = f32[48,128]{1,0:T(8,128)S(1)} collective-permute-done((f32[48,128]{1,0:T(8,128)S(1)}, f32[48,128]{1,0:T(8,128)S(1)}, u32[]{:S(2)}, u32[]{:S(2)}) %collective-permute-start.7) | collective-permute-done | bytes 24608 | tf_op jit(solution)/shard_map/ppermute | solution.py:261
  24.7 3.5 %collective-permute-done.8.refs_3_ = f32[48,128]{1,0:T(8,128)S(1)} collective-permute-done((f32[48,128]{1,0:T(8,128)S(1)}, f32[48,128]{1,0:T(8,128)S(1)}, u32[]{:S(2)}, u32[]{:S(2)}) %collective-permute-start.8) | collective-permute-done | bytes 24608 | tf_op jit(solution)/shard_map/ppermute | solution.py:261
  28.2 0.8 %finish.1 = f32[192,128]{1,0:T(8,128)} custom-call(f32[192,128]{1,0:T(8,128)S(1)} %wall.1.after.total, f32[48,128]{1,0:T(8,128)S(1)} %get-tuple-element.31.refs_0_, f32[48,128]{1,0:T(8,128)S(1)} %collective-permute-done.6.refs_1_, f32[48,128]{1,0:T(8,128)S(1)} %collective-permute-done.7.refs_2_, f32[48,128]{1,0:T(8,128)S(1)} %collective-permute-done.8.refs_3_), custom_call_target="tpu_custom_call" | custom-call | tf_op jit(solution)/shard_map/finish/pallas_call | solution.py:228
  (22 shorter events, 0.1 us)
Async XLA Ops:
  0.0 13.9 %collective-permute-start.3 = (f32[192,128]{1,0:T(8,128)}, f32[192,128]{1,0:T(8,128)S(1)}, u32[]{:S(2)}, u32[]{:S(2)}) collective-permute-start(f32[192,128]{1,0:T(8,128)} %bitcast.4), channel_id=1, source_target_pairs={{0,16},{8,24},{16,0},{24,8},{1,17},{9,25},{17,1},{25,9},{2,18},{10... | collective-permute-start | bytes 294920 | tf_op jit(solution)/shard_map/ppermute | solution.py:264
  3.0 0.9 %copy-start = (f32[3,16,4,128]{3,2,1,0:T(4,128)S(1)}, f32[3,16,4,128]{3,2,1,0:T(4,128)}, u32[]{:S(2)}) copy-start(f32[3,16,4,128]{3,2,1,0:T(4,128)} %param.10) | copy-start | bytes 294916
  3.9 4.7 %copy-start.1 = (f32[3,16,4,128]{3,2,1,0:T(4,128)S(1)}, f32[3,16,4,128]{3,2,1,0:T(4,128)}, u32[]{:S(2)}) copy-start(f32[3,16,4,128]{3,2,1,0:T(4,128)} %param.10) | copy-start | bytes 294916
  4.1 8.7 %collective-permute-start = (f32[48,128]{1,0:T(8,128)S(1)}, f32[48,128]{1,0:T(8,128)S(1)}, u32[]{:S(2)}, u32[]{:S(2)}) collective-permute-start(f32[48,128]{1,0:T(8,128)S(1)} %get-tuple-element.25), channel_id=1, source_target_pairs={{0,2},{1,3},{2,0},{3,1},{4,6},{5,7},{6,4},{7,5},{8,10},{9,11},{10,... | collective-permute-start | bytes 73736 | tf_op jit(solution)/shard_map/ppermute | solution.py:261
  5.7 7.0 %collective-permute-start.1 = (f32[48,128]{1,0:T(8,128)S(1)}, f32[48,128]{1,0:T(8,128)S(1)}, u32[]{:S(2)}, u32[]{:S(2)}) collective-permute-start(f32[48,128]{1,0:T(8,128)S(1)} %get-tuple-element.26), channel_id=1, source_target_pairs={{0,4},{1,5},{2,6},{3,7},{4,0},{5,1},{6,2},{7,3},{8,12},{9,13},{10,... | collective-permute-start | bytes 73736 | tf_op jit(solution)/shard_map/ppermute | solution.py:261
  8.3 5.6 %collective-permute-start.2 = (f32[48,128]{1,0:T(8,128)S(1)}, f32[48,128]{1,0:T(8,128)S(1)}, u32[]{:S(2)}, u32[]{:S(2)}) collective-permute-start(f32[48,128]{1,0:T(8,128)S(1)} %get-tuple-element.27), channel_id=1, source_target_pairs={{0,6},{1,7},{2,4},{3,5},{4,2},{5,3},{6,0},{7,1},{8,14},{9,15},{10,... | collective-permute-start | bytes 73736 | tf_op jit(solution)/shard_map/ppermute | solution.py:261
  8.5 0.7 %copy-start.7 = (f32[64]{0:T(128)S(1)}, f32[64]{0:T(128)}, u32[]{:S(2)}) copy-start(f32[64]{0:T(128)} %metric_table.1) | copy-start | bytes 772
  8.5 0.7 %copy-start.8 = (s32[32]{0:T(128)S(1)}, s32[32]{0:T(128)}, u32[]{:S(2)}) copy-start(s32[32]{0:T(128)} %metric_index.1) | copy-start | bytes 388
  8.5 0.7 %copy-start.9 = (f32[128]{0:T(128)S(1)}, f32[128]{0:T(128)}, u32[]{:S(2)}) copy-start(f32[128]{0:T(128)} %param.12) | copy-start | bytes 1540
  8.5 0.7 %copy-start.10 = (f32[128]{0:T(128)S(1)}, f32[128]{0:T(128)}, u32[]{:S(2)}) copy-start(f32[128]{0:T(128)} %param.13) | copy-start | bytes 1540
  8.5 0.7 %copy-start.4 = (s32[4]{0:T(128)S(1)}, s32[4]{0:T(128)}, u32[]{:S(2)}) copy-start(s32[4]{0:T(128)} %wall_counts.1) | copy-start | bytes 52
  8.6 0.7 %copy-start.5 = (f32[32]{0:T(128)S(1)}, f32[32]{0:T(128)}, u32[]{:S(2)}) copy-start(f32[32]{0:T(128)} %z_first.1) | copy-start | bytes 388
  8.6 0.7 %copy-start.6 = (f32[32]{0:T(128)S(1)}, f32[32]{0:T(128)}, u32[]{:S(2)}) copy-start(f32[32]{0:T(128)} %z_second.1) | copy-start | bytes 388
  9.3 0.7 %copy-start.2 = (f32[32,32]{1,0:T(8,128)S(1)}, f32[32,32]{1,0:T(8,128)}, u32[]{:S(2)}) copy-start(f32[32,32]{1,0:T(8,128)} %y_first.1) | copy-start | bytes 12292
  10.0 0.7 %copy-start.3 = (f32[32,32]{1,0:T(8,128)S(1)}, f32[32,32]{1,0:T(8,128)}, u32[]{:S(2)}) copy-start(f32[32,32]{1,0:T(8,128)} %y_second.1) | copy-start | bytes 12292
  14.2 1.6 %collective-permute-start.4 = (f32[2,192,128]{2,1,0:T(8,128)S(1)}, f32[2,192,128]{2,1,0:T(8,128)S(1)}, u32[]{:S(2)}, u32[]{:S(2)}) collective-permute-start(f32[2,192,128]{2,1,0:T(8,128)S(1)} %get-tuple-element.28.ours), channel_id=1, source_target_pairs={{0,8},{8,0},{16,24},{24,16},{1,9},{9,1},{17,25},{25,17},{2,10},{10... | collective-permute-start | bytes 589832 | tf_op jit(solution)/shard_map/ppermute | solution.py:264
  14.3 5.2 %collective-permute-start.5 = (f32[3,64,128]{2,1,0:T(8,128)S(1)}, f32[3,64,128]{2,1,0:T(8,128)S(1)}, u32[]{:S(2)}, u32[]{:S(2)}) collective-permute-start(f32[3,64,128]{2,1,0:T(8,128)S(1)} %get-tuple-element.30), channel_id=1, source_target_pairs={{0,1},{1,0},{2,3},{3,2},{4,5},{5,4},{6,7},{7,6},{8,9},{9,8},{10,11... | collective-permute-start | bytes 294920 | tf_op jit(solution)/shard_map/ppermute | solution.py:261
  19.5 4.5 %collective-permute-start.6 = (f32[48,128]{1,0:T(8,128)S(1)}, f32[48,128]{1,0:T(8,128)S(1)}, u32[]{:S(2)}, u32[]{:S(2)}) collective-permute-start(f32[48,128]{1,0:T(8,128)S(1)} %get-tuple-element.32), channel_id=1, source_target_pairs={{0,2},{1,3},{2,0},{3,1},{4,6},{5,7},{6,4},{7,5},{8,10},{9,11},{10,... | collective-permute-start | bytes 73736 | tf_op jit(solution)/shard_map/ppermute | solution.py:261
  19.6 5.1 %collective-permute-start.7 = (f32[48,128]{1,0:T(8,128)S(1)}, f32[48,128]{1,0:T(8,128)S(1)}, u32[]{:S(2)}, u32[]{:S(2)}) collective-permute-start(f32[48,128]{1,0:T(8,128)S(1)} %get-tuple-element.33), channel_id=1, source_target_pairs={{0,4},{1,5},{2,6},{3,7},{4,0},{5,1},{6,2},{7,3},{8,12},{9,13},{10,... | collective-permute-start | bytes 73736 | tf_op jit(solution)/shard_map/ppermute | solution.py:261
  22.6 5.6 %collective-permute-start.8 = (f32[48,128]{1,0:T(8,128)S(1)}, f32[48,128]{1,0:T(8,128)S(1)}, u32[]{:S(2)}, u32[]{:S(2)}) collective-permute-start(f32[48,128]{1,0:T(8,128)S(1)} %get-tuple-element.34), channel_id=1, source_target_pairs={{0,6},{1,7},{2,4},{3,5},{4,2},{5,3},{6,0},{7,1},{8,14},{9,15},{10,... | collective-permute-start | bytes 73736 | tf_op jit(solution)/shard_map/ppermute | solution.py:261

commit v7 on v5

v7 whole, which is shorter than its diff:
```python
import functools
import math

import jax
import jax.numpy as jnp
from jax import lax
from jax.experimental import pallas as pl
from jax.experimental.pallas import tpu as pltpu
from jax.sharding import PartitionSpec as P

viscosity = 0.4
quad = 4

VMEM = pltpu.VMEM
SMEM = pltpu.SMEM


def halves(value):
    high = value.astype(jnp.bfloat16)
    low = (value - high.astype(jnp.float32)).astype(jnp.bfloat16)
    return high, low


def dot_split(left, right, transposed=False):
    dims = (((1,), (1 if transposed else 0,)), ((), ()))
    mul = functools.partial(lax.dot_general, dimension_numbers=dims, preferred_element_type=jnp.float32)
    lh, ll = halves(left)
    rh, rl = halves(right)
    return mul(lh, rh) + (mul(lh, rl) + mul(ll, rh))


def span_kernel(comps, matrix, field, *refs):
    parts, pair = refs[-quad - 1 : -1], refs[-1]
    pair[0] = field[...]
    for i in range(1, pair.shape[0]):
        pair[i] = refs[i - 1][...]
    sources = (field,) + refs[pair.shape[0] - 1 : -quad - 1]
    depth, length = field.shape[0] // comps, field.shape[1]
    group = matrix.shape[0] // quad
    right = []
    for comp in range(comps):
        for at in range(0, depth, group):
            stack = [source[comp * depth + at : comp * depth + at + group] for source in sources]
            stack += [value * source[2 * depth + at : 2 * depth + at + group] for value, source in zip(stack, sources)]
            right.append(jnp.concatenate(stack, axis=0))
    result = dot_split(matrix[...], jnp.concatenate(right, axis=1))
    for t in range(quad):
        for i in range(len(right)):
            parts[t][i * group : (i + 1) * group] = result[
                t * group : (t + 1) * group, i * length : (i + 1) * length
            ]


def circulant_rows(row, length):
    return pltpu.roll(jnp.broadcast_to(row, (length, length)), 0, 1, stride=1, stride_axis=0)


def stream_kernel(
    rows,
    cols,
    comps,
    slots,
    zloc,
    wall_counts,
    z_first,
    z_second,
    metric_table,
    metric_index,
    field,
    x_first,
    x_second,
    y_first,
    y_second,
    x_part,
    y_matrix,
    z_matrix,
    mask,
    scaled,
):
    depth = slots * zloc
    length = field.shape[1]
    cells = y_first.shape[0]
    me = lax.axis_index("row")
    mask[...] = (lax.broadcasted_iota(jnp.int32, mask.shape, 0) // zloc < wall_counts[me]).astype(jnp.float32)

    cells_z = cols * zloc
    shape = z_matrix.shape
    half = shape[1] // 2
    group = shape[0] // quad
    mine = lax.axis_index("col")
    r = lax.broadcasted_iota(jnp.int32, shape, 0)
    q = lax.broadcasted_iota(jnp.int32, shape, 1)
    q = jnp.where(q < half, q, q - half)
    out_cell = ((r // group) ^ mine) * zloc + r % zloc
    in_cell = ((quad * (q // group)) ^ mine) * zloc + q % zloc
    same = (r % group) // zloc == (q % group) // zloc
    gap = jnp.where(same, (in_cell - out_cell + cells_z) % cells_z, -1)
    kind = lax.broadcasted_iota(jnp.int32, (1, shape[1]), 1) < half

    def fill(k, total):
        value = jnp.where(kind, viscosity * z_second[k], -z_first[k])
        return jnp.where(gap == k, value, total)

    z_matrix[...] = lax.fori_loop(0, cells_z, fill, jnp.zeros(shape, jnp.float32), unroll=8)

    u = field[...]
    lead = u[:depth]
    left = jnp.concatenate(
        [u, jnp.concatenate([lead * u[c * depth : (c + 1) * depth] for c in range(comps)], axis=0)], axis=1
    )
    right = jnp.concatenate(
        [viscosity * circulant_rows(x_second[...], length), -circulant_rows(x_first[...], length)], axis=1
    )
    x_part[...] = dot_split(left, right, transposed=True)

    def scale(j, carry):
        scaled[pl.ds(j, 1), :] = y_first[pl.ds(j, 1), :] * -metric_table[metric_index[j]]
        return carry

    lax.fori_loop(0, cells, scale, 0, unroll=8)

    def start_of(index):
        return lax.fori_loop(0, rows, lambda i, acc: acc + jnp.where(i < index, wall_counts[i], 0), 0, unroll=True)

    own = lax.broadcasted_iota(jnp.int32, (depth, cells), 0) // zloc
    cell = lax.broadcasted_iota(jnp.int32, (depth, cells), 1)
    mine = ((own < wall_counts[me]) & (own + start_of(me) == cell)).astype(jnp.float32)
    exact = functools.partial(
        lax.dot_general, precision=lax.Precision.HIGHEST, preferred_element_type=jnp.float32
    )
    plain = (((1,), (0,)), ((), ()))
    turned = (((1,), (1,)), ((), ()))
    both = [exact(mine, viscosity * y_second[...], plain), exact(mine, scaled[...], plain)]
    r = lax.broadcasted_iota(jnp.int32, (depth, depth), 0) % zloc
    q = lax.broadcasted_iota(jnp.int32, (depth, depth), 1) % zloc
    match = r == q
    for b in range(rows):
        other = me ^ (2 * b if b < rows // 2 else 2 * b + 1 - rows)
        theirs = ((own < wall_counts[other]) & (own + start_of(other) == cell)).astype(jnp.float32)
        for k in range(2):
            block = jnp.where(match, exact(both[k], theirs, turned), 0.0)
            y_matrix[:, (2 * b + k) * depth : (2 * b + k + 1) * depth] = block


def wall_kernel(comps, matrix, x_part, z_part, ours, theirs, out):
    depth = x_part.shape[0] // comps
    for comp in range(comps):
        at = slice(comp * depth, (comp + 1) * depth)
        stack = []
        for fields in (ours, theirs):
            for i in range(fields.shape[0]):
                value = fields[i, at]
                stack += [value, fields[i, depth : 2 * depth] * value]
        out[at] = x_part[at] + z_part[at] + dot_split(matrix[...], jnp.concatenate(stack, axis=0))


def finish_kernel(comps, mask, *refs):
    parts, out = refs[:-1], refs[-1]
    depth = mask.shape[0]
    for comp in range(comps):
        at = slice(comp * depth, (comp + 1) * depth)
        out[at] = jnp.where(mask[...] > 0, sum(part[at] for part in parts[1:]) + parts[0][at], 0.0)


def call(kernel, operands, spaces, results, name, scratch=()):
    results = [jax.ShapeDtypeStruct(shape, jnp.float32) for shape in results]
    held = sum(4 * math.prod(array.shape) for array in list(operands) + results)
    return pl.pallas_call(
        kernel,
        out_shape=results,
        in_specs=[pl.BlockSpec(memory_space=space) for space in spaces],
        out_specs=[pl.BlockSpec(memory_space=VMEM)] * len(results),
        scratch_shapes=[pltpu.VMEM(shape, jnp.float32) for shape in scratch],
        compiler_params=pltpu.CompilerParams(vmem_limit_bytes=(4 << 20) + 3 * held),
        name=name,
    )(*operands)


def local(
    velocity,
    wall_counts,
    x_first,
    x_second,
    y_first,
    y_second,
    z_first,
    z_second,
    metric_table,
    metric_index,
):
    rows = lax.axis_size("row")
    cols = lax.axis_size("col")
    comps, slots, zloc, length = velocity.shape
    depth = slots * zloc
    field = velocity.reshape(comps * depth, length)
    group = min(depth, 32)
    sources = cols // quad

    def along(value, step):
        return lax.ppermute(value, "col", [(i, i ^ step) for i in range(cols)])

    def across(value, step):
        return lax.ppermute(value, "row", [(i, i ^ step) for i in range(rows)])

    gathered = [along(field, quad * i) for i in range(1, sources)]
    far = [across(field, step) for step in range(2, rows, 2)]
    x_part, y_matrix, z_matrix, mask = call(
        functools.partial(stream_kernel, rows, cols, comps, slots, zloc),
        [
            wall_counts,
            z_first,
            z_second,
            metric_table,
            metric_index,
            field,
            x_first.reshape(1, length),
            x_second.reshape(1, length),
            y_first,
            y_second,
        ],
        [SMEM] * 5 + [VMEM] * 5,
        [field.shape, (depth, 2 * rows * depth), (quad * group, 2 * sources * group), (depth, length)],
        "stream",
        [y_first.shape],
    )
    *parts, pair = call(
        functools.partial(span_kernel, comps),
        [z_matrix, field] + far + gathered,
        [VMEM] * (rows // 2 + sources),
        [field.shape] * quad + [(rows // 2,) + field.shape],
        "span",
    )
    returned = [along(parts[t], t) for t in reversed(range(1, quad))]
    other = across(pair, 1)
    (total,) = call(
        functools.partial(wall_kernel, comps),
        [y_matrix, x_part, parts[0], pair, other],
        [VMEM] * 5,
        [field.shape],
        "wall",
    )
    (result,) = call(
        functools.partial(finish_kernel, comps),
        [mask, total] + returned,
        [VMEM] * (quad + 1),
        [field.shape],
        "finish",
    )
    return result.reshape(velocity.shape)


def solution(mesh):
    in_specs = (P(None, "row", "col", None), P(), P(), P(), P(), P(), P(), P(), P(), P())
    out_specs = P(None, "row", "col", None)
    return jax.shard_map(local, mesh=mesh, in_specs=in_specs, out_specs=out_specs, check_vma=False)
```

time: 27.7 us -> 20.4 us (0.74)
  starting transfers between devices: 13.4 us -> 9.18 us
  waiting for transfers between devices: 8.4 us -> 4.34 us
  local copies, waits for them, and re-layouts: 1.57 us -> 3.05 us
  Pallas kernels: 4.11 us -> 3.38 us
    ppermute x7 -> x4, starting transfers between devices: 10.5 us -> 7.59 us  [along(): return lax.ppermute(value, 'col', [(i, i ^ step) for i in range(cols)])]
    ppermute x7 -> x4, waiting for transfers between devices: 6.88 us -> 4.33 us  [along(): return lax.ppermute(value, 'col', [(i, i ^ step) for i in range(cols)])]
    ppermute x3 -> x2, waiting for transfers between devices: 1.51 us -> 0.01 us  [across(): return lax.ppermute(value, 'row', [(i, i ^ step) for i in range(rows)])]
    unnamed x22, local copies, waits for them, and re-layouts: 1.57 us -> 3.05 us
    ppermute x3 -> x2, starting transfers between devices: 2.97 us -> 1.59 us  [across(): return lax.ppermute(value, 'row', [(i, i ^ step) for i in range(rows)])]
    pallas_call x5 -> x4, Pallas kernels: 4.11 us -> 3.38 us  [call(): pl.pallas_call(kernel, out_shape=results, in_specs=[pl.BlockSpec(memory_s...]
  transfers between devices with their start and end apart: 10 -> 6, of which waited for: 5 -> 2; matrix products, arithmetic and copies ran while one was open for 0% -> 0% of each run, Pallas kernels for 10% -> 12%
where the time goes in v7:
time: 20.4 us; the launch traced here: 20 us
  starting transfers between devices  9.18 us (45%)
  waiting for transfers between devices  4.34 us (21%)
  Pallas kernels  3.38 us (17%)
  local copies, waits for them, and re-layouts  3.05 us (15%)
    ppermute x4, starting transfers between devices, along(): return lax.ppermute(value, 'col', [(i, i ^ step) for i in range(cols)])  7.59 us
    ppermute x4, waiting for transfers between devices, along(): return lax.ppermute(value, 'col', [(i, i ^ step) for i in range(cols)])  4.33 us
    pallas_call x4, Pallas kernels, call(): pl.pallas_call(kernel, out_shape=results, in_specs=[pl.BlockSpec(memory_s...  3.38 us
    unnamed x22, local copies, waits for them, and re-layouts  3.05 us
    ppermute x2, starting transfers between devices, across(): return lax.ppermute(value, 'row', [(i, i ^ step) for i in range(rows)])  1.59 us
  transfers between devices with their start and end apart: 6, of which 2 were waited for; matrix products, arithmetic and copies ran while one was open for 0% of the time, Pallas kernels for 12%

profile of v7, /device:TPU:0, one launch (start us, length us, event | category | flops | bytes accessed | tf_op | source)
XLA Modules:
  0.0 20.0 jit_solution(10010536059981610488)
XLA Ops:
  0.0 4.0 %collective-permute-start.1 = (f32[192,128]{1,0:T(8,128)}, f32[192,128]{1,0:T(8,128)S(1)}, u32[]{:S(2)}, u32[]{:S(2)}) collective-permute-start(f32[192,128]{1,0:T(8,128)} %bitcast.4), channel_id=1, source_target_pairs={{0,4},{1,5},{2,6},{3,7},{4,0},{5,1},{6,2},{7,3},{8,12},{9,13},{10,... | collective-permute-start | bytes 294920 | tf_op jit(solution)/shard_map/ppermute | solution.py:200
  4.0 1.5 %collective-permute-start = (f32[192,128]{1,0:T(8,128)}, f32[192,128]{1,0:T(8,128)S(1)}, u32[]{:S(2)}, u32[]{:S(2)}) collective-permute-start(f32[192,128]{1,0:T(8,128)} %bitcast.5), channel_id=1, source_target_pairs={{0,16},{8,24},{16,0},{24,8},{1,17},{9,25},{17,1},{25,9},{2,18},{10... | collective-permute-start | bytes 294920 | tf_op jit(solution)/shard_map/ppermute | solution.py:203
  5.6 0.6 %copy-done.7 = f32[64]{0:T(128)S(1)} copy-done((f32[64]{0:T(128)S(1)}, f32[64]{0:T(128)}, u32[]{:S(2)}) %copy-start.7) | copy-done | bytes 280
  6.2 0.0 copy-done.8
  6.2 0.0 copy-done.9
  6.2 0.0 copy-done.10
  6.3 0.0 copy-done.4
  6.3 0.0 copy-done.5
  6.3 0.0 copy-done.6
  6.3 0.9 %copy-done = f32[3,16,4,128]{3,2,1,0:T(4,128)S(1)} copy-done((f32[3,16,4,128]{3,2,1,0:T(4,128)S(1)}, f32[3,16,4,128]{3,2,1,0:T(4,128)}, u32[]{:S(2)}) %copy-start) | copy-done | bytes 98328
  7.2 0.7 %copy-done.2 = f32[32,32]{1,0:T(8,128)S(1)} copy-done((f32[32,32]{1,0:T(8,128)S(1)}, f32[32,32]{1,0:T(8,128)}, u32[]{:S(2)}) %copy-start.2) | copy-done | bytes 4120
  7.9 0.7 %copy-done.3 = f32[32,32]{1,0:T(8,128)S(1)} copy-done((f32[32,32]{1,0:T(8,128)S(1)}, f32[32,32]{1,0:T(8,128)}, u32[]{:S(2)}) %copy-start.3) | copy-done | bytes 4120
  8.6 2.0 %stream.1 = (f32[192,128]{1,0:T(8,128)S(1)}, f32[64,512]{1,0:T(8,128)S(1)}, f32[128,128]{1,0:T(8,128)S(1)}, f32[64,128]{1,0:T(8,128)S(1)}) custom-call(s32[4]{0:T(128)S(1)} %copy-done.4, f32[32]{0:T(128)S(1)} %copy-done.5, f32[32]{0:T(128)S(1)} %copy-done.6, f32[64]{0:T(128)S(1)} %copy-done.7, s32[32]{0:T(128)S(1)} %copy-done.8, f32[192,128]{1,0:T(8,128)S(1)} %bitcast.6, ...), custom_call_target="tpu_custom_call" | custom-call | tf_op jit(solution)/shard_map/stream/pallas_call | solution.py:168
  10.7 0.0 collective-permute-done.1.refs_1_
  10.7 0.3 %span.1 = (f32[192,128]{1,0:T(8,128)S(1)}, f32[192,128]{1,0:T(8,128)S(1)}, f32[192,128]{1,0:T(8,128)S(1)}, f32[192,128]{1,0:T(8,128)S(1)}, f32[2,192,128]{2,1,0:T(8,128)S(1)}) custom-call(f32[128,128]{1,0:T(8,128)S(1)} %get-tuple-element.17.matrix, f32[192,128]{1,0:T(8,128)S(1)} %bitcast.7, f32[192,128]{1,0:T(8,128)S(1)} %collective-permute-done.refs_0_, ...), custom_call_target="tpu_custom_call" | custom-call | tf_op jit(solution)/shard_map/span/pallas_call | solution.py:168
  11.0 0.1 collective-permute-start.2
  11.1 2.6 %collective-permute-start.3 = (f32[192,128]{1,0:T(8,128)S(1)}, f32[192,128]{1,0:T(8,128)S(1)}, u32[]{:S(2)}, u32[]{:S(2)}) collective-permute-start(f32[192,128]{1,0:T(8,128)S(1)} %get-tuple-element.20), channel_id=1, source_target_pairs={{0,3},{1,2},{2,1},{3,0},{4,7},{5,6},{6,5},{7,4},{8,11},{9,10},{10,... | collective-permute-start | bytes 294920 | tf_op jit(solution)/shard_map/ppermute | solution.py:200
  13.7 0.5 %collective-permute-start.4 = (f32[192,128]{1,0:T(8,128)S(1)}, f32[192,128]{1,0:T(8,128)S(1)}, u32[]{:S(2)}, u32[]{:S(2)}) collective-permute-start(f32[192,128]{1,0:T(8,128)S(1)} %get-tuple-element.21), channel_id=1, source_target_pairs={{0,2},{1,3},{2,0},{3,1},{4,6},{5,7},{6,4},{7,5},{8,10},{9,11},{10,... | collective-permute-start | bytes 294920 | tf_op jit(solution)/shard_map/ppermute | solution.py:200
  14.1 0.5 %collective-permute-start.5 = (f32[192,128]{1,0:T(8,128)S(1)}, f32[192,128]{1,0:T(8,128)S(1)}, u32[]{:S(2)}, u32[]{:S(2)}) collective-permute-start(f32[192,128]{1,0:T(8,128)S(1)} %get-tuple-element.22), channel_id=1, source_target_pairs={{0,1},{1,0},{2,3},{3,2},{4,5},{5,4},{6,7},{7,6},{8,9},{9,8},{10,11... | collective-permute-start | bytes 294920 | tf_op jit(solution)/shard_map/ppermute | solution.py:200
  14.7 0.0 collective-permute-done.2.theirs
  14.7 0.4 %wall.1.refs_0_ = f32[192,128]{1,0:T(8,128)S(1)} custom-call(f32[64,512]{1,0:T(8,128)S(1)} %get-tuple-element.15.matrix, f32[192,128]{1,0:T(8,128)S(1)} %get-tuple-element.16.x_part, f32[192,128]{1,0:T(8,128)S(1)} %get-tuple-element.18.z_part, f32[2,192,128]{2,1,0:T(8,128)S(1)} %get-tuple-element.19.ours, f32[2,192,128]{2,1,0:T(8,128)S(1)} %collective-permute-done.2.theirs), custom_call_target="tpu_custom_call" | custom-call | tf_op jit(solution)/shard_map/wall/pallas_call | solution.py:168
  15.0 2.6 %collective-permute-done.3.refs_1_ = f32[192,128]{1,0:T(8,128)S(1)} collective-permute-done((f32[192,128]{1,0:T(8,128)S(1)}, f32[192,128]{1,0:T(8,128)S(1)}, u32[]{:S(2)}, u32[]{:S(2)}) %collective-permute-start.3) | collective-permute-done | bytes 98336 | tf_op jit(solution)/shard_map/ppermute | solution.py:200
  17.7 1.7 %collective-permute-done.4.refs_2_ = f32[192,128]{1,0:T(8,128)S(1)} collective-permute-done((f32[192,128]{1,0:T(8,128)S(1)}, f32[192,128]{1,0:T(8,128)S(1)}, u32[]{:S(2)}, u32[]{:S(2)}) %collective-permute-start.4) | collective-permute-done | bytes 98336 | tf_op jit(solution)/shard_map/ppermute | solution.py:200
  19.4 0.7 %finish.1 = f32[192,128]{1,0:T(8,128)} custom-call(f32[64,128]{1,0:T(8,128)S(1)} %get-tuple-element.14.mask, f32[192,128]{1,0:T(8,128)S(1)} %wall.1.refs_0_, f32[192,128]{1,0:T(8,128)S(1)} %collective-permute-done.3.refs_1_, f32[192,128]{1,0:T(8,128)S(1)} %collective-permute-done.4.refs_2_, f32[192,128]{1,0:T(8,128)S(1)} %collective-permute-done.5.refs_3_), custom_call_target="tpu_custom_call" | custom-call | tf_op jit(solution)/shard_map/finish/pallas_call | solution.py:168
  (14 shorter events, 0.0 us)
Async XLA Ops:
  0.0 10.7 %collective-permute-start.1 = (f32[192,128]{1,0:T(8,128)}, f32[192,128]{1,0:T(8,128)S(1)}, u32[]{:S(2)}, u32[]{:S(2)}) collective-permute-start(f32[192,128]{1,0:T(8,128)} %bitcast.4), channel_id=1, source_target_pairs={{0,4},{1,5},{2,6},{3,7},{4,0},{5,1},{6,2},{7,3},{8,12},{9,13},{10,... | collective-permute-start | bytes 294920 | tf_op jit(solution)/shard_map/ppermute | solution.py:200
  4.0 6.6 %collective-permute-start = (f32[192,128]{1,0:T(8,128)}, f32[192,128]{1,0:T(8,128)S(1)}, u32[]{:S(2)}, u32[]{:S(2)}) collective-permute-start(f32[192,128]{1,0:T(8,128)} %bitcast.5), channel_id=1, source_target_pairs={{0,16},{8,24},{16,0},{24,8},{1,17},{9,25},{17,1},{25,9},{2,18},{10... | collective-permute-start | bytes 294920 | tf_op jit(solution)/shard_map/ppermute | solution.py:203
  5.6 0.7 %copy-start.7 = (f32[64]{0:T(128)S(1)}, f32[64]{0:T(128)}, u32[]{:S(2)}) copy-start(f32[64]{0:T(128)} %metric_table.1) | copy-start | bytes 772
  5.6 0.7 %copy-start.8 = (s32[32]{0:T(128)S(1)}, s32[32]{0:T(128)}, u32[]{:S(2)}) copy-start(s32[32]{0:T(128)} %metric_index.1) | copy-start | bytes 388
  5.6 0.7 %copy-start.9 = (f32[128]{0:T(128)S(1)}, f32[128]{0:T(128)}, u32[]{:S(2)}) copy-start(f32[128]{0:T(128)} %param.12) | copy-start | bytes 1540
  5.6 0.7 %copy-start.10 = (f32[128]{0:T(128)S(1)}, f32[128]{0:T(128)}, u32[]{:S(2)}) copy-start(f32[128]{0:T(128)} %param.13) | copy-start | bytes 1540
  5.6 0.7 %copy-start.4 = (s32[4]{0:T(128)S(1)}, s32[4]{0:T(128)}, u32[]{:S(2)}) copy-start(s32[4]{0:T(128)} %wall_counts.1) | copy-start | bytes 52
  5.6 0.7 %copy-start.5 = (f32[32]{0:T(128)S(1)}, f32[32]{0:T(128)}, u32[]{:S(2)}) copy-start(f32[32]{0:T(128)} %z_first.1) | copy-start | bytes 388
  5.6 0.7 %copy-start.6 = (f32[32]{0:T(128)S(1)}, f32[32]{0:T(128)}, u32[]{:S(2)}) copy-start(f32[32]{0:T(128)} %z_second.1) | copy-start | bytes 388
  6.3 0.9 %copy-start = (f32[3,16,4,128]{3,2,1,0:T(4,128)S(1)}, f32[3,16,4,128]{3,2,1,0:T(4,128)}, u32[]{:S(2)}) copy-start(f32[3,16,4,128]{3,2,1,0:T(4,128)} %param.10) | copy-start | bytes 294916
  7.2 0.7 %copy-start.2 = (f32[32,32]{1,0:T(8,128)S(1)}, f32[32,32]{1,0:T(8,128)}, u32[]{:S(2)}) copy-start(f32[32,32]{1,0:T(8,128)} %y_first.1) | copy-start | bytes 12292
  7.9 0.7 %copy-start.3 = (f32[32,32]{1,0:T(8,128)S(1)}, f32[32,32]{1,0:T(8,128)}, u32[]{:S(2)}) copy-start(f32[32,32]{1,0:T(8,128)} %y_second.1) | copy-start | bytes 12292
  8.6 2.1 %copy-start.1 = (f32[3,16,4,128]{3,2,1,0:T(4,128)S(1)}, f32[3,16,4,128]{3,2,1,0:T(4,128)}, u32[]{:S(2)}) copy-start(f32[3,16,4,128]{3,2,1,0:T(4,128)} %param.10) | copy-start | bytes 294916
  11.0 3.6 %collective-permute-start.2 = (f32[2,192,128]{2,1,0:T(8,128)S(1)}, f32[2,192,128]{2,1,0:T(8,128)S(1)}, u32[]{:S(2)}, u32[]{:S(2)}) collective-permute-start(f32[2,192,128]{2,1,0:T(8,128)S(1)} %get-tuple-element.19.ours), channel_id=1, source_target_pairs={{0,8},{8,0},{16,24},{24,16},{1,9},{9,1},{17,25},{25,17},{2,10},{10... | collective-permute-start | bytes 589832 | tf_op jit(solution)/shard_map/ppermute | solution.py:203
  11.1 6.6 %collective-permute-start.3 = (f32[192,128]{1,0:T(8,128)S(1)}, f32[192,128]{1,0:T(8,128)S(1)}, u32[]{:S(2)}, u32[]{:S(2)}) collective-permute-start(f32[192,128]{1,0:T(8,128)S(1)} %get-tuple-element.20), channel_id=1, source_target_pairs={{0,3},{1,2},{2,1},{3,0},{4,7},{5,6},{6,5},{7,4},{8,11},{9,10},{10,... | collective-permute-start | bytes 294920 | tf_op jit(solution)/shard_map/ppermute | solution.py:200
  13.7 5.7 %collective-permute-start.4 = (f32[192,128]{1,0:T(8,128)S(1)}, f32[192,128]{1,0:T(8,128)S(1)}, u32[]{:S(2)}, u32[]{:S(2)}) collective-permute-start(f32[192,128]{1,0:T(8,128)S(1)} %get-tuple-element.21), channel_id=1, source_target_pairs={{0,2},{1,3},{2,0},{3,1},{4,6},{5,7},{6,4},{7,5},{8,10},{9,11},{10,... | collective-permute-start | bytes 294920 | tf_op jit(solution)/shard_map/ppermute | solution.py:200
  14.1 5.2 %collective-permute-start.5 = (f32[192,128]{1,0:T(8,128)S(1)}, f32[192,128]{1,0:T(8,128)S(1)}, u32[]{:S(2)}, u32[]{:S(2)}) collective-permute-start(f32[192,128]{1,0:T(8,128)S(1)} %get-tuple-element.22), channel_id=1, source_target_pairs={{0,1},{1,0},{2,3},{3,2},{4,5},{5,4},{6,7},{7,6},{8,9},{9,8},{10,11... | collective-permute-start | bytes 294920 | tf_op jit(solution)/shard_map/ppermute | solution.py:200

commit v8 on v7

--- a/solution.py
+++ b/solution.py
@@ -56,32 +56,12 @@
 
 
 def stream_kernel(
-    rows,
-    cols,
-    comps,
-    slots,
-    zloc,
-    wall_counts,
-    z_first,
-    z_second,
-    metric_table,
-    metric_index,
-    field,
-    x_first,
-    x_second,
-    y_first,
-    y_second,
-    x_part,
-    y_matrix,
-    z_matrix,
-    mask,
-    scaled,
+    cols, comps, zloc, wall_counts, z_first, z_second, field, x_first, x_second, x_part, z_matrix, mask
 ):
-    depth = slots * zloc
+    depth = mask.shape[0]
     length = field.shape[1]
-    cells = y_first.shape[0]
-    me = lax.axis_index("row")
-    mask[...] = (lax.broadcasted_iota(jnp.int32, mask.shape, 0) // zloc < wall_counts[me]).astype(jnp.float32)
+    count = wall_counts[lax.axis_index("row")]
+    mask[...] = (lax.broadcasted_iota(jnp.int32, mask.shape, 0) // zloc < count).astype(jnp.float32)
 
     cells_z = cols * zloc
     shape = z_matrix.shape
@@ -113,11 +93,33 @@
     )
     x_part[...] = dot_split(left, right, transposed=True)
 
+
+def wall_kernel(
+    rows,
+    comps,
+    zloc,
+    wall_counts,
+    metric_table,
+    metric_index,
+    y_first,
+    y_second,
+    x_part,
+    z_part,
+    ours,
+    theirs,
+    out,
+    matrix,
+    scaled,
+):
+    depth = x_part.shape[0] // comps
+    cells = y_first.shape[0]
+
     def scale(j, carry):
         scaled[pl.ds(j, 1), :] = y_first[pl.ds(j, 1), :] * -metric_table[metric_index[j]]
         return carry
 
     lax.fori_loop(0, cells, scale, 0, unroll=8)
+    me = lax.axis_index("row")
 
     def start_of(index):
         return lax.fori_loop(0, rows, lambda i, acc: acc + jnp.where(i < index, wall_counts[i], 0), 0, unroll=True)
@@ -136,14 +138,11 @@
     match = r == q
     for b in range(rows):
         other = me ^ (2 * b if b < rows // 2 else 2 * b + 1 - rows)
-        theirs = ((own < wall_counts[other]) & (own + start_of(other) == cell)).astype(jnp.float32)
+        spots = ((own < wall_counts[other]) & (own + start_of(other) == cell)).astype(jnp.float32)
         for k in range(2):
-            block = jnp.where(match, exact(both[k], theirs, turned), 0.0)
-            y_matrix[:, (2 * b + k) * depth : (2 * b + k + 1) * depth] = block
-
-
-def wall_kernel(comps, matrix, x_part, z_part, ours, theirs, out):
-    depth = x_part.shape[0] // comps
+            block = jnp.where(match, exact(both[k], spots, turned), 0.0)
+            matrix[:, (2 * b + k) * depth : (2 * b + k + 1) * depth] = block
+
     for comp in range(comps):
         at = slice(comp * depth, (comp + 1) * depth)
         stack = []
@@ -204,24 +203,12 @@
 
     gathered = [along(field, quad * i) for i in range(1, sources)]
     far = [across(field, step) for step in range(2, rows, 2)]
-    x_part, y_matrix, z_matrix, mask = call(
-        functools.partial(stream_kernel, rows, cols, comps, slots, zloc),
-        [
-            wall_counts,
-            z_first,
-            z_second,
-            metric_table,
-            metric_index,
-            field,
-            x_first.reshape(1, length),
-            x_second.reshape(1, length),
-            y_first,
-            y_second,
-        ],
-        [SMEM] * 5 + [VMEM] * 5,
-        [field.shape, (depth, 2 * rows * depth), (quad * group, 2 * sources * group), (depth, length)],
+    x_part, z_matrix, mask = call(
+        functools.partial(stream_kernel, cols, comps, zloc),
+        [wall_counts, z_first, z_second, field, x_first.reshape(1, length), x_second.reshape(1, length)],
+        [SMEM] * 3 + [VMEM] * 3,
+        [field.shape, (quad * group, 2 * sources * group), (depth, length)],
         "stream",
-        [y_first.shape],
     )
     *parts, pair = call(
         functools.partial(span_kernel, comps),
@@ -233,11 +220,12 @@
     returned = [along(parts[t], t) for t in reversed(range(1, quad))]
     other = across(pair, 1)
     (total,) = call(
-        functools.partial(wall_kernel, comps),
-        [y_matrix, x_part, parts[0], pair, other],
-        [VMEM] * 5,
+        functools.partial(wall_kernel, rows, comps, zloc),
+        [wall_counts, metric_table, metric_index, y_first, y_second, x_part, parts[0], pair, other],
+        [SMEM] * 3 + [VMEM] * 6,
         [field.shape],
         "wall",
+        [(depth, 2 * rows * depth), y_first.shape],
     )
     (result,) = call(
         functools.partial(finish_kernel, comps),

time: 20.4 us -> 18.7 us (0.917); the launches traced: 20 us -> 18.6 us
  waiting for transfers between devices: 4.34 us -> 3.24 us
  local copies, waits for them, and re-layouts: 3.05 us -> 2.26 us
  Pallas kernels: 3.38 us -> 3.8 us
    ppermute x4, waiting for transfers between devices: 4.33 us -> 3.23 us  [along(): return lax.ppermute(value, 'col', [(i, i ^ step) for i in range(cols)])]
    unnamed x22, local copies, waits for them, and re-layouts: 3.05 us -> 2.26 us
    pallas_call x4, Pallas kernels: 3.38 us -> 3.8 us  [call(): pl.pallas_call(kernel, out_shape=results, in_specs=[pl.BlockSpec(memory_s...]
  transfers between devices with their start and end apart: 6 -> 6, of which waited for: 2 -> 3; matrix products, arithmetic and copies ran while one was open for 0% -> 0% of each run, Pallas kernels for 12% -> 15%
where the time goes in v8:
time: 18.7 us; the launch traced here: 18.6 us
  starting transfers between devices  9.18 us (49%)
  Pallas kernels  3.8 us (20%)
  waiting for transfers between devices  3.24 us (17%)
  local copies, waits for them, and re-layouts  2.26 us (12%)
    ppermute x4, starting transfers between devices, along(): return lax.ppermute(value, 'col', [(i, i ^ step) for i in range(cols)])  7.59 us
    pallas_call x4, Pallas kernels, call(): pl.pallas_call(kernel, out_shape=results, in_specs=[pl.BlockSpec(memory_s...  3.8 us
    ppermute x4, waiting for transfers between devices, along(): return lax.ppermute(value, 'col', [(i, i ^ step) for i in range(cols)])  3.23 us
    unnamed x22, local copies, waits for them, and re-layouts  2.26 us
    ppermute x2, starting transfers between devices, across(): return lax.ppermute(value, 'row', [(i, i ^ step) for i in range(rows)])  1.59 us
  transfers between devices with their start and end apart: 6, of which 3 were waited for; matrix products, arithmetic and copies ran while one was open for 0% of the time, Pallas kernels for 15%

profile of v8, /device:TPU:0, one launch (start us, length us, event | category | flops | bytes accessed | tf_op | source)
XLA Modules:
  0.0 18.6 jit_solution(1032550862856752501)
XLA Ops:
  0.0 4.0 %collective-permute-start.1 = (f32[192,128]{1,0:T(8,128)}, f32[192,128]{1,0:T(8,128)S(1)}, u32[]{:S(2)}, u32[]{:S(2)}) collective-permute-start(f32[192,128]{1,0:T(8,128)} %bitcast.4), channel_id=1, source_target_pairs={{0,4},{1,5},{2,6},{3,7},{4,0},{5,1},{6,2},{7,3},{8,12},{9,13},{10,... | collective-permute-start | bytes 294920 | tf_op jit(solution)/shard_map/ppermute | solution.py:199
  4.0 1.5 %collective-permute-start = (f32[192,128]{1,0:T(8,128)}, f32[192,128]{1,0:T(8,128)S(1)}, u32[]{:S(2)}, u32[]{:S(2)}) collective-permute-start(f32[192,128]{1,0:T(8,128)} %bitcast.5), channel_id=1, source_target_pairs={{0,16},{8,24},{16,0},{24,8},{1,17},{9,25},{17,1},{25,9},{2,18},{10... | collective-permute-start | bytes 294920 | tf_op jit(solution)/shard_map/ppermute | solution.py:202
  5.6 0.6 %copy-done.7 = f32[128]{0:T(128)S(1)} copy-done((f32[128]{0:T(128)S(1)}, f32[128]{0:T(128)}, u32[]{:S(2)}) %copy-start.7) | copy-done | bytes 536
  6.2 0.0 copy-done.8
  6.2 0.0 copy-done.4
  6.2 0.0 copy-done.5
  6.3 0.0 copy-done.6
  6.3 0.9 %copy-done = f32[3,16,4,128]{3,2,1,0:T(4,128)S(1)} copy-done((f32[3,16,4,128]{3,2,1,0:T(4,128)S(1)}, f32[3,16,4,128]{3,2,1,0:T(4,128)}, u32[]{:S(2)}) %copy-start) | copy-done | bytes 98328
  7.2 1.1 %stream.1 = (f32[192,128]{1,0:T(8,128)S(1)}, f32[128,128]{1,0:T(8,128)S(1)}, f32[64,128]{1,0:T(8,128)S(1)}) custom-call(s32[4]{0:T(128)S(1)} %copy-done.4, f32[32]{0:T(128)S(1)} %copy-done.5, f32[32]{0:T(128)S(1)} %copy-done.6, f32[192,128]{1,0:T(8,128)S(1)} %bitcast.6, f32[1,128]{1,0:T(1,128)S(1)} %bitcast.8, f32[1,128]{1,0:T(1,128)S(1)} %bitcast.9), custom_call_target="tpu_custom_call" | custom-call | tf_op jit(solution)/shard_map/stream/pallas_call | solution.py:167
  8.3 0.9 %collective-permute-done.1.refs_1_ = f32[192,128]{1,0:T(8,128)S(1)} collective-permute-done((f32[192,128]{1,0:T(8,128)}, f32[192,128]{1,0:T(8,128)S(1)}, u32[]{:S(2)}, u32[]{:S(2)}) %collective-permute-start.1) | collective-permute-done | bytes 98336 | tf_op jit(solution)/shard_map/ppermute | solution.py:199
  9.1 0.0 collective-permute-done.refs_0_
  9.2 0.0 copy-start.3
  9.2 0.3 %span.1 = (f32[192,128]{1,0:T(8,128)S(1)}, f32[192,128]{1,0:T(8,128)S(1)}, f32[192,128]{1,0:T(8,128)S(1)}, f32[192,128]{1,0:T(8,128)S(1)}, f32[2,192,128]{2,1,0:T(8,128)S(1)}) custom-call(f32[128,128]{1,0:T(8,128)S(1)} %get-tuple-element.15.matrix, f32[192,128]{1,0:T(8,128)S(1)} %bitcast.7, f32[192,128]{1,0:T(8,128)S(1)} %collective-permute-done.refs_0_, ...), custom_call_target="tpu_custom_call" | custom-call | tf_op jit(solution)/shard_map/span/pallas_call | solution.py:167
  9.5 0.1 collective-permute-start.2
  9.6 2.3 %collective-permute-start.3 = (f32[192,128]{1,0:T(8,128)S(1)}, f32[192,128]{1,0:T(8,128)S(1)}, u32[]{:S(2)}, u32[]{:S(2)}) collective-permute-start(f32[192,128]{1,0:T(8,128)S(1)} %get-tuple-element.18), channel_id=1, source_target_pairs={{0,3},{1,2},{2,1},{3,0},{4,7},{5,6},{6,5},{7,4},{8,11},{9,10},{10,... | collective-permute-start | bytes 294920 | tf_op jit(solution)/shard_map/ppermute | solution.py:199
  11.9 0.8 %collective-permute-start.4 = (f32[192,128]{1,0:T(8,128)S(1)}, f32[192,128]{1,0:T(8,128)S(1)}, u32[]{:S(2)}, u32[]{:S(2)}) collective-permute-start(f32[192,128]{1,0:T(8,128)S(1)} %get-tuple-element.19), channel_id=1, source_target_pairs={{0,2},{1,3},{2,0},{3,1},{4,6},{5,7},{6,4},{7,5},{8,10},{9,11},{10,... | collective-permute-start | bytes 294920 | tf_op jit(solution)/shard_map/ppermute | solution.py:199
  12.7 0.5 %collective-permute-start.5 = (f32[192,128]{1,0:T(8,128)S(1)}, f32[192,128]{1,0:T(8,128)S(1)}, u32[]{:S(2)}, u32[]{:S(2)}) collective-permute-start(f32[192,128]{1,0:T(8,128)S(1)} %get-tuple-element.20), channel_id=1, source_target_pairs={{0,1},{1,0},{2,3},{3,2},{4,5},{5,4},{6,7},{7,6},{8,9},{9,8},{10,11... | collective-permute-start | bytes 294920 | tf_op jit(solution)/shard_map/ppermute | solution.py:199
  13.1 0.0 collective-permute-done.2.theirs
  13.2 0.6 %copy-done.9 = f32[64]{0:T(128)S(1)} copy-done((f32[64]{0:T(128)S(1)}, f32[64]{0:T(128)}, u32[]{:S(2)}) %copy-start.9) | copy-done | bytes 280
  13.8 0.0 copy-done.10
  13.8 1.7 %wall.1.refs_0_ = f32[192,128]{1,0:T(8,128)S(1)} custom-call(s32[4]{0:T(128)S(1)} %copy-done.4, f32[64]{0:T(128)S(1)} %copy-done.9, s32[32]{0:T(128)S(1)} %copy-done.10, f32[32,32]{1,0:T(8,128)S(1)} %copy-done.2, f32[32,32]{1,0:T(8,128)S(1)} %copy-done.3, f32[192,128]{1,0:T(8,128)S(1)} %get-tuple-element.14.x_part, f32[192,128]{1,0:T(8,128)S(1)} %get-tuple-element.16.z_part, ...), custom_call_target="tpu_custom_call" | custom-call | tf_op jit(solution)/shard_map/wall/pallas_call | solution.py:167
  15.5 0.6 %collective-permute-done.3.refs_1_ = f32[192,128]{1,0:T(8,128)S(1)} collective-permute-done((f32[192,128]{1,0:T(8,128)S(1)}, f32[192,128]{1,0:T(8,128)S(1)}, u32[]{:S(2)}, u32[]{:S(2)}) %collective-permute-start.3) | collective-permute-done | bytes 98336 | tf_op jit(solution)/shard_map/ppermute | solution.py:199
  16.1 1.7 %collective-permute-done.4.refs_2_ = f32[192,128]{1,0:T(8,128)S(1)} collective-permute-done((f32[192,128]{1,0:T(8,128)S(1)}, f32[192,128]{1,0:T(8,128)S(1)}, u32[]{:S(2)}, u32[]{:S(2)}) %collective-permute-start.4) | collective-permute-done | bytes 98336 | tf_op jit(solution)/shard_map/ppermute | solution.py:199
  17.9 0.7 %finish.1 = f32[192,128]{1,0:T(8,128)} custom-call(f32[64,128]{1,0:T(8,128)S(1)} %get-tuple-element.13.mask, f32[192,128]{1,0:T(8,128)S(1)} %wall.1.refs_0_, f32[192,128]{1,0:T(8,128)S(1)} %collective-permute-done.3.refs_1_, f32[192,128]{1,0:T(8,128)S(1)} %collective-permute-done.4.refs_2_, f32[192,128]{1,0:T(8,128)S(1)} %collective-permute-done.5.refs_3_), custom_call_target="tpu_custom_call" | custom-call | tf_op jit(solution)/shard_map/finish/pallas_call | solution.py:167
  (14 shorter events, 0.0 us)
Async XLA Ops:
  0.0 9.1 %collective-permute-start.1 = (f32[192,128]{1,0:T(8,128)}, f32[192,128]{1,0:T(8,128)S(1)}, u32[]{:S(2)}, u32[]{:S(2)}) collective-permute-start(f32[192,128]{1,0:T(8,128)} %bitcast.4), channel_id=1, source_target_pairs={{0,4},{1,5},{2,6},{3,7},{4,0},{5,1},{6,2},{7,3},{8,12},{9,13},{10,... | collective-permute-start | bytes 294920 | tf_op jit(solution)/shard_map/ppermute | solution.py:199
  4.0 5.1 %collective-permute-start = (f32[192,128]{1,0:T(8,128)}, f32[192,128]{1,0:T(8,128)S(1)}, u32[]{:S(2)}, u32[]{:S(2)}) collective-permute-start(f32[192,128]{1,0:T(8,128)} %bitcast.5), channel_id=1, source_target_pairs={{0,16},{8,24},{16,0},{24,8},{1,17},{9,25},{17,1},{25,9},{2,18},{10... | collective-permute-start | bytes 294920 | tf_op jit(solution)/shard_map/ppermute | solution.py:202
  5.6 0.7 %copy-start.7 = (f32[128]{0:T(128)S(1)}, f32[128]{0:T(128)}, u32[]{:S(2)}) copy-start(f32[128]{0:T(128)} %param.12) | copy-start | bytes 1540
  5.6 0.7 %copy-start.8 = (f32[128]{0:T(128)S(1)}, f32[128]{0:T(128)}, u32[]{:S(2)}) copy-start(f32[128]{0:T(128)} %param.13) | copy-start | bytes 1540
  5.6 0.7 %copy-start.4 = (s32[4]{0:T(128)S(1)}, s32[4]{0:T(128)}, u32[]{:S(2)}) copy-start(s32[4]{0:T(128)} %wall_counts.3) | copy-start | bytes 52
  5.6 0.7 %copy-start.5 = (f32[32]{0:T(128)S(1)}, f32[32]{0:T(128)}, u32[]{:S(2)}) copy-start(f32[32]{0:T(128)} %z_first.1) | copy-start | bytes 388
  5.6 0.7 %copy-start.6 = (f32[32]{0:T(128)S(1)}, f32[32]{0:T(128)}, u32[]{:S(2)}) copy-start(f32[32]{0:T(128)} %z_second.1) | copy-start | bytes 388
  6.3 0.9 %copy-start = (f32[3,16,4,128]{3,2,1,0:T(4,128)S(1)}, f32[3,16,4,128]{3,2,1,0:T(4,128)}, u32[]{:S(2)}) copy-start(f32[3,16,4,128]{3,2,1,0:T(4,128)} %param.10) | copy-start | bytes 294916
  7.2 2.0 %copy-start.1 = (f32[3,16,4,128]{3,2,1,0:T(4,128)S(1)}, f32[3,16,4,128]{3,2,1,0:T(4,128)}, u32[]{:S(2)}) copy-start(f32[3,16,4,128]{3,2,1,0:T(4,128)} %param.10) | copy-start | bytes 294916
  9.2 4.0 %copy-start.2 = (f32[32,32]{1,0:T(8,128)S(1)}, f32[32,32]{1,0:T(8,128)}, u32[]{:S(2)}) copy-start(f32[32,32]{1,0:T(8,128)} %y_first.1) | copy-start | bytes 12292
  9.2 4.0 %copy-start.3 = (f32[32,32]{1,0:T(8,128)S(1)}, f32[32,32]{1,0:T(8,128)}, u32[]{:S(2)}) copy-start(f32[32,32]{1,0:T(8,128)} %y_second.1) | copy-start | bytes 12292
  9.5 3.6 %collective-permute-start.2 = (f32[2,192,128]{2,1,0:T(8,128)S(1)}, f32[2,192,128]{2,1,0:T(8,128)S(1)}, u32[]{:S(2)}, u32[]{:S(2)}) collective-permute-start(f32[2,192,128]{2,1,0:T(8,128)S(1)} %get-tuple-element.17.ours), channel_id=1, source_target_pairs={{0,8},{8,0},{16,24},{24,16},{1,9},{9,1},{17,25},{25,17},{2,10},{10... | collective-permute-start | bytes 589832 | tf_op jit(solution)/shard_map/ppermute | solution.py:202
  9.6 6.6 %collective-permute-start.3 = (f32[192,128]{1,0:T(8,128)S(1)}, f32[192,128]{1,0:T(8,128)S(1)}, u32[]{:S(2)}, u32[]{:S(2)}) collective-permute-start(f32[192,128]{1,0:T(8,128)S(1)} %get-tuple-element.18), channel_id=1, source_target_pairs={{0,3},{1,2},{2,1},{3,0},{4,7},{5,6},{6,5},{7,4},{8,11},{9,10},{10,... | collective-permute-start | bytes 294920 | tf_op jit(solution)/shard_map/ppermute | solution.py:199
  11.9 6.0 %collective-permute-start.4 = (f32[192,128]{1,0:T(8,128)S(1)}, f32[192,128]{1,0:T(8,128)S(1)}, u32[]{:S(2)}, u32[]{:S(2)}) collective-permute-start(f32[192,128]{1,0:T(8,128)S(1)} %get-tuple-element.19), channel_id=1, source_target_pairs={{0,2},{1,3},{2,0},{3,1},{4,6},{5,7},{6,4},{7,5},{8,10},{9,11},{10,... | collective-permute-start | bytes 294920 | tf_op jit(solution)/shard_map/ppermute | solution.py:199
  12.7 5.2 %collective-permute-start.5 = (f32[192,128]{1,0:T(8,128)S(1)}, f32[192,128]{1,0:T(8,128)S(1)}, u32[]{:S(2)}, u32[]{:S(2)}) collective-permute-start(f32[192,128]{1,0:T(8,128)S(1)} %get-tuple-element.20), channel_id=1, source_target_pairs={{0,1},{1,0},{2,3},{3,2},{4,5},{5,4},{6,7},{7,6},{8,9},{9,8},{10,11... | collective-permute-start | bytes 294920 | tf_op jit(solution)/shard_map/ppermute | solution.py:199
  13.1 0.7 %copy-start.9 = (f32[64]{0:T(128)S(1)}, f32[64]{0:T(128)}, u32[]{:S(2)}) copy-start(f32[64]{0:T(128)} %metric_table.1) | copy-start | bytes 772
  13.1 0.7 %copy-start.10 = (s32[32]{0:T(128)S(1)}, s32[32]{0:T(128)}, u32[]{:S(2)}) copy-start(s32[32]{0:T(128)} %metric_index.1) | copy-start | bytes 388

commit v9 on v8

--- a/solution.py
+++ b/solution.py
@@ -29,14 +29,18 @@
     return mul(lh, rh) + (mul(lh, rl) + mul(ll, rh))
 
 
-def span_kernel(comps, matrix, field, *refs):
-    parts, pair = refs[-quad - 1 : -1], refs[-1]
+def fan(cols):
+    return max(quad, cols // quad)
+
+
+def span_kernel(comps, count, matrix, field, *refs):
+    parts, pair = refs[-count - 1 : -1], refs[-1]
     pair[0] = field[...]
     for i in range(1, pair.shape[0]):
         pair[i] = refs[i - 1][...]
-    sources = (field,) + refs[pair.shape[0] - 1 : -quad - 1]
+    sources = (field,) + refs[pair.shape[0] - 1 : -count - 1]
     depth, length = field.shape[0] // comps, field.shape[1]
-    group = matrix.shape[0] // quad
+    group = matrix.shape[0] // count
     right = []
     for comp in range(comps):
         for at in range(0, depth, group):
@@ -44,7 +48,7 @@
             stack += [value * source[2 * depth + at : 2 * depth + at + group] for value, source in zip(stack, sources)]
             right.append(jnp.concatenate(stack, axis=0))
     result = dot_split(matrix[...], jnp.concatenate(right, axis=1))
-    for t in range(quad):
+    for t in range(count):
         for i in range(len(right)):
             parts[t][i * group : (i + 1) * group] = result[
                 t * group : (t + 1) * group, i * length : (i + 1) * length
@@ -66,15 +70,20 @@
     cells_z = cols * zloc
     shape = z_matrix.shape
     half = shape[1] // 2
-    group = shape[0] // quad
+    group = half // fan(cols)
     mine = lax.axis_index("col")
+    odd = lax.axis_index("row") % 2
+    wide = cols // quad
+    far_step, far_count = jnp.where(odd == 0, quad, 1), jnp.where(odd == 0, wide, quad)
+    near_step, near_count = jnp.where(odd == 0, 1, quad), jnp.where(odd == 0, quad, wide)
     r = lax.broadcasted_iota(jnp.int32, shape, 0)
     q = lax.broadcasted_iota(jnp.int32, shape, 1)
     q = jnp.where(q < half, q, q - half)
-    out_cell = ((r // group) ^ mine) * zloc + r % zloc
-    in_cell = ((quad * (q // group)) ^ mine) * zloc + q % zloc
-    same = (r % group) // zloc == (q % group) // zloc
-    gap = jnp.where(same, (in_cell - out_cell + cells_z) % cells_z, -1)
+    t, s = r // group, q // group
+    out_cell = ((near_step * t) ^ mine) * zloc + r % zloc
+    in_cell = ((far_step * s) ^ mine) * zloc + q % zloc
+    used = (t < near_count) & (s < far_count) & ((r % group) // zloc == (q % group) // zloc)
+    gap = jnp.where(used, (in_cell - out_cell + cells_z) % cells_z, -1)
     kind = lax.broadcasted_iota(jnp.int32, (1, shape[1]), 1) < half
 
     def fill(k, total):
@@ -193,31 +202,41 @@
     depth = slots * zloc
     field = velocity.reshape(comps * depth, length)
     group = min(depth, 32)
-    sources = cols // quad
-
-    def along(value, step):
-        return lax.ppermute(value, "col", [(i, i ^ step) for i in range(cols)])
+    count = fan(cols)
+
+    def along(value, index, steps):
+        limits = [cols // quad if step == quad else quad for step in steps]
+        return lax.ppermute(
+            value,
+            ("row", "col"),
+            [
+                (r * cols + c, r * cols + (c ^ (steps[r % 2] * index)))
+                for r in range(rows)
+                for c in range(cols)
+                if index < limits[r % 2]
+            ],
+        )
 
     def across(value, step):
         return lax.ppermute(value, "row", [(i, i ^ step) for i in range(rows)])
 
-    gathered = [along(field, quad * i) for i in range(1, sources)]
+    gathered = [along(field, i, (quad, 1)) for i in range(1, count)]
     far = [across(field, step) for step in range(2, rows, 2)]
     x_part, z_matrix, mask = call(
         functools.partial(stream_kernel, cols, comps, zloc),
         [wall_counts, z_first, z_second, field, x_first.reshape(1, length), x_second.reshape(1, length)],
         [SMEM] * 3 + [VMEM] * 3,
-        [field.shape, (quad * group, 2 * sources * group), (depth, length)],
+        [field.shape, (count * group, 2 * count * group), (depth, length)],
         "stream",
     )
     *parts, pair = call(
-        functools.partial(span_kernel, comps),
+        functools.partial(span_kernel, comps, count),
         [z_matrix, field] + far + gathered,
-        [VMEM] * (rows // 2 + sources),
-        [field.shape] * quad + [(rows // 2,) + field.shape],
+        [VMEM] * (rows // 2 + count),
+        [field.shape] * count + [(rows // 2,) + field.shape],
         "span",
     )
-    returned = [along(parts[t], t) for t in reversed(range(1, quad))]
+    returned = [along(parts[t], t, (1, quad)) for t in range(1, count)]
     other = across(pair, 1)
     (total,) = call(
         functools.partial(wall_kernel, rows, comps, zloc),
@@ -230,7 +249,7 @@
     (result,) = call(
         functools.partial(finish_kernel, comps),
         [mask, total] + returned,
-        [VMEM] * (quad + 1),
+        [VMEM] * (count + 1),
         [field.shape],
         "finish",
     )

time: 18.7 us -> 25.7 us (1.37)
  starting transfers between devices: 9.18 us -> 16 us
    ppermute x4 -> x6, starting transfers between devices: 7.59 us -> 12.7 us  [along(): lax.ppermute(value, ('row', 'col'), [(r * cols + c, r * cols + (c ^ steps...]
    ppermute x2, starting transfers between devices: 1.59 us -> 3.27 us  [across(): return lax.ppermute(value, 'row', [(i, i ^ step) for i in range(rows)])]
    ppermute x4 -> x6, waiting for transfers between devices: 3.23 us -> 2.67 us  [along(): lax.ppermute(value, ('row', 'col'), [(r * cols + c, r * cols + (c ^ steps...]
    ppermute x2, waiting for transfers between devices: 0.01 us -> 0.46 us  [across(): return lax.ppermute(value, 'row', [(i, i ^ step) for i in range(rows)])]
  transfers between devices with their start and end apart: 6 -> 8, of which waited for: 3 -> 2; matrix products, arithmetic and copies ran while one was open for 0% -> 0% of each run, Pallas kernels for 15% -> 11%
where the time goes in v9:
time: 25.7 us; the launch traced here: 25.5 us
  starting transfers between devices  16 us (62%)
  Pallas kernels  3.96 us (15%)
  waiting for transfers between devices  3.13 us (12%)
  local copies, waits for them, and re-layouts  2.24 us (9%)
    ppermute x6, starting transfers between devices, along(): lax.ppermute(value, ('row', 'col'), [(r * cols + c, r * cols + (c ^ steps...  12.7 us
    pallas_call x4, Pallas kernels, call(): pl.pallas_call(kernel, out_shape=results, in_specs=[pl.BlockSpec(memory_s...  3.96 us
    ppermute x2, starting transfers between devices, across(): return lax.ppermute(value, 'row', [(i, i ^ step) for i in range(rows)])  3.27 us
    ppermute x6, waiting for transfers between devices, along(): lax.ppermute(value, ('row', 'col'), [(r * cols + c, r * cols + (c ^ steps...  2.67 us
    unnamed x22, local copies, waits for them, and re-layouts  2.24 us
  transfers between devices with their start and end apart: 8, of which 2 were waited for; matrix products, arithmetic and copies ran while one was open for 0% of the time, Pallas kernels for 11%

profile of v9, /device:TPU:0, one launch (start us, length us, event | category | flops | bytes accessed | tf_op | source)
XLA Modules:
  0.0 25.5 jit_solution(10166688789699949998)
XLA Ops:
  0.0 0.7 %collective-permute-start.3 = (f32[192,128]{1,0:T(8,128)}, f32[192,128]{1,0:T(8,128)S(1)}, u32[]{:S(2)}, u32[]{:S(2)}) collective-permute-start(f32[192,128]{1,0:T(8,128)} %bitcast.4), channel_id=1, source_target_pairs={{8,11},{9,10},{10,9},{11,8},{12,15},{13,14},{14,13},{15,12},{24,27... | collective-permute-start | bytes 294920 | tf_op jit(solution)/shard_map/ppermute | solution.py:209
  0.7 0.7 %collective-permute-start.2 = (f32[192,128]{1,0:T(8,128)}, f32[192,128]{1,0:T(8,128)S(1)}, u32[]{:S(2)}, u32[]{:S(2)}) collective-permute-start(f32[192,128]{1,0:T(8,128)} %bitcast.5), channel_id=1, source_target_pairs={{8,10},{9,11},{10,8},{11,9},{12,14},{13,15},{14,12},{15,13},{24,26... | collective-permute-start | bytes 294920 | tf_op jit(solution)/shard_map/ppermute | solution.py:209
  1.3 4.1 %collective-permute-start.1 = (f32[192,128]{1,0:T(8,128)}, f32[192,128]{1,0:T(8,128)S(1)}, u32[]{:S(2)}, u32[]{:S(2)}) collective-permute-start(f32[192,128]{1,0:T(8,128)} %bitcast.6), channel_id=1, source_target_pairs={{0,4},{1,5},{2,6},{3,7},{4,0},{5,1},{6,2},{7,3},{8,9},{9,8},{10,11... | collective-permute-start | bytes 294920 | tf_op jit(solution)/shard_map/ppermute | solution.py:209
  5.4 1.5 %collective-permute-start = (f32[192,128]{1,0:T(8,128)}, f32[192,128]{1,0:T(8,128)S(1)}, u32[]{:S(2)}, u32[]{:S(2)}) collective-permute-start(f32[192,128]{1,0:T(8,128)} %bitcast.7), channel_id=1, source_target_pairs={{0,16},{8,24},{16,0},{24,8},{1,17},{9,25},{17,1},{25,9},{2,18},{10... | collective-permute-start | bytes 294920 | tf_op jit(solution)/shard_map/ppermute | solution.py:221
  7.0 0.6 %copy-done.7 = f32[128]{0:T(128)S(1)} copy-done((f32[128]{0:T(128)S(1)}, f32[128]{0:T(128)}, u32[]{:S(2)}) %copy-start.7) | copy-done | bytes 536
  7.6 0.0 copy-done.8
  7.6 0.0 copy-done.4
  7.6 0.0 copy-done.5
  7.7 0.0 copy-done.6
  7.7 0.9 %copy-done = f32[3,16,4,128]{3,2,1,0:T(4,128)S(1)} copy-done((f32[3,16,4,128]{3,2,1,0:T(4,128)S(1)}, f32[3,16,4,128]{3,2,1,0:T(4,128)}, u32[]{:S(2)}) %copy-start) | copy-done | bytes 98328
  8.6 1.2 %stream.1 = (f32[192,128]{1,0:T(8,128)S(1)}, f32[128,256]{1,0:T(8,128)S(1)}, f32[64,128]{1,0:T(8,128)S(1)}) custom-call(s32[4]{0:T(128)S(1)} %copy-done.4, f32[32]{0:T(128)S(1)} %copy-done.5, f32[32]{0:T(128)S(1)} %copy-done.6, f32[192,128]{1,0:T(8,128)S(1)} %bitcast.8, f32[1,128]{1,0:T(1,128)S(1)} %bitcast.10, f32[1,128]{1,0:T(1,128)S(1)} %bitcast.11), custom_call_target="tpu_custom_call" | custom-call | tf_op jit(solution)/shard_map/stream/pallas_call | solution.py:176
  9.8 0.5 %collective-permute-done.refs_0_ = f32[192,128]{1,0:T(8,128)S(1)} collective-permute-done((f32[192,128]{1,0:T(8,128)}, f32[192,128]{1,0:T(8,128)S(1)}, u32[]{:S(2)}, u32[]{:S(2)}) %collective-permute-start) | collective-permute-done | bytes 98336 | tf_op jit(solution)/shard_map/ppermute | solution.py:221
  10.3 0.4 %span.1 = (f32[192,128]{1,0:T(8,128)S(1)}, f32[192,128]{1,0:T(8,128)S(1)}, f32[192,128]{1,0:T(8,128)S(1)}, f32[192,128]{1,0:T(8,128)S(1)}, f32[2,192,128]{2,1,0:T(8,128)S(1)}) custom-call(f32[128,256]{1,0:T(8,128)S(1)} %get-tuple-element.15.matrix, f32[192,128]{1,0:T(8,128)S(1)} %bitcast.9, f32[192,128]{1,0:T(8,128)S(1)} %collective-permute-done.refs_0_, ...), custom_call_target="tpu_custom_call" | custom-call | tf_op jit(solution)/shard_map/span/pallas_call | solution.py:176
  10.7 1.8 %collective-permute-start.4 = (f32[2,192,128]{2,1,0:T(8,128)S(1)}, f32[2,192,128]{2,1,0:T(8,128)S(1)}, u32[]{:S(2)}, u32[]{:S(2)}) collective-permute-start(f32[2,192,128]{2,1,0:T(8,128)S(1)} %get-tuple-element.17.ours), channel_id=1, source_target_pairs={{0,8},{8,0},{16,24},{24,16},{1,9},{9,1},{17,25},{25,17},{2,10},{10... | collective-permute-start | bytes 589832 | tf_op jit(solution)/shard_map/ppermute | solution.py:221
  12.4 1.5 %collective-permute-start.5 = (f32[192,128]{1,0:T(8,128)S(1)}, f32[192,128]{1,0:T(8,128)S(1)}, u32[]{:S(2)}, u32[]{:S(2)}) collective-permute-start(f32[192,128]{1,0:T(8,128)S(1)} %get-tuple-element.18), channel_id=1, source_target_pairs={{0,1},{1,0},{2,3},{3,2},{4,5},{5,4},{6,7},{7,6},{8,12},{9,13},{10,... | collective-permute-start | bytes 294920 | tf_op jit(solution)/shard_map/ppermute | solution.py:209
  13.9 3.5 %collective-permute-start.6 = (f32[192,128]{1,0:T(8,128)S(1)}, f32[192,128]{1,0:T(8,128)S(1)}, u32[]{:S(2)}, u32[]{:S(2)}) collective-permute-start(f32[192,128]{1,0:T(8,128)S(1)} %get-tuple-element.19), channel_id=1, source_target_pairs={{0,2},{1,3},{2,0},{3,1},{4,6},{5,7},{6,4},{7,5},{16,18},{17,19},{1... | collective-permute-start | bytes 294920 | tf_op jit(solution)/shard_map/ppermute | solution.py:209
  17.4 2.3 %collective-permute-start.7 = (f32[192,128]{1,0:T(8,128)S(1)}, f32[192,128]{1,0:T(8,128)S(1)}, u32[]{:S(2)}, u32[]{:S(2)}) collective-permute-start(f32[192,128]{1,0:T(8,128)S(1)} %get-tuple-element.20), channel_id=1, source_target_pairs={{0,3},{1,2},{2,1},{3,0},{4,7},{5,6},{6,5},{7,4},{16,19},{17,18},{1... | collective-permute-start | bytes 294920 | tf_op jit(solution)/shard_map/ppermute | solution.py:209
  19.7 0.0 copy-start.9
  19.7 0.0 copy-start.10
  19.8 0.6 %copy-done.9 = f32[64]{0:T(128)S(1)} copy-done((f32[64]{0:T(128)S(1)}, f32[64]{0:T(128)}, u32[]{:S(2)}) %copy-start.9) | copy-done | bytes 280
  20.4 0.0 copy-done.10
  20.4 1.7 %wall.1.refs_0_ = f32[192,128]{1,0:T(8,128)S(1)} custom-call(s32[4]{0:T(128)S(1)} %copy-done.4, f32[64]{0:T(128)S(1)} %copy-done.9, s32[32]{0:T(128)S(1)} %copy-done.10, f32[32,32]{1,0:T(8,128)S(1)} %copy-done.2, f32[32,32]{1,0:T(8,128)S(1)} %copy-done.3, f32[192,128]{1,0:T(8,128)S(1)} %get-tuple-element.14.x_part, f32[192,128]{1,0:T(8,128)S(1)} %get-tuple-element.16.z_part, ...), custom_call_target="tpu_custom_call" | custom-call | tf_op jit(solution)/shard_map/wall/pallas_call | solution.py:176
  22.1 2.7 %collective-permute-done.7.refs_3_ = f32[192,128]{1,0:T(8,128)S(1)} collective-permute-done((f32[192,128]{1,0:T(8,128)S(1)}, f32[192,128]{1,0:T(8,128)S(1)}, u32[]{:S(2)}, u32[]{:S(2)}) %collective-permute-start.7) | collective-permute-done | bytes 98336 | tf_op jit(solution)/shard_map/ppermute | solution.py:209
  24.8 0.7 %finish.1 = f32[192,128]{1,0:T(8,128)} custom-call(f32[64,128]{1,0:T(8,128)S(1)} %get-tuple-element.13.mask, f32[192,128]{1,0:T(8,128)S(1)} %wall.1.refs_0_, f32[192,128]{1,0:T(8,128)S(1)} %collective-permute-done.5.refs_1_, f32[192,128]{1,0:T(8,128)S(1)} %collective-permute-done.6.refs_2_, f32[192,128]{1,0:T(8,128)S(1)} %collective-permute-done.7.refs_3_), custom_call_target="tpu_custom_call" | custom-call | tf_op jit(solution)/shard_map/finish/pallas_call | solution.py:176
  (18 shorter events, 0.0 us)
Async XLA Ops:
  0.0 9.8 %collective-permute-start.3 = (f32[192,128]{1,0:T(8,128)}, f32[192,128]{1,0:T(8,128)S(1)}, u32[]{:S(2)}, u32[]{:S(2)}) collective-permute-start(f32[192,128]{1,0:T(8,128)} %bitcast.4), channel_id=1, source_target_pairs={{8,11},{9,10},{10,9},{11,8},{12,15},{13,14},{14,13},{15,12},{24,27... | collective-permute-start | bytes 294920 | tf_op jit(solution)/shard_map/ppermute | solution.py:209
  0.7 9.1 %collective-permute-start.2 = (f32[192,128]{1,0:T(8,128)}, f32[192,128]{1,0:T(8,128)S(1)}, u32[]{:S(2)}, u32[]{:S(2)}) collective-permute-start(f32[192,128]{1,0:T(8,128)} %bitcast.5), channel_id=1, source_target_pairs={{8,10},{9,11},{10,8},{11,9},{12,14},{13,15},{14,12},{15,13},{24,26... | collective-permute-start | bytes 294920 | tf_op jit(solution)/shard_map/ppermute | solution.py:209
  1.3 8.5 %collective-permute-start.1 = (f32[192,128]{1,0:T(8,128)}, f32[192,128]{1,0:T(8,128)S(1)}, u32[]{:S(2)}, u32[]{:S(2)}) collective-permute-start(f32[192,128]{1,0:T(8,128)} %bitcast.6), channel_id=1, source_target_pairs={{0,4},{1,5},{2,6},{3,7},{4,0},{5,1},{6,2},{7,3},{8,9},{9,8},{10,11... | collective-permute-start | bytes 294920 | tf_op jit(solution)/shard_map/ppermute | solution.py:209
  5.4 4.8 %collective-permute-start = (f32[192,128]{1,0:T(8,128)}, f32[192,128]{1,0:T(8,128)S(1)}, u32[]{:S(2)}, u32[]{:S(2)}) collective-permute-start(f32[192,128]{1,0:T(8,128)} %bitcast.7), channel_id=1, source_target_pairs={{0,16},{8,24},{16,0},{24,8},{1,17},{9,25},{17,1},{25,9},{2,18},{10... | collective-permute-start | bytes 294920 | tf_op jit(solution)/shard_map/ppermute | solution.py:221
  7.0 0.7 %copy-start.7 = (f32[128]{0:T(128)S(1)}, f32[128]{0:T(128)}, u32[]{:S(2)}) copy-start(f32[128]{0:T(128)} %param.12) | copy-start | bytes 1540
  7.0 0.7 %copy-start.8 = (f32[128]{0:T(128)S(1)}, f32[128]{0:T(128)}, u32[]{:S(2)}) copy-start(f32[128]{0:T(128)} %param.13) | copy-start | bytes 1540
  7.0 0.7 %copy-start.4 = (s32[4]{0:T(128)S(1)}, s32[4]{0:T(128)}, u32[]{:S(2)}) copy-start(s32[4]{0:T(128)} %wall_counts.3) | copy-start | bytes 52
  7.0 0.7 %copy-start.5 = (f32[32]{0:T(128)S(1)}, f32[32]{0:T(128)}, u32[]{:S(2)}) copy-start(f32[32]{0:T(128)} %z_first.1) | copy-start | bytes 388
  7.0 0.7 %copy-start.6 = (f32[32]{0:T(128)S(1)}, f32[32]{0:T(128)}, u32[]{:S(2)}) copy-start(f32[32]{0:T(128)} %z_second.1) | copy-start | bytes 388
  7.7 0.9 %copy-start = (f32[3,16,4,128]{3,2,1,0:T(4,128)S(1)}, f32[3,16,4,128]{3,2,1,0:T(4,128)}, u32[]{:S(2)}) copy-start(f32[3,16,4,128]{3,2,1,0:T(4,128)} %param.10) | copy-start | bytes 294916
  8.6 1.7 %copy-start.1 = (f32[3,16,4,128]{3,2,1,0:T(4,128)S(1)}, f32[3,16,4,128]{3,2,1,0:T(4,128)}, u32[]{:S(2)}) copy-start(f32[3,16,4,128]{3,2,1,0:T(4,128)} %param.10) | copy-start | bytes 294916
  10.3 9.5 %copy-start.2 = (f32[32,32]{1,0:T(8,128)S(1)}, f32[32,32]{1,0:T(8,128)}, u32[]{:S(2)}) copy-start(f32[32,32]{1,0:T(8,128)} %y_first.1) | copy-start | bytes 12292
  10.3 9.5 %copy-start.3 = (f32[32,32]{1,0:T(8,128)S(1)}, f32[32,32]{1,0:T(8,128)}, u32[]{:S(2)}) copy-start(f32[32,32]{1,0:T(8,128)} %y_second.1) | copy-start | bytes 12292
  10.7 9.1 %collective-permute-start.4 = (f32[2,192,128]{2,1,0:T(8,128)S(1)}, f32[2,192,128]{2,1,0:T(8,128)S(1)}, u32[]{:S(2)}, u32[]{:S(2)}) collective-permute-start(f32[2,192,128]{2,1,0:T(8,128)S(1)} %get-tuple-element.17.ours), channel_id=1, source_target_pairs={{0,8},{8,0},{16,24},{24,16},{1,9},{9,1},{17,25},{25,17},{2,10},{10... | collective-permute-start | bytes 589832 | tf_op jit(solution)/shard_map/ppermute | solution.py:221
  12.4 9.7 %collective-permute-start.5 = (f32[192,128]{1,0:T(8,128)S(1)}, f32[192,128]{1,0:T(8,128)S(1)}, u32[]{:S(2)}, u32[]{:S(2)}) collective-permute-start(f32[192,128]{1,0:T(8,128)S(1)} %get-tuple-element.18), channel_id=1, source_target_pairs={{0,1},{1,0},{2,3},{3,2},{4,5},{5,4},{6,7},{7,6},{8,12},{9,13},{10,... | collective-permute-start | bytes 294920 | tf_op jit(solution)/shard_map/ppermute | solution.py:209
  13.9 8.2 %collective-permute-start.6 = (f32[192,128]{1,0:T(8,128)S(1)}, f32[192,128]{1,0:T(8,128)S(1)}, u32[]{:S(2)}, u32[]{:S(2)}) collective-permute-start(f32[192,128]{1,0:T(8,128)S(1)} %get-tuple-element.19), channel_id=1, source_target_pairs={{0,2},{1,3},{2,0},{3,1},{4,6},{5,7},{6,4},{7,5},{16,18},{17,19},{1... | collective-permute-start | bytes 294920 | tf_op jit(solution)/shard_map/ppermute | solution.py:209
  17.4 7.4 %collective-permute-start.7 = (f32[192,128]{1,0:T(8,128)S(1)}, f32[192,128]{1,0:T(8,128)S(1)}, u32[]{:S(2)}, u32[]{:S(2)}) collective-permute-start(f32[192,128]{1,0:T(8,128)S(1)} %get-tuple-element.20), channel_id=1, source_target_pairs={{0,3},{1,2},{2,1},{3,0},{4,7},{5,6},{6,5},{7,4},{16,19},{17,18},{1... | collective-permute-start | bytes 294920 | tf_op jit(solution)/shard_map/ppermute | solution.py:209
  19.7 0.7 %copy-start.9 = (f32[64]{0:T(128)S(1)}, f32[64]{0:T(128)}, u32[]{:S(2)}) copy-start(f32[64]{0:T(128)} %metric_table.1) | copy-start | bytes 772
  19.7 0.7 %copy-start.10 = (s32[32]{0:T(128)S(1)}, s32[32]{0:T(128)}, u32[]{:S(2)}) copy-start(s32[32]{0:T(128)} %metric_index.1) | copy-start | bytes 388

commit v10 on v9

--- a/solution.py
+++ b/solution.py
@@ -210,10 +210,9 @@
             value,
             ("row", "col"),
             [
-                (r * cols + c, r * cols + (c ^ (steps[r % 2] * index)))
+                (r * cols + c, r * cols + (c ^ (steps[r % 2] * index if index < limits[r % 2] else 0)))
                 for r in range(rows)
                 for c in range(cols)
-                if index < limits[r % 2]
             ],
         )
 

time: 25.7 us -> 26.6 us (1.035)
  waiting for transfers between devices: 3.13 us -> 3.91 us
    ppermute x6, starting transfers between devices: 12.7 us -> 14.5 us  [along(): lax.ppermute(value, ('row', 'col'), [(r * cols + c, r * cols + (c ^ (step...]
    ppermute x2, starting transfers between devices: 3.27 us -> 1.59 us  [across(): return lax.ppermute(value, 'row', [(i, i ^ step) for i in range(rows)])]
    ppermute x2, waiting for transfers between devices: 0.46 us -> 1.11 us  [across(): return lax.ppermute(value, 'row', [(i, i ^ step) for i in range(rows)])]
where the time goes in v10:
time: 26.6 us; the launch traced here: 26.3 us
  starting transfers between devices  16.1 us (61%)
  Pallas kernels  3.95 us (15%)
  waiting for transfers between devices  3.91 us (15%)
  local copies, waits for them, and re-layouts  2.24 us (8%)
    ppermute x6, starting transfers between devices, along(): lax.ppermute(value, ('row', 'col'), [(r * cols + c, r * cols + (c ^ (step...  14.5 us
    pallas_call x4, Pallas kernels, call(): pl.pallas_call(kernel, out_shape=results, in_specs=[pl.BlockSpec(memory_s...  3.95 us
    ppermute x6, waiting for transfers between devices, along(): lax.ppermute(value, ('row', 'col'), [(r * cols + c, r * cols + (c ^ (step...  2.8 us
    unnamed x22, local copies, waits for them, and re-layouts  2.24 us
    ppermute x2, starting transfers between devices, across(): return lax.ppermute(value, 'row', [(i, i ^ step) for i in range(rows)])  1.59 us
    ppermute x2, waiting for transfers between devices, across(): return lax.ppermute(value, 'row', [(i, i ^ step) for i in range(rows)])  1.11 us
  transfers between devices with their start and end apart: 8, of which 2 were waited for; matrix products, arithmetic and copies ran while one was open for 0% of the time, Pallas kernels for 11%

profile of v10, /device:TPU:0, one launch (start us, length us, event | category | flops | bytes accessed | tf_op | source)
XLA Modules:
  0.0 26.3 jit_solution(14414952589207479908)
XLA Ops:
  0.0 1.5 %collective-permute-start.3 = (f32[192,128]{1,0:T(8,128)}, f32[192,128]{1,0:T(8,128)S(1)}, u32[]{:S(2)}, u32[]{:S(2)}) collective-permute-start(f32[192,128]{1,0:T(8,128)} %bitcast.4), channel_id=1, source_target_pairs={{0,0},{1,1},{2,2},{3,3},{4,4},{5,5},{6,6},{7,7},{8,11},{9,10},{10,... | collective-permute-start | bytes 294920 | tf_op jit(solution)/shard_map/ppermute | solution.py:209
  1.5 1.5 %collective-permute-start.2 = (f32[192,128]{1,0:T(8,128)}, f32[192,128]{1,0:T(8,128)S(1)}, u32[]{:S(2)}, u32[]{:S(2)}) collective-permute-start(f32[192,128]{1,0:T(8,128)} %bitcast.5), channel_id=1, source_target_pairs={{0,0},{1,1},{2,2},{3,3},{4,4},{5,5},{6,6},{7,7},{8,10},{9,11},{10,... | collective-permute-start | bytes 294920 | tf_op jit(solution)/shard_map/ppermute | solution.py:209
  3.1 4.0 %collective-permute-start.1 = (f32[192,128]{1,0:T(8,128)}, f32[192,128]{1,0:T(8,128)S(1)}, u32[]{:S(2)}, u32[]{:S(2)}) collective-permute-start(f32[192,128]{1,0:T(8,128)} %bitcast.6), channel_id=1, source_target_pairs={{0,4},{1,5},{2,6},{3,7},{4,0},{5,1},{6,2},{7,3},{8,9},{9,8},{10,11... | collective-permute-start | bytes 294920 | tf_op jit(solution)/shard_map/ppermute | solution.py:209
  7.1 1.5 %collective-permute-start = (f32[192,128]{1,0:T(8,128)}, f32[192,128]{1,0:T(8,128)S(1)}, u32[]{:S(2)}, u32[]{:S(2)}) collective-permute-start(f32[192,128]{1,0:T(8,128)} %bitcast.7), channel_id=1, source_target_pairs={{0,16},{8,24},{16,0},{24,8},{1,17},{9,25},{17,1},{25,9},{2,18},{10... | collective-permute-start | bytes 294920 | tf_op jit(solution)/shard_map/ppermute | solution.py:220
  8.7 0.6 %copy-done.7 = f32[128]{0:T(128)S(1)} copy-done((f32[128]{0:T(128)S(1)}, f32[128]{0:T(128)}, u32[]{:S(2)}) %copy-start.7) | copy-done | bytes 536
  9.3 0.0 copy-done.8
  9.3 0.0 copy-done.4
  9.3 0.0 copy-done.5
  9.3 0.0 copy-done.6
  9.4 0.9 %copy-done = f32[3,16,4,128]{3,2,1,0:T(4,128)S(1)} copy-done((f32[3,16,4,128]{3,2,1,0:T(4,128)S(1)}, f32[3,16,4,128]{3,2,1,0:T(4,128)}, u32[]{:S(2)}) %copy-start) | copy-done | bytes 98328
  10.2 1.2 %stream.1 = (f32[192,128]{1,0:T(8,128)S(1)}, f32[128,256]{1,0:T(8,128)S(1)}, f32[64,128]{1,0:T(8,128)S(1)}) custom-call(s32[4]{0:T(128)S(1)} %copy-done.4, f32[32]{0:T(128)S(1)} %copy-done.5, f32[32]{0:T(128)S(1)} %copy-done.6, f32[192,128]{1,0:T(8,128)S(1)} %bitcast.8, f32[1,128]{1,0:T(1,128)S(1)} %bitcast.10, f32[1,128]{1,0:T(1,128)S(1)} %bitcast.11), custom_call_target="tpu_custom_call" | custom-call | tf_op jit(solution)/shard_map/stream/pallas_call | solution.py:176
  11.5 1.1 %collective-permute-done.refs_0_ = f32[192,128]{1,0:T(8,128)S(1)} collective-permute-done((f32[192,128]{1,0:T(8,128)}, f32[192,128]{1,0:T(8,128)S(1)}, u32[]{:S(2)}, u32[]{:S(2)}) %collective-permute-start) | collective-permute-done | bytes 98336 | tf_op jit(solution)/shard_map/ppermute | solution.py:220
  12.6 0.4 %span.1 = (f32[192,128]{1,0:T(8,128)S(1)}, f32[192,128]{1,0:T(8,128)S(1)}, f32[192,128]{1,0:T(8,128)S(1)}, f32[192,128]{1,0:T(8,128)S(1)}, f32[2,192,128]{2,1,0:T(8,128)S(1)}) custom-call(f32[128,256]{1,0:T(8,128)S(1)} %get-tuple-element.15.matrix, f32[192,128]{1,0:T(8,128)S(1)} %bitcast.9, f32[192,128]{1,0:T(8,128)S(1)} %collective-permute-done.refs_0_, ...), custom_call_target="tpu_custom_call" | custom-call | tf_op jit(solution)/shard_map/span/pallas_call | solution.py:176
  13.0 0.1 collective-permute-start.4
  13.1 1.7 %collective-permute-start.5 = (f32[192,128]{1,0:T(8,128)S(1)}, f32[192,128]{1,0:T(8,128)S(1)}, u32[]{:S(2)}, u32[]{:S(2)}) collective-permute-start(f32[192,128]{1,0:T(8,128)S(1)} %get-tuple-element.18), channel_id=1, source_target_pairs={{0,1},{1,0},{2,3},{3,2},{4,5},{5,4},{6,7},{7,6},{8,12},{9,13},{10,... | collective-permute-start | bytes 294920 | tf_op jit(solution)/shard_map/ppermute | solution.py:209
  14.8 3.5 %collective-permute-start.6 = (f32[192,128]{1,0:T(8,128)S(1)}, f32[192,128]{1,0:T(8,128)S(1)}, u32[]{:S(2)}, u32[]{:S(2)}) collective-permute-start(f32[192,128]{1,0:T(8,128)S(1)} %get-tuple-element.19), channel_id=1, source_target_pairs={{0,2},{1,3},{2,0},{3,1},{4,6},{5,7},{6,4},{7,5},{8,8},{9,9},{10,10... | collective-permute-start | bytes 294920 | tf_op jit(solution)/shard_map/ppermute | solution.py:209
  18.2 2.2 %collective-permute-start.7 = (f32[192,128]{1,0:T(8,128)S(1)}, f32[192,128]{1,0:T(8,128)S(1)}, u32[]{:S(2)}, u32[]{:S(2)}) collective-permute-start(f32[192,128]{1,0:T(8,128)S(1)} %get-tuple-element.20), channel_id=1, source_target_pairs={{0,3},{1,2},{2,1},{3,0},{4,7},{5,6},{6,5},{7,4},{8,8},{9,9},{10,10... | collective-permute-start | bytes 294920 | tf_op jit(solution)/shard_map/ppermute | solution.py:209
  20.4 0.0 copy-start.9
  20.5 0.0 copy-start.10
  20.5 0.6 %copy-done.9 = f32[64]{0:T(128)S(1)} copy-done((f32[64]{0:T(128)S(1)}, f32[64]{0:T(128)}, u32[]{:S(2)}) %copy-start.9) | copy-done | bytes 280
  21.1 0.0 copy-done.10
  21.1 1.7 %wall.1.refs_0_ = f32[192,128]{1,0:T(8,128)S(1)} custom-call(s32[4]{0:T(128)S(1)} %copy-done.4, f32[64]{0:T(128)S(1)} %copy-done.9, s32[32]{0:T(128)S(1)} %copy-done.10, f32[32,32]{1,0:T(8,128)S(1)} %copy-done.2, f32[32,32]{1,0:T(8,128)S(1)} %copy-done.3, f32[192,128]{1,0:T(8,128)S(1)} %get-tuple-element.14.x_part, f32[192,128]{1,0:T(8,128)S(1)} %get-tuple-element.16.z_part, ...), custom_call_target="tpu_custom_call" | custom-call | tf_op jit(solution)/shard_map/wall/pallas_call | solution.py:176
  22.9 2.8 %collective-permute-done.7.refs_3_ = f32[192,128]{1,0:T(8,128)S(1)} collective-permute-done((f32[192,128]{1,0:T(8,128)S(1)}, f32[192,128]{1,0:T(8,128)S(1)}, u32[]{:S(2)}, u32[]{:S(2)}) %collective-permute-start.7) | collective-permute-done | bytes 98336 | tf_op jit(solution)/shard_map/ppermute | solution.py:209
  25.6 0.7 %finish.1 = f32[192,128]{1,0:T(8,128)} custom-call(f32[64,128]{1,0:T(8,128)S(1)} %get-tuple-element.13.mask, f32[192,128]{1,0:T(8,128)S(1)} %wall.1.refs_0_, f32[192,128]{1,0:T(8,128)S(1)} %collective-permute-done.5.refs_1_, f32[192,128]{1,0:T(8,128)S(1)} %collective-permute-done.6.refs_2_, f32[192,128]{1,0:T(8,128)S(1)} %collective-permute-done.7.refs_3_), custom_call_target="tpu_custom_call" | custom-call | tf_op jit(solution)/shard_map/finish/pallas_call | solution.py:176
  (18 shorter events, 0.0 us)
Async XLA Ops:
  0.0 11.5 %collective-permute-start.3 = (f32[192,128]{1,0:T(8,128)}, f32[192,128]{1,0:T(8,128)S(1)}, u32[]{:S(2)}, u32[]{:S(2)}) collective-permute-start(f32[192,128]{1,0:T(8,128)} %bitcast.4), channel_id=1, source_target_pairs={{0,0},{1,1},{2,2},{3,3},{4,4},{5,5},{6,6},{7,7},{8,11},{9,10},{10,... | collective-permute-start | bytes 294920 | tf_op jit(solution)/shard_map/ppermute | solution.py:209
  1.5 9.9 %collective-permute-start.2 = (f32[192,128]{1,0:T(8,128)}, f32[192,128]{1,0:T(8,128)S(1)}, u32[]{:S(2)}, u32[]{:S(2)}) collective-permute-start(f32[192,128]{1,0:T(8,128)} %bitcast.5), channel_id=1, source_target_pairs={{0,0},{1,1},{2,2},{3,3},{4,4},{5,5},{6,6},{7,7},{8,10},{9,11},{10,... | collective-permute-start | bytes 294920 | tf_op jit(solution)/shard_map/ppermute | solution.py:209
  3.1 8.4 %collective-permute-start.1 = (f32[192,128]{1,0:T(8,128)}, f32[192,128]{1,0:T(8,128)S(1)}, u32[]{:S(2)}, u32[]{:S(2)}) collective-permute-start(f32[192,128]{1,0:T(8,128)} %bitcast.6), channel_id=1, source_target_pairs={{0,4},{1,5},{2,6},{3,7},{4,0},{5,1},{6,2},{7,3},{8,9},{9,8},{10,11... | collective-permute-start | bytes 294920 | tf_op jit(solution)/shard_map/ppermute | solution.py:209
  7.1 5.5 %collective-permute-start = (f32[192,128]{1,0:T(8,128)}, f32[192,128]{1,0:T(8,128)S(1)}, u32[]{:S(2)}, u32[]{:S(2)}) collective-permute-start(f32[192,128]{1,0:T(8,128)} %bitcast.7), channel_id=1, source_target_pairs={{0,16},{8,24},{16,0},{24,8},{1,17},{9,25},{17,1},{25,9},{2,18},{10... | collective-permute-start | bytes 294920 | tf_op jit(solution)/shard_map/ppermute | solution.py:220
  8.6 0.7 %copy-start.7 = (f32[128]{0:T(128)S(1)}, f32[128]{0:T(128)}, u32[]{:S(2)}) copy-start(f32[128]{0:T(128)} %param.12) | copy-start | bytes 1540
  8.6 0.7 %copy-start.8 = (f32[128]{0:T(128)S(1)}, f32[128]{0:T(128)}, u32[]{:S(2)}) copy-start(f32[128]{0:T(128)} %param.13) | copy-start | bytes 1540
  8.6 0.7 %copy-start.4 = (s32[4]{0:T(128)S(1)}, s32[4]{0:T(128)}, u32[]{:S(2)}) copy-start(s32[4]{0:T(128)} %wall_counts.3) | copy-start | bytes 52
  8.6 0.7 %copy-start.5 = (f32[32]{0:T(128)S(1)}, f32[32]{0:T(128)}, u32[]{:S(2)}) copy-start(f32[32]{0:T(128)} %z_first.1) | copy-start | bytes 388
  8.6 0.7 %copy-start.6 = (f32[32]{0:T(128)S(1)}, f32[32]{0:T(128)}, u32[]{:S(2)}) copy-start(f32[32]{0:T(128)} %z_second.1) | copy-start | bytes 388
  9.4 0.9 %copy-start = (f32[3,16,4,128]{3,2,1,0:T(4,128)S(1)}, f32[3,16,4,128]{3,2,1,0:T(4,128)}, u32[]{:S(2)}) copy-start(f32[3,16,4,128]{3,2,1,0:T(4,128)} %param.10) | copy-start | bytes 294916
  10.2 2.4 %copy-start.1 = (f32[3,16,4,128]{3,2,1,0:T(4,128)S(1)}, f32[3,16,4,128]{3,2,1,0:T(4,128)}, u32[]{:S(2)}) copy-start(f32[3,16,4,128]{3,2,1,0:T(4,128)} %param.10) | copy-start | bytes 294916
  12.6 7.9 %copy-start.2 = (f32[32,32]{1,0:T(8,128)S(1)}, f32[32,32]{1,0:T(8,128)}, u32[]{:S(2)}) copy-start(f32[32,32]{1,0:T(8,128)} %y_first.1) | copy-start | bytes 12292
  12.6 7.9 %copy-start.3 = (f32[32,32]{1,0:T(8,128)S(1)}, f32[32,32]{1,0:T(8,128)}, u32[]{:S(2)}) copy-start(f32[32,32]{1,0:T(8,128)} %y_second.1) | copy-start | bytes 12292
  13.0 7.5 %collective-permute-start.4 = (f32[2,192,128]{2,1,0:T(8,128)S(1)}, f32[2,192,128]{2,1,0:T(8,128)S(1)}, u32[]{:S(2)}, u32[]{:S(2)}) collective-permute-start(f32[2,192,128]{2,1,0:T(8,128)S(1)} %get-tuple-element.17.ours), channel_id=1, source_target_pairs={{0,8},{8,0},{16,24},{24,16},{1,9},{9,1},{17,25},{25,17},{2,10},{10... | collective-permute-start | bytes 589832 | tf_op jit(solution)/shard_map/ppermute | solution.py:220
  13.1 9.8 %collective-permute-start.5 = (f32[192,128]{1,0:T(8,128)S(1)}, f32[192,128]{1,0:T(8,128)S(1)}, u32[]{:S(2)}, u32[]{:S(2)}) collective-permute-start(f32[192,128]{1,0:T(8,128)S(1)} %get-tuple-element.18), channel_id=1, source_target_pairs={{0,1},{1,0},{2,3},{3,2},{4,5},{5,4},{6,7},{7,6},{8,12},{9,13},{10,... | collective-permute-start | bytes 294920 | tf_op jit(solution)/shard_map/ppermute | solution.py:209
  14.8 8.1 %collective-permute-start.6 = (f32[192,128]{1,0:T(8,128)S(1)}, f32[192,128]{1,0:T(8,128)S(1)}, u32[]{:S(2)}, u32[]{:S(2)}) collective-permute-start(f32[192,128]{1,0:T(8,128)S(1)} %get-tuple-element.19), channel_id=1, source_target_pairs={{0,2},{1,3},{2,0},{3,1},{4,6},{5,7},{6,4},{7,5},{8,8},{9,9},{10,10... | collective-permute-start | bytes 294920 | tf_op jit(solution)/shard_map/ppermute | solution.py:209
  18.2 7.4 %collective-permute-start.7 = (f32[192,128]{1,0:T(8,128)S(1)}, f32[192,128]{1,0:T(8,128)S(1)}, u32[]{:S(2)}, u32[]{:S(2)}) collective-permute-start(f32[192,128]{1,0:T(8,128)S(1)} %get-tuple-element.20), channel_id=1, source_target_pairs={{0,3},{1,2},{2,1},{3,0},{4,7},{5,6},{6,5},{7,4},{8,8},{9,9},{10,10... | collective-permute-start | bytes 294920 | tf_op jit(solution)/shard_map/ppermute | solution.py:209
  20.4 0.7 %copy-start.9 = (f32[64]{0:T(128)S(1)}, f32[64]{0:T(128)}, u32[]{:S(2)}) copy-start(f32[64]{0:T(128)} %metric_table.1) | copy-start | bytes 772
  20.5 0.7 %copy-start.10 = (s32[32]{0:T(128)S(1)}, s32[32]{0:T(128)}, u32[]{:S(2)}) copy-start(s32[32]{0:T(128)} %metric_index.1) | copy-start | bytes 388

commit v11 on v8

v11 whole, which is shorter than its diff:
```python
import functools
import math

import jax
import jax.numpy as jnp
from jax import lax
from jax.experimental import pallas as pl
from jax.experimental.pallas import tpu as pltpu
from jax.sharding import PartitionSpec as P

viscosity = 0.4
quad = 4

VMEM = pltpu.VMEM
SMEM = pltpu.SMEM


def halves(value):
    high = value.astype(jnp.bfloat16)
    low = (value - high.astype(jnp.float32)).astype(jnp.bfloat16)
    return high, low


def by_parity(odd, pair):
    return jnp.where(odd == 1, *reversed(pair))


def dot_split(left, right, transposed=False):
    dims = (((1,), (1 if transposed else 0,)), ((), ()))
    mul = functools.partial(lax.dot_general, dimension_numbers=dims, preferred_element_type=jnp.float32)
    lh, ll = halves(left)
    rh, rl = halves(right)
    return mul(lh, rh) + (mul(lh, rl) + mul(ll, rh))


def span_kernel(comps, hand_on, matrix, field, *refs):
    count = len(hand_on)
    sources, parts = (field,) + refs[-count - 1 :: -1], refs[-count:]
    odd = lax.axis_index("row") % 2
    depth, length = field.shape[0] // comps, field.shape[1]
    group = matrix.shape[0] // count
    right = []
    for comp in range(comps):
        for at in range(0, depth, group):
            stack = [source[comp * depth + at : comp * depth + at + group] for source in sources]
            stack += [value * source[2 * depth + at : 2 * depth + at + group] for value, source in zip(stack, sources)]
            right.append(jnp.concatenate(stack, axis=0))
    result = dot_split(matrix[...], jnp.concatenate(right, axis=1))
    for t in range(count):
        for i in range(len(right)):
            at = slice(i * group, (i + 1) * group)
            value = result[t * group : (t + 1) * group, i * length : (i + 1) * length]
            if any(hand_on[t]):
                value = jnp.where(by_parity(odd, hand_on[t]), field[at], value)
            parts[t][at] = value


def circulant_rows(row, length):
    return pltpu.roll(jnp.broadcast_to(row, (length, length)), 0, 1, stride=1, stride_axis=0)


def stream_kernel(
    cols, comps, zloc, wall_counts, z_first, z_second, field, x_first, x_second, x_part, z_matrix, mask
):
    depth = mask.shape[0]
    length = field.shape[1]
    count = wall_counts[lax.axis_index("row")]
    mask[...] = (lax.broadcasted_iota(jnp.int32, mask.shape, 0) // zloc < count).astype(jnp.float32)

    cells_z = cols * zloc
    shape = z_matrix.shape
    half = shape[1] // 2
    group = half // max(quad, cols // quad)
    mine = lax.axis_index("col")
    odd = lax.axis_index("row") % 2
    r = lax.broadcasted_iota(jnp.int32, shape, 0)
    q = lax.broadcasted_iota(jnp.int32, shape, 1)
    q = jnp.where(q < half, q, q - half)
    t, s = r // group, q // group
    into = by_parity(odd, (inner_step(t), quad * t))
    outof = by_parity(odd, (quad * s, inner_step(s)))
    out_cell = (into ^ mine) * zloc + r % zloc
    in_cell = (outof ^ mine) * zloc + q % zloc
    used = (t < by_parity(odd, (quad, cols // quad))) & (s < by_parity(odd, (cols // quad, quad)))
    used &= (r % group) // zloc == (q % group) // zloc
    gap = jnp.where(used, (in_cell - out_cell + cells_z) % cells_z, -1)
    kind = lax.broadcasted_iota(jnp.int32, (1, shape[1]), 1) < half

    def fill(k, total):
        value = jnp.where(kind, viscosity * z_second[k], -z_first[k])
        return jnp.where(gap == k, value, total)

    z_matrix[...] = lax.fori_loop(0, cells_z, fill, jnp.zeros(shape, jnp.float32), unroll=8)

    u = field[...]
    lead = u[:depth]
    left = jnp.concatenate(
        [u, jnp.concatenate([lead * u[c * depth : (c + 1) * depth] for c in range(comps)], axis=0)], axis=1
    )
    right = jnp.concatenate(
        [viscosity * circulant_rows(x_second[...], length), -circulant_rows(x_first[...], length)], axis=1
    )
    x_part[...] = dot_split(left, right, transposed=True)


def wall_matrix_kernel(rows, zloc, wall_counts, metric_table, metric_index, y_first, y_second, after, matrix):
    cells = y_first.shape[0]
    depth = matrix.shape[0] // 2
    me = lax.axis_index("row")
    plain = functools.partial(
        lax.dot_general, dimension_numbers=(((1,), (0,)), ((), ())), preferred_element_type=jnp.float32
    )
    turned = functools.partial(
        lax.dot_general, dimension_numbers=(((1,), (1,)), ((), ())), preferred_element_type=jnp.float32
    )

    def spots(index):
        start = lax.fori_loop(0, rows, lambda i, acc: acc + jnp.where(i < index, wall_counts[i], 0), 0, unroll=True)
        plane = lax.broadcasted_iota(jnp.int32, (depth, cells), 0) // zloc
        cell = lax.broadcasted_iota(jnp.int32, (depth, cells), 1)
        return ((plane < wall_counts[index]) & (plane + start == cell)).astype(jnp.float32)

    levels = metric_table.shape[1]
    entry = (lax.broadcasted_iota(jnp.int32, (levels, cells), 0) == metric_index[...]).astype(jnp.float32)
    table = jnp.broadcast_to(metric_table[...], (8, levels))
    metric = plain(table, entry, precision=lax.Precision.HIGHEST)[:1]
    ends = jnp.concatenate([spots(me), spots(me ^ 1)], axis=0)
    scale = jnp.sum(ends * metric, axis=1, keepdims=True)
    pick = ends.astype(jnp.bfloat16)
    second = sum(plain(pick, part) for part in halves(viscosity * y_second[...]))
    first = -scale * sum(plain(pick, part) for part in halves(y_first[...]))
    other = jnp.concatenate([spots(me ^ step) for step in range(0, rows, 2)], axis=0).astype(jnp.bfloat16)
    wide = sum(turned(part, other) for part in halves(jnp.concatenate([second, first], axis=0)))
    match = lax.broadcasted_iota(jnp.int32, wide.shape, 0) % zloc == lax.broadcasted_iota(jnp.int32, wide.shape, 1) % zloc
    wide = jnp.where(match, wide, 0.0)
    for b in range(rows // 2):
        for k in range(2):
            matrix[:, (2 * b + k) * depth : (2 * b + k + 1) * depth] = wide[
                2 * k * depth : 2 * (k + 1) * depth, b * depth : (b + 1) * depth
            ]


def wall_kernel(comps, matrix, x_part, z_part, field, *refs):
    far, (total, away) = refs[:-2], refs[-2:]
    odd = lax.axis_index("row") % 2
    depth = x_part.shape[0] // comps
    fields = [field[...]] + [by_parity(odd, (even[...], other[...])) for even, other in zip(far[::2], far[1::2])]
    for comp in range(comps):
        at = slice(comp * depth, (comp + 1) * depth)
        stack = []
        for value in fields:
            stack += [value[at], value[depth : 2 * depth] * value[at]]
        result = dot_split(matrix[...], jnp.concatenate(stack, axis=0))
        total[at] = x_part[at] + z_part[at] + result[:depth]
        away[at] = result[depth:]


def finish_kernel(comps, use, mask, total, near, *refs):
    parts, out = refs[:-1], refs[-1]
    odd = lax.axis_index("row") % 2
    depth = mask.shape[0]
    for comp in range(comps):
        at = slice(comp * depth, (comp + 1) * depth)
        value = total[at] + near[at]
        for part, pair in zip(parts, use):
            value += part[at] if all(pair) else jnp.where(by_parity(odd, pair), part[at], 0.0)
        out[at] = jnp.where(mask[...] > 0, value, 0.0)


def inner_step(index):
    return (quad - index) % quad


def plan(rows, cols):
    wide = cols // quad
    steps = {"outer": [quad * i for i in range(1, wide)], "inner": [inner_step(i) for i in range(1, quad)]}
    order = (("outer", "inner"), ("inner", "outer"))
    count = max(wide, quad) - 1
    stages = [[[None, None] for _ in range(count)] for _ in range(2)] + [[]]
    found = []
    for parity in range(2):
        wanted = list(range(2, rows, 2))
        spots = {}
        for stage in range(2):
            own = steps[order[parity][stage]]
            for i in range(count):
                if i < len(own):
                    stages[stage][i][parity] = ("col", own[i])
                else:
                    step = wanted.pop(0) if wanted else None
                    stages[stage][i][parity] = ("row", step or 2)
                    if step:
                        spots[step] = (stage, i)
        for i, step in enumerate(wanted):
            if i == len(stages[2]):
                stages[2].append([("row", 2), ("row", 2)])
            stages[2][i][parity] = ("row", step)
            spots[step] = (2, i)
        found.append(spots)
    return stages, found


def call(kernel, operands, spaces, results, name, scratch=()):
    results = [jax.ShapeDtypeStruct(shape, jnp.float32) for shape in results]
    held = sum(4 * math.prod(array.shape) for array in list(operands) + results)
    return pl.pallas_call(
        kernel,
        out_shape=results,
        in_specs=[pl.BlockSpec(memory_space=space) for space in spaces],
        out_specs=[pl.BlockSpec(memory_space=VMEM)] * len(results),
        scratch_shapes=[pltpu.VMEM(shape, jnp.float32) for shape in scratch],
        compiler_params=pltpu.CompilerParams(vmem_limit_bytes=(4 << 20) + 3 * held),
        name=name,
    )(*operands)


def local(
    velocity,
    wall_counts,
    x_first,
    x_second,
    y_first,
    y_second,
    z_first,
    z_second,
    metric_table,
    metric_index,
):
    rows = lax.axis_size("row")
    cols = lax.axis_size("col")
    comps, slots, zloc, length = velocity.shape
    depth = slots * zloc
    field = velocity.reshape(comps * depth, length)
    group = min(depth, 32)
    stages, found = plan(rows, cols)
    count = len(stages[0]) + 1

    def trade(value, moves):
        pairs = []
        for r in range(rows):
            for c in range(cols):
                axis, step = moves[r % 2]
                to = (r ^ step, c) if axis == "row" else (r, c ^ step)
                pairs.append((r * cols + c, to[0] * cols + to[1]))
        return lax.ppermute(value, ("row", "col"), pairs)

    gathered = [trade(field, moves) for moves in stages[0]]
    extra = [trade(field, moves) for moves in stages[2]]
    x_part, z_matrix, mask = call(
        functools.partial(stream_kernel, cols, comps, zloc),
        [wall_counts, z_first, z_second, field, x_first.reshape(1, length), x_second.reshape(1, length)],
        [SMEM] * 3 + [VMEM] * 3,
        [field.shape, (count * group, 2 * count * group), (depth, length)],
        "stream",
    )
    hand_on = [(False, False)] + [
        tuple((1, i) in found[parity].values() for parity in range(2)) for i in range(count - 1)
    ]
    parts = call(
        functools.partial(span_kernel, comps, hand_on),
        [z_matrix, field] + gathered[::-1],
        [VMEM] * (count + 1),
        [field.shape] * count,
        "span",
    )
    returned = [trade(part, moves) for part, moves in zip(parts[1:], stages[1])]
    (y_matrix,) = call(
        functools.partial(wall_matrix_kernel, rows, zloc),
        [wall_counts, metric_table.reshape(1, -1), metric_index.reshape(1, -1), y_first, y_second, parts[0]],
        [SMEM] + [VMEM] * 4 + [pl.ANY],
        [(2 * depth, rows * depth)],
        "wall_matrix",
    )
    arrived = (gathered, returned, extra)
    far = [arrived[stage][i] for step in range(2, rows, 2) for stage, i in (found[0][step], found[1][step])]
    total, away = call(
        functools.partial(wall_kernel, comps),
        [y_matrix, x_part, parts[0], field] + far,
        [VMEM] * (4 + len(far)),
        [field.shape] * 2,
        "wall",
    )
    near = trade(away, (("row", 1), ("row", 1)))
    use = [tuple(moves[parity][0] == "col" for parity in range(2)) for moves in stages[1]]
    (result,) = call(
        functools.partial(finish_kernel, comps, use),
        [mask, total, near] + returned,
        [VMEM] * (count + 2),
        [field.shape],
        "finish",
    )
    return result.reshape(velocity.shape)


def solution(mesh):
    in_specs = (P(None, "row", "col", None), P(), P(), P(), P(), P(), P(), P(), P(), P())
    out_specs = P(None, "row", "col", None)
    return jax.shard_map(local, mesh=mesh, in_specs=in_specs, out_specs=out_specs, check_vma=False)
```

time: 18.7 us -> 19.8 us (1.059)
  waiting for transfers between devices: 3.24 us -> 4.01 us
  starting transfers between devices: 9.18 us -> 9.69 us
  Pallas kernels: 3.8 us -> 3.6 us
    ppermute x6 -> x7, waiting for transfers between devices: 3.24 us -> 4.01 us  [trade(): return lax.ppermute(value, ('row', 'col'), pairs)]
    ppermute x6 -> x7, starting transfers between devices: 9.18 us -> 9.69 us  [trade(): return lax.ppermute(value, ('row', 'col'), pairs)]
    pallas_call x4 -> x5, Pallas kernels: 3.8 us -> 3.6 us  [call(): pl.pallas_call(kernel, out_shape=results, in_specs=[pl.BlockSpec(memory_s...]
  transfers between devices with their start and end apart: 6 -> 7, of which waited for: 3 -> 3; matrix products, arithmetic and copies ran while one was open for 0% -> 0% of each run, Pallas kernels for 15% -> 13%
where the time goes in v11:
time: 19.8 us; the launch traced here: 19.6 us
  starting transfers between devices  9.69 us (49%)
  waiting for transfers between devices  4.01 us (20%)
  Pallas kernels  3.6 us (18%)
  local copies, waits for them, and re-layouts  2.27 us (11%)
    ppermute x7, starting transfers between devices, trade(): return lax.ppermute(value, ('row', 'col'), pairs)  9.69 us
    ppermute x7, waiting for transfers between devices, trade(): return lax.ppermute(value, ('row', 'col'), pairs)  4.01 us
    pallas_call x5, Pallas kernels, call(): pl.pallas_call(kernel, out_shape=results, in_specs=[pl.BlockSpec(memory_s...  3.6 us
    unnamed x22, local copies, waits for them, and re-layouts  2.27 us
  transfers between devices with their start and end apart: 7, of which 3 were waited for; matrix products, arithmetic and copies ran while one was open for 0% of the time, Pallas kernels for 13%

profile of v11, /device:TPU:0, one launch (start us, length us, event | category | flops | bytes accessed | tf_op | source)
XLA Modules:
  0.0 19.6 jit_solution(16100527153922187992)
XLA Ops:
  0.0 4.0 %collective-permute-start.2 = (f32[192,128]{1,0:T(8,128)}, f32[192,128]{1,0:T(8,128)S(1)}, u32[]{:S(2)}, u32[]{:S(2)}) collective-permute-start(f32[192,128]{1,0:T(8,128)} %bitcast.6), channel_id=1, source_target_pairs={{0,4},{1,5},{2,6},{3,7},{4,0},{5,1},{6,2},{7,3},{8,11},{9,10},{10,... | collective-permute-start | bytes 294920 | tf_op jit(solution)/shard_map/ppermute | solution.py:245
  4.0 1.5 %collective-permute-start.1 = (f32[192,128]{1,0:T(8,128)}, f32[192,128]{1,0:T(8,128)S(1)}, u32[]{:S(2)}, u32[]{:S(2)}) collective-permute-start(f32[192,128]{1,0:T(8,128)} %bitcast.7), channel_id=1, source_target_pairs={{0,16},{1,17},{2,18},{3,19},{4,20},{5,21},{6,22},{7,23},{8,10},{9,... | collective-permute-start | bytes 294920 | tf_op jit(solution)/shard_map/ppermute | solution.py:245
  5.6 0.5 %collective-permute-start = (f32[192,128]{1,0:T(8,128)}, f32[192,128]{1,0:T(8,128)S(1)}, u32[]{:S(2)}, u32[]{:S(2)}) collective-permute-start(f32[192,128]{1,0:T(8,128)} %bitcast.8), channel_id=1, source_target_pairs={{0,16},{1,17},{2,18},{3,19},{4,20},{5,21},{6,22},{7,23},{8,9},{9,8... | collective-permute-start | bytes 294920 | tf_op jit(solution)/shard_map/ppermute | solution.py:245
  6.1 0.6 %copy-done.7 = f32[128]{0:T(128)S(1)} copy-done((f32[128]{0:T(128)S(1)}, f32[128]{0:T(128)}, u32[]{:S(2)}) %copy-start.7) | copy-done | bytes 536
  6.7 0.0 copy-done.8
  6.7 0.0 copy-done.4
  6.8 0.0 copy-done.5
  6.8 0.0 copy-done.6
  6.8 0.9 %copy-done = f32[3,16,4,128]{3,2,1,0:T(4,128)S(1)} copy-done((f32[3,16,4,128]{3,2,1,0:T(4,128)S(1)}, f32[3,16,4,128]{3,2,1,0:T(4,128)}, u32[]{:S(2)}) %copy-start) | copy-done | bytes 98328
  7.7 1.2 %stream.1 = (f32[192,128]{1,0:T(8,128)S(1)}, f32[128,256]{1,0:T(8,128)S(1)}, f32[64,128]{1,0:T(8,128)S(1)}) custom-call(s32[4]{0:T(128)S(1)} %copy-done.4, f32[32]{0:T(128)S(1)} %copy-done.5, f32[32]{0:T(128)S(1)} %copy-done.6, f32[192,128]{1,0:T(8,128)S(1)} %bitcast.9, f32[1,128]{1,0:T(1,128)S(1)} %bitcast.12, f32[1,128]{1,0:T(1,128)S(1)} %bitcast.13), custom_call_target="tpu_custom_call" | custom-call | tf_op jit(solution)/shard_map/stream/pallas_call | solution.py:206
  8.9 1.5 %collective-permute-done.refs_0_ = f32[192,128]{1,0:T(8,128)S(1)} collective-permute-done((f32[192,128]{1,0:T(8,128)}, f32[192,128]{1,0:T(8,128)S(1)}, u32[]{:S(2)}, u32[]{:S(2)}) %collective-permute-start) | collective-permute-done | bytes 98336 | tf_op jit(solution)/shard_map/ppermute | solution.py:245
  10.4 0.4 %span.1 = (f32[192,128]{1,0:T(8,128)S(1)}, f32[192,128]{1,0:T(8,128)S(1)}, f32[192,128]{1,0:T(8,128)S(1)}, f32[192,128]{1,0:T(8,128)S(1)}) custom-call(f32[128,256]{1,0:T(8,128)S(1)} %get-tuple-element.15.matrix, f32[192,128]{1,0:T(8,128)S(1)} %bitcast.10, f32[192,128]{1,0:T(8,128)S(1)} %collective-permute-done.refs_0_, ...), custom_call_target="tpu_custom_call" | custom-call | tf_op jit(solution)/shard_map/span/pallas_call | solution.py:206
  10.8 1.6 %collective-permute-start.3 = (f32[192,128]{1,0:T(8,128)S(1)}, f32[192,128]{1,0:T(8,128)S(1)}, u32[]{:S(2)}, u32[]{:S(2)}) collective-permute-start(f32[192,128]{1,0:T(8,128)S(1)} %get-tuple-element.18), channel_id=1, source_target_pairs={{0,2},{1,3},{2,0},{3,1},{4,6},{5,7},{6,4},{7,5},{8,24},{9,25},{10,... | collective-permute-start | bytes 294920 | tf_op jit(solution)/shard_map/ppermute | solution.py:245
  12.4 1.4 %collective-permute-start.5 = (f32[192,128]{1,0:T(8,128)S(1)}, f32[192,128]{1,0:T(8,128)S(1)}, u32[]{:S(2)}, u32[]{:S(2)}) collective-permute-start(f32[192,128]{1,0:T(8,128)S(1)} %get-tuple-element.21), channel_id=1, source_target_pairs={{0,3},{1,2},{2,1},{3,0},{4,7},{5,6},{6,5},{7,4},{8,12},{9,13},{10,... | collective-permute-start | bytes 294920 | tf_op jit(solution)/shard_map/ppermute | solution.py:245
  13.8 0.5 %collective-permute-start.6 = (f32[192,128]{1,0:T(8,128)S(1)}, f32[192,128]{1,0:T(8,128)S(1)}, u32[]{:S(2)}, u32[]{:S(2)}) collective-permute-start(f32[192,128]{1,0:T(8,128)S(1)} %get-tuple-element.22), channel_id=1, source_target_pairs={{0,1},{1,0},{2,3},{3,2},{4,5},{5,4},{6,7},{7,6},{8,24},{9,25},{10,... | collective-permute-start | bytes 294920 | tf_op jit(solution)/shard_map/ppermute | solution.py:245
  14.3 0.6 %copy-done.9 = f32[64]{0:T(128)S(1)} copy-done((f32[64]{0:T(128)S(1)}, f32[64]{0:T(128)}, u32[]{:S(2)}) %copy-start.9) | copy-done | bytes 280
  15.0 0.0 copy-done.10
  15.0 1.0 %wall_matrix.1.matrix = f32[128,256]{1,0:T(8,128)S(1)} custom-call(s32[4]{0:T(128)S(1)} %copy-done.4, f32[1,64]{1,0:T(1,128)S(1)} %bitcast.14, s32[1,32]{1,0:T(1,128)S(1)} %bitcast.15, f32[32,32]{1,0:T(8,128)S(1)} %copy-done.2, f32[32,32]{1,0:T(8,128)S(1)} %copy-done.3, f32[192,128]{1,0:T(8,128)S(1)} %get-tuple-element.16.after.z_part), custom_call_target="tpu_custom_call" | custom-call | tf_op jit(solution)/shard_map/wall_matrix/pallas_call | solution.py:206
  16.0 0.0 collective-permute-done.3.refs_1_
  16.0 0.3 %wall.1 = (f32[192,128]{1,0:T(8,128)S(1)}, f32[192,128]{1,0:T(8,128)S(1)}) custom-call(f32[128,256]{1,0:T(8,128)S(1)} %wall_matrix.1.matrix, f32[192,128]{1,0:T(8,128)S(1)} %get-tuple-element.17.x_part, f32[192,128]{1,0:T(8,128)S(1)} %get-tuple-element.16.after.z_part, f32[192,128]{1,0:T(8,128)S(1)} %bitcast.11, ...), custom_call_target="tpu_custom_call" | custom-call | tf_op jit(solution)/shard_map/wall/pallas_call | solution.py:206
  16.4 0.1 collective-permute-start.4
  16.4 1.6 %collective-permute-done.5.refs_0_ = f32[192,128]{1,0:T(8,128)S(1)} collective-permute-done((f32[192,128]{1,0:T(8,128)S(1)}, f32[192,128]{1,0:T(8,128)S(1)}, u32[]{:S(2)}, u32[]{:S(2)}) %collective-permute-start.5) | collective-permute-done | bytes 98336 | tf_op jit(solution)/shard_map/ppermute | solution.py:245
  18.0 1.0 %collective-permute-done.6.refs_2_ = f32[192,128]{1,0:T(8,128)S(1)} collective-permute-done((f32[192,128]{1,0:T(8,128)S(1)}, f32[192,128]{1,0:T(8,128)S(1)}, u32[]{:S(2)}, u32[]{:S(2)}) %collective-permute-start.6) | collective-permute-done | bytes 98336 | tf_op jit(solution)/shard_map/ppermute | solution.py:245
  19.0 0.7 %finish.1 = f32[192,128]{1,0:T(8,128)} custom-call(f32[64,128]{1,0:T(8,128)S(1)} %get-tuple-element.14.mask, f32[192,128]{1,0:T(8,128)S(1)} %get-tuple-element.19.total, f32[192,128]{1,0:T(8,128)S(1)} %collective-permute-done.4.near, f32[192,128]{1,0:T(8,128)S(1)} %collective-permute-done.5.refs_0_, f32[192,128]{1,0:T(8,128)S(1)} %collective-permute-done.3.refs_1_, ...), custom_call_target="tpu_custom_call" | custom-call | tf_op jit(solution)/shard_map/finish/pallas_call | solution.py:206
  (17 shorter events, 0.0 us)
Async XLA Ops:
  0.0 8.9 %collective-permute-start.2 = (f32[192,128]{1,0:T(8,128)}, f32[192,128]{1,0:T(8,128)S(1)}, u32[]{:S(2)}, u32[]{:S(2)}) collective-permute-start(f32[192,128]{1,0:T(8,128)} %bitcast.6), channel_id=1, source_target_pairs={{0,4},{1,5},{2,6},{3,7},{4,0},{5,1},{6,2},{7,3},{8,11},{9,10},{10,... | collective-permute-start | bytes 294920 | tf_op jit(solution)/shard_map/ppermute | solution.py:245
  4.0 4.9 %collective-permute-start.1 = (f32[192,128]{1,0:T(8,128)}, f32[192,128]{1,0:T(8,128)S(1)}, u32[]{:S(2)}, u32[]{:S(2)}) collective-permute-start(f32[192,128]{1,0:T(8,128)} %bitcast.7), channel_id=1, source_target_pairs={{0,16},{1,17},{2,18},{3,19},{4,20},{5,21},{6,22},{7,23},{8,10},{9,... | collective-permute-start | bytes 294920 | tf_op jit(solution)/shard_map/ppermute | solution.py:245
  5.6 4.8 %collective-permute-start = (f32[192,128]{1,0:T(8,128)}, f32[192,128]{1,0:T(8,128)S(1)}, u32[]{:S(2)}, u32[]{:S(2)}) collective-permute-start(f32[192,128]{1,0:T(8,128)} %bitcast.8), channel_id=1, source_target_pairs={{0,16},{1,17},{2,18},{3,19},{4,20},{5,21},{6,22},{7,23},{8,9},{9,8... | collective-permute-start | bytes 294920 | tf_op jit(solution)/shard_map/ppermute | solution.py:245
  6.1 0.7 %copy-start.7 = (f32[128]{0:T(128)S(1)}, f32[128]{0:T(128)}, u32[]{:S(2)}) copy-start(f32[128]{0:T(128)} %param.12) | copy-start | bytes 1540
  6.1 0.7 %copy-start.8 = (f32[128]{0:T(128)S(1)}, f32[128]{0:T(128)}, u32[]{:S(2)}) copy-start(f32[128]{0:T(128)} %param.13) | copy-start | bytes 1540
  6.1 0.7 %copy-start.4 = (s32[4]{0:T(128)S(1)}, s32[4]{0:T(128)}, u32[]{:S(2)}) copy-start(s32[4]{0:T(128)} %wall_counts.3) | copy-start | bytes 52
  6.1 0.7 %copy-start.5 = (f32[32]{0:T(128)S(1)}, f32[32]{0:T(128)}, u32[]{:S(2)}) copy-start(f32[32]{0:T(128)} %z_first.1) | copy-start | bytes 388
  6.1 0.7 %copy-start.6 = (f32[32]{0:T(128)S(1)}, f32[32]{0:T(128)}, u32[]{:S(2)}) copy-start(f32[32]{0:T(128)} %z_second.1) | copy-start | bytes 388
  6.8 0.9 %copy-start = (f32[3,16,4,128]{3,2,1,0:T(4,128)S(1)}, f32[3,16,4,128]{3,2,1,0:T(4,128)}, u32[]{:S(2)}) copy-start(f32[3,16,4,128]{3,2,1,0:T(4,128)} %param.10) | copy-start | bytes 294916
  7.7 2.7 %copy-start.1 = (f32[3,16,4,128]{3,2,1,0:T(4,128)S(1)}, f32[3,16,4,128]{3,2,1,0:T(4,128)}, u32[]{:S(2)}) copy-start(f32[3,16,4,128]{3,2,1,0:T(4,128)} %param.10) | copy-start | bytes 294916
  10.4 3.9 %copy-start.2 = (f32[32,32]{1,0:T(8,128)S(1)}, f32[32,32]{1,0:T(8,128)}, u32[]{:S(2)}) copy-start(f32[32,32]{1,0:T(8,128)} %y_first.1) | copy-start | bytes 12292
  10.4 3.9 %copy-start.3 = (f32[32,32]{1,0:T(8,128)S(1)}, f32[32,32]{1,0:T(8,128)}, u32[]{:S(2)}) copy-start(f32[32,32]{1,0:T(8,128)} %y_second.1) | copy-start | bytes 12292
  10.8 5.2 %collective-permute-start.3 = (f32[192,128]{1,0:T(8,128)S(1)}, f32[192,128]{1,0:T(8,128)S(1)}, u32[]{:S(2)}, u32[]{:S(2)}) collective-permute-start(f32[192,128]{1,0:T(8,128)S(1)} %get-tuple-element.18), channel_id=1, source_target_pairs={{0,2},{1,3},{2,0},{3,1},{4,6},{5,7},{6,4},{7,5},{8,24},{9,25},{10,... | collective-permute-start | bytes 294920 | tf_op jit(solution)/shard_map/ppermute | solution.py:245
  12.4 5.6 %collective-permute-start.5 = (f32[192,128]{1,0:T(8,128)S(1)}, f32[192,128]{1,0:T(8,128)S(1)}, u32[]{:S(2)}, u32[]{:S(2)}) collective-permute-start(f32[192,128]{1,0:T(8,128)S(1)} %get-tuple-element.21), channel_id=1, source_target_pairs={{0,3},{1,2},{2,1},{3,0},{4,7},{5,6},{6,5},{7,4},{8,12},{9,13},{10,... | collective-permute-start | bytes 294920 | tf_op jit(solution)/shard_map/ppermute | solution.py:245
  13.8 5.2 %collective-permute-start.6 = (f32[192,128]{1,0:T(8,128)S(1)}, f32[192,128]{1,0:T(8,128)S(1)}, u32[]{:S(2)}, u32[]{:S(2)}) collective-permute-start(f32[192,128]{1,0:T(8,128)S(1)} %get-tuple-element.22), channel_id=1, source_target_pairs={{0,1},{1,0},{2,3},{3,2},{4,5},{5,4},{6,7},{7,6},{8,24},{9,25},{10,... | collective-permute-start | bytes 294920 | tf_op jit(solution)/shard_map/ppermute | solution.py:245
  14.3 0.7 %copy-start.9 = (f32[64]{0:T(128)S(1)}, f32[64]{0:T(128)}, u32[]{:S(2)}) copy-start(f32[64]{0:T(128)} %param.18) | copy-start | bytes 772
  14.3 0.7 %copy-start.10 = (s32[32]{0:T(128)S(1)}, s32[32]{0:T(128)}, u32[]{:S(2)}) copy-start(s32[32]{0:T(128)} %param.19) | copy-start | bytes 388
  16.4 2.6 %collective-permute-start.4 = (f32[192,128]{1,0:T(8,128)S(1)}, f32[192,128]{1,0:T(8,128)S(1)}, u32[]{:S(2)}, u32[]{:S(2)}) collective-permute-start(f32[192,128]{1,0:T(8,128)S(1)} %get-tuple-element.20), channel_id=1, source_target_pairs={{0,8},{1,9},{2,10},{3,11},{4,12},{5,13},{6,14},{7,15},{8,0},{9,1},... | collective-permute-start | bytes 294920 | tf_op jit(solution)/shard_map/ppermute | solution.py:245

commit v12 on v11

v12 whole, which is shorter than its diff:
```python
import functools
import math

import jax
import jax.numpy as jnp
from jax import lax
from jax.experimental import pallas as pl
from jax.experimental.pallas import tpu as pltpu
from jax.sharding import PartitionSpec as P

viscosity = 0.4
quad = 4

VMEM = pltpu.VMEM
SMEM = pltpu.SMEM


def halves(value):
    high = value.astype(jnp.bfloat16)
    low = (value - high.astype(jnp.float32)).astype(jnp.bfloat16)
    return high, low


def dot_split(left, right, transposed=False):
    dims = (((1,), (1 if transposed else 0,)), ((), ()))
    mul = functools.partial(lax.dot_general, dimension_numbers=dims, preferred_element_type=jnp.float32)
    lh, ll = halves(left)
    rh, rl = halves(right)
    return mul(lh, rh) + (mul(lh, rl) + mul(ll, rh))


def span_kernel(comps, sources, matrix, *refs):
    fields, parts = refs[:sources], refs[-quad:]
    depth, length = fields[0].shape[0] // comps, fields[0].shape[1]
    group = matrix.shape[0] // quad
    right = []
    for comp in range(comps):
        for at in range(0, depth, group):
            stack = [field[comp * depth + at : comp * depth + at + group] for field in fields]
            stack += [value * field[2 * depth + at : 2 * depth + at + group] for value, field in zip(stack, fields)]
            right.append(jnp.concatenate(stack, axis=0))
    result = dot_split(matrix[...], jnp.concatenate(right, axis=1))
    for t in range(quad):
        for i in range(len(right)):
            parts[t][i * group : (i + 1) * group] = result[
                t * group : (t + 1) * group, i * length : (i + 1) * length
            ]


def circulant_rows(row, length):
    return pltpu.roll(jnp.broadcast_to(row, (length, length)), 0, 1, stride=1, stride_axis=0)


def stream_kernel(
    cols, comps, zloc, wall_counts, z_first, z_second, field, x_first, x_second, x_part, z_matrix, mask
):
    depth = mask.shape[0]
    length = field.shape[1]
    count = wall_counts[lax.axis_index("row")]
    mask[...] = (lax.broadcasted_iota(jnp.int32, mask.shape, 0) // zloc < count).astype(jnp.float32)

    cells_z = cols * zloc
    shape = z_matrix.shape
    half = shape[1] // 2
    group = shape[0] // quad
    mine = lax.axis_index("col")
    r = lax.broadcasted_iota(jnp.int32, shape, 0)
    q = lax.broadcasted_iota(jnp.int32, shape, 1)
    q = jnp.where(q < half, q, q - half)
    out_cell = ((r // group) ^ mine) * zloc + r % zloc
    in_cell = ((quad * (q // group)) ^ mine) * zloc + q % zloc
    same = (r % group) // zloc == (q % group) // zloc
    gap = jnp.where(same, (in_cell - out_cell + cells_z) % cells_z, -1)
    kind = lax.broadcasted_iota(jnp.int32, (1, shape[1]), 1) < half

    def fill(k, total):
        value = jnp.where(kind, viscosity * z_second[k], -z_first[k])
        return jnp.where(gap == k, value, total)

    z_matrix[...] = lax.fori_loop(0, cells_z, fill, jnp.zeros(shape, jnp.float32), unroll=8)

    u = field[...]
    lead = u[:depth]
    left = jnp.concatenate(
        [u, jnp.concatenate([lead * u[c * depth : (c + 1) * depth] for c in range(comps)], axis=0)], axis=1
    )
    right = jnp.concatenate(
        [viscosity * circulant_rows(x_second[...], length), -circulant_rows(x_first[...], length)], axis=1
    )
    x_part[...] = dot_split(left, right, transposed=True)


def wall_matrix_kernel(rows, zloc, wall_counts, metric_table, metric_index, y_first, y_second, after, matrix):
    cells = y_first.shape[0]
    depth = matrix.shape[0] // 2
    me = lax.axis_index("row")
    plain = functools.partial(
        lax.dot_general, dimension_numbers=(((1,), (0,)), ((), ())), preferred_element_type=jnp.float32
    )
    turned = functools.partial(
        lax.dot_general, dimension_numbers=(((1,), (1,)), ((), ())), preferred_element_type=jnp.float32
    )

    def spots(index):
        start = lax.fori_loop(0, rows, lambda i, acc: acc + jnp.where(i < index, wall_counts[i], 0), 0, unroll=True)
        plane = lax.broadcasted_iota(jnp.int32, (depth, cells), 0) // zloc
        cell = lax.broadcasted_iota(jnp.int32, (depth, cells), 1)
        return ((plane < wall_counts[index]) & (plane + start == cell)).astype(jnp.float32)

    levels = metric_table.shape[1]
    entry = (lax.broadcasted_iota(jnp.int32, (levels, cells), 0) == metric_index[...]).astype(jnp.float32)
    table = jnp.broadcast_to(metric_table[...], (8, levels))
    metric = plain(table, entry, precision=lax.Precision.HIGHEST)[:1]
    ends = jnp.concatenate([spots(me), spots(me ^ 1)], axis=0)
    scale = jnp.sum(ends * metric, axis=1, keepdims=True)
    pick = ends.astype(jnp.bfloat16)
    second = sum(plain(pick, part) for part in halves(viscosity * y_second[...]))
    first = -scale * sum(plain(pick, part) for part in halves(y_first[...]))
    other = jnp.concatenate([spots(me ^ step) for step in range(0, rows, 2)], axis=0).astype(jnp.bfloat16)
    wide = sum(turned(part, other) for part in halves(jnp.concatenate([second, first], axis=0)))
    match = lax.broadcasted_iota(jnp.int32, wide.shape, 0) % zloc == lax.broadcasted_iota(jnp.int32, wide.shape, 1) % zloc
    wide = jnp.where(match, wide, 0.0)
    for b in range(rows // 2):
        for k in range(2):
            matrix[:, (2 * b + k) * depth : (2 * b + k + 1) * depth] = wide[
                2 * k * depth : 2 * (k + 1) * depth, b * depth : (b + 1) * depth
            ]


def wall_kernel(comps, matrix, x_part, z_part, *refs):
    fields, (total, away) = refs[:-2], refs[-2:]
    depth = x_part.shape[0] // comps
    for comp in range(comps):
        at = slice(comp * depth, (comp + 1) * depth)
        stack = []
        for field in fields:
            stack += [field[at], field[depth : 2 * depth] * field[at]]
        result = dot_split(matrix[...], jnp.concatenate(stack, axis=0))
        total[at] = x_part[at] + z_part[at] + result[:depth]
        away[at] = result[depth:]


def finish_kernel(comps, mask, *refs):
    parts, out = refs[:-1], refs[-1]
    depth = mask.shape[0]
    for comp in range(comps):
        at = slice(comp * depth, (comp + 1) * depth)
        out[at] = jnp.where(mask[...] > 0, sum(part[at] for part in parts[1:]) + parts[0][at], 0.0)


def call(kernel, operands, spaces, results, name, scratch=()):
    results = [jax.ShapeDtypeStruct(shape, jnp.float32) for shape in results]
    held = sum(4 * math.prod(array.shape) for array in list(operands) + results)
    return pl.pallas_call(
        kernel,
        out_shape=results,
        in_specs=[pl.BlockSpec(memory_space=space) for space in spaces],
        out_specs=[pl.BlockSpec(memory_space=VMEM)] * len(results),
        scratch_shapes=[pltpu.VMEM(shape, jnp.float32) for shape in scratch],
        compiler_params=pltpu.CompilerParams(vmem_limit_bytes=(4 << 20) + 3 * held),
        name=name,
    )(*operands)


def local(
    velocity,
    wall_counts,
    x_first,
    x_second,
    y_first,
    y_second,
    z_first,
    z_second,
    metric_table,
    metric_index,
):
    rows = lax.axis_size("row")
    cols = lax.axis_size("col")
    comps, slots, zloc, length = velocity.shape
    depth = slots * zloc
    field = velocity.reshape(comps * depth, length)
    group = min(depth, 32)
    sources = cols // quad

    def along(value, step):
        return lax.ppermute(value, "col", [(i, i ^ step) for i in range(cols)])

    def across(value, step):
        return lax.ppermute(value, "row", [(i, i ^ step) for i in range(rows)])

    gathered = [along(field, quad * i) for i in range(1, sources)]
    far = [across(field, step) for step in range(2, rows, 2)]
    x_part, z_matrix, mask = call(
        functools.partial(stream_kernel, cols, comps, zloc),
        [wall_counts, z_first, z_second, field, x_first.reshape(1, length), x_second.reshape(1, length)],
        [SMEM] * 3 + [VMEM] * 3,
        [field.shape, (quad * group, 2 * sources * group), (depth, length)],
        "stream",
    )
    parts = call(
        functools.partial(span_kernel, comps, sources),
        [z_matrix, field] + gathered + far,
        [VMEM] * (1 + sources) + [pl.ANY] * len(far),
        [field.shape] * quad,
        "span",
    )
    returned = [along(parts[t], t) for t in reversed(range(1, quad))]
    (y_matrix,) = call(
        functools.partial(wall_matrix_kernel, rows, zloc),
        [wall_counts, metric_table.reshape(1, -1), metric_index.reshape(1, -1), y_first, y_second, parts[0]],
        [SMEM] + [VMEM] * 4 + [pl.ANY],
        [(2 * depth, rows * depth)],
        "wall_matrix",
    )
    total, away = call(
        functools.partial(wall_kernel, comps),
        [y_matrix, x_part, parts[0], field] + far,
        [VMEM] * (4 + len(far)),
        [field.shape] * 2,
        "wall",
    )
    near = across(away, 1)
    (result,) = call(
        functools.partial(finish_kernel, comps),
        [mask, total, near] + returned,
        [VMEM] * (quad + 2),
        [field.shape],
        "finish",
    )
    return result.reshape(velocity.shape)


def solution(mesh):
    in_specs = (P(None, "row", "col", None), P(), P(), P(), P(), P(), P(), P(), P(), P())
    out_specs = P(None, "row", "col", None)
    return jax.shard_map(local, mesh=mesh, in_specs=in_specs, out_specs=out_specs, check_vma=False)
```

time: 19.8 us -> 19.3 us (0.975)
  starting transfers between devices: 9.69 us -> 9.18 us
    ppermute x7 -> x6, starting transfers between devices: 9.69 us -> 9.18 us  [the longest x4 6.14 us: along(): return lax.ppermute(value, 'col', [(i, i ^ step) for i in range(cols)])]
    ppermute x7 -> x6, waiting for transfers between devices: 4.01 us -> 4.17 us  [the longest x4 4.17 us: along(): return lax.ppermute(value, 'col', [(i, i ^ step) for i in range(cols)])]
  transfers between devices with their start and end apart: 7 -> 6, of which waited for: 3 -> 4; matrix products, arithmetic and copies ran while one was open for 0% -> 0% of each run, Pallas kernels for 13% -> 13%
where the time goes in v12:
time: 19.3 us; the launch traced here: 19.1 us
  starting transfers between devices  9.18 us (48%)
  waiting for transfers between devices  4.17 us (22%)
  Pallas kernels  3.41 us (18%)
  local copies, waits for them, and re-layouts  2.27 us (12%)
    ppermute x4, starting transfers between devices, along(): return lax.ppermute(value, 'col', [(i, i ^ step) for i in range(cols)])  6.14 us
    ppermute x4, waiting for transfers between devices, along(): return lax.ppermute(value, 'col', [(i, i ^ step) for i in range(cols)])  4.17 us
    pallas_call x5, Pallas kernels, call(): pl.pallas_call(kernel, out_shape=results, in_specs=[pl.BlockSpec(memory_s...  3.41 us
    ppermute x2, starting transfers between devices, across(): return lax.ppermute(value, 'row', [(i, i ^ step) for i in range(rows)])  3.04 us
    unnamed x22, local copies, waits for them, and re-layouts  2.27 us
  transfers between devices with their start and end apart: 6, of which 4 were waited for; matrix products, arithmetic and copies ran while one was open for 0% of the time, Pallas kernels for 13%

profile of v12, /device:TPU:0, one launch (start us, length us, event | category | flops | bytes accessed | tf_op | source)
XLA Modules:
  0.0 19.1 jit_solution(9589708499342074819)
XLA Ops:
  0.0 3.0 %collective-permute-start.1 = (f32[192,128]{1,0:T(8,128)}, f32[192,128]{1,0:T(8,128)S(1)}, u32[]{:S(2)}, u32[]{:S(2)}) collective-permute-start(f32[192,128]{1,0:T(8,128)} %bitcast.6), channel_id=1, source_target_pairs={{0,16},{8,24},{16,0},{24,8},{1,17},{9,25},{17,1},{25,9},{2,18},{10... | collective-permute-start | bytes 294920 | tf_op jit(solution)/shard_map/ppermute | solution.py:189
  3.0 2.6 %collective-permute-start = (f32[192,128]{1,0:T(8,128)}, f32[192,128]{1,0:T(8,128)S(1)}, u32[]{:S(2)}, u32[]{:S(2)}) collective-permute-start(f32[192,128]{1,0:T(8,128)} %bitcast.7), channel_id=1, source_target_pairs={{0,4},{1,5},{2,6},{3,7},{4,0},{5,1},{6,2},{7,3},{8,12},{9,13},{10,... | collective-permute-start | bytes 294920 | tf_op jit(solution)/shard_map/ppermute | solution.py:186
  5.6 0.6 %copy-done.7 = f32[128]{0:T(128)S(1)} copy-done((f32[128]{0:T(128)S(1)}, f32[128]{0:T(128)}, u32[]{:S(2)}) %copy-start.7) | copy-done | bytes 536
  6.2 0.0 copy-done.8
  6.2 0.0 copy-done.4
  6.2 0.0 copy-done.5
  6.3 0.0 copy-done.6
  6.3 0.9 %copy-done = f32[3,16,4,128]{3,2,1,0:T(4,128)S(1)} copy-done((f32[3,16,4,128]{3,2,1,0:T(4,128)S(1)}, f32[3,16,4,128]{3,2,1,0:T(4,128)}, u32[]{:S(2)}) %copy-start) | copy-done | bytes 98328
  7.2 1.1 %stream.1 = (f32[192,128]{1,0:T(8,128)S(1)}, f32[128,128]{1,0:T(8,128)S(1)}, f32[64,128]{1,0:T(8,128)S(1)}) custom-call(s32[4]{0:T(128)S(1)} %copy-done.4, f32[32]{0:T(128)S(1)} %copy-done.5, f32[32]{0:T(128)S(1)} %copy-done.6, f32[192,128]{1,0:T(8,128)S(1)} %bitcast.8, f32[1,128]{1,0:T(1,128)S(1)} %bitcast.11, f32[1,128]{1,0:T(1,128)S(1)} %bitcast.12), custom_call_target="tpu_custom_call" | custom-call | tf_op jit(solution)/shard_map/stream/pallas_call | solution.py:154
  8.3 0.0 collective-permute-done.1.refs_2_.refs_1_
  8.3 2.2 %collective-permute-done.refs_1_ = f32[192,128]{1,0:T(8,128)S(1)} collective-permute-done((f32[192,128]{1,0:T(8,128)}, f32[192,128]{1,0:T(8,128)S(1)}, u32[]{:S(2)}, u32[]{:S(2)}) %collective-permute-start) | collective-permute-done | bytes 98336 | tf_op jit(solution)/shard_map/ppermute | solution.py:186
  10.5 0.3 %span.1 = (f32[192,128]{1,0:T(8,128)S(1)}, f32[192,128]{1,0:T(8,128)S(1)}, f32[192,128]{1,0:T(8,128)S(1)}, f32[192,128]{1,0:T(8,128)S(1)}) custom-call(f32[128,128]{1,0:T(8,128)S(1)} %get-tuple-element.15.matrix, f32[192,128]{1,0:T(8,128)S(1)} %bitcast.9, f32[192,128]{1,0:T(8,128)S(1)} %collective-permute-done.refs_1_, ...), custom_call_target="tpu_custom_call" | custom-call | tf_op jit(solution)/shard_map/span/pallas_call | solution.py:154
  10.8 1.8 %collective-permute-start.3 = (f32[192,128]{1,0:T(8,128)S(1)}, f32[192,128]{1,0:T(8,128)S(1)}, u32[]{:S(2)}, u32[]{:S(2)}) collective-permute-start(f32[192,128]{1,0:T(8,128)S(1)} %get-tuple-element.20), channel_id=1, source_target_pairs={{0,3},{1,2},{2,1},{3,0},{4,7},{5,6},{6,5},{7,4},{8,11},{9,10},{10,... | collective-permute-start | bytes 294920 | tf_op jit(solution)/shard_map/ppermute | solution.py:186
  12.5 1.3 %collective-permute-start.4 = (f32[192,128]{1,0:T(8,128)S(1)}, f32[192,128]{1,0:T(8,128)S(1)}, u32[]{:S(2)}, u32[]{:S(2)}) collective-permute-start(f32[192,128]{1,0:T(8,128)S(1)} %get-tuple-element.21), channel_id=1, source_target_pairs={{0,2},{1,3},{2,0},{3,1},{4,6},{5,7},{6,4},{7,5},{8,10},{9,11},{10,... | collective-permute-start | bytes 294920 | tf_op jit(solution)/shard_map/ppermute | solution.py:186
  13.8 0.5 %collective-permute-start.5 = (f32[192,128]{1,0:T(8,128)S(1)}, f32[192,128]{1,0:T(8,128)S(1)}, u32[]{:S(2)}, u32[]{:S(2)}) collective-permute-start(f32[192,128]{1,0:T(8,128)S(1)} %get-tuple-element.22), channel_id=1, source_target_pairs={{0,1},{1,0},{2,3},{3,2},{4,5},{5,4},{6,7},{7,6},{8,9},{9,8},{10,11... | collective-permute-start | bytes 294920 | tf_op jit(solution)/shard_map/ppermute | solution.py:186
  14.4 0.6 %copy-done.9 = f32[64]{0:T(128)S(1)} copy-done((f32[64]{0:T(128)S(1)}, f32[64]{0:T(128)}, u32[]{:S(2)}) %copy-start.9) | copy-done | bytes 280
  15.0 0.0 copy-done.10
  15.0 1.0 %wall_matrix.1.matrix = f32[128,256]{1,0:T(8,128)S(1)} custom-call(s32[4]{0:T(128)S(1)} %copy-done.4, f32[1,64]{1,0:T(1,128)S(1)} %bitcast.13, s32[1,32]{1,0:T(1,128)S(1)} %bitcast.14, f32[32,32]{1,0:T(8,128)S(1)} %copy-done.2, f32[32,32]{1,0:T(8,128)S(1)} %copy-done.3, f32[192,128]{1,0:T(8,128)S(1)} %get-tuple-element.16.after.z_part), custom_call_target="tpu_custom_call" | custom-call | tf_op jit(solution)/shard_map/wall_matrix/pallas_call | solution.py:154
  16.0 0.3 %wall.1 = (f32[192,128]{1,0:T(8,128)S(1)}, f32[192,128]{1,0:T(8,128)S(1)}) custom-call(f32[128,256]{1,0:T(8,128)S(1)} %wall_matrix.1.matrix, f32[192,128]{1,0:T(8,128)S(1)} %get-tuple-element.17.x_part, f32[192,128]{1,0:T(8,128)S(1)} %get-tuple-element.16.after.z_part, f32[192,128]{1,0:T(8,128)S(1)} %bitcast.10, ...), custom_call_target="tpu_custom_call" | custom-call | tf_op jit(solution)/shard_map/wall/pallas_call | solution.py:154
  16.4 0.1 collective-permute-start.2
  16.4 0.2 %collective-permute-done.3.refs_2_ = f32[192,128]{1,0:T(8,128)S(1)} collective-permute-done((f32[192,128]{1,0:T(8,128)S(1)}, f32[192,128]{1,0:T(8,128)S(1)}, u32[]{:S(2)}, u32[]{:S(2)}) %collective-permute-start.3) | collective-permute-done | bytes 98336 | tf_op jit(solution)/shard_map/ppermute | solution.py:186
  16.7 1.0 %collective-permute-done.4.refs_3_ = f32[192,128]{1,0:T(8,128)S(1)} collective-permute-done((f32[192,128]{1,0:T(8,128)S(1)}, f32[192,128]{1,0:T(8,128)S(1)}, u32[]{:S(2)}, u32[]{:S(2)}) %collective-permute-start.4) | collective-permute-done | bytes 98336 | tf_op jit(solution)/shard_map/ppermute | solution.py:186
  17.7 0.7 %collective-permute-done.5.refs_4_ = f32[192,128]{1,0:T(8,128)S(1)} collective-permute-done((f32[192,128]{1,0:T(8,128)S(1)}, f32[192,128]{1,0:T(8,128)S(1)}, u32[]{:S(2)}, u32[]{:S(2)}) %collective-permute-start.5) | collective-permute-done | bytes 98336 | tf_op jit(solution)/shard_map/ppermute | solution.py:186
  18.4 0.7 %finish.1 = f32[192,128]{1,0:T(8,128)} custom-call(f32[64,128]{1,0:T(8,128)S(1)} %get-tuple-element.14.mask, f32[192,128]{1,0:T(8,128)S(1)} %get-tuple-element.18.refs_0_, f32[192,128]{1,0:T(8,128)S(1)} %collective-permute-done.2.refs_1_, f32[192,128]{1,0:T(8,128)S(1)} %collective-permute-done.3.refs_2_, f32[192,128]{1,0:T(8,128)S(1)} %collective-permute-done.4.refs_3_, ...), custom_call_target="tpu_custom_call" | custom-call | tf_op jit(solution)/shard_map/finish/pallas_call | solution.py:154
  (15 shorter events, 0.0 us)
Async XLA Ops:
  0.0 8.3 %collective-permute-start.1 = (f32[192,128]{1,0:T(8,128)}, f32[192,128]{1,0:T(8,128)S(1)}, u32[]{:S(2)}, u32[]{:S(2)}) collective-permute-start(f32[192,128]{1,0:T(8,128)} %bitcast.6), channel_id=1, source_target_pairs={{0,16},{8,24},{16,0},{24,8},{1,17},{9,25},{17,1},{25,9},{2,18},{10... | collective-permute-start | bytes 294920 | tf_op jit(solution)/shard_map/ppermute | solution.py:189
  3.0 7.5 %collective-permute-start = (f32[192,128]{1,0:T(8,128)}, f32[192,128]{1,0:T(8,128)S(1)}, u32[]{:S(2)}, u32[]{:S(2)}) collective-permute-start(f32[192,128]{1,0:T(8,128)} %bitcast.7), channel_id=1, source_target_pairs={{0,4},{1,5},{2,6},{3,7},{4,0},{5,1},{6,2},{7,3},{8,12},{9,13},{10,... | collective-permute-start | bytes 294920 | tf_op jit(solution)/shard_map/ppermute | solution.py:186
  5.6 0.7 %copy-start.7 = (f32[128]{0:T(128)S(1)}, f32[128]{0:T(128)}, u32[]{:S(2)}) copy-start(f32[128]{0:T(128)} %param.12) | copy-start | bytes 1540
  5.6 0.7 %copy-start.8 = (f32[128]{0:T(128)S(1)}, f32[128]{0:T(128)}, u32[]{:S(2)}) copy-start(f32[128]{0:T(128)} %param.13) | copy-start | bytes 1540
  5.6 0.7 %copy-start.4 = (s32[4]{0:T(128)S(1)}, s32[4]{0:T(128)}, u32[]{:S(2)}) copy-start(s32[4]{0:T(128)} %wall_counts.3) | copy-start | bytes 52
  5.6 0.7 %copy-start.5 = (f32[32]{0:T(128)S(1)}, f32[32]{0:T(128)}, u32[]{:S(2)}) copy-start(f32[32]{0:T(128)} %z_first.1) | copy-start | bytes 388
  5.6 0.7 %copy-start.6 = (f32[32]{0:T(128)S(1)}, f32[32]{0:T(128)}, u32[]{:S(2)}) copy-start(f32[32]{0:T(128)} %z_second.1) | copy-start | bytes 388
  6.3 0.9 %copy-start = (f32[3,16,4,128]{3,2,1,0:T(4,128)S(1)}, f32[3,16,4,128]{3,2,1,0:T(4,128)}, u32[]{:S(2)}) copy-start(f32[3,16,4,128]{3,2,1,0:T(4,128)} %param.10) | copy-start | bytes 294916
  7.2 3.3 %copy-start.1 = (f32[3,16,4,128]{3,2,1,0:T(4,128)S(1)}, f32[3,16,4,128]{3,2,1,0:T(4,128)}, u32[]{:S(2)}) copy-start(f32[3,16,4,128]{3,2,1,0:T(4,128)} %param.10) | copy-start | bytes 294916
  10.5 3.9 %copy-start.2 = (f32[32,32]{1,0:T(8,128)S(1)}, f32[32,32]{1,0:T(8,128)}, u32[]{:S(2)}) copy-start(f32[32,32]{1,0:T(8,128)} %y_first.1) | copy-start | bytes 12292
  10.5 3.9 %copy-start.3 = (f32[32,32]{1,0:T(8,128)S(1)}, f32[32,32]{1,0:T(8,128)}, u32[]{:S(2)}) copy-start(f32[32,32]{1,0:T(8,128)} %y_second.1) | copy-start | bytes 12292
  10.8 5.9 %collective-permute-start.3 = (f32[192,128]{1,0:T(8,128)S(1)}, f32[192,128]{1,0:T(8,128)S(1)}, u32[]{:S(2)}, u32[]{:S(2)}) collective-permute-start(f32[192,128]{1,0:T(8,128)S(1)} %get-tuple-element.20), channel_id=1, source_target_pairs={{0,3},{1,2},{2,1},{3,0},{4,7},{5,6},{6,5},{7,4},{8,11},{9,10},{10,... | collective-permute-start | bytes 294920 | tf_op jit(solution)/shard_map/ppermute | solution.py:186
  12.5 5.2 %collective-permute-start.4 = (f32[192,128]{1,0:T(8,128)S(1)}, f32[192,128]{1,0:T(8,128)S(1)}, u32[]{:S(2)}, u32[]{:S(2)}) collective-permute-start(f32[192,128]{1,0:T(8,128)S(1)} %get-tuple-element.21), channel_id=1, source_target_pairs={{0,2},{1,3},{2,0},{3,1},{4,6},{5,7},{6,4},{7,5},{8,10},{9,11},{10,... | collective-permute-start | bytes 294920 | tf_op jit(solution)/shard_map/ppermute | solution.py:186
  13.8 4.6 %collective-permute-start.5 = (f32[192,128]{1,0:T(8,128)S(1)}, f32[192,128]{1,0:T(8,128)S(1)}, u32[]{:S(2)}, u32[]{:S(2)}) collective-permute-start(f32[192,128]{1,0:T(8,128)S(1)} %get-tuple-element.22), channel_id=1, source_target_pairs={{0,1},{1,0},{2,3},{3,2},{4,5},{5,4},{6,7},{7,6},{8,9},{9,8},{10,11... | collective-permute-start | bytes 294920 | tf_op jit(solution)/shard_map/ppermute | solution.py:186
  14.3 0.7 %copy-start.9 = (f32[64]{0:T(128)S(1)}, f32[64]{0:T(128)}, u32[]{:S(2)}) copy-start(f32[64]{0:T(128)} %param.18) | copy-start | bytes 772
  14.3 0.7 %copy-start.10 = (s32[32]{0:T(128)S(1)}, s32[32]{0:T(128)}, u32[]{:S(2)}) copy-start(s32[32]{0:T(128)} %param.19) | copy-start | bytes 388
  16.4 2.1 %collective-permute-start.2 = (f32[192,128]{1,0:T(8,128)S(1)}, f32[192,128]{1,0:T(8,128)S(1)}, u32[]{:S(2)}, u32[]{:S(2)}) collective-permute-start(f32[192,128]{1,0:T(8,128)S(1)} %get-tuple-element.19), channel_id=1, source_target_pairs={{0,8},{8,0},{16,24},{24,16},{1,9},{9,1},{17,25},{25,17},{2,10},{10... | collective-permute-start | bytes 294920 | tf_op jit(solution)/shard_map/ppermute | solution.py:189

commit v13 on v12

--- a/solution.py
+++ b/solution.py
@@ -30,7 +30,7 @@
 
 
 def span_kernel(comps, sources, matrix, *refs):
-    fields, parts = refs[:sources], refs[-quad:]
+    fields, parts = refs[-quad - sources : -quad], refs[-quad:]
     depth, length = fields[0].shape[0] // comps, fields[0].shape[1]
     group = matrix.shape[0] // quad
     right = []
@@ -199,8 +199,8 @@
     )
     parts = call(
         functools.partial(span_kernel, comps, sources),
-        [z_matrix, field] + gathered + far,
-        [VMEM] * (1 + sources) + [pl.ANY] * len(far),
+        [z_matrix] + far + [field] + gathered,
+        [VMEM] + [pl.ANY] * len(far) + [VMEM] * sources,
         [field.shape] * quad,
         "span",
     )

time: 19.3 us -> 18 us (0.933)
  waiting for transfers between devices: 4.17 us -> 2.92 us
    ppermute x2, starting transfers between devices: 3.04 us -> 1.59 us  [across(): return lax.ppermute(value, 'row', [(i, i ^ step) for i in range(rows)])]
    ppermute x4, starting transfers between devices: 6.14 us -> 7.59 us  [along(): return lax.ppermute(value, 'col', [(i, i ^ step) for i in range(cols)])]
    ppermute x4, waiting for transfers between devices: 4.17 us -> 2.92 us  [along(): return lax.ppermute(value, 'col', [(i, i ^ step) for i in range(cols)])]
  transfers between devices with their start and end apart: 6 -> 6, of which waited for: 4 -> 4; matrix products, arithmetic and copies ran while one was open for 0% -> 0% of each run, Pallas kernels for 13% -> 14%
where the time goes in v13:
time: 18 us; the launch traced here: 17.8 us
  starting transfers between devices  9.18 us (51%)
  Pallas kernels  3.4 us (19%)
  waiting for transfers between devices  2.92 us (16%)
  local copies, waits for them, and re-layouts  2.27 us (13%)
    ppermute x4, starting transfers between devices, along(): return lax.ppermute(value, 'col', [(i, i ^ step) for i in range(cols)])  7.59 us
    pallas_call x5, Pallas kernels, call(): pl.pallas_call(kernel, out_shape=results, in_specs=[pl.BlockSpec(memory_s...  3.4 us
    ppermute x4, waiting for transfers between devices, along(): return lax.ppermute(value, 'col', [(i, i ^ step) for i in range(cols)])  2.92 us
    unnamed x22, local copies, waits for them, and re-layouts  2.27 us
    ppermute x2, starting transfers between devices, across(): return lax.ppermute(value, 'row', [(i, i ^ step) for i in range(rows)])  1.59 us
  transfers between devices with their start and end apart: 6, of which 4 were waited for; matrix products, arithmetic and copies ran while one was open for 0% of the time, Pallas kernels for 14%

profile of v13, /device:TPU:0, one launch (start us, length us, event | category | flops | bytes accessed | tf_op | source)
XLA Modules:
  0.0 17.8 jit_solution(12887323041677017686)
XLA Ops:
  0.0 4.0 %collective-permute-start.1 = (f32[192,128]{1,0:T(8,128)}, f32[192,128]{1,0:T(8,128)S(1)}, u32[]{:S(2)}, u32[]{:S(2)}) collective-permute-start(f32[192,128]{1,0:T(8,128)} %bitcast.6), channel_id=1, source_target_pairs={{0,4},{1,5},{2,6},{3,7},{4,0},{5,1},{6,2},{7,3},{8,12},{9,13},{10,... | collective-permute-start | bytes 294920 | tf_op jit(solution)/shard_map/ppermute | solution.py:186
  4.0 1.5 %collective-permute-start = (f32[192,128]{1,0:T(8,128)}, f32[192,128]{1,0:T(8,128)S(1)}, u32[]{:S(2)}, u32[]{:S(2)}) collective-permute-start(f32[192,128]{1,0:T(8,128)} %bitcast.7), channel_id=1, source_target_pairs={{0,16},{8,24},{16,0},{24,8},{1,17},{9,25},{17,1},{25,9},{2,18},{10... | collective-permute-start | bytes 294920 | tf_op jit(solution)/shard_map/ppermute | solution.py:189
  5.6 0.6 %copy-done.7 = f32[128]{0:T(128)S(1)} copy-done((f32[128]{0:T(128)S(1)}, f32[128]{0:T(128)}, u32[]{:S(2)}) %copy-start.7) | copy-done | bytes 536
  6.2 0.0 copy-done.8
  6.2 0.0 copy-done.4
  6.2 0.0 copy-done.5
  6.3 0.0 copy-done.6
  6.3 0.9 %copy-done = f32[3,16,4,128]{3,2,1,0:T(4,128)S(1)} copy-done((f32[3,16,4,128]{3,2,1,0:T(4,128)S(1)}, f32[3,16,4,128]{3,2,1,0:T(4,128)}, u32[]{:S(2)}) %copy-start) | copy-done | bytes 98328
  7.2 1.1 %stream.1 = (f32[192,128]{1,0:T(8,128)S(1)}, f32[128,128]{1,0:T(8,128)S(1)}, f32[64,128]{1,0:T(8,128)S(1)}) custom-call(s32[4]{0:T(128)S(1)} %copy-done.4, f32[32]{0:T(128)S(1)} %copy-done.5, f32[32]{0:T(128)S(1)} %copy-done.6, f32[192,128]{1,0:T(8,128)S(1)} %bitcast.8, f32[1,128]{1,0:T(1,128)S(1)} %bitcast.11, f32[1,128]{1,0:T(1,128)S(1)} %bitcast.12), custom_call_target="tpu_custom_call" | custom-call | tf_op jit(solution)/shard_map/stream/pallas_call | solution.py:154
  8.3 0.9 %collective-permute-done.1.refs_2_ = f32[192,128]{1,0:T(8,128)S(1)} collective-permute-done((f32[192,128]{1,0:T(8,128)}, f32[192,128]{1,0:T(8,128)S(1)}, u32[]{:S(2)}, u32[]{:S(2)}) %collective-permute-start.1) | collective-permute-done | bytes 98336 | tf_op jit(solution)/shard_map/ppermute | solution.py:186
  9.2 0.0 copy-start.3
  9.2 0.3 %span.1 = (f32[192,128]{1,0:T(8,128)S(1)}, f32[192,128]{1,0:T(8,128)S(1)}, f32[192,128]{1,0:T(8,128)S(1)}, f32[192,128]{1,0:T(8,128)S(1)}) custom-call(f32[128,128]{1,0:T(8,128)S(1)} %get-tuple-element.15.matrix, f32[192,128]{1,0:T(8,128)S(1)} %collective-permute-done.refs_0_.refs_1_, f32[192,128]{1,0:T(8,128)S(1)} %bitcast.9, ...), custom_call_target="tpu_custom_call" | custom-call | tf_op jit(solution)/shard_map/span/pallas_call | solution.py:154
  9.5 2.3 %collective-permute-start.3 = (f32[192,128]{1,0:T(8,128)S(1)}, f32[192,128]{1,0:T(8,128)S(1)}, u32[]{:S(2)}, u32[]{:S(2)}) collective-permute-start(f32[192,128]{1,0:T(8,128)S(1)} %get-tuple-element.20), channel_id=1, source_target_pairs={{0,3},{1,2},{2,1},{3,0},{4,7},{5,6},{6,5},{7,4},{8,11},{9,10},{10,... | collective-permute-start | bytes 294920 | tf_op jit(solution)/shard_map/ppermute | solution.py:186
  11.8 0.8 %collective-permute-start.4 = (f32[192,128]{1,0:T(8,128)S(1)}, f32[192,128]{1,0:T(8,128)S(1)}, u32[]{:S(2)}, u32[]{:S(2)}) collective-permute-start(f32[192,128]{1,0:T(8,128)S(1)} %get-tuple-element.21), channel_id=1, source_target_pairs={{0,2},{1,3},{2,0},{3,1},{4,6},{5,7},{6,4},{7,5},{8,10},{9,11},{10,... | collective-permute-start | bytes 294920 | tf_op jit(solution)/shard_map/ppermute | solution.py:186
  12.6 0.5 %collective-permute-start.5 = (f32[192,128]{1,0:T(8,128)S(1)}, f32[192,128]{1,0:T(8,128)S(1)}, u32[]{:S(2)}, u32[]{:S(2)}) collective-permute-start(f32[192,128]{1,0:T(8,128)S(1)} %get-tuple-element.22), channel_id=1, source_target_pairs={{0,1},{1,0},{2,3},{3,2},{4,5},{5,4},{6,7},{7,6},{8,9},{9,8},{10,11... | collective-permute-start | bytes 294920 | tf_op jit(solution)/shard_map/ppermute | solution.py:186
  13.1 0.6 %copy-done.9 = f32[64]{0:T(128)S(1)} copy-done((f32[64]{0:T(128)S(1)}, f32[64]{0:T(128)}, u32[]{:S(2)}) %copy-start.9) | copy-done | bytes 280
  13.7 0.0 copy-done.10
  13.7 1.0 %wall_matrix.1.matrix = f32[128,256]{1,0:T(8,128)S(1)} custom-call(s32[4]{0:T(128)S(1)} %copy-done.4, f32[1,64]{1,0:T(1,128)S(1)} %bitcast.13, s32[1,32]{1,0:T(1,128)S(1)} %bitcast.14, f32[32,32]{1,0:T(8,128)S(1)} %copy-done.2, f32[32,32]{1,0:T(8,128)S(1)} %copy-done.3, f32[192,128]{1,0:T(8,128)S(1)} %get-tuple-element.16.after.z_part), custom_call_target="tpu_custom_call" | custom-call | tf_op jit(solution)/shard_map/wall_matrix/pallas_call | solution.py:154
  14.7 0.3 %wall.1 = (f32[192,128]{1,0:T(8,128)S(1)}, f32[192,128]{1,0:T(8,128)S(1)}) custom-call(f32[128,256]{1,0:T(8,128)S(1)} %wall_matrix.1.matrix, f32[192,128]{1,0:T(8,128)S(1)} %get-tuple-element.17.x_part, f32[192,128]{1,0:T(8,128)S(1)} %get-tuple-element.16.after.z_part, f32[192,128]{1,0:T(8,128)S(1)} %bitcast.10, ...), custom_call_target="tpu_custom_call" | custom-call | tf_op jit(solution)/shard_map/wall/pallas_call | solution.py:154
  15.1 0.1 collective-permute-start.2
  15.1 0.6 %collective-permute-done.3.refs_2_ = f32[192,128]{1,0:T(8,128)S(1)} collective-permute-done((f32[192,128]{1,0:T(8,128)S(1)}, f32[192,128]{1,0:T(8,128)S(1)}, u32[]{:S(2)}, u32[]{:S(2)}) %collective-permute-start.3) | collective-permute-done | bytes 98336 | tf_op jit(solution)/shard_map/ppermute | solution.py:186
  15.7 1.0 %collective-permute-done.4.refs_3_ = f32[192,128]{1,0:T(8,128)S(1)} collective-permute-done((f32[192,128]{1,0:T(8,128)S(1)}, f32[192,128]{1,0:T(8,128)S(1)}, u32[]{:S(2)}, u32[]{:S(2)}) %collective-permute-start.4) | collective-permute-done | bytes 98336 | tf_op jit(solution)/shard_map/ppermute | solution.py:186
  16.8 0.4 %collective-permute-done.5.refs_4_ = f32[192,128]{1,0:T(8,128)S(1)} collective-permute-done((f32[192,128]{1,0:T(8,128)S(1)}, f32[192,128]{1,0:T(8,128)S(1)}, u32[]{:S(2)}, u32[]{:S(2)}) %collective-permute-start.5) | collective-permute-done | bytes 98336 | tf_op jit(solution)/shard_map/ppermute | solution.py:186
  17.2 0.7 %finish.1 = f32[192,128]{1,0:T(8,128)} custom-call(f32[64,128]{1,0:T(8,128)S(1)} %get-tuple-element.14.mask, f32[192,128]{1,0:T(8,128)S(1)} %get-tuple-element.18.refs_0_, f32[192,128]{1,0:T(8,128)S(1)} %collective-permute-done.2.refs_1_, f32[192,128]{1,0:T(8,128)S(1)} %collective-permute-done.3.refs_2_, f32[192,128]{1,0:T(8,128)S(1)} %collective-permute-done.4.refs_3_, ...), custom_call_target="tpu_custom_call" | custom-call | tf_op jit(solution)/shard_map/finish/pallas_call | solution.py:154
  (15 shorter events, 0.0 us)
Async XLA Ops:
  0.0 9.1 %collective-permute-start.1 = (f32[192,128]{1,0:T(8,128)}, f32[192,128]{1,0:T(8,128)S(1)}, u32[]{:S(2)}, u32[]{:S(2)}) collective-permute-start(f32[192,128]{1,0:T(8,128)} %bitcast.6), channel_id=1, source_target_pairs={{0,4},{1,5},{2,6},{3,7},{4,0},{5,1},{6,2},{7,3},{8,12},{9,13},{10,... | collective-permute-start | bytes 294920 | tf_op jit(solution)/shard_map/ppermute | solution.py:186
  4.0 5.1 %collective-permute-start = (f32[192,128]{1,0:T(8,128)}, f32[192,128]{1,0:T(8,128)S(1)}, u32[]{:S(2)}, u32[]{:S(2)}) collective-permute-start(f32[192,128]{1,0:T(8,128)} %bitcast.7), channel_id=1, source_target_pairs={{0,16},{8,24},{16,0},{24,8},{1,17},{9,25},{17,1},{25,9},{2,18},{10... | collective-permute-start | bytes 294920 | tf_op jit(solution)/shard_map/ppermute | solution.py:189
  5.6 0.7 %copy-start.7 = (f32[128]{0:T(128)S(1)}, f32[128]{0:T(128)}, u32[]{:S(2)}) copy-start(f32[128]{0:T(128)} %param.12) | copy-start | bytes 1540
  5.6 0.7 %copy-start.8 = (f32[128]{0:T(128)S(1)}, f32[128]{0:T(128)}, u32[]{:S(2)}) copy-start(f32[128]{0:T(128)} %param.13) | copy-start | bytes 1540
  5.6 0.7 %copy-start.4 = (s32[4]{0:T(128)S(1)}, s32[4]{0:T(128)}, u32[]{:S(2)}) copy-start(s32[4]{0:T(128)} %wall_counts.3) | copy-start | bytes 52
  5.6 0.7 %copy-start.5 = (f32[32]{0:T(128)S(1)}, f32[32]{0:T(128)}, u32[]{:S(2)}) copy-start(f32[32]{0:T(128)} %z_first.1) | copy-start | bytes 388
  5.6 0.7 %copy-start.6 = (f32[32]{0:T(128)S(1)}, f32[32]{0:T(128)}, u32[]{:S(2)}) copy-start(f32[32]{0:T(128)} %z_second.1) | copy-start | bytes 388
  6.3 0.9 %copy-start = (f32[3,16,4,128]{3,2,1,0:T(4,128)S(1)}, f32[3,16,4,128]{3,2,1,0:T(4,128)}, u32[]{:S(2)}) copy-start(f32[3,16,4,128]{3,2,1,0:T(4,128)} %param.10) | copy-start | bytes 294916
  7.2 2.0 %copy-start.1 = (f32[3,16,4,128]{3,2,1,0:T(4,128)S(1)}, f32[3,16,4,128]{3,2,1,0:T(4,128)}, u32[]{:S(2)}) copy-start(f32[3,16,4,128]{3,2,1,0:T(4,128)} %param.10) | copy-start | bytes 294916
  9.2 3.9 %copy-start.2 = (f32[32,32]{1,0:T(8,128)S(1)}, f32[32,32]{1,0:T(8,128)}, u32[]{:S(2)}) copy-start(f32[32,32]{1,0:T(8,128)} %y_first.1) | copy-start | bytes 12292
  9.2 3.9 %copy-start.3 = (f32[32,32]{1,0:T(8,128)S(1)}, f32[32,32]{1,0:T(8,128)}, u32[]{:S(2)}) copy-start(f32[32,32]{1,0:T(8,128)} %y_second.1) | copy-start | bytes 12292
  9.5 6.3 %collective-permute-start.3 = (f32[192,128]{1,0:T(8,128)S(1)}, f32[192,128]{1,0:T(8,128)S(1)}, u32[]{:S(2)}, u32[]{:S(2)}) collective-permute-start(f32[192,128]{1,0:T(8,128)S(1)} %get-tuple-element.20), channel_id=1, source_target_pairs={{0,3},{1,2},{2,1},{3,0},{4,7},{5,6},{6,5},{7,4},{8,11},{9,10},{10,... | collective-permute-start | bytes 294920 | tf_op jit(solution)/shard_map/ppermute | solution.py:186
  11.8 5.0 %collective-permute-start.4 = (f32[192,128]{1,0:T(8,128)S(1)}, f32[192,128]{1,0:T(8,128)S(1)}, u32[]{:S(2)}, u32[]{:S(2)}) collective-permute-start(f32[192,128]{1,0:T(8,128)S(1)} %get-tuple-element.21), channel_id=1, source_target_pairs={{0,2},{1,3},{2,0},{3,1},{4,6},{5,7},{6,4},{7,5},{8,10},{9,11},{10,... | collective-permute-start | bytes 294920 | tf_op jit(solution)/shard_map/ppermute | solution.py:186
  12.6 4.6 %collective-permute-start.5 = (f32[192,128]{1,0:T(8,128)S(1)}, f32[192,128]{1,0:T(8,128)S(1)}, u32[]{:S(2)}, u32[]{:S(2)}) collective-permute-start(f32[192,128]{1,0:T(8,128)S(1)} %get-tuple-element.22), channel_id=1, source_target_pairs={{0,1},{1,0},{2,3},{3,2},{4,5},{5,4},{6,7},{7,6},{8,9},{9,8},{10,11... | collective-permute-start | bytes 294920 | tf_op jit(solution)/shard_map/ppermute | solution.py:186
  13.0 0.7 %copy-start.9 = (f32[64]{0:T(128)S(1)}, f32[64]{0:T(128)}, u32[]{:S(2)}) copy-start(f32[64]{0:T(128)} %param.18) | copy-start | bytes 772
  13.0 0.7 %copy-start.10 = (s32[32]{0:T(128)S(1)}, s32[32]{0:T(128)}, u32[]{:S(2)}) copy-start(s32[32]{0:T(128)} %param.19) | copy-start | bytes 388
  15.1 2.1 %collective-permute-start.2 = (f32[192,128]{1,0:T(8,128)S(1)}, f32[192,128]{1,0:T(8,128)S(1)}, u32[]{:S(2)}, u32[]{:S(2)}) collective-permute-start(f32[192,128]{1,0:T(8,128)S(1)} %get-tuple-element.19), channel_id=1, source_target_pairs={{0,8},{8,0},{16,24},{24,16},{1,9},{9,1},{17,25},{25,17},{2,10},{10... | collective-permute-start | bytes 294920 | tf_op jit(solution)/shard_map/ppermute | solution.py:189

commit v14 on v13

--- a/solution.py
+++ b/solution.py
@@ -204,7 +204,7 @@
         [field.shape] * quad,
         "span",
     )
-    returned = [along(parts[t], t) for t in reversed(range(1, quad))]
+    returned = [along(parts[t], t) for t in range(1, quad)]
     (y_matrix,) = call(
         functools.partial(wall_matrix_kernel, rows, zloc),
         [wall_counts, metric_table.reshape(1, -1), metric_index.reshape(1, -1), y_first, y_second, parts[0]],

time: 18 us -> 18.7 us (1.039)
  waiting for transfers between devices: 2.92 us -> 3.58 us
    ppermute x4, waiting for transfers between devices: 2.92 us -> 3.58 us  [along(): return lax.ppermute(value, 'col', [(i, i ^ step) for i in range(cols)])]
  transfers between devices with their start and end apart: 6 -> 6, of which waited for: 4 -> 3; matrix products, arithmetic and copies ran while one was open for 0% -> 0% of each run, Pallas kernels for 14% -> 13%
where the time goes in v14:
time: 18.7 us; the launch traced here: 18.5 us
  starting transfers between devices  9.18 us (49%)
  waiting for transfers between devices  3.58 us (19%)
  Pallas kernels  3.4 us (18%)
  local copies, waits for them, and re-layouts  2.27 us (12%)
    ppermute x4, starting transfers between devices, along(): return lax.ppermute(value, 'col', [(i, i ^ step) for i in range(cols)])  7.59 us
    ppermute x4, waiting for transfers between devices, along(): return lax.ppermute(value, 'col', [(i, i ^ step) for i in range(cols)])  3.58 us
    pallas_call x5, Pallas kernels, call(): pl.pallas_call(kernel, out_shape=results, in_specs=[pl.BlockSpec(memory_s...  3.4 us
    unnamed x22, local copies, waits for them, and re-layouts  2.27 us
    ppermute x2, starting transfers between devices, across(): return lax.ppermute(value, 'row', [(i, i ^ step) for i in range(rows)])  1.59 us
  transfers between devices with their start and end apart: 6, of which 3 were waited for; matrix products, arithmetic and copies ran while one was open for 0% of the time, Pallas kernels for 13%

profile of v14, /device:TPU:0, one launch (start us, length us, event | category | flops | bytes accessed | tf_op | source)
XLA Modules:
  0.0 18.5 jit_solution(13884772791288868734)
XLA Ops:
  0.0 4.0 %collective-permute-start.1 = (f32[192,128]{1,0:T(8,128)}, f32[192,128]{1,0:T(8,128)S(1)}, u32[]{:S(2)}, u32[]{:S(2)}) collective-permute-start(f32[192,128]{1,0:T(8,128)} %bitcast.6), channel_id=1, source_target_pairs={{0,4},{1,5},{2,6},{3,7},{4,0},{5,1},{6,2},{7,3},{8,12},{9,13},{10,... | collective-permute-start | bytes 294920 | tf_op jit(solution)/shard_map/ppermute | solution.py:186
  4.0 1.5 %collective-permute-start = (f32[192,128]{1,0:T(8,128)}, f32[192,128]{1,0:T(8,128)S(1)}, u32[]{:S(2)}, u32[]{:S(2)}) collective-permute-start(f32[192,128]{1,0:T(8,128)} %bitcast.7), channel_id=1, source_target_pairs={{0,16},{8,24},{16,0},{24,8},{1,17},{9,25},{17,1},{25,9},{2,18},{10... | collective-permute-start | bytes 294920 | tf_op jit(solution)/shard_map/ppermute | solution.py:189
  5.6 0.6 %copy-done.7 = f32[128]{0:T(128)S(1)} copy-done((f32[128]{0:T(128)S(1)}, f32[128]{0:T(128)}, u32[]{:S(2)}) %copy-start.7) | copy-done | bytes 536
  6.2 0.0 copy-done.8
  6.2 0.0 copy-done.4
  6.2 0.0 copy-done.5
  6.3 0.0 copy-done.6
  6.3 0.9 %copy-done = f32[3,16,4,128]{3,2,1,0:T(4,128)S(1)} copy-done((f32[3,16,4,128]{3,2,1,0:T(4,128)S(1)}, f32[3,16,4,128]{3,2,1,0:T(4,128)}, u32[]{:S(2)}) %copy-start) | copy-done | bytes 98328
  7.2 1.1 %stream.1 = (f32[192,128]{1,0:T(8,128)S(1)}, f32[128,128]{1,0:T(8,128)S(1)}, f32[64,128]{1,0:T(8,128)S(1)}) custom-call(s32[4]{0:T(128)S(1)} %copy-done.4, f32[32]{0:T(128)S(1)} %copy-done.5, f32[32]{0:T(128)S(1)} %copy-done.6, f32[192,128]{1,0:T(8,128)S(1)} %bitcast.8, f32[1,128]{1,0:T(1,128)S(1)} %bitcast.11, f32[1,128]{1,0:T(1,128)S(1)} %bitcast.12), custom_call_target="tpu_custom_call" | custom-call | tf_op jit(solution)/shard_map/stream/pallas_call | solution.py:154
  8.3 0.9 %collective-permute-done.1.refs_2_ = f32[192,128]{1,0:T(8,128)S(1)} collective-permute-done((f32[192,128]{1,0:T(8,128)}, f32[192,128]{1,0:T(8,128)S(1)}, u32[]{:S(2)}, u32[]{:S(2)}) %collective-permute-start.1) | collective-permute-done | bytes 98336 | tf_op jit(solution)/shard_map/ppermute | solution.py:186
  9.1 0.0 collective-permute-done.refs_0_.refs_1_
  9.2 0.0 copy-start.3
  9.2 0.3 %span.1 = (f32[192,128]{1,0:T(8,128)S(1)}, f32[192,128]{1,0:T(8,128)S(1)}, f32[192,128]{1,0:T(8,128)S(1)}, f32[192,128]{1,0:T(8,128)S(1)}) custom-call(f32[128,128]{1,0:T(8,128)S(1)} %get-tuple-element.15.matrix, f32[192,128]{1,0:T(8,128)S(1)} %collective-permute-done.refs_0_.refs_1_, f32[192,128]{1,0:T(8,128)S(1)} %bitcast.9, ...), custom_call_target="tpu_custom_call" | custom-call | tf_op jit(solution)/shard_map/span/pallas_call | solution.py:154
  9.5 1.6 %collective-permute-start.3 = (f32[192,128]{1,0:T(8,128)S(1)}, f32[192,128]{1,0:T(8,128)S(1)}, u32[]{:S(2)}, u32[]{:S(2)}) collective-permute-start(f32[192,128]{1,0:T(8,128)S(1)} %get-tuple-element.20), channel_id=1, source_target_pairs={{0,1},{1,0},{2,3},{3,2},{4,5},{5,4},{6,7},{7,6},{8,9},{9,8},{10,11... | collective-permute-start | bytes 294920 | tf_op jit(solution)/shard_map/ppermute | solution.py:186
  11.1 1.2 %collective-permute-start.4 = (f32[192,128]{1,0:T(8,128)S(1)}, f32[192,128]{1,0:T(8,128)S(1)}, u32[]{:S(2)}, u32[]{:S(2)}) collective-permute-start(f32[192,128]{1,0:T(8,128)S(1)} %get-tuple-element.21), channel_id=1, source_target_pairs={{0,2},{1,3},{2,0},{3,1},{4,6},{5,7},{6,4},{7,5},{8,10},{9,11},{10,... | collective-permute-start | bytes 294920 | tf_op jit(solution)/shard_map/ppermute | solution.py:186
  12.3 0.7 %collective-permute-start.5 = (f32[192,128]{1,0:T(8,128)S(1)}, f32[192,128]{1,0:T(8,128)S(1)}, u32[]{:S(2)}, u32[]{:S(2)}) collective-permute-start(f32[192,128]{1,0:T(8,128)S(1)} %get-tuple-element.22), channel_id=1, source_target_pairs={{0,3},{1,2},{2,1},{3,0},{4,7},{5,6},{6,5},{7,4},{8,11},{9,10},{10,... | collective-permute-start | bytes 294920 | tf_op jit(solution)/shard_map/ppermute | solution.py:186
  13.1 0.6 %copy-done.9 = f32[64]{0:T(128)S(1)} copy-done((f32[64]{0:T(128)S(1)}, f32[64]{0:T(128)}, u32[]{:S(2)}) %copy-start.9) | copy-done | bytes 280
  13.7 0.0 copy-done.10
  13.7 1.0 %wall_matrix.1.matrix = f32[128,256]{1,0:T(8,128)S(1)} custom-call(s32[4]{0:T(128)S(1)} %copy-done.4, f32[1,64]{1,0:T(1,128)S(1)} %bitcast.13, s32[1,32]{1,0:T(1,128)S(1)} %bitcast.14, f32[32,32]{1,0:T(8,128)S(1)} %copy-done.2, f32[32,32]{1,0:T(8,128)S(1)} %copy-done.3, f32[192,128]{1,0:T(8,128)S(1)} %get-tuple-element.16.after.z_part), custom_call_target="tpu_custom_call" | custom-call | tf_op jit(solution)/shard_map/wall_matrix/pallas_call | solution.py:154
  14.7 0.3 %wall.1 = (f32[192,128]{1,0:T(8,128)S(1)}, f32[192,128]{1,0:T(8,128)S(1)}) custom-call(f32[128,256]{1,0:T(8,128)S(1)} %wall_matrix.1.matrix, f32[192,128]{1,0:T(8,128)S(1)} %get-tuple-element.17.x_part, f32[192,128]{1,0:T(8,128)S(1)} %get-tuple-element.16.after.z_part, f32[192,128]{1,0:T(8,128)S(1)} %bitcast.10, ...), custom_call_target="tpu_custom_call" | custom-call | tf_op jit(solution)/shard_map/wall/pallas_call | solution.py:154
  15.1 0.1 collective-permute-start.2
  15.1 0.9 %collective-permute-done.4.refs_3_ = f32[192,128]{1,0:T(8,128)S(1)} collective-permute-done((f32[192,128]{1,0:T(8,128)S(1)}, f32[192,128]{1,0:T(8,128)S(1)}, u32[]{:S(2)}, u32[]{:S(2)}) %collective-permute-start.4) | collective-permute-done | bytes 98336 | tf_op jit(solution)/shard_map/ppermute | solution.py:186
  16.0 1.8 %collective-permute-done.5.refs_4_ = f32[192,128]{1,0:T(8,128)S(1)} collective-permute-done((f32[192,128]{1,0:T(8,128)S(1)}, f32[192,128]{1,0:T(8,128)S(1)}, u32[]{:S(2)}, u32[]{:S(2)}) %collective-permute-start.5) | collective-permute-done | bytes 98336 | tf_op jit(solution)/shard_map/ppermute | solution.py:186
  17.8 0.7 %finish.1 = f32[192,128]{1,0:T(8,128)} custom-call(f32[64,128]{1,0:T(8,128)S(1)} %get-tuple-element.14.mask, f32[192,128]{1,0:T(8,128)S(1)} %get-tuple-element.18.refs_0_, f32[192,128]{1,0:T(8,128)S(1)} %collective-permute-done.2.refs_1_, f32[192,128]{1,0:T(8,128)S(1)} %collective-permute-done.3.refs_2_, f32[192,128]{1,0:T(8,128)S(1)} %collective-permute-done.4.refs_3_, ...), custom_call_target="tpu_custom_call" | custom-call | tf_op jit(solution)/shard_map/finish/pallas_call | solution.py:154
  (15 shorter events, 0.0 us)
Async XLA Ops:
  0.0 9.1 %collective-permute-start.1 = (f32[192,128]{1,0:T(8,128)}, f32[192,128]{1,0:T(8,128)S(1)}, u32[]{:S(2)}, u32[]{:S(2)}) collective-permute-start(f32[192,128]{1,0:T(8,128)} %bitcast.6), channel_id=1, source_target_pairs={{0,4},{1,5},{2,6},{3,7},{4,0},{5,1},{6,2},{7,3},{8,12},{9,13},{10,... | collective-permute-start | bytes 294920 | tf_op jit(solution)/shard_map/ppermute | solution.py:186
  4.0 5.1 %collective-permute-start = (f32[192,128]{1,0:T(8,128)}, f32[192,128]{1,0:T(8,128)S(1)}, u32[]{:S(2)}, u32[]{:S(2)}) collective-permute-start(f32[192,128]{1,0:T(8,128)} %bitcast.7), channel_id=1, source_target_pairs={{0,16},{8,24},{16,0},{24,8},{1,17},{9,25},{17,1},{25,9},{2,18},{10... | collective-permute-start | bytes 294920 | tf_op jit(solution)/shard_map/ppermute | solution.py:189
  5.6 0.7 %copy-start.7 = (f32[128]{0:T(128)S(1)}, f32[128]{0:T(128)}, u32[]{:S(2)}) copy-start(f32[128]{0:T(128)} %param.12) | copy-start | bytes 1540
  5.6 0.7 %copy-start.8 = (f32[128]{0:T(128)S(1)}, f32[128]{0:T(128)}, u32[]{:S(2)}) copy-start(f32[128]{0:T(128)} %param.13) | copy-start | bytes 1540
  5.6 0.7 %copy-start.4 = (s32[4]{0:T(128)S(1)}, s32[4]{0:T(128)}, u32[]{:S(2)}) copy-start(s32[4]{0:T(128)} %wall_counts.3) | copy-start | bytes 52
  5.6 0.7 %copy-start.5 = (f32[32]{0:T(128)S(1)}, f32[32]{0:T(128)}, u32[]{:S(2)}) copy-start(f32[32]{0:T(128)} %z_first.1) | copy-start | bytes 388
  5.6 0.7 %copy-start.6 = (f32[32]{0:T(128)S(1)}, f32[32]{0:T(128)}, u32[]{:S(2)}) copy-start(f32[32]{0:T(128)} %z_second.1) | copy-start | bytes 388
  6.3 0.9 %copy-start = (f32[3,16,4,128]{3,2,1,0:T(4,128)S(1)}, f32[3,16,4,128]{3,2,1,0:T(4,128)}, u32[]{:S(2)}) copy-start(f32[3,16,4,128]{3,2,1,0:T(4,128)} %param.10) | copy-start | bytes 294916
  7.2 2.0 %copy-start.1 = (f32[3,16,4,128]{3,2,1,0:T(4,128)S(1)}, f32[3,16,4,128]{3,2,1,0:T(4,128)}, u32[]{:S(2)}) copy-start(f32[3,16,4,128]{3,2,1,0:T(4,128)} %param.10) | copy-start | bytes 294916
  9.2 3.9 %copy-start.2 = (f32[32,32]{1,0:T(8,128)S(1)}, f32[32,32]{1,0:T(8,128)}, u32[]{:S(2)}) copy-start(f32[32,32]{1,0:T(8,128)} %y_first.1) | copy-start | bytes 12292
  9.2 3.9 %copy-start.3 = (f32[32,32]{1,0:T(8,128)S(1)}, f32[32,32]{1,0:T(8,128)}, u32[]{:S(2)}) copy-start(f32[32,32]{1,0:T(8,128)} %y_second.1) | copy-start | bytes 12292
  9.5 5.6 %collective-permute-start.3 = (f32[192,128]{1,0:T(8,128)S(1)}, f32[192,128]{1,0:T(8,128)S(1)}, u32[]{:S(2)}, u32[]{:S(2)}) collective-permute-start(f32[192,128]{1,0:T(8,128)S(1)} %get-tuple-element.20), channel_id=1, source_target_pairs={{0,1},{1,0},{2,3},{3,2},{4,5},{5,4},{6,7},{7,6},{8,9},{9,8},{10,11... | collective-permute-start | bytes 294920 | tf_op jit(solution)/shard_map/ppermute | solution.py:186
  11.1 4.9 %collective-permute-start.4 = (f32[192,128]{1,0:T(8,128)S(1)}, f32[192,128]{1,0:T(8,128)S(1)}, u32[]{:S(2)}, u32[]{:S(2)}) collective-permute-start(f32[192,128]{1,0:T(8,128)S(1)} %get-tuple-element.21), channel_id=1, source_target_pairs={{0,2},{1,3},{2,0},{3,1},{4,6},{5,7},{6,4},{7,5},{8,10},{9,11},{10,... | collective-permute-start | bytes 294920 | tf_op jit(solution)/shard_map/ppermute | solution.py:186
  12.3 5.5 %collective-permute-start.5 = (f32[192,128]{1,0:T(8,128)S(1)}, f32[192,128]{1,0:T(8,128)S(1)}, u32[]{:S(2)}, u32[]{:S(2)}) collective-permute-start(f32[192,128]{1,0:T(8,128)S(1)} %get-tuple-element.22), channel_id=1, source_target_pairs={{0,3},{1,2},{2,1},{3,0},{4,7},{5,6},{6,5},{7,4},{8,11},{9,10},{10,... | collective-permute-start | bytes 294920 | tf_op jit(solution)/shard_map/ppermute | solution.py:186
  13.0 0.7 %copy-start.9 = (f32[64]{0:T(128)S(1)}, f32[64]{0:T(128)}, u32[]{:S(2)}) copy-start(f32[64]{0:T(128)} %param.18) | copy-start | bytes 772
  13.0 0.7 %copy-start.10 = (s32[32]{0:T(128)S(1)}, s32[32]{0:T(128)}, u32[]{:S(2)}) copy-start(s32[32]{0:T(128)} %param.19) | copy-start | bytes 388
  15.1 2.8 %collective-permute-start.2 = (f32[192,128]{1,0:T(8,128)S(1)}, f32[192,128]{1,0:T(8,128)S(1)}, u32[]{:S(2)}, u32[]{:S(2)}) collective-permute-start(f32[192,128]{1,0:T(8,128)S(1)} %get-tuple-element.19), channel_id=1, source_target_pairs={{0,8},{8,0},{16,24},{24,16},{1,9},{9,1},{17,25},{25,17},{2,10},{10... | collective-permute-start | bytes 294920 | tf_op jit(solution)/shard_map/ppermute | solution.py:189

commit v15 on v13

--- a/solution.py
+++ b/solution.py
@@ -199,8 +199,8 @@
     )
     parts = call(
         functools.partial(span_kernel, comps, sources),
-        [z_matrix] + far + [field] + gathered,
-        [VMEM] + [pl.ANY] * len(far) + [VMEM] * sources,
+        [z_matrix, field] + gathered,
+        [VMEM] * (1 + sources),
         [field.shape] * quad,
         "span",
     )

time: 18 us -> 18 us (level)
  transfers between devices with their start and end apart: 6 -> 6, of which waited for: 4 -> 4; matrix products, arithmetic and copies ran while one was open for 0% -> 0% of each run, Pallas kernels for 14% -> 15%
where the time goes in v15:
time: 18 us; the launch traced here: 17.8 us
  starting transfers between devices  9.18 us (51%)
  Pallas kernels  3.41 us (19%)
  waiting for transfers between devices  2.9 us (16%)
  local copies, waits for them, and re-layouts  2.27 us (13%)
    ppermute x4, starting transfers between devices, along(): return lax.ppermute(value, 'col', [(i, i ^ step) for i in range(cols)])  7.59 us
    pallas_call x5, Pallas kernels, call(): pl.pallas_call(kernel, out_shape=results, in_specs=[pl.BlockSpec(memory_s...  3.41 us
    ppermute x4, waiting for transfers between devices, along(): return lax.ppermute(value, 'col', [(i, i ^ step) for i in range(cols)])  2.9 us
    unnamed x22, local copies, waits for them, and re-layouts  2.27 us
    ppermute x2, starting transfers between devices, across(): return lax.ppermute(value, 'row', [(i, i ^ step) for i in range(rows)])  1.59 us
  transfers between devices with their start and end apart: 6, of which 4 were waited for; matrix products, arithmetic and copies ran while one was open for 0% of the time, Pallas kernels for 15%

profile of v15, /device:TPU:0, one launch (start us, length us, event | category | flops | bytes accessed | tf_op | source)
XLA Modules:
  0.0 17.8 jit_solution(15822467731205905010)
XLA Ops:
  0.0 4.0 %collective-permute-start = (f32[192,128]{1,0:T(8,128)}, f32[192,128]{1,0:T(8,128)S(1)}, u32[]{:S(2)}, u32[]{:S(2)}) collective-permute-start(f32[192,128]{1,0:T(8,128)} %bitcast.6), channel_id=1, source_target_pairs={{0,4},{1,5},{2,6},{3,7},{4,0},{5,1},{6,2},{7,3},{8,12},{9,13},{10,... | collective-permute-start | bytes 294920 | tf_op jit(solution)/shard_map/ppermute | solution.py:186
  4.0 1.5 %collective-permute-start.1 = (f32[192,128]{1,0:T(8,128)}, f32[192,128]{1,0:T(8,128)S(1)}, u32[]{:S(2)}, u32[]{:S(2)}) collective-permute-start(f32[192,128]{1,0:T(8,128)} %bitcast.7), channel_id=1, source_target_pairs={{0,16},{8,24},{16,0},{24,8},{1,17},{9,25},{17,1},{25,9},{2,18},{10... | collective-permute-start | bytes 294920 | tf_op jit(solution)/shard_map/ppermute | solution.py:189
  5.6 0.6 %copy-done.7 = f32[128]{0:T(128)S(1)} copy-done((f32[128]{0:T(128)S(1)}, f32[128]{0:T(128)}, u32[]{:S(2)}) %copy-start.7) | copy-done | bytes 536
  6.2 0.0 copy-done.8
  6.2 0.0 copy-done.4
  6.2 0.0 copy-done.5
  6.3 0.0 copy-done.6
  6.3 0.9 %copy-done = f32[3,16,4,128]{3,2,1,0:T(4,128)S(1)} copy-done((f32[3,16,4,128]{3,2,1,0:T(4,128)S(1)}, f32[3,16,4,128]{3,2,1,0:T(4,128)}, u32[]{:S(2)}) %copy-start) | copy-done | bytes 98328
  7.2 1.1 %stream.1 = (f32[192,128]{1,0:T(8,128)S(1)}, f32[128,128]{1,0:T(8,128)S(1)}, f32[64,128]{1,0:T(8,128)S(1)}) custom-call(s32[4]{0:T(128)S(1)} %copy-done.4, f32[32]{0:T(128)S(1)} %copy-done.5, f32[32]{0:T(128)S(1)} %copy-done.6, f32[192,128]{1,0:T(8,128)S(1)} %bitcast.8, f32[1,128]{1,0:T(1,128)S(1)} %bitcast.11, f32[1,128]{1,0:T(1,128)S(1)} %bitcast.12), custom_call_target="tpu_custom_call" | custom-call | tf_op jit(solution)/shard_map/stream/pallas_call | solution.py:154
  8.3 0.9 %collective-permute-done.refs_1_ = f32[192,128]{1,0:T(8,128)S(1)} collective-permute-done((f32[192,128]{1,0:T(8,128)}, f32[192,128]{1,0:T(8,128)S(1)}, u32[]{:S(2)}, u32[]{:S(2)}) %collective-permute-start) | collective-permute-done | bytes 98336 | tf_op jit(solution)/shard_map/ppermute | solution.py:186
  9.2 0.3 %span.1 = (f32[192,128]{1,0:T(8,128)S(1)}, f32[192,128]{1,0:T(8,128)S(1)}, f32[192,128]{1,0:T(8,128)S(1)}, f32[192,128]{1,0:T(8,128)S(1)}) custom-call(f32[128,128]{1,0:T(8,128)S(1)} %get-tuple-element.15.matrix, f32[192,128]{1,0:T(8,128)S(1)} %bitcast.9, f32[192,128]{1,0:T(8,128)S(1)} %collective-permute-done.refs_1_), custom_call_target="tpu_custom_call" | custom-call | tf_op jit(solution)/shard_map/span/pallas_call | solution.py:154
  9.5 1.8 %collective-permute-start.3 = (f32[192,128]{1,0:T(8,128)S(1)}, f32[192,128]{1,0:T(8,128)S(1)}, u32[]{:S(2)}, u32[]{:S(2)}) collective-permute-start(f32[192,128]{1,0:T(8,128)S(1)} %get-tuple-element.20), channel_id=1, source_target_pairs={{0,3},{1,2},{2,1},{3,0},{4,7},{5,6},{6,5},{7,4},{8,11},{9,10},{10,... | collective-permute-start | bytes 294920 | tf_op jit(solution)/shard_map/ppermute | solution.py:186
  11.3 1.3 %collective-permute-start.4 = (f32[192,128]{1,0:T(8,128)S(1)}, f32[192,128]{1,0:T(8,128)S(1)}, u32[]{:S(2)}, u32[]{:S(2)}) collective-permute-start(f32[192,128]{1,0:T(8,128)S(1)} %get-tuple-element.21), channel_id=1, source_target_pairs={{0,2},{1,3},{2,0},{3,1},{4,6},{5,7},{6,4},{7,5},{8,10},{9,11},{10,... | collective-permute-start | bytes 294920 | tf_op jit(solution)/shard_map/ppermute | solution.py:186
  12.5 0.5 %collective-permute-start.5 = (f32[192,128]{1,0:T(8,128)S(1)}, f32[192,128]{1,0:T(8,128)S(1)}, u32[]{:S(2)}, u32[]{:S(2)}) collective-permute-start(f32[192,128]{1,0:T(8,128)S(1)} %get-tuple-element.22), channel_id=1, source_target_pairs={{0,1},{1,0},{2,3},{3,2},{4,5},{5,4},{6,7},{7,6},{8,9},{9,8},{10,11... | collective-permute-start | bytes 294920 | tf_op jit(solution)/shard_map/ppermute | solution.py:186
  13.0 0.6 %copy-done.9 = f32[64]{0:T(128)S(1)} copy-done((f32[64]{0:T(128)S(1)}, f32[64]{0:T(128)}, u32[]{:S(2)}) %copy-start.9) | copy-done | bytes 280
  13.7 0.0 copy-done.10
  13.7 1.0 %wall_matrix.1.matrix = f32[128,256]{1,0:T(8,128)S(1)} custom-call(s32[4]{0:T(128)S(1)} %copy-done.4, f32[1,64]{1,0:T(1,128)S(1)} %bitcast.13, s32[1,32]{1,0:T(1,128)S(1)} %bitcast.14, f32[32,32]{1,0:T(8,128)S(1)} %copy-done.2, f32[32,32]{1,0:T(8,128)S(1)} %copy-done.3, f32[192,128]{1,0:T(8,128)S(1)} %get-tuple-element.16.after.z_part), custom_call_target="tpu_custom_call" | custom-call | tf_op jit(solution)/shard_map/wall_matrix/pallas_call | solution.py:154
  14.7 0.0 collective-permute-done.1.refs_1_
  14.7 0.3 %wall.1 = (f32[192,128]{1,0:T(8,128)S(1)}, f32[192,128]{1,0:T(8,128)S(1)}) custom-call(f32[128,256]{1,0:T(8,128)S(1)} %wall_matrix.1.matrix, f32[192,128]{1,0:T(8,128)S(1)} %get-tuple-element.17.x_part, f32[192,128]{1,0:T(8,128)S(1)} %get-tuple-element.16.after.z_part, f32[192,128]{1,0:T(8,128)S(1)} %bitcast.10, f32[192,128]{1,0:T(8,128)S(1)} %collective-permute-done.1.refs_1_), custom_call_target="tpu_custom_call" | custom-call | tf_op jit(solution)/shard_map/wall/pallas_call | solution.py:154
  15.1 0.1 collective-permute-start.2
  15.1 0.6 %collective-permute-done.3.refs_2_ = f32[192,128]{1,0:T(8,128)S(1)} collective-permute-done((f32[192,128]{1,0:T(8,128)S(1)}, f32[192,128]{1,0:T(8,128)S(1)}, u32[]{:S(2)}, u32[]{:S(2)}) %collective-permute-start.3) | collective-permute-done | bytes 98336 | tf_op jit(solution)/shard_map/ppermute | solution.py:186
  15.7 1.0 %collective-permute-done.4.refs_3_ = f32[192,128]{1,0:T(8,128)S(1)} collective-permute-done((f32[192,128]{1,0:T(8,128)S(1)}, f32[192,128]{1,0:T(8,128)S(1)}, u32[]{:S(2)}, u32[]{:S(2)}) %collective-permute-start.4) | collective-permute-done | bytes 98336 | tf_op jit(solution)/shard_map/ppermute | solution.py:186
  16.8 0.4 %collective-permute-done.5.refs_4_ = f32[192,128]{1,0:T(8,128)S(1)} collective-permute-done((f32[192,128]{1,0:T(8,128)S(1)}, f32[192,128]{1,0:T(8,128)S(1)}, u32[]{:S(2)}, u32[]{:S(2)}) %collective-permute-start.5) | collective-permute-done | bytes 98336 | tf_op jit(solution)/shard_map/ppermute | solution.py:186
  17.2 0.7 %finish.1 = f32[192,128]{1,0:T(8,128)} custom-call(f32[64,128]{1,0:T(8,128)S(1)} %get-tuple-element.14.mask, f32[192,128]{1,0:T(8,128)S(1)} %get-tuple-element.18.refs_0_, f32[192,128]{1,0:T(8,128)S(1)} %collective-permute-done.2.refs_1_, f32[192,128]{1,0:T(8,128)S(1)} %collective-permute-done.3.refs_2_, f32[192,128]{1,0:T(8,128)S(1)} %collective-permute-done.4.refs_3_, ...), custom_call_target="tpu_custom_call" | custom-call | tf_op jit(solution)/shard_map/finish/pallas_call | solution.py:154
  (15 shorter events, 0.0 us)
Async XLA Ops:
  0.0 9.1 %collective-permute-start = (f32[192,128]{1,0:T(8,128)}, f32[192,128]{1,0:T(8,128)S(1)}, u32[]{:S(2)}, u32[]{:S(2)}) collective-permute-start(f32[192,128]{1,0:T(8,128)} %bitcast.6), channel_id=1, source_target_pairs={{0,4},{1,5},{2,6},{3,7},{4,0},{5,1},{6,2},{7,3},{8,12},{9,13},{10,... | collective-permute-start | bytes 294920 | tf_op jit(solution)/shard_map/ppermute | solution.py:186
  4.0 10.7 %collective-permute-start.1 = (f32[192,128]{1,0:T(8,128)}, f32[192,128]{1,0:T(8,128)S(1)}, u32[]{:S(2)}, u32[]{:S(2)}) collective-permute-start(f32[192,128]{1,0:T(8,128)} %bitcast.7), channel_id=1, source_target_pairs={{0,16},{8,24},{16,0},{24,8},{1,17},{9,25},{17,1},{25,9},{2,18},{10... | collective-permute-start | bytes 294920 | tf_op jit(solution)/shard_map/ppermute | solution.py:189
  5.6 0.7 %copy-start.7 = (f32[128]{0:T(128)S(1)}, f32[128]{0:T(128)}, u32[]{:S(2)}) copy-start(f32[128]{0:T(128)} %param.12) | copy-start | bytes 1540
  5.6 0.7 %copy-start.8 = (f32[128]{0:T(128)S(1)}, f32[128]{0:T(128)}, u32[]{:S(2)}) copy-start(f32[128]{0:T(128)} %param.13) | copy-start | bytes 1540
  5.6 0.7 %copy-start.4 = (s32[4]{0:T(128)S(1)}, s32[4]{0:T(128)}, u32[]{:S(2)}) copy-start(s32[4]{0:T(128)} %wall_counts.3) | copy-start | bytes 52
  5.6 0.7 %copy-start.5 = (f32[32]{0:T(128)S(1)}, f32[32]{0:T(128)}, u32[]{:S(2)}) copy-start(f32[32]{0:T(128)} %z_first.1) | copy-start | bytes 388
  5.6 0.7 %copy-start.6 = (f32[32]{0:T(128)S(1)}, f32[32]{0:T(128)}, u32[]{:S(2)}) copy-start(f32[32]{0:T(128)} %z_second.1) | copy-start | bytes 388
  6.3 0.9 %copy-start = (f32[3,16,4,128]{3,2,1,0:T(4,128)S(1)}, f32[3,16,4,128]{3,2,1,0:T(4,128)}, u32[]{:S(2)}) copy-start(f32[3,16,4,128]{3,2,1,0:T(4,128)} %param.10) | copy-start | bytes 294916
  7.2 2.0 %copy-start.1 = (f32[3,16,4,128]{3,2,1,0:T(4,128)S(1)}, f32[3,16,4,128]{3,2,1,0:T(4,128)}, u32[]{:S(2)}) copy-start(f32[3,16,4,128]{3,2,1,0:T(4,128)} %param.10) | copy-start | bytes 294916
  9.1 3.9 %copy-start.2 = (f32[32,32]{1,0:T(8,128)S(1)}, f32[32,32]{1,0:T(8,128)}, u32[]{:S(2)}) copy-start(f32[32,32]{1,0:T(8,128)} %y_first.1) | copy-start | bytes 12292
  9.2 3.9 %copy-start.3 = (f32[32,32]{1,0:T(8,128)S(1)}, f32[32,32]{1,0:T(8,128)}, u32[]{:S(2)}) copy-start(f32[32,32]{1,0:T(8,128)} %y_second.1) | copy-start | bytes 12292
  9.5 6.3 %collective-permute-start.3 = (f32[192,128]{1,0:T(8,128)S(1)}, f32[192,128]{1,0:T(8,128)S(1)}, u32[]{:S(2)}, u32[]{:S(2)}) collective-permute-start(f32[192,128]{1,0:T(8,128)S(1)} %get-tuple-element.20), channel_id=1, source_target_pairs={{0,3},{1,2},{2,1},{3,0},{4,7},{5,6},{6,5},{7,4},{8,11},{9,10},{10,... | collective-permute-start | bytes 294920 | tf_op jit(solution)/shard_map/ppermute | solution.py:186
  11.3 5.5 %collective-permute-start.4 = (f32[192,128]{1,0:T(8,128)S(1)}, f32[192,128]{1,0:T(8,128)S(1)}, u32[]{:S(2)}, u32[]{:S(2)}) collective-permute-start(f32[192,128]{1,0:T(8,128)S(1)} %get-tuple-element.21), channel_id=1, source_target_pairs={{0,2},{1,3},{2,0},{3,1},{4,6},{5,7},{6,4},{7,5},{8,10},{9,11},{10,... | collective-permute-start | bytes 294920 | tf_op jit(solution)/shard_map/ppermute | solution.py:186
  12.5 4.6 %collective-permute-start.5 = (f32[192,128]{1,0:T(8,128)S(1)}, f32[192,128]{1,0:T(8,128)S(1)}, u32[]{:S(2)}, u32[]{:S(2)}) collective-permute-start(f32[192,128]{1,0:T(8,128)S(1)} %get-tuple-element.22), channel_id=1, source_target_pairs={{0,1},{1,0},{2,3},{3,2},{4,5},{5,4},{6,7},{7,6},{8,9},{9,8},{10,11... | collective-permute-start | bytes 294920 | tf_op jit(solution)/shard_map/ppermute | solution.py:186
  13.0 0.7 %copy-start.9 = (f32[64]{0:T(128)S(1)}, f32[64]{0:T(128)}, u32[]{:S(2)}) copy-start(f32[64]{0:T(128)} %param.18) | copy-start | bytes 772
  13.0 0.7 %copy-start.10 = (s32[32]{0:T(128)S(1)}, s32[32]{0:T(128)}, u32[]{:S(2)}) copy-start(s32[32]{0:T(128)} %param.19) | copy-start | bytes 388
  15.1 2.1 %collective-permute-start.2 = (f32[192,128]{1,0:T(8,128)S(1)}, f32[192,128]{1,0:T(8,128)S(1)}, u32[]{:S(2)}, u32[]{:S(2)}) collective-permute-start(f32[192,128]{1,0:T(8,128)S(1)} %get-tuple-element.19), channel_id=1, source_target_pairs={{0,8},{8,0},{16,24},{24,16},{1,9},{9,1},{17,25},{25,17},{2,10},{10... | collective-permute-start | bytes 294920 | tf_op jit(solution)/shard_map/ppermute | solution.py:189

commit v16 on v15

--- a/solution.py
+++ b/solution.py
@@ -52,8 +52,9 @@
 
 
 def stream_kernel(
-    cols, comps, zloc, wall_counts, z_first, z_second, field, x_first, x_second, x_part, z_matrix, mask
+    cols, comps, zloc, wall_counts, z_first, z_second, field, x_first, x_second, x_part, z_matrix, mask, held
 ):
+    held[...] = field[...]
     depth = mask.shape[0]
     length = field.shape[1]
     count = wall_counts[lax.axis_index("row")]
@@ -189,14 +190,14 @@
         return lax.ppermute(value, "row", [(i, i ^ step) for i in range(rows)])
 
     gathered = [along(field, quad * i) for i in range(1, sources)]
-    far = [across(field, step) for step in range(2, rows, 2)]
-    x_part, z_matrix, mask = call(
+    x_part, z_matrix, mask, held = call(
         functools.partial(stream_kernel, cols, comps, zloc),
         [wall_counts, z_first, z_second, field, x_first.reshape(1, length), x_second.reshape(1, length)],
         [SMEM] * 3 + [VMEM] * 3,
-        [field.shape, (quad * group, 2 * sources * group), (depth, length)],
+        [field.shape, (quad * group, 2 * sources * group), (depth, length), field.shape],
         "stream",
     )
+    far = [across(held, step) for step in range(2, rows, 2)]
     parts = call(
         functools.partial(span_kernel, comps, sources),
         [z_matrix, field] + gathered,

time: 18 us -> 18 us (level)
  no operation moved by 1% of the time
where the time goes in v16:
time: 18 us; the launch traced here: 17.8 us
  starting transfers between devices  9.24 us (51%)
  Pallas kernels  3.41 us (19%)
  waiting for transfers between devices  2.84 us (16%)
  local copies, waits for them, and re-layouts  2.27 us (13%)
    ppermute x4, starting transfers between devices, along(): return lax.ppermute(value, 'col', [(i, i ^ step) for i in range(cols)])  7.59 us
    pallas_call x5, Pallas kernels, call(): pl.pallas_call(kernel, out_shape=results, in_specs=[pl.BlockSpec(memory_s...  3.41 us
    ppermute x4, waiting for transfers between devices, along(): return lax.ppermute(value, 'col', [(i, i ^ step) for i in range(cols)])  2.83 us
    unnamed x22, local copies, waits for them, and re-layouts  2.27 us
    ppermute x2, starting transfers between devices, across(): return lax.ppermute(value, 'row', [(i, i ^ step) for i in range(rows)])  1.65 us
  transfers between devices with their start and end apart: 6, of which 4 were waited for; matrix products, arithmetic and copies ran while one was open for 0% of the time, Pallas kernels for 15%

profile of v16, /device:TPU:0, one launch (start us, length us, event | category | flops | bytes accessed | tf_op | source)
XLA Modules:
  0.0 17.8 jit_solution(10062771072052600286)
XLA Ops:
  0.0 4.0 %collective-permute-start = (f32[192,128]{1,0:T(8,128)}, f32[192,128]{1,0:T(8,128)S(1)}, u32[]{:S(2)}, u32[]{:S(2)}) collective-permute-start(f32[192,128]{1,0:T(8,128)} %bitcast.6), channel_id=1, source_target_pairs={{0,4},{1,5},{2,6},{3,7},{4,0},{5,1},{6,2},{7,3},{8,12},{9,13},{10,... | collective-permute-start | bytes 294920 | tf_op jit(solution)/shard_map/ppermute | solution.py:187
  4.1 0.6 %copy-done.7 = f32[128]{0:T(128)S(1)} copy-done((f32[128]{0:T(128)S(1)}, f32[128]{0:T(128)}, u32[]{:S(2)}) %copy-start.7) | copy-done | bytes 536
  4.7 0.0 copy-done.8
  4.7 0.0 copy-done.4
  4.7 0.0 copy-done.5
  4.7 0.0 copy-done.6
  4.8 0.9 %copy-done = f32[3,16,4,128]{3,2,1,0:T(4,128)S(1)} copy-done((f32[3,16,4,128]{3,2,1,0:T(4,128)S(1)}, f32[3,16,4,128]{3,2,1,0:T(4,128)}, u32[]{:S(2)}) %copy-start) | copy-done | bytes 98328
  5.7 1.1 %stream.1 = (f32[192,128]{1,0:T(8,128)S(1)}, f32[128,128]{1,0:T(8,128)S(1)}, f32[64,128]{1,0:T(8,128)S(1)}, f32[192,128]{1,0:T(8,128)S(1)}) custom-call(s32[4]{0:T(128)S(1)} %copy-done.4, f32[32]{0:T(128)S(1)} %copy-done.5, f32[32]{0:T(128)S(1)} %copy-done.6, f32[192,128]{1,0:T(8,128)S(1)} %bitcast.7, f32[1,128]{1,0:T(1,128)S(1)} %bitcast.10, ...), custom_call_target="tpu_custom_call" | custom-call | tf_op jit(solution)/shard_map/stream/pallas_call | solution.py:155
  6.8 1.6 %collective-permute-start.1 = (f32[192,128]{1,0:T(8,128)S(1)}, f32[192,128]{1,0:T(8,128)S(1)}, u32[]{:S(2)}, u32[]{:S(2)}) collective-permute-start(f32[192,128]{1,0:T(8,128)S(1)} %get-tuple-element.19), channel_id=1, source_target_pairs={{0,16},{8,24},{16,0},{24,8},{1,17},{9,25},{17,1},{25,9},{2,18},{10... | collective-permute-start | bytes 294920 | tf_op jit(solution)/shard_map/ppermute | solution.py:190
  8.3 0.8 %collective-permute-done.refs_1_ = f32[192,128]{1,0:T(8,128)S(1)} collective-permute-done((f32[192,128]{1,0:T(8,128)}, f32[192,128]{1,0:T(8,128)S(1)}, u32[]{:S(2)}, u32[]{:S(2)}) %collective-permute-start) | collective-permute-done | bytes 98336 | tf_op jit(solution)/shard_map/ppermute | solution.py:187
  9.2 0.3 %span.1 = (f32[192,128]{1,0:T(8,128)S(1)}, f32[192,128]{1,0:T(8,128)S(1)}, f32[192,128]{1,0:T(8,128)S(1)}, f32[192,128]{1,0:T(8,128)S(1)}) custom-call(f32[128,128]{1,0:T(8,128)S(1)} %get-tuple-element.16.matrix, f32[192,128]{1,0:T(8,128)S(1)} %bitcast.8, f32[192,128]{1,0:T(8,128)S(1)} %collective-permute-done.refs_1_), custom_call_target="tpu_custom_call" | custom-call | tf_op jit(solution)/shard_map/span/pallas_call | solution.py:155
  9.5 1.8 %collective-permute-start.3 = (f32[192,128]{1,0:T(8,128)S(1)}, f32[192,128]{1,0:T(8,128)S(1)}, u32[]{:S(2)}, u32[]{:S(2)}) collective-permute-start(f32[192,128]{1,0:T(8,128)S(1)} %get-tuple-element.22), channel_id=1, source_target_pairs={{0,3},{1,2},{2,1},{3,0},{4,7},{5,6},{6,5},{7,4},{8,11},{9,10},{10,... | collective-permute-start | bytes 294920 | tf_op jit(solution)/shard_map/ppermute | solution.py:187
  11.3 1.3 %collective-permute-start.4 = (f32[192,128]{1,0:T(8,128)S(1)}, f32[192,128]{1,0:T(8,128)S(1)}, u32[]{:S(2)}, u32[]{:S(2)}) collective-permute-start(f32[192,128]{1,0:T(8,128)S(1)} %get-tuple-element.23), channel_id=1, source_target_pairs={{0,2},{1,3},{2,0},{3,1},{4,6},{5,7},{6,4},{7,5},{8,10},{9,11},{10,... | collective-permute-start | bytes 294920 | tf_op jit(solution)/shard_map/ppermute | solution.py:187
  12.5 0.5 %collective-permute-start.5 = (f32[192,128]{1,0:T(8,128)S(1)}, f32[192,128]{1,0:T(8,128)S(1)}, u32[]{:S(2)}, u32[]{:S(2)}) collective-permute-start(f32[192,128]{1,0:T(8,128)S(1)} %get-tuple-element.24), channel_id=1, source_target_pairs={{0,1},{1,0},{2,3},{3,2},{4,5},{5,4},{6,7},{7,6},{8,9},{9,8},{10,11... | collective-permute-start | bytes 294920 | tf_op jit(solution)/shard_map/ppermute | solution.py:187
  13.0 0.6 %copy-done.9 = f32[64]{0:T(128)S(1)} copy-done((f32[64]{0:T(128)S(1)}, f32[64]{0:T(128)}, u32[]{:S(2)}) %copy-start.9) | copy-done | bytes 280
  13.7 0.0 copy-done.10
  13.7 1.0 %wall_matrix.1.matrix = f32[128,256]{1,0:T(8,128)S(1)} custom-call(s32[4]{0:T(128)S(1)} %copy-done.4, f32[1,64]{1,0:T(1,128)S(1)} %bitcast.12, s32[1,32]{1,0:T(1,128)S(1)} %bitcast.13, f32[32,32]{1,0:T(8,128)S(1)} %copy-done.2, f32[32,32]{1,0:T(8,128)S(1)} %copy-done.3, f32[192,128]{1,0:T(8,128)S(1)} %get-tuple-element.17.after.z_part), custom_call_target="tpu_custom_call" | custom-call | tf_op jit(solution)/shard_map/wall_matrix/pallas_call | solution.py:155
  14.7 0.0 collective-permute-done.1.refs_1_
  14.7 0.3 %wall.1 = (f32[192,128]{1,0:T(8,128)S(1)}, f32[192,128]{1,0:T(8,128)S(1)}) custom-call(f32[128,256]{1,0:T(8,128)S(1)} %wall_matrix.1.matrix, f32[192,128]{1,0:T(8,128)S(1)} %get-tuple-element.18.x_part, f32[192,128]{1,0:T(8,128)S(1)} %get-tuple-element.17.after.z_part, f32[192,128]{1,0:T(8,128)S(1)} %bitcast.9, f32[192,128]{1,0:T(8,128)S(1)} %collective-permute-done.1.refs_1_), custom_call_target="tpu_custom_call" | custom-call | tf_op jit(solution)/shard_map/wall/pallas_call | solution.py:155
  15.1 0.1 collective-permute-start.2
  15.1 0.6 %collective-permute-done.3.refs_2_ = f32[192,128]{1,0:T(8,128)S(1)} collective-permute-done((f32[192,128]{1,0:T(8,128)S(1)}, f32[192,128]{1,0:T(8,128)S(1)}, u32[]{:S(2)}, u32[]{:S(2)}) %collective-permute-start.3) | collective-permute-done | bytes 98336 | tf_op jit(solution)/shard_map/ppermute | solution.py:187
  15.7 1.0 %collective-permute-done.4.refs_3_ = f32[192,128]{1,0:T(8,128)S(1)} collective-permute-done((f32[192,128]{1,0:T(8,128)S(1)}, f32[192,128]{1,0:T(8,128)S(1)}, u32[]{:S(2)}, u32[]{:S(2)}) %collective-permute-start.4) | collective-permute-done | bytes 98336 | tf_op jit(solution)/shard_map/ppermute | solution.py:187
  16.8 0.4 %collective-permute-done.5.refs_4_ = f32[192,128]{1,0:T(8,128)S(1)} collective-permute-done((f32[192,128]{1,0:T(8,128)S(1)}, f32[192,128]{1,0:T(8,128)S(1)}, u32[]{:S(2)}, u32[]{:S(2)}) %collective-permute-start.5) | collective-permute-done | bytes 98336 | tf_op jit(solution)/shard_map/ppermute | solution.py:187
  17.2 0.7 %finish.1 = f32[192,128]{1,0:T(8,128)} custom-call(f32[64,128]{1,0:T(8,128)S(1)} %get-tuple-element.15.mask, f32[192,128]{1,0:T(8,128)S(1)} %get-tuple-element.20.refs_0_, f32[192,128]{1,0:T(8,128)S(1)} %collective-permute-done.2.refs_1_, f32[192,128]{1,0:T(8,128)S(1)} %collective-permute-done.3.refs_2_, f32[192,128]{1,0:T(8,128)S(1)} %collective-permute-done.4.refs_3_, ...), custom_call_target="tpu_custom_call" | custom-call | tf_op jit(solution)/shard_map/finish/pallas_call | solution.py:155
  (15 shorter events, 0.0 us)
Async XLA Ops:
  0.0 9.1 %collective-permute-start = (f32[192,128]{1,0:T(8,128)}, f32[192,128]{1,0:T(8,128)S(1)}, u32[]{:S(2)}, u32[]{:S(2)}) collective-permute-start(f32[192,128]{1,0:T(8,128)} %bitcast.6), channel_id=1, source_target_pairs={{0,4},{1,5},{2,6},{3,7},{4,0},{5,1},{6,2},{7,3},{8,12},{9,13},{10,... | collective-permute-start | bytes 294920 | tf_op jit(solution)/shard_map/ppermute | solution.py:187
  4.0 0.7 %copy-start.7 = (f32[128]{0:T(128)S(1)}, f32[128]{0:T(128)}, u32[]{:S(2)}) copy-start(f32[128]{0:T(128)} %param.12) | copy-start | bytes 1540
  4.0 0.7 %copy-start.8 = (f32[128]{0:T(128)S(1)}, f32[128]{0:T(128)}, u32[]{:S(2)}) copy-start(f32[128]{0:T(128)} %param.13) | copy-start | bytes 1540
  4.0 0.7 %copy-start.4 = (s32[4]{0:T(128)S(1)}, s32[4]{0:T(128)}, u32[]{:S(2)}) copy-start(s32[4]{0:T(128)} %wall_counts.3) | copy-start | bytes 52
  4.0 0.7 %copy-start.5 = (f32[32]{0:T(128)S(1)}, f32[32]{0:T(128)}, u32[]{:S(2)}) copy-start(f32[32]{0:T(128)} %z_first.1) | copy-start | bytes 388
  4.0 0.7 %copy-start.6 = (f32[32]{0:T(128)S(1)}, f32[32]{0:T(128)}, u32[]{:S(2)}) copy-start(f32[32]{0:T(128)} %z_second.1) | copy-start | bytes 388
  4.8 0.9 %copy-start = (f32[3,16,4,128]{3,2,1,0:T(4,128)S(1)}, f32[3,16,4,128]{3,2,1,0:T(4,128)}, u32[]{:S(2)}) copy-start(f32[3,16,4,128]{3,2,1,0:T(4,128)} %param.10) | copy-start | bytes 294916
  5.6 3.5 %copy-start.1 = (f32[3,16,4,128]{3,2,1,0:T(4,128)S(1)}, f32[3,16,4,128]{3,2,1,0:T(4,128)}, u32[]{:S(2)}) copy-start(f32[3,16,4,128]{3,2,1,0:T(4,128)} %param.10) | copy-start | bytes 294916
  6.8 8.0 %collective-permute-start.1 = (f32[192,128]{1,0:T(8,128)S(1)}, f32[192,128]{1,0:T(8,128)S(1)}, u32[]{:S(2)}, u32[]{:S(2)}) collective-permute-start(f32[192,128]{1,0:T(8,128)S(1)} %get-tuple-element.19), channel_id=1, source_target_pairs={{0,16},{8,24},{16,0},{24,8},{1,17},{9,25},{17,1},{25,9},{2,18},{10... | collective-permute-start | bytes 294920 | tf_op jit(solution)/shard_map/ppermute | solution.py:190
  9.1 3.9 %copy-start.2 = (f32[32,32]{1,0:T(8,128)S(1)}, f32[32,32]{1,0:T(8,128)}, u32[]{:S(2)}) copy-start(f32[32,32]{1,0:T(8,128)} %y_first.1) | copy-start | bytes 12292
  9.2 3.9 %copy-start.3 = (f32[32,32]{1,0:T(8,128)S(1)}, f32[32,32]{1,0:T(8,128)}, u32[]{:S(2)}) copy-start(f32[32,32]{1,0:T(8,128)} %y_second.1) | copy-start | bytes 12292
  9.5 6.3 %collective-permute-start.3 = (f32[192,128]{1,0:T(8,128)S(1)}, f32[192,128]{1,0:T(8,128)S(1)}, u32[]{:S(2)}, u32[]{:S(2)}) collective-permute-start(f32[192,128]{1,0:T(8,128)S(1)} %get-tuple-element.22), channel_id=1, source_target_pairs={{0,3},{1,2},{2,1},{3,0},{4,7},{5,6},{6,5},{7,4},{8,11},{9,10},{10,... | collective-permute-start | bytes 294920 | tf_op jit(solution)/shard_map/ppermute | solution.py:187
  11.3 5.5 %collective-permute-start.4 = (f32[192,128]{1,0:T(8,128)S(1)}, f32[192,128]{1,0:T(8,128)S(1)}, u32[]{:S(2)}, u32[]{:S(2)}) collective-permute-start(f32[192,128]{1,0:T(8,128)S(1)} %get-tuple-element.23), channel_id=1, source_target_pairs={{0,2},{1,3},{2,0},{3,1},{4,6},{5,7},{6,4},{7,5},{8,10},{9,11},{10,... | collective-permute-start | bytes 294920 | tf_op jit(solution)/shard_map/ppermute | solution.py:187
  12.5 4.6 %collective-permute-start.5 = (f32[192,128]{1,0:T(8,128)S(1)}, f32[192,128]{1,0:T(8,128)S(1)}, u32[]{:S(2)}, u32[]{:S(2)}) collective-permute-start(f32[192,128]{1,0:T(8,128)S(1)} %get-tuple-element.24), channel_id=1, source_target_pairs={{0,1},{1,0},{2,3},{3,2},{4,5},{5,4},{6,7},{7,6},{8,9},{9,8},{10,11... | collective-permute-start | bytes 294920 | tf_op jit(solution)/shard_map/ppermute | solution.py:187
  13.0 0.7 %copy-start.9 = (f32[64]{0:T(128)S(1)}, f32[64]{0:T(128)}, u32[]{:S(2)}) copy-start(f32[64]{0:T(128)} %param.18) | copy-start | bytes 772
  13.0 0.7 %copy-start.10 = (s32[32]{0:T(128)S(1)}, s32[32]{0:T(128)}, u32[]{:S(2)}) copy-start(s32[32]{0:T(128)} %param.19) | copy-start | bytes 388
  15.1 2.1 %collective-permute-start.2 = (f32[192,128]{1,0:T(8,128)S(1)}, f32[192,128]{1,0:T(8,128)S(1)}, u32[]{:S(2)}, u32[]{:S(2)}) collective-permute-start(f32[192,128]{1,0:T(8,128)S(1)} %get-tuple-element.21), channel_id=1, source_target_pairs={{0,8},{8,0},{16,24},{24,16},{1,9},{9,1},{17,25},{25,17},{2,10},{10... | collective-permute-start | bytes 294920 | tf_op jit(solution)/shard_map/ppermute | solution.py:190

commit v17 on v16

--- a/solution.py
+++ b/solution.py
@@ -29,8 +29,8 @@
     return mul(lh, rh) + (mul(lh, rl) + mul(ll, rh))
 
 
-def span_kernel(comps, sources, matrix, *refs):
-    fields, parts = refs[-quad - sources : -quad], refs[-quad:]
+def span_kernel(comps, sources, pieces, matrix, *refs):
+    fields, parts = refs[:sources], refs[sources:]
     depth, length = fields[0].shape[0] // comps, fields[0].shape[1]
     group = matrix.shape[0] // quad
     right = []
@@ -40,11 +40,10 @@
             stack += [value * field[2 * depth + at : 2 * depth + at + group] for value, field in zip(stack, fields)]
             right.append(jnp.concatenate(stack, axis=0))
     result = dot_split(matrix[...], jnp.concatenate(right, axis=1))
-    for t in range(quad):
-        for i in range(len(right)):
-            parts[t][i * group : (i + 1) * group] = result[
-                t * group : (t + 1) * group, i * length : (i + 1) * length
-            ]
+    for part, (t, low, high) in zip(parts, pieces):
+        for at in range(low, high, group):
+            i = at // group
+            part[at - low : at - low + group] = result[t * group : (t + 1) * group, i * length : (i + 1) * length]
 
 
 def circulant_rows(row, length):
@@ -141,12 +140,16 @@
         away[at] = result[depth:]
 
 
-def finish_kernel(comps, mask, *refs):
+def finish_kernel(comps, pieces, mask, total, near, *refs):
     parts, out = refs[:-1], refs[-1]
     depth = mask.shape[0]
     for comp in range(comps):
         at = slice(comp * depth, (comp + 1) * depth)
-        out[at] = jnp.where(mask[...] > 0, sum(part[at] for part in parts[1:]) + parts[0][at], 0.0)
+        value = total[at] + near[at]
+        for part, (_, low, high) in zip(parts, pieces):
+            if low <= at.start and at.stop <= high:
+                value += part[at.start - low : at.stop - low]
+        out[at] = jnp.where(mask[...] > 0, value, 0.0)
 
 
 def call(kernel, operands, spaces, results, name, scratch=()):
@@ -182,6 +185,8 @@
     field = velocity.reshape(comps * depth, length)
     group = min(depth, 32)
     sources = cols // quad
+    rest = comps * depth
+    pieces = [(t, 0, rest) for t in (0, 3, 2)] + [(1, 0, rest - depth), (1, rest - depth, rest)]
 
     def along(value, step):
         return lax.ppermute(value, "col", [(i, i ^ step) for i in range(cols)])
@@ -199,13 +204,13 @@
     )
     far = [across(held, step) for step in range(2, rows, 2)]
     parts = call(
-        functools.partial(span_kernel, comps, sources),
+        functools.partial(span_kernel, comps, sources, pieces),
         [z_matrix, field] + gathered,
         [VMEM] * (1 + sources),
-        [field.shape] * quad,
+        [(high - low, length) for _, low, high in pieces],
         "span",
     )
-    returned = [along(parts[t], t) for t in reversed(range(1, quad))]
+    returned = [along(part, t) for part, (t, _, _) in zip(parts[1:], pieces[1:])]
     (y_matrix,) = call(
         functools.partial(wall_matrix_kernel, rows, zloc),
         [wall_counts, metric_table.reshape(1, -1), metric_index.reshape(1, -1), y_first, y_second, parts[0]],
@@ -222,9 +227,9 @@
     )
     near = across(away, 1)
     (result,) = call(
-        functools.partial(finish_kernel, comps),
+        functools.partial(finish_kernel, comps, pieces[1:]),
         [mask, total, near] + returned,
-        [VMEM] * (quad + 2),
+        [VMEM] * (3 + len(returned)),
         [field.shape],
         "finish",
     )

time: 18 us -> 20.7 us (1.15)
  starting transfers between devices: 9.24 us -> 10.8 us
  waiting for transfers between devices: 2.84 us -> 3.94 us
    ppermute x4 -> x5, starting transfers between devices: 7.59 us -> 9.19 us  [along(): return lax.ppermute(value, 'col', [(i, i ^ step) for i in range(cols)])]
    ppermute x4 -> x5, waiting for transfers between devices: 2.83 us -> 3.93 us  [along(): return lax.ppermute(value, 'col', [(i, i ^ step) for i in range(cols)])]
  transfers between devices with their start and end apart: 6 -> 7, of which waited for: 4 -> 2; matrix products, arithmetic and copies ran while one was open for 0% -> 0% of each run, Pallas kernels for 15% -> 13%
where the time goes in v17:
time: 20.7 us; the launch traced here: 20.5 us
  starting transfers between devices  10.8 us (52%)
  waiting for transfers between devices  3.94 us (19%)
  Pallas kernels  3.41 us (16%)
  local copies, waits for them, and re-layouts  2.27 us (11%)
    ppermute x5, starting transfers between devices, along(): return lax.ppermute(value, 'col', [(i, i ^ step) for i in range(cols)])  9.19 us
    ppermute x5, waiting for transfers between devices, along(): return lax.ppermute(value, 'col', [(i, i ^ step) for i in range(cols)])  3.93 us
    pallas_call x5, Pallas kernels, call(): pl.pallas_call(kernel, out_shape=results, in_specs=[pl.BlockSpec(memory_s...  3.41 us
    unnamed x22, local copies, waits for them, and re-layouts  2.27 us
    ppermute x2, starting transfers between devices, across(): return lax.ppermute(value, 'row', [(i, i ^ step) for i in range(rows)])  1.65 us
  transfers between devices with their start and end apart: 7, of which 2 were waited for; matrix products, arithmetic and copies ran while one was open for 0% of the time, Pallas kernels for 13%

profile of v17, /device:TPU:0, one launch (start us, length us, event | category | flops | bytes accessed | tf_op | source)
XLA Modules:
  0.0 20.5 jit_solution(11691249934748237437)
XLA Ops:
  0.0 4.0 %collective-permute-start = (f32[192,128]{1,0:T(8,128)}, f32[192,128]{1,0:T(8,128)S(1)}, u32[]{:S(2)}, u32[]{:S(2)}) collective-permute-start(f32[192,128]{1,0:T(8,128)} %bitcast.6), channel_id=1, source_target_pairs={{0,4},{1,5},{2,6},{3,7},{4,0},{5,1},{6,2},{7,3},{8,12},{9,13},{10,... | collective-permute-start | bytes 294920 | tf_op jit(solution)/shard_map/ppermute | solution.py:192
  4.1 0.6 %copy-done.7 = f32[128]{0:T(128)S(1)} copy-done((f32[128]{0:T(128)S(1)}, f32[128]{0:T(128)}, u32[]{:S(2)}) %copy-start.7) | copy-done | bytes 536
  4.7 0.0 copy-done.8
  4.7 0.0 copy-done.4
  4.7 0.0 copy-done.5
  4.7 0.0 copy-done.6
  4.8 0.9 %copy-done = f32[3,16,4,128]{3,2,1,0:T(4,128)S(1)} copy-done((f32[3,16,4,128]{3,2,1,0:T(4,128)S(1)}, f32[3,16,4,128]{3,2,1,0:T(4,128)}, u32[]{:S(2)}) %copy-start) | copy-done | bytes 98328
  5.7 1.1 %stream.1 = (f32[192,128]{1,0:T(8,128)S(1)}, f32[128,128]{1,0:T(8,128)S(1)}, f32[64,128]{1,0:T(8,128)S(1)}, f32[192,128]{1,0:T(8,128)S(1)}) custom-call(s32[4]{0:T(128)S(1)} %copy-done.4, f32[32]{0:T(128)S(1)} %copy-done.5, f32[32]{0:T(128)S(1)} %copy-done.6, f32[192,128]{1,0:T(8,128)S(1)} %bitcast.7, f32[1,128]{1,0:T(1,128)S(1)} %bitcast.10, ...), custom_call_target="tpu_custom_call" | custom-call | tf_op jit(solution)/shard_map/stream/pallas_call | solution.py:158
  6.8 1.6 %collective-permute-start.1 = (f32[192,128]{1,0:T(8,128)S(1)}, f32[192,128]{1,0:T(8,128)S(1)}, u32[]{:S(2)}, u32[]{:S(2)}) collective-permute-start(f32[192,128]{1,0:T(8,128)S(1)} %get-tuple-element.20), channel_id=1, source_target_pairs={{0,16},{8,24},{16,0},{24,8},{1,17},{9,25},{17,1},{25,9},{2,18},{10... | collective-permute-start | bytes 294920 | tf_op jit(solution)/shard_map/ppermute | solution.py:195
  8.3 0.8 %collective-permute-done.refs_1_ = f32[192,128]{1,0:T(8,128)S(1)} collective-permute-done((f32[192,128]{1,0:T(8,128)}, f32[192,128]{1,0:T(8,128)S(1)}, u32[]{:S(2)}, u32[]{:S(2)}) %collective-permute-start) | collective-permute-done | bytes 98336 | tf_op jit(solution)/shard_map/ppermute | solution.py:192
  9.2 0.3 %span.1 = (f32[192,128]{1,0:T(8,128)S(1)}, f32[192,128]{1,0:T(8,128)S(1)}, f32[192,128]{1,0:T(8,128)S(1)}, f32[128,128]{1,0:T(8,128)S(1)}, f32[64,128]{1,0:T(8,128)S(1)}) custom-call(f32[128,128]{1,0:T(8,128)S(1)} %get-tuple-element.17.matrix, f32[192,128]{1,0:T(8,128)S(1)} %bitcast.8, f32[192,128]{1,0:T(8,128)S(1)} %collective-permute-done.refs_1_), custom_call_target="tpu_custom_call" | custom-call | tf_op jit(solution)/shard_map/span/pallas_call | solution.py:158
  9.5 1.8 %collective-permute-start.3 = (f32[192,128]{1,0:T(8,128)S(1)}, f32[192,128]{1,0:T(8,128)S(1)}, u32[]{:S(2)}, u32[]{:S(2)}) collective-permute-start(f32[192,128]{1,0:T(8,128)S(1)} %get-tuple-element.23), channel_id=1, source_target_pairs={{0,3},{1,2},{2,1},{3,0},{4,7},{5,6},{6,5},{7,4},{8,11},{9,10},{10,... | collective-permute-start | bytes 294920 | tf_op jit(solution)/shard_map/ppermute | solution.py:192
  11.3 1.3 %collective-permute-start.4 = (f32[192,128]{1,0:T(8,128)S(1)}, f32[192,128]{1,0:T(8,128)S(1)}, u32[]{:S(2)}, u32[]{:S(2)}) collective-permute-start(f32[192,128]{1,0:T(8,128)S(1)} %get-tuple-element.24), channel_id=1, source_target_pairs={{0,2},{1,3},{2,0},{3,1},{4,6},{5,7},{6,4},{7,5},{8,10},{9,11},{10,... | collective-permute-start | bytes 294920 | tf_op jit(solution)/shard_map/ppermute | solution.py:192
  12.6 0.6 %copy-done.9 = f32[64]{0:T(128)S(1)} copy-done((f32[64]{0:T(128)S(1)}, f32[64]{0:T(128)}, u32[]{:S(2)}) %copy-start.9) | copy-done | bytes 280
  13.2 0.0 copy-done.10
  13.2 1.0 %wall_matrix.1.matrix = f32[128,256]{1,0:T(8,128)S(1)} custom-call(s32[4]{0:T(128)S(1)} %copy-done.4, f32[1,64]{1,0:T(1,128)S(1)} %bitcast.12, s32[1,32]{1,0:T(1,128)S(1)} %bitcast.13, f32[32,32]{1,0:T(8,128)S(1)} %copy-done.2, f32[32,32]{1,0:T(8,128)S(1)} %copy-done.3, f32[192,128]{1,0:T(8,128)S(1)} %get-tuple-element.18.after.z_part), custom_call_target="tpu_custom_call" | custom-call | tf_op jit(solution)/shard_map/wall_matrix/pallas_call | solution.py:158
  14.2 0.3 %wall.1 = (f32[192,128]{1,0:T(8,128)S(1)}, f32[192,128]{1,0:T(8,128)S(1)}) custom-call(f32[128,256]{1,0:T(8,128)S(1)} %wall_matrix.1.matrix, f32[192,128]{1,0:T(8,128)S(1)} %get-tuple-element.19.x_part, f32[192,128]{1,0:T(8,128)S(1)} %get-tuple-element.18.after.z_part, f32[192,128]{1,0:T(8,128)S(1)} %bitcast.9, f32[192,128]{1,0:T(8,128)S(1)} %collective-permute-done.1.refs_1_), custom_call_target="tpu_custom_call" | custom-call | tf_op jit(solution)/shard_map/wall/pallas_call | solution.py:158
  14.6 0.1 collective-permute-start.2
  14.6 0.6 %collective-permute-start.5 = (f32[128,128]{1,0:T(8,128)S(1)}, f32[128,128]{1,0:T(8,128)S(1)}, u32[]{:S(2)}, u32[]{:S(2)}) collective-permute-start(f32[128,128]{1,0:T(8,128)S(1)} %get-tuple-element.25), channel_id=1, source_target_pairs={{0,1},{1,0},{2,3},{3,2},{4,5},{5,4},{6,7},{7,6},{8,9},{9,8},{10,11... | collective-permute-start | bytes 196616 | tf_op jit(solution)/shard_map/ppermute | solution.py:192
  15.2 1.5 %collective-permute-start.6 = (f32[64,128]{1,0:T(8,128)S(1)}, f32[64,128]{1,0:T(8,128)S(1)}, u32[]{:S(2)}, u32[]{:S(2)}) collective-permute-start(f32[64,128]{1,0:T(8,128)S(1)} %get-tuple-element.26), channel_id=1, source_target_pairs={{0,1},{1,0},{2,3},{3,2},{4,5},{5,4},{6,7},{7,6},{8,9},{9,8},{10,11... | collective-permute-start | bytes 98312 | tf_op jit(solution)/shard_map/ppermute | solution.py:192
  16.7 3.1 %collective-permute-done.6.refs_3_ = f32[64,128]{1,0:T(8,128)S(1)} collective-permute-done((f32[64,128]{1,0:T(8,128)S(1)}, f32[64,128]{1,0:T(8,128)S(1)}, u32[]{:S(2)}, u32[]{:S(2)}) %collective-permute-start.6) | collective-permute-done | bytes 32800 | tf_op jit(solution)/shard_map/ppermute | solution.py:192
  19.9 0.0 collective-permute-done.4.refs_1_
  19.9 0.0 collective-permute-done.2.near
  19.9 0.7 %finish.1 = f32[192,128]{1,0:T(8,128)} custom-call(f32[64,128]{1,0:T(8,128)S(1)} %get-tuple-element.16.mask, f32[192,128]{1,0:T(8,128)S(1)} %get-tuple-element.21.total, f32[192,128]{1,0:T(8,128)S(1)} %collective-permute-done.2.near, f32[192,128]{1,0:T(8,128)S(1)} %collective-permute-done.3.refs_0_, f32[192,128]{1,0:T(8,128)S(1)} %collective-permute-done.4.refs_1_, ...), custom_call_target="tpu_custom_call" | custom-call | tf_op jit(solution)/shard_map/finish/pallas_call | solution.py:158
  (17 shorter events, 0.0 us)
Async XLA Ops:
  0.0 9.1 %collective-permute-start = (f32[192,128]{1,0:T(8,128)}, f32[192,128]{1,0:T(8,128)S(1)}, u32[]{:S(2)}, u32[]{:S(2)}) collective-permute-start(f32[192,128]{1,0:T(8,128)} %bitcast.6), channel_id=1, source_target_pairs={{0,4},{1,5},{2,6},{3,7},{4,0},{5,1},{6,2},{7,3},{8,12},{9,13},{10,... | collective-permute-start | bytes 294920 | tf_op jit(solution)/shard_map/ppermute | solution.py:192
  4.0 0.7 %copy-start.7 = (f32[128]{0:T(128)S(1)}, f32[128]{0:T(128)}, u32[]{:S(2)}) copy-start(f32[128]{0:T(128)} %param.12) | copy-start | bytes 1540
  4.0 0.7 %copy-start.8 = (f32[128]{0:T(128)S(1)}, f32[128]{0:T(128)}, u32[]{:S(2)}) copy-start(f32[128]{0:T(128)} %param.13) | copy-start | bytes 1540
  4.0 0.7 %copy-start.4 = (s32[4]{0:T(128)S(1)}, s32[4]{0:T(128)}, u32[]{:S(2)}) copy-start(s32[4]{0:T(128)} %wall_counts.3) | copy-start | bytes 52
  4.0 0.7 %copy-start.5 = (f32[32]{0:T(128)S(1)}, f32[32]{0:T(128)}, u32[]{:S(2)}) copy-start(f32[32]{0:T(128)} %z_first.1) | copy-start | bytes 388
  4.0 0.7 %copy-start.6 = (f32[32]{0:T(128)S(1)}, f32[32]{0:T(128)}, u32[]{:S(2)}) copy-start(f32[32]{0:T(128)} %z_second.1) | copy-start | bytes 388
  4.8 0.9 %copy-start = (f32[3,16,4,128]{3,2,1,0:T(4,128)S(1)}, f32[3,16,4,128]{3,2,1,0:T(4,128)}, u32[]{:S(2)}) copy-start(f32[3,16,4,128]{3,2,1,0:T(4,128)} %param.10) | copy-start | bytes 294916
  5.6 3.5 %copy-start.1 = (f32[3,16,4,128]{3,2,1,0:T(4,128)S(1)}, f32[3,16,4,128]{3,2,1,0:T(4,128)}, u32[]{:S(2)}) copy-start(f32[3,16,4,128]{3,2,1,0:T(4,128)} %param.10) | copy-start | bytes 294916
  6.8 7.5 %collective-permute-start.1 = (f32[192,128]{1,0:T(8,128)S(1)}, f32[192,128]{1,0:T(8,128)S(1)}, u32[]{:S(2)}, u32[]{:S(2)}) collective-permute-start(f32[192,128]{1,0:T(8,128)S(1)} %get-tuple-element.20), channel_id=1, source_target_pairs={{0,16},{8,24},{16,0},{24,8},{1,17},{9,25},{17,1},{25,9},{2,18},{10... | collective-permute-start | bytes 294920 | tf_op jit(solution)/shard_map/ppermute | solution.py:195
  9.1 3.4 %copy-start.2 = (f32[32,32]{1,0:T(8,128)S(1)}, f32[32,32]{1,0:T(8,128)}, u32[]{:S(2)}) copy-start(f32[32,32]{1,0:T(8,128)} %y_first.1) | copy-start | bytes 12292
  9.2 3.4 %copy-start.3 = (f32[32,32]{1,0:T(8,128)S(1)}, f32[32,32]{1,0:T(8,128)}, u32[]{:S(2)}) copy-start(f32[32,32]{1,0:T(8,128)} %y_second.1) | copy-start | bytes 12292
  9.5 10.4 %collective-permute-start.3 = (f32[192,128]{1,0:T(8,128)S(1)}, f32[192,128]{1,0:T(8,128)S(1)}, u32[]{:S(2)}, u32[]{:S(2)}) collective-permute-start(f32[192,128]{1,0:T(8,128)S(1)} %get-tuple-element.23), channel_id=1, source_target_pairs={{0,3},{1,2},{2,1},{3,0},{4,7},{5,6},{6,5},{7,4},{8,11},{9,10},{10,... | collective-permute-start | bytes 294920 | tf_op jit(solution)/shard_map/ppermute | solution.py:192
  11.3 8.6 %collective-permute-start.4 = (f32[192,128]{1,0:T(8,128)S(1)}, f32[192,128]{1,0:T(8,128)S(1)}, u32[]{:S(2)}, u32[]{:S(2)}) collective-permute-start(f32[192,128]{1,0:T(8,128)S(1)} %get-tuple-element.24), channel_id=1, source_target_pairs={{0,2},{1,3},{2,0},{3,1},{4,6},{5,7},{6,4},{7,5},{8,10},{9,11},{10,... | collective-permute-start | bytes 294920 | tf_op jit(solution)/shard_map/ppermute | solution.py:192
  12.5 0.7 %copy-start.9 = (f32[64]{0:T(128)S(1)}, f32[64]{0:T(128)}, u32[]{:S(2)}) copy-start(f32[64]{0:T(128)} %param.18) | copy-start | bytes 772
  12.5 0.7 %copy-start.10 = (s32[32]{0:T(128)S(1)}, s32[32]{0:T(128)}, u32[]{:S(2)}) copy-start(s32[32]{0:T(128)} %param.19) | copy-start | bytes 388
  14.6 5.3 %collective-permute-start.2 = (f32[192,128]{1,0:T(8,128)S(1)}, f32[192,128]{1,0:T(8,128)S(1)}, u32[]{:S(2)}, u32[]{:S(2)}) collective-permute-start(f32[192,128]{1,0:T(8,128)S(1)} %get-tuple-element.22), channel_id=1, source_target_pairs={{0,8},{8,0},{16,24},{24,16},{1,9},{9,1},{17,25},{25,17},{2,10},{10... | collective-permute-start | bytes 294920 | tf_op jit(solution)/shard_map/ppermute | solution.py:195
  14.6 5.2 %collective-permute-start.5 = (f32[128,128]{1,0:T(8,128)S(1)}, f32[128,128]{1,0:T(8,128)S(1)}, u32[]{:S(2)}, u32[]{:S(2)}) collective-permute-start(f32[128,128]{1,0:T(8,128)S(1)} %get-tuple-element.25), channel_id=1, source_target_pairs={{0,1},{1,0},{2,3},{3,2},{4,5},{5,4},{6,7},{7,6},{8,9},{9,8},{10,11... | collective-permute-start | bytes 196616 | tf_op jit(solution)/shard_map/ppermute | solution.py:192
  15.2 4.7 %collective-permute-start.6 = (f32[64,128]{1,0:T(8,128)S(1)}, f32[64,128]{1,0:T(8,128)S(1)}, u32[]{:S(2)}, u32[]{:S(2)}) collective-permute-start(f32[64,128]{1,0:T(8,128)S(1)} %get-tuple-element.26), channel_id=1, source_target_pairs={{0,1},{1,0},{2,3},{3,2},{4,5},{5,4},{6,7},{7,6},{8,9},{9,8},{10,11... | collective-permute-start | bytes 98312 | tf_op jit(solution)/shard_map/ppermute | solution.py:192

commit v18 on v17

--- a/solution.py
+++ b/solution.py
@@ -140,19 +140,23 @@
         away[at] = result[depth:]
 
 
-def finish_kernel(comps, pieces, mask, total, near, *refs):
+def sum_kernel(comps, pieces, mask, total, *refs):
     parts, out = refs[:-1], refs[-1]
     depth = mask.shape[0]
     for comp in range(comps):
         at = slice(comp * depth, (comp + 1) * depth)
-        value = total[at] + near[at]
+        value = total[at]
         for part, (_, low, high) in zip(parts, pieces):
             if low <= at.start and at.stop <= high:
                 value += part[at.start - low : at.stop - low]
         out[at] = jnp.where(mask[...] > 0, value, 0.0)
 
 
-def call(kernel, operands, spaces, results, name, scratch=()):
+def finish_kernel(total, near, out):
+    out[...] = total[...] + near[...]
+
+
+def call(kernel, operands, spaces, results, name, scratch=(), cost=None):
     results = [jax.ShapeDtypeStruct(shape, jnp.float32) for shape in results]
     held = sum(4 * math.prod(array.shape) for array in list(operands) + results)
     return pl.pallas_call(
@@ -162,6 +166,7 @@
         out_specs=[pl.BlockSpec(memory_space=VMEM)] * len(results),
         scratch_shapes=[pltpu.VMEM(shape, jnp.float32) for shape in scratch],
         compiler_params=pltpu.CompilerParams(vmem_limit_bytes=(4 << 20) + 3 * held),
+        cost_estimate=cost,
         name=name,
     )(*operands)
 
@@ -226,13 +231,15 @@
         "wall",
     )
     near = across(away, 1)
-    (result,) = call(
-        functools.partial(finish_kernel, comps, pieces[1:]),
-        [mask, total, near] + returned,
-        [VMEM] * (3 + len(returned)),
+    (summed,) = call(
+        functools.partial(sum_kernel, comps, pieces[1:]),
+        [mask, total] + returned,
+        [VMEM] * (2 + len(returned)),
         [field.shape],
-        "finish",
-    )
+        "sum",
+        cost=pl.CostEstimate(flops=1 << 30, bytes_accessed=1 << 22, transcendentals=0),
+    )
+    (result,) = call(finish_kernel, [summed, near], [VMEM] * 2, [field.shape], "finish")
     return result.reshape(velocity.shape)
 
 

time: 20.7 us -> 18.8 us (0.908)
  waiting for transfers between devices: 3.94 us -> 2.06 us
    ppermute x5, waiting for transfers between devices: 3.93 us -> 1.31 us  [along(): return lax.ppermute(value, 'col', [(i, i ^ step) for i in range(cols)])]
    ppermute x2, waiting for transfers between devices: 0.01 us -> 0.75 us  [across(): return lax.ppermute(value, 'row', [(i, i ^ step) for i in range(rows)])]
    pallas_call x5 -> x6, Pallas kernels: 3.41 us -> 3.42 us  [call(): pl.pallas_call(kernel, out_shape=results, in_specs=[pl.BlockSpec(memory_s...]
  transfers between devices with their start and end apart: 7 -> 7, of which waited for: 2 -> 3; matrix products, arithmetic and copies ran while one was open for 0% -> 0% of each run, Pallas kernels for 13% -> 15%
where the time goes in v18:
time: 18.8 us; the launch traced here: 18.6 us
  starting transfers between devices  10.8 us (57%)
  Pallas kernels  3.42 us (18%)
  local copies, waits for them, and re-layouts  2.27 us (12%)
  waiting for transfers between devices  2.06 us (11%)
    ppermute x5, starting transfers between devices, along(): return lax.ppermute(value, 'col', [(i, i ^ step) for i in range(cols)])  9.12 us
    pallas_call x6, Pallas kernels, call(): pl.pallas_call(kernel, out_shape=results, in_specs=[pl.BlockSpec(memory_s...  3.42 us
    unnamed x22, local copies, waits for them, and re-layouts  2.27 us
    ppermute x2, starting transfers between devices, across(): return lax.ppermute(value, 'row', [(i, i ^ step) for i in range(rows)])  1.65 us
    ppermute x5, waiting for transfers between devices, along(): return lax.ppermute(value, 'col', [(i, i ^ step) for i in range(cols)])  1.31 us
    ppermute x2, waiting for transfers between devices, across(): return lax.ppermute(value, 'row', [(i, i ^ step) for i in range(rows)])  0.75 us
  transfers between devices with their start and end apart: 7, of which 3 were waited for; matrix products, arithmetic and copies ran while one was open for 0% of the time, Pallas kernels for 15%

profile of v18, /device:TPU:0, one launch (start us, length us, event | category | flops | bytes accessed | tf_op | source)
XLA Modules:
  0.0 18.6 jit_solution(4108112182996913153)
XLA Ops:
  0.0 4.0 %collective-permute-start = (f32[192,128]{1,0:T(8,128)}, f32[192,128]{1,0:T(8,128)S(1)}, u32[]{:S(2)}, u32[]{:S(2)}) collective-permute-start(f32[192,128]{1,0:T(8,128)} %bitcast.6), channel_id=1, source_target_pairs={{0,4},{1,5},{2,6},{3,7},{4,0},{5,1},{6,2},{7,3},{8,12},{9,13},{10,... | collective-permute-start | bytes 294920 | tf_op jit(solution)/shard_map/ppermute | solution.py:197
  4.1 0.6 %copy-done.7 = f32[128]{0:T(128)S(1)} copy-done((f32[128]{0:T(128)S(1)}, f32[128]{0:T(128)}, u32[]{:S(2)}) %copy-start.7) | copy-done | bytes 536
  4.7 0.0 copy-done.8
  4.7 0.0 copy-done.4
  4.7 0.0 copy-done.5
  4.7 0.0 copy-done.6
  4.8 0.9 %copy-done = f32[3,16,4,128]{3,2,1,0:T(4,128)S(1)} copy-done((f32[3,16,4,128]{3,2,1,0:T(4,128)S(1)}, f32[3,16,4,128]{3,2,1,0:T(4,128)}, u32[]{:S(2)}) %copy-start) | copy-done | bytes 98328
  5.7 1.1 %stream.1 = (f32[192,128]{1,0:T(8,128)S(1)}, f32[128,128]{1,0:T(8,128)S(1)}, f32[64,128]{1,0:T(8,128)S(1)}, f32[192,128]{1,0:T(8,128)S(1)}) custom-call(s32[4]{0:T(128)S(1)} %copy-done.4, f32[32]{0:T(128)S(1)} %copy-done.5, f32[32]{0:T(128)S(1)} %copy-done.6, f32[192,128]{1,0:T(8,128)S(1)} %bitcast.7, f32[1,128]{1,0:T(1,128)S(1)} %bitcast.10, ...), custom_call_target="tpu_custom_call" | custom-call | tf_op jit(solution)/shard_map/stream/pallas_call | solution.py:162
  6.8 1.6 %collective-permute-start.1 = (f32[192,128]{1,0:T(8,128)S(1)}, f32[192,128]{1,0:T(8,128)S(1)}, u32[]{:S(2)}, u32[]{:S(2)}) collective-permute-start(f32[192,128]{1,0:T(8,128)S(1)} %get-tuple-element.20), channel_id=1, source_target_pairs={{0,16},{8,24},{16,0},{24,8},{1,17},{9,25},{17,1},{25,9},{2,18},{10... | collective-permute-start | bytes 294920 | tf_op jit(solution)/shard_map/ppermute | solution.py:200
  8.3 0.8 %collective-permute-done.refs_1_ = f32[192,128]{1,0:T(8,128)S(1)} collective-permute-done((f32[192,128]{1,0:T(8,128)}, f32[192,128]{1,0:T(8,128)S(1)}, u32[]{:S(2)}, u32[]{:S(2)}) %collective-permute-start) | collective-permute-done | bytes 98336 | tf_op jit(solution)/shard_map/ppermute | solution.py:197
  9.2 0.3 %span.1 = (f32[192,128]{1,0:T(8,128)S(1)}, f32[192,128]{1,0:T(8,128)S(1)}, f32[192,128]{1,0:T(8,128)S(1)}, f32[128,128]{1,0:T(8,128)S(1)}, f32[64,128]{1,0:T(8,128)S(1)}) custom-call(f32[128,128]{1,0:T(8,128)S(1)} %get-tuple-element.17.matrix, f32[192,128]{1,0:T(8,128)S(1)} %bitcast.8, f32[192,128]{1,0:T(8,128)S(1)} %collective-permute-done.refs_1_), custom_call_target="tpu_custom_call" | custom-call | tf_op jit(solution)/shard_map/span/pallas_call | solution.py:162
  9.5 1.8 %collective-permute-start.2 = (f32[192,128]{1,0:T(8,128)S(1)}, f32[192,128]{1,0:T(8,128)S(1)}, u32[]{:S(2)}, u32[]{:S(2)}) collective-permute-start(f32[192,128]{1,0:T(8,128)S(1)} %get-tuple-element.22), channel_id=1, source_target_pairs={{0,3},{1,2},{2,1},{3,0},{4,7},{5,6},{6,5},{7,4},{8,11},{9,10},{10,... | collective-permute-start | bytes 294920 | tf_op jit(solution)/shard_map/ppermute | solution.py:197
  11.3 1.3 %collective-permute-start.3 = (f32[192,128]{1,0:T(8,128)S(1)}, f32[192,128]{1,0:T(8,128)S(1)}, u32[]{:S(2)}, u32[]{:S(2)}) collective-permute-start(f32[192,128]{1,0:T(8,128)S(1)} %get-tuple-element.23), channel_id=1, source_target_pairs={{0,2},{1,3},{2,0},{3,1},{4,6},{5,7},{6,4},{7,5},{8,10},{9,11},{10,... | collective-permute-start | bytes 294920 | tf_op jit(solution)/shard_map/ppermute | solution.py:197
  12.5 0.5 %collective-permute-start.4 = (f32[128,128]{1,0:T(8,128)S(1)}, f32[128,128]{1,0:T(8,128)S(1)}, u32[]{:S(2)}, u32[]{:S(2)}) collective-permute-start(f32[128,128]{1,0:T(8,128)S(1)} %get-tuple-element.24), channel_id=1, source_target_pairs={{0,1},{1,0},{2,3},{3,2},{4,5},{5,4},{6,7},{7,6},{8,9},{9,8},{10,11... | collective-permute-start | bytes 196616 | tf_op jit(solution)/shard_map/ppermute | solution.py:197
  13.0 1.5 %collective-permute-start.5 = (f32[64,128]{1,0:T(8,128)S(1)}, f32[64,128]{1,0:T(8,128)S(1)}, u32[]{:S(2)}, u32[]{:S(2)}) collective-permute-start(f32[64,128]{1,0:T(8,128)S(1)} %get-tuple-element.25), channel_id=1, source_target_pairs={{0,1},{1,0},{2,3},{3,2},{4,5},{5,4},{6,7},{7,6},{8,9},{9,8},{10,11... | collective-permute-start | bytes 98312 | tf_op jit(solution)/shard_map/ppermute | solution.py:197
  14.6 0.6 %copy-done.9 = f32[64]{0:T(128)S(1)} copy-done((f32[64]{0:T(128)S(1)}, f32[64]{0:T(128)}, u32[]{:S(2)}) %copy-start.9) | copy-done | bytes 280
  15.2 0.0 copy-done.10
  15.2 1.0 %wall_matrix.1.matrix = f32[128,256]{1,0:T(8,128)S(1)} custom-call(s32[4]{0:T(128)S(1)} %copy-done.4, f32[1,64]{1,0:T(1,128)S(1)} %bitcast.12, s32[1,32]{1,0:T(1,128)S(1)} %bitcast.13, f32[32,32]{1,0:T(8,128)S(1)} %copy-done.2, f32[32,32]{1,0:T(8,128)S(1)} %copy-done.3, f32[192,128]{1,0:T(8,128)S(1)} %get-tuple-element.18.after.z_part), custom_call_target="tpu_custom_call" | custom-call | tf_op jit(solution)/shard_map/wall_matrix/pallas_call | solution.py:162
  16.3 0.0 collective-permute-done.1.refs_1_
  16.3 0.3 %wall.1 = (f32[192,128]{1,0:T(8,128)S(1)}, f32[192,128]{1,0:T(8,128)S(1)}) custom-call(f32[128,256]{1,0:T(8,128)S(1)} %wall_matrix.1.matrix, f32[192,128]{1,0:T(8,128)S(1)} %get-tuple-element.19.x_part, f32[192,128]{1,0:T(8,128)S(1)} %get-tuple-element.18.after.z_part, f32[192,128]{1,0:T(8,128)S(1)} %bitcast.9, f32[192,128]{1,0:T(8,128)S(1)} %collective-permute-done.1.refs_1_), custom_call_target="tpu_custom_call" | custom-call | tf_op jit(solution)/shard_map/wall/pallas_call | solution.py:162
  16.6 0.1 collective-permute-start.6
  16.7 0.5 %collective-permute-done.5.refs_3_ = f32[64,128]{1,0:T(8,128)S(1)} collective-permute-done((f32[64,128]{1,0:T(8,128)S(1)}, f32[64,128]{1,0:T(8,128)S(1)}, u32[]{:S(2)}, u32[]{:S(2)}) %collective-permute-start.5) | collective-permute-done | bytes 32800 | tf_op jit(solution)/shard_map/ppermute | solution.py:197
  17.2 0.7 %collective-permute-done.6.near = f32[192,128]{1,0:T(8,128)S(1)} collective-permute-done((f32[192,128]{1,0:T(8,128)S(1)}, f32[192,128]{1,0:T(8,128)S(1)}, u32[]{:S(2)}, u32[]{:S(2)}) %collective-permute-start.6) | collective-permute-done | bytes 98336 | tf_op jit(solution)/shard_map/ppermute | solution.py:200
  18.0 0.7 %finish.1 = f32[192,128]{1,0:T(8,128)} custom-call(f32[192,128]{1,0:T(8,128)S(1)} %sum.1.total, f32[192,128]{1,0:T(8,128)S(1)} %collective-permute-done.6.near), custom_call_target="tpu_custom_call" | custom-call | tf_op jit(solution)/shard_map/finish/pallas_call | solution.py:162
  (18 shorter events, 0.1 us)
Async XLA Ops:
  0.0 9.1 %collective-permute-start = (f32[192,128]{1,0:T(8,128)}, f32[192,128]{1,0:T(8,128)S(1)}, u32[]{:S(2)}, u32[]{:S(2)}) collective-permute-start(f32[192,128]{1,0:T(8,128)} %bitcast.6), channel_id=1, source_target_pairs={{0,4},{1,5},{2,6},{3,7},{4,0},{5,1},{6,2},{7,3},{8,12},{9,13},{10,... | collective-permute-start | bytes 294920 | tf_op jit(solution)/shard_map/ppermute | solution.py:197
  4.0 0.7 %copy-start.7 = (f32[128]{0:T(128)S(1)}, f32[128]{0:T(128)}, u32[]{:S(2)}) copy-start(f32[128]{0:T(128)} %param.12) | copy-start | bytes 1540
  4.0 0.7 %copy-start.8 = (f32[128]{0:T(128)S(1)}, f32[128]{0:T(128)}, u32[]{:S(2)}) copy-start(f32[128]{0:T(128)} %param.13) | copy-start | bytes 1540
  4.0 0.7 %copy-start.4 = (s32[4]{0:T(128)S(1)}, s32[4]{0:T(128)}, u32[]{:S(2)}) copy-start(s32[4]{0:T(128)} %wall_counts.3) | copy-start | bytes 52
  4.0 0.7 %copy-start.5 = (f32[32]{0:T(128)S(1)}, f32[32]{0:T(128)}, u32[]{:S(2)}) copy-start(f32[32]{0:T(128)} %z_first.1) | copy-start | bytes 388
  4.0 0.7 %copy-start.6 = (f32[32]{0:T(128)S(1)}, f32[32]{0:T(128)}, u32[]{:S(2)}) copy-start(f32[32]{0:T(128)} %z_second.1) | copy-start | bytes 388
  4.8 0.9 %copy-start = (f32[3,16,4,128]{3,2,1,0:T(4,128)S(1)}, f32[3,16,4,128]{3,2,1,0:T(4,128)}, u32[]{:S(2)}) copy-start(f32[3,16,4,128]{3,2,1,0:T(4,128)} %param.10) | copy-start | bytes 294916
  5.6 3.5 %copy-start.1 = (f32[3,16,4,128]{3,2,1,0:T(4,128)S(1)}, f32[3,16,4,128]{3,2,1,0:T(4,128)}, u32[]{:S(2)}) copy-start(f32[3,16,4,128]{3,2,1,0:T(4,128)} %param.10) | copy-start | bytes 294916
  6.8 9.5 %collective-permute-start.1 = (f32[192,128]{1,0:T(8,128)S(1)}, f32[192,128]{1,0:T(8,128)S(1)}, u32[]{:S(2)}, u32[]{:S(2)}) collective-permute-start(f32[192,128]{1,0:T(8,128)S(1)} %get-tuple-element.20), channel_id=1, source_target_pairs={{0,16},{8,24},{16,0},{24,8},{1,17},{9,25},{17,1},{25,9},{2,18},{10... | collective-permute-start | bytes 294920 | tf_op jit(solution)/shard_map/ppermute | solution.py:200
  9.1 5.4 %copy-start.2 = (f32[32,32]{1,0:T(8,128)S(1)}, f32[32,32]{1,0:T(8,128)}, u32[]{:S(2)}) copy-start(f32[32,32]{1,0:T(8,128)} %y_first.1) | copy-start | bytes 12292
  9.2 5.4 %copy-start.3 = (f32[32,32]{1,0:T(8,128)S(1)}, f32[32,32]{1,0:T(8,128)}, u32[]{:S(2)}) copy-start(f32[32,32]{1,0:T(8,128)} %y_second.1) | copy-start | bytes 12292
  9.5 7.7 %collective-permute-start.2 = (f32[192,128]{1,0:T(8,128)S(1)}, f32[192,128]{1,0:T(8,128)S(1)}, u32[]{:S(2)}, u32[]{:S(2)}) collective-permute-start(f32[192,128]{1,0:T(8,128)S(1)} %get-tuple-element.22), channel_id=1, source_target_pairs={{0,3},{1,2},{2,1},{3,0},{4,7},{5,6},{6,5},{7,4},{8,11},{9,10},{10,... | collective-permute-start | bytes 294920 | tf_op jit(solution)/shard_map/ppermute | solution.py:197
  11.3 5.9 %collective-permute-start.3 = (f32[192,128]{1,0:T(8,128)S(1)}, f32[192,128]{1,0:T(8,128)S(1)}, u32[]{:S(2)}, u32[]{:S(2)}) collective-permute-start(f32[192,128]{1,0:T(8,128)S(1)} %get-tuple-element.23), channel_id=1, source_target_pairs={{0,2},{1,3},{2,0},{3,1},{4,6},{5,7},{6,4},{7,5},{8,10},{9,11},{10,... | collective-permute-start | bytes 294920 | tf_op jit(solution)/shard_map/ppermute | solution.py:197
  12.5 4.6 %collective-permute-start.4 = (f32[128,128]{1,0:T(8,128)S(1)}, f32[128,128]{1,0:T(8,128)S(1)}, u32[]{:S(2)}, u32[]{:S(2)}) collective-permute-start(f32[128,128]{1,0:T(8,128)S(1)} %get-tuple-element.24), channel_id=1, source_target_pairs={{0,1},{1,0},{2,3},{3,2},{4,5},{5,4},{6,7},{7,6},{8,9},{9,8},{10,11... | collective-permute-start | bytes 196616 | tf_op jit(solution)/shard_map/ppermute | solution.py:197
  13.0 4.1 %collective-permute-start.5 = (f32[64,128]{1,0:T(8,128)S(1)}, f32[64,128]{1,0:T(8,128)S(1)}, u32[]{:S(2)}, u32[]{:S(2)}) collective-permute-start(f32[64,128]{1,0:T(8,128)S(1)} %get-tuple-element.25), channel_id=1, source_target_pairs={{0,1},{1,0},{2,3},{3,2},{4,5},{5,4},{6,7},{7,6},{8,9},{9,8},{10,11... | collective-permute-start | bytes 98312 | tf_op jit(solution)/shard_map/ppermute | solution.py:197
  14.6 0.7 %copy-start.9 = (f32[64]{0:T(128)S(1)}, f32[64]{0:T(128)}, u32[]{:S(2)}) copy-start(f32[64]{0:T(128)} %param.18) | copy-start | bytes 772
  14.6 0.7 %copy-start.10 = (s32[32]{0:T(128)S(1)}, s32[32]{0:T(128)}, u32[]{:S(2)}) copy-start(s32[32]{0:T(128)} %param.19) | copy-start | bytes 388
  16.6 1.4 %collective-permute-start.6 = (f32[192,128]{1,0:T(8,128)S(1)}, f32[192,128]{1,0:T(8,128)S(1)}, u32[]{:S(2)}, u32[]{:S(2)}) collective-permute-start(f32[192,128]{1,0:T(8,128)S(1)} %get-tuple-element.26), channel_id=1, source_target_pairs={{0,8},{8,0},{16,24},{24,16},{1,9},{9,1},{17,25},{25,17},{2,10},{10... | collective-permute-start | bytes 294920 | tf_op jit(solution)/shard_map/ppermute | solution.py:200

commit v19 on v18

--- a/solution.py
+++ b/solution.py
@@ -29,10 +29,10 @@
     return mul(lh, rh) + (mul(lh, rl) + mul(ll, rh))
 
 
-def span_kernel(comps, sources, pieces, matrix, *refs):
-    fields, parts = refs[:sources], refs[sources:]
+def span_kernel(comps, across, pieces, matrix, *refs):
+    fields, parts = refs[:quad], refs[quad:]
     depth, length = fields[0].shape[0] // comps, fields[0].shape[1]
-    group = matrix.shape[0] // quad
+    group = matrix.shape[0] // across
     right = []
     for comp in range(comps):
         for at in range(0, depth, group):
@@ -62,13 +62,13 @@
     cells_z = cols * zloc
     shape = z_matrix.shape
     half = shape[1] // 2
-    group = shape[0] // quad
+    group = half // quad
     mine = lax.axis_index("col")
     r = lax.broadcasted_iota(jnp.int32, shape, 0)
     q = lax.broadcasted_iota(jnp.int32, shape, 1)
     q = jnp.where(q < half, q, q - half)
-    out_cell = ((r // group) ^ mine) * zloc + r % zloc
-    in_cell = ((quad * (q // group)) ^ mine) * zloc + q % zloc
+    out_cell = ((quad * (r // group)) ^ mine) * zloc + r % zloc
+    in_cell = ((q // group) ^ mine) * zloc + q % zloc
     same = (r % group) // zloc == (q % group) // zloc
     gap = jnp.where(same, (in_cell - out_cell + cells_z) % cells_z, -1)
     kind = lax.broadcasted_iota(jnp.int32, (1, shape[1]), 1) < half
@@ -189,9 +189,11 @@
     depth = slots * zloc
     field = velocity.reshape(comps * depth, length)
     group = min(depth, 32)
-    sources = cols // quad
+    wide = cols // quad
     rest = comps * depth
-    pieces = [(t, 0, rest) for t in (0, 3, 2)] + [(1, 0, rest - depth), (1, rest - depth, rest)]
+    pieces = [(0, 0, rest)]
+    for t in range(1, wide):
+        pieces += [(t, 0, rest - depth), (t, rest - depth, rest)]
 
     def along(value, step):
         return lax.ppermute(value, "col", [(i, i ^ step) for i in range(cols)])
@@ -199,23 +201,23 @@
     def across(value, step):
         return lax.ppermute(value, "row", [(i, i ^ step) for i in range(rows)])
 
-    gathered = [along(field, quad * i) for i in range(1, sources)]
+    gathered = [along(field, t) for t in range(1, quad)]
     x_part, z_matrix, mask, held = call(
         functools.partial(stream_kernel, cols, comps, zloc),
         [wall_counts, z_first, z_second, field, x_first.reshape(1, length), x_second.reshape(1, length)],
         [SMEM] * 3 + [VMEM] * 3,
-        [field.shape, (quad * group, 2 * sources * group), (depth, length), field.shape],
+        [field.shape, (wide * group, 2 * quad * group), (depth, length), field.shape],
         "stream",
     )
     far = [across(held, step) for step in range(2, rows, 2)]
     parts = call(
-        functools.partial(span_kernel, comps, sources, pieces),
+        functools.partial(span_kernel, comps, wide, pieces),
         [z_matrix, field] + gathered,
-        [VMEM] * (1 + sources),
+        [VMEM] * (1 + quad),
         [(high - low, length) for _, low, high in pieces],
         "span",
     )
-    returned = [along(part, t) for part, (t, _, _) in zip(parts[1:], pieces[1:])]
+    returned = [along(part, quad * t) for part, (t, _, _) in zip(parts[1:], pieces[1:])]
     (y_matrix,) = call(
         functools.partial(wall_matrix_kernel, rows, zloc),
         [wall_counts, metric_table.reshape(1, -1), metric_index.reshape(1, -1), y_first, y_second, parts[0]],

time: 18.8 us -> 18.1 us (0.963)
  starting transfers between devices: 10.8 us -> 9.56 us
  waiting for transfers between devices: 2.06 us -> 2.57 us
    ppermute x5, starting transfers between devices: 9.12 us -> 7.49 us  [along(): return lax.ppermute(value, 'col', [(i, i ^ step) for i in range(cols)])]
    ppermute x5, waiting for transfers between devices: 1.31 us -> 2.57 us  [along(): return lax.ppermute(value, 'col', [(i, i ^ step) for i in range(cols)])]
    ppermute x2, waiting for transfers between devices: 0.75 us -> 0.01 us  [across(): return lax.ppermute(value, 'row', [(i, i ^ step) for i in range(rows)])]
    ppermute x2, starting transfers between devices: 1.65 us -> 2.07 us  [across(): return lax.ppermute(value, 'row', [(i, i ^ step) for i in range(rows)])]
  transfers between devices with their start and end apart: 7 -> 7, of which waited for: 3 -> 2; matrix products, arithmetic and copies ran while one was open for 0% -> 0% of each run, Pallas kernels for 15% -> 15%
where the time goes in v19:
time: 18.1 us; the launch traced here: 17.9 us
  starting transfers between devices  9.56 us (53%)
  Pallas kernels  3.42 us (19%)
  waiting for transfers between devices  2.57 us (14%)
  local copies, waits for them, and re-layouts  2.27 us (13%)
    ppermute x5, starting transfers between devices, along(): return lax.ppermute(value, 'col', [(i, i ^ step) for i in range(cols)])  7.49 us
    pallas_call x6, Pallas kernels, call(): pl.pallas_call(kernel, out_shape=results, in_specs=[pl.BlockSpec(memory_s...  3.42 us
    ppermute x5, waiting for transfers between devices, along(): return lax.ppermute(value, 'col', [(i, i ^ step) for i in range(cols)])  2.57 us
    unnamed x22, local copies, waits for them, and re-layouts  2.27 us
    ppermute x2, starting transfers between devices, across(): return lax.ppermute(value, 'row', [(i, i ^ step) for i in range(rows)])  2.07 us
  transfers between devices with their start and end apart: 7, of which 2 were waited for; matrix products, arithmetic and copies ran while one was open for 0% of the time, Pallas kernels for 15%

profile of v19, /device:TPU:0, one launch (start us, length us, event | category | flops | bytes accessed | tf_op | source)
XLA Modules:
  0.0 17.9 jit_solution(17240319196361574478)
XLA Ops:
  0.0 4.0 %collective-permute-start.2 = (f32[192,128]{1,0:T(8,128)}, f32[192,128]{1,0:T(8,128)S(1)}, u32[]{:S(2)}, u32[]{:S(2)}) collective-permute-start(f32[192,128]{1,0:T(8,128)} %bitcast.6), channel_id=1, source_target_pairs={{0,3},{1,2},{2,1},{3,0},{4,7},{5,6},{6,5},{7,4},{8,11},{9,10},{10,... | collective-permute-start | bytes 294920 | tf_op jit(solution)/shard_map/ppermute | solution.py:199
  4.0 0.4 %collective-permute-start.1 = (f32[192,128]{1,0:T(8,128)}, f32[192,128]{1,0:T(8,128)S(1)}, u32[]{:S(2)}, u32[]{:S(2)}) collective-permute-start(f32[192,128]{1,0:T(8,128)} %bitcast.7), channel_id=1, source_target_pairs={{0,2},{1,3},{2,0},{3,1},{4,6},{5,7},{6,4},{7,5},{8,10},{9,11},{10,... | collective-permute-start | bytes 294920 | tf_op jit(solution)/shard_map/ppermute | solution.py:199
  4.4 0.1 collective-permute-start
  4.5 0.6 %copy-done.7 = f32[128]{0:T(128)S(1)} copy-done((f32[128]{0:T(128)S(1)}, f32[128]{0:T(128)}, u32[]{:S(2)}) %copy-start.7) | copy-done | bytes 536
  5.2 0.0 copy-done.8
  5.2 0.0 copy-done.4
  5.2 0.0 copy-done.5
  5.2 0.0 copy-done.6
  5.2 0.9 %copy-done = f32[3,16,4,128]{3,2,1,0:T(4,128)S(1)} copy-done((f32[3,16,4,128]{3,2,1,0:T(4,128)S(1)}, f32[3,16,4,128]{3,2,1,0:T(4,128)}, u32[]{:S(2)}) %copy-start) | copy-done | bytes 98328
  6.1 1.0 %stream.1 = (f32[192,128]{1,0:T(8,128)S(1)}, f32[64,256]{1,0:T(8,128)S(1)}, f32[64,128]{1,0:T(8,128)S(1)}, f32[192,128]{1,0:T(8,128)S(1)}) custom-call(s32[4]{0:T(128)S(1)} %copy-done.4, f32[32]{0:T(128)S(1)} %copy-done.5, f32[32]{0:T(128)S(1)} %copy-done.6, f32[192,128]{1,0:T(8,128)S(1)} %bitcast.9, f32[1,128]{1,0:T(1,128)S(1)} %bitcast.12, ...), custom_call_target="tpu_custom_call" | custom-call | tf_op jit(solution)/shard_map/stream/pallas_call | solution.py:162
  7.2 2.0 %collective-permute-start.3 = (f32[192,128]{1,0:T(8,128)S(1)}, f32[192,128]{1,0:T(8,128)S(1)}, u32[]{:S(2)}, u32[]{:S(2)}) collective-permute-start(f32[192,128]{1,0:T(8,128)S(1)} %get-tuple-element.18), channel_id=1, source_target_pairs={{0,16},{8,24},{16,0},{24,8},{1,17},{9,25},{17,1},{25,9},{2,18},{10... | collective-permute-start | bytes 294920 | tf_op jit(solution)/shard_map/ppermute | solution.py:202
  9.2 0.0 collective-permute-done.2.refs_3_
  9.2 0.1 collective-permute-done.1.refs_2_
  9.3 0.0 copy-start.3
  9.3 0.4 %span.1 = (f32[192,128]{1,0:T(8,128)S(1)}, f32[128,128]{1,0:T(8,128)S(1)}, f32[64,128]{1,0:T(8,128)S(1)}) custom-call(f32[64,256]{1,0:T(8,128)S(1)} %get-tuple-element.15.matrix, f32[192,128]{1,0:T(8,128)S(1)} %bitcast.10, f32[192,128]{1,0:T(8,128)S(1)} %collective-permute-done.refs_1_, f32[192,128]{1,0:T(8,128)S(1)} %collective-permute-done.1.refs_2_, ...), custom_call_target="tpu_custom_call" | custom-call | tf_op jit(solution)/shard_map/span/pallas_call | solution.py:162
  9.7 2.7 %collective-permute-start.4 = (f32[128,128]{1,0:T(8,128)S(1)}, f32[128,128]{1,0:T(8,128)S(1)}, u32[]{:S(2)}, u32[]{:S(2)}) collective-permute-start(f32[128,128]{1,0:T(8,128)S(1)} %get-tuple-element.20), channel_id=1, source_target_pairs={{0,4},{1,5},{2,6},{3,7},{4,0},{5,1},{6,2},{7,3},{8,12},{9,13},{10,... | collective-permute-start | bytes 196616 | tf_op jit(solution)/shard_map/ppermute | solution.py:199
  12.4 0.3 %collective-permute-start.5 = (f32[64,128]{1,0:T(8,128)S(1)}, f32[64,128]{1,0:T(8,128)S(1)}, u32[]{:S(2)}, u32[]{:S(2)}) collective-permute-start(f32[64,128]{1,0:T(8,128)S(1)} %get-tuple-element.21), channel_id=1, source_target_pairs={{0,4},{1,5},{2,6},{3,7},{4,0},{5,1},{6,2},{7,3},{8,12},{9,13},{10,... | collective-permute-start | bytes 98312 | tf_op jit(solution)/shard_map/ppermute | solution.py:199
  12.7 0.6 %copy-done.9 = f32[64]{0:T(128)S(1)} copy-done((f32[64]{0:T(128)S(1)}, f32[64]{0:T(128)}, u32[]{:S(2)}) %copy-start.9) | copy-done | bytes 280
  13.3 0.0 copy-done.10
  13.4 1.0 %wall_matrix.1.matrix = f32[128,256]{1,0:T(8,128)S(1)} custom-call(s32[4]{0:T(128)S(1)} %copy-done.4, f32[1,64]{1,0:T(1,128)S(1)} %bitcast.14, s32[1,32]{1,0:T(1,128)S(1)} %bitcast.15, f32[32,32]{1,0:T(8,128)S(1)} %copy-done.2, f32[32,32]{1,0:T(8,128)S(1)} %copy-done.3, f32[192,128]{1,0:T(8,128)S(1)} %get-tuple-element.16.after.z_part), custom_call_target="tpu_custom_call" | custom-call | tf_op jit(solution)/shard_map/wall_matrix/pallas_call | solution.py:162
  14.4 0.3 %wall.1 = (f32[192,128]{1,0:T(8,128)S(1)}, f32[192,128]{1,0:T(8,128)S(1)}) custom-call(f32[128,256]{1,0:T(8,128)S(1)} %wall_matrix.1.matrix, f32[192,128]{1,0:T(8,128)S(1)} %get-tuple-element.17.x_part, f32[192,128]{1,0:T(8,128)S(1)} %get-tuple-element.16.after.z_part, f32[192,128]{1,0:T(8,128)S(1)} %bitcast.11, f32[192,128]{1,0:T(8,128)S(1)} %collective-permute-done.3.refs_1_), custom_call_target="tpu_custom_call" | custom-call | tf_op jit(solution)/shard_map/wall/pallas_call | solution.py:162
  14.7 0.1 collective-permute-start.6
  14.8 2.4 %collective-permute-done.5.refs_1_ = f32[64,128]{1,0:T(8,128)S(1)} collective-permute-done((f32[64,128]{1,0:T(8,128)S(1)}, f32[64,128]{1,0:T(8,128)S(1)}, u32[]{:S(2)}, u32[]{:S(2)}) %collective-permute-start.5) | collective-permute-done | bytes 32800 | tf_op jit(solution)/shard_map/ppermute | solution.py:199
  17.2 0.7 %finish.1 = f32[192,128]{1,0:T(8,128)} custom-call(f32[192,128]{1,0:T(8,128)S(1)} %sum.1.total, f32[192,128]{1,0:T(8,128)S(1)} %collective-permute-done.6.near), custom_call_target="tpu_custom_call" | custom-call | tf_op jit(solution)/shard_map/finish/pallas_call | solution.py:162
  (18 shorter events, 0.1 us)
Async XLA Ops:
  0.0 9.2 %collective-permute-start.2 = (f32[192,128]{1,0:T(8,128)}, f32[192,128]{1,0:T(8,128)S(1)}, u32[]{:S(2)}, u32[]{:S(2)}) collective-permute-start(f32[192,128]{1,0:T(8,128)} %bitcast.6), channel_id=1, source_target_pairs={{0,3},{1,2},{2,1},{3,0},{4,7},{5,6},{6,5},{7,4},{8,11},{9,10},{10,... | collective-permute-start | bytes 294920 | tf_op jit(solution)/shard_map/ppermute | solution.py:199
  4.0 5.4 %collective-permute-start.1 = (f32[192,128]{1,0:T(8,128)}, f32[192,128]{1,0:T(8,128)S(1)}, u32[]{:S(2)}, u32[]{:S(2)}) collective-permute-start(f32[192,128]{1,0:T(8,128)} %bitcast.7), channel_id=1, source_target_pairs={{0,2},{1,3},{2,0},{3,1},{4,6},{5,7},{6,4},{7,5},{8,10},{9,11},{10,... | collective-permute-start | bytes 294920 | tf_op jit(solution)/shard_map/ppermute | solution.py:199
  4.4 4.9 %collective-permute-start = (f32[192,128]{1,0:T(8,128)}, f32[192,128]{1,0:T(8,128)S(1)}, u32[]{:S(2)}, u32[]{:S(2)}) collective-permute-start(f32[192,128]{1,0:T(8,128)} %bitcast.8), channel_id=1, source_target_pairs={{0,1},{1,0},{2,3},{3,2},{4,5},{5,4},{6,7},{7,6},{8,9},{9,8},{10,11... | collective-permute-start | bytes 294920 | tf_op jit(solution)/shard_map/ppermute | solution.py:199
  4.5 0.7 %copy-start.7 = (f32[128]{0:T(128)S(1)}, f32[128]{0:T(128)}, u32[]{:S(2)}) copy-start(f32[128]{0:T(128)} %param.12) | copy-start | bytes 1540
  4.5 0.7 %copy-start.8 = (f32[128]{0:T(128)S(1)}, f32[128]{0:T(128)}, u32[]{:S(2)}) copy-start(f32[128]{0:T(128)} %param.13) | copy-start | bytes 1540
  4.5 0.7 %copy-start.4 = (s32[4]{0:T(128)S(1)}, s32[4]{0:T(128)}, u32[]{:S(2)}) copy-start(s32[4]{0:T(128)} %wall_counts.3) | copy-start | bytes 52
  4.5 0.7 %copy-start.5 = (f32[32]{0:T(128)S(1)}, f32[32]{0:T(128)}, u32[]{:S(2)}) copy-start(f32[32]{0:T(128)} %z_first.1) | copy-start | bytes 388
  4.5 0.7 %copy-start.6 = (f32[32]{0:T(128)S(1)}, f32[32]{0:T(128)}, u32[]{:S(2)}) copy-start(f32[32]{0:T(128)} %z_second.1) | copy-start | bytes 388
  5.2 0.9 %copy-start = (f32[3,16,4,128]{3,2,1,0:T(4,128)S(1)}, f32[3,16,4,128]{3,2,1,0:T(4,128)}, u32[]{:S(2)}) copy-start(f32[3,16,4,128]{3,2,1,0:T(4,128)} %param.10) | copy-start | bytes 294916
  6.1 3.2 %copy-start.1 = (f32[3,16,4,128]{3,2,1,0:T(4,128)S(1)}, f32[3,16,4,128]{3,2,1,0:T(4,128)}, u32[]{:S(2)}) copy-start(f32[3,16,4,128]{3,2,1,0:T(4,128)} %param.10) | copy-start | bytes 294916
  7.2 7.2 %collective-permute-start.3 = (f32[192,128]{1,0:T(8,128)S(1)}, f32[192,128]{1,0:T(8,128)S(1)}, u32[]{:S(2)}, u32[]{:S(2)}) collective-permute-start(f32[192,128]{1,0:T(8,128)S(1)} %get-tuple-element.18), channel_id=1, source_target_pairs={{0,16},{8,24},{16,0},{24,8},{1,17},{9,25},{17,1},{25,9},{2,18},{10... | collective-permute-start | bytes 294920 | tf_op jit(solution)/shard_map/ppermute | solution.py:202
  9.3 3.4 %copy-start.2 = (f32[32,32]{1,0:T(8,128)S(1)}, f32[32,32]{1,0:T(8,128)}, u32[]{:S(2)}) copy-start(f32[32,32]{1,0:T(8,128)} %y_first.1) | copy-start | bytes 12292
  9.3 3.4 %copy-start.3 = (f32[32,32]{1,0:T(8,128)S(1)}, f32[32,32]{1,0:T(8,128)}, u32[]{:S(2)}) copy-start(f32[32,32]{1,0:T(8,128)} %y_second.1) | copy-start | bytes 12292
  9.7 7.5 %collective-permute-start.4 = (f32[128,128]{1,0:T(8,128)S(1)}, f32[128,128]{1,0:T(8,128)S(1)}, u32[]{:S(2)}, u32[]{:S(2)}) collective-permute-start(f32[128,128]{1,0:T(8,128)S(1)} %get-tuple-element.20), channel_id=1, source_target_pairs={{0,4},{1,5},{2,6},{3,7},{4,0},{5,1},{6,2},{7,3},{8,12},{9,13},{10,... | collective-permute-start | bytes 196616 | tf_op jit(solution)/shard_map/ppermute | solution.py:199
  12.4 4.8 %collective-permute-start.5 = (f32[64,128]{1,0:T(8,128)S(1)}, f32[64,128]{1,0:T(8,128)S(1)}, u32[]{:S(2)}, u32[]{:S(2)}) collective-permute-start(f32[64,128]{1,0:T(8,128)S(1)} %get-tuple-element.21), channel_id=1, source_target_pairs={{0,4},{1,5},{2,6},{3,7},{4,0},{5,1},{6,2},{7,3},{8,12},{9,13},{10,... | collective-permute-start | bytes 98312 | tf_op jit(solution)/shard_map/ppermute | solution.py:199
  12.7 0.7 %copy-start.9 = (f32[64]{0:T(128)S(1)}, f32[64]{0:T(128)}, u32[]{:S(2)}) copy-start(f32[64]{0:T(128)} %param.18) | copy-start | bytes 772
  12.7 0.7 %copy-start.10 = (s32[32]{0:T(128)S(1)}, s32[32]{0:T(128)}, u32[]{:S(2)}) copy-start(s32[32]{0:T(128)} %param.19) | copy-start | bytes 388
  14.7 2.5 %collective-permute-start.6 = (f32[192,128]{1,0:T(8,128)S(1)}, f32[192,128]{1,0:T(8,128)S(1)}, u32[]{:S(2)}, u32[]{:S(2)}) collective-permute-start(f32[192,128]{1,0:T(8,128)S(1)} %get-tuple-element.22), channel_id=1, source_target_pairs={{0,8},{8,0},{16,24},{24,16},{1,9},{9,1},{17,25},{25,17},{2,10},{10... | collective-permute-start | bytes 294920 | tf_op jit(solution)/shard_map/ppermute | solution.py:202

commit v20 on v19

--- a/solution.py
+++ b/solution.py
@@ -50,12 +50,8 @@
     return pltpu.roll(jnp.broadcast_to(row, (length, length)), 0, 1, stride=1, stride_axis=0)
 
 
-def stream_kernel(
-    cols, comps, zloc, wall_counts, z_first, z_second, field, x_first, x_second, x_part, z_matrix, mask, held
-):
+def span_matrix_kernel(cols, zloc, wall_counts, z_first, z_second, field, z_matrix, mask, held):
     held[...] = field[...]
-    depth = mask.shape[0]
-    length = field.shape[1]
     count = wall_counts[lax.axis_index("row")]
     mask[...] = (lax.broadcasted_iota(jnp.int32, mask.shape, 0) // zloc < count).astype(jnp.float32)
 
@@ -79,6 +75,10 @@
 
     z_matrix[...] = lax.fori_loop(0, cells_z, fill, jnp.zeros(shape, jnp.float32), unroll=8)
 
+
+def stream_kernel(comps, field, x_first, x_second, after, x_part):
+    length = field.shape[1]
+    depth = field.shape[0] // comps
     u = field[...]
     lead = u[:depth]
     left = jnp.concatenate(
@@ -190,10 +190,7 @@
     field = velocity.reshape(comps * depth, length)
     group = min(depth, 32)
     wide = cols // quad
-    rest = comps * depth
-    pieces = [(0, 0, rest)]
-    for t in range(1, wide):
-        pieces += [(t, 0, rest - depth), (t, rest - depth, rest)]
+    pieces = [(t, 0, comps * depth) for t in range(wide)]
 
     def along(value, step):
         return lax.ppermute(value, "col", [(i, i ^ step) for i in range(cols)])
@@ -202,12 +199,12 @@
         return lax.ppermute(value, "row", [(i, i ^ step) for i in range(rows)])
 
     gathered = [along(field, t) for t in range(1, quad)]
-    x_part, z_matrix, mask, held = call(
-        functools.partial(stream_kernel, cols, comps, zloc),
-        [wall_counts, z_first, z_second, field, x_first.reshape(1, length), x_second.reshape(1, length)],
-        [SMEM] * 3 + [VMEM] * 3,
-        [field.shape, (wide * group, 2 * quad * group), (depth, length), field.shape],
-        "stream",
+    z_matrix, mask, held = call(
+        functools.partial(span_matrix_kernel, cols, zloc),
+        [wall_counts, z_first, z_second, field],
+        [SMEM] * 3 + [VMEM],
+        [(wide * group, 2 * quad * group), (depth, length), field.shape],
+        "span_matrix",
     )
     far = [across(held, step) for step in range(2, rows, 2)]
     parts = call(
@@ -218,6 +215,13 @@
         "span",
     )
     returned = [along(part, quad * t) for part, (t, _, _) in zip(parts[1:], pieces[1:])]
+    (x_part,) = call(
+        functools.partial(stream_kernel, comps),
+        [field, x_first.reshape(1, length), x_second.reshape(1, length), parts[0]],
+        [VMEM] * 3 + [pl.ANY],
+        [field.shape],
+        "stream",
+    )
     (y_matrix,) = call(
         functools.partial(wall_matrix_kernel, rows, zloc),
         [wall_counts, metric_table.reshape(1, -1), metric_index.reshape(1, -1), y_first, y_second, parts[0]],

time: 18.1 us -> 17.7 us (0.978)
  starting transfers between devices: 9.56 us -> 9.36 us
    ppermute x5 -> x4, waiting for transfers between devices: 2.57 us -> 2.36 us  [along(): return lax.ppermute(value, 'col', [(i, i ^ step) for i in range(cols)])]
    ppermute x5 -> x4, starting transfers between devices: 7.49 us -> 7.36 us  [along(): return lax.ppermute(value, 'col', [(i, i ^ step) for i in range(cols)])]
    pallas_call x6 -> x7, Pallas kernels: 3.42 us -> 3.4 us  [call(): pl.pallas_call(kernel, out_shape=results, in_specs=[pl.BlockSpec(memory_s...]
  transfers between devices with their start and end apart: 7 -> 6, of which waited for: 2 -> 2; matrix products, arithmetic and copies ran while one was open for 0% -> 0% of each run, Pallas kernels for 15% -> 16%
where the time goes in v20:
time: 17.7 us; the launch traced here: 17.5 us
  starting transfers between devices  9.36 us (53%)
  Pallas kernels  3.4 us (19%)
  waiting for transfers between devices  2.4 us (14%)
  local copies, waits for them, and re-layouts  2.26 us (13%)
    ppermute x4, starting transfers between devices, along(): return lax.ppermute(value, 'col', [(i, i ^ step) for i in range(cols)])  7.36 us
    pallas_call x7, Pallas kernels, call(): pl.pallas_call(kernel, out_shape=results, in_specs=[pl.BlockSpec(memory_s...  3.4 us
    ppermute x4, waiting for transfers between devices, along(): return lax.ppermute(value, 'col', [(i, i ^ step) for i in range(cols)])  2.36 us
    unnamed x22, local copies, waits for them, and re-layouts  2.26 us
    ppermute x2, starting transfers between devices, across(): return lax.ppermute(value, 'row', [(i, i ^ step) for i in range(rows)])  2 us
  transfers between devices with their start and end apart: 6, of which 2 were waited for; matrix products, arithmetic and copies ran while one was open for 0% of the time, Pallas kernels for 16%

profile of v20, /device:TPU:0, one launch (start us, length us, event | category | flops | bytes accessed | tf_op | source)
XLA Modules:
  0.0 17.5 jit_solution(3445522766784445539)
XLA Ops:
  0.0 4.0 %collective-permute-start.2 = (f32[192,128]{1,0:T(8,128)}, f32[192,128]{1,0:T(8,128)S(1)}, u32[]{:S(2)}, u32[]{:S(2)}) collective-permute-start(f32[192,128]{1,0:T(8,128)} %bitcast.6), channel_id=1, source_target_pairs={{0,3},{1,2},{2,1},{3,0},{4,7},{5,6},{6,5},{7,4},{8,11},{9,10},{10,... | collective-permute-start | bytes 294920 | tf_op jit(solution)/shard_map/ppermute | solution.py:196
  4.0 0.4 %collective-permute-start.1 = (f32[192,128]{1,0:T(8,128)}, f32[192,128]{1,0:T(8,128)S(1)}, u32[]{:S(2)}, u32[]{:S(2)}) collective-permute-start(f32[192,128]{1,0:T(8,128)} %bitcast.7), channel_id=1, source_target_pairs={{0,2},{1,3},{2,0},{3,1},{4,6},{5,7},{6,4},{7,5},{8,10},{9,11},{10,... | collective-permute-start | bytes 294920 | tf_op jit(solution)/shard_map/ppermute | solution.py:196
  4.5 0.2 %collective-permute-start = (f32[192,128]{1,0:T(8,128)}, f32[192,128]{1,0:T(8,128)S(1)}, u32[]{:S(2)}, u32[]{:S(2)}) collective-permute-start(f32[192,128]{1,0:T(8,128)} %bitcast.8), channel_id=1, source_target_pairs={{0,1},{1,0},{2,3},{3,2},{4,5},{5,4},{6,7},{7,6},{8,9},{9,8},{10,11... | collective-permute-start | bytes 294920 | tf_op jit(solution)/shard_map/ppermute | solution.py:196
  4.7 0.9 %copy-done = f32[3,16,4,128]{3,2,1,0:T(4,128)S(1)} copy-done((f32[3,16,4,128]{3,2,1,0:T(4,128)S(1)}, f32[3,16,4,128]{3,2,1,0:T(4,128)}, u32[]{:S(2)}) %copy-start) | copy-done | bytes 98328
  5.6 0.7 %span_matrix.1 = (f32[64,256]{1,0:T(8,128)S(1)}, f32[64,128]{1,0:T(8,128)S(1)}, f32[192,128]{1,0:T(8,128)S(1)}) custom-call(s32[4]{0:T(128)S(1)} %copy-done.4, f32[32]{0:T(128)S(1)} %copy-done.5, f32[32]{0:T(128)S(1)} %copy-done.6, f32[192,128]{1,0:T(8,128)S(1)} %bitcast.9), custom_call_target="tpu_custom_call" | custom-call | tf_op jit(solution)/shard_map/span_matrix/pallas_call | solution.py:162
  6.3 1.9 %collective-permute-start.3 = (f32[192,128]{1,0:T(8,128)S(1)}, f32[192,128]{1,0:T(8,128)S(1)}, u32[]{:S(2)}, u32[]{:S(2)}) collective-permute-start(f32[192,128]{1,0:T(8,128)S(1)} %get-tuple-element.15), channel_id=1, source_target_pairs={{0,16},{8,24},{16,0},{24,8},{1,17},{9,25},{17,1},{25,9},{2,18},{10... | collective-permute-start | bytes 294920 | tf_op jit(solution)/shard_map/ppermute | solution.py:199
  8.3 1.1 %collective-permute-done.1.refs_2_ = f32[192,128]{1,0:T(8,128)S(1)} collective-permute-done((f32[192,128]{1,0:T(8,128)}, f32[192,128]{1,0:T(8,128)S(1)}, u32[]{:S(2)}, u32[]{:S(2)}) %collective-permute-start.1) | collective-permute-done | bytes 98336 | tf_op jit(solution)/shard_map/ppermute | solution.py:196
  9.4 0.4 %span.1 = (f32[192,128]{1,0:T(8,128)S(1)}, f32[192,128]{1,0:T(8,128)S(1)}) custom-call(f32[64,256]{1,0:T(8,128)S(1)} %get-tuple-element.13.matrix, f32[192,128]{1,0:T(8,128)S(1)} %bitcast.10, f32[192,128]{1,0:T(8,128)S(1)} %collective-permute-done.refs_1_, f32[192,128]{1,0:T(8,128)S(1)} %collective-permute-done.1.refs_2_, ...), custom_call_target="tpu_custom_call" | custom-call | tf_op jit(solution)/shard_map/span/pallas_call | solution.py:162
  9.8 2.7 %collective-permute-start.4 = (f32[192,128]{1,0:T(8,128)S(1)}, f32[192,128]{1,0:T(8,128)S(1)}, u32[]{:S(2)}, u32[]{:S(2)}) collective-permute-start(f32[192,128]{1,0:T(8,128)S(1)} %get-tuple-element.17), channel_id=1, source_target_pairs={{0,4},{1,5},{2,6},{3,7},{4,0},{5,1},{6,2},{7,3},{8,12},{9,13},{10,... | collective-permute-start | bytes 294920 | tf_op jit(solution)/shard_map/ppermute | solution.py:196
  12.5 0.7 %copy-done.7 = f32[128]{0:T(128)S(1)} copy-done((f32[128]{0:T(128)S(1)}, f32[128]{0:T(128)}, u32[]{:S(2)}) %copy-start.7) | copy-done | bytes 536
  13.1 0.0 copy-done.8
  13.1 0.3 %stream.1.x_part = f32[192,128]{1,0:T(8,128)S(1)} custom-call(f32[192,128]{1,0:T(8,128)S(1)} %bitcast.11, f32[1,128]{1,0:T(1,128)S(1)} %bitcast.13, f32[1,128]{1,0:T(1,128)S(1)} %bitcast.14, f32[192,128]{1,0:T(8,128)S(1)} %get-tuple-element.14.after.z_part), custom_call_target="tpu_custom_call" | custom-call | tf_op jit(solution)/shard_map/stream/pallas_call | solution.py:162
  13.5 0.0 copy-start.9
  13.5 0.0 copy-start.10
  13.5 0.4 %copy-done.2 = f32[32,32]{1,0:T(8,128)S(1)} copy-done((f32[32,32]{1,0:T(8,128)S(1)}, f32[32,32]{1,0:T(8,128)}, u32[]{:S(2)}) %copy-start.2) | copy-done | bytes 4120
  13.9 0.0 copy-done.3
  13.9 0.2 %copy-done.9 = f32[64]{0:T(128)S(1)} copy-done((f32[64]{0:T(128)S(1)}, f32[64]{0:T(128)}, u32[]{:S(2)}) %copy-start.9) | copy-done | bytes 280
  14.1 0.0 copy-done.10
  14.1 1.0 %wall_matrix.1.matrix = f32[128,256]{1,0:T(8,128)S(1)} custom-call(s32[4]{0:T(128)S(1)} %copy-done.4, f32[1,64]{1,0:T(1,128)S(1)} %bitcast.15, s32[1,32]{1,0:T(1,128)S(1)} %bitcast.16, f32[32,32]{1,0:T(8,128)S(1)} %copy-done.2, f32[32,32]{1,0:T(8,128)S(1)} %copy-done.3, f32[192,128]{1,0:T(8,128)S(1)} %get-tuple-element.14.after.z_part), custom_call_target="tpu_custom_call" | custom-call | tf_op jit(solution)/shard_map/wall_matrix/pallas_call | solution.py:162
  15.2 0.3 %wall.1 = (f32[192,128]{1,0:T(8,128)S(1)}, f32[192,128]{1,0:T(8,128)S(1)}) custom-call(f32[128,256]{1,0:T(8,128)S(1)} %wall_matrix.1.matrix, f32[192,128]{1,0:T(8,128)S(1)} %stream.1.x_part, f32[192,128]{1,0:T(8,128)S(1)} %get-tuple-element.14.after.z_part, f32[192,128]{1,0:T(8,128)S(1)} %bitcast.12, f32[192,128]{1,0:T(8,128)S(1)} %collective-permute-done.3.refs_1_), custom_call_target="tpu_custom_call" | custom-call | tf_op jit(solution)/shard_map/wall/pallas_call | solution.py:162
  15.5 0.1 collective-permute-start.5
  15.6 1.2 %collective-permute-done.4.refs_0_ = f32[192,128]{1,0:T(8,128)S(1)} collective-permute-done((f32[192,128]{1,0:T(8,128)S(1)}, f32[192,128]{1,0:T(8,128)S(1)}, u32[]{:S(2)}, u32[]{:S(2)}) %collective-permute-start.4) | collective-permute-done | bytes 98336 | tf_op jit(solution)/shard_map/ppermute | solution.py:196
  16.8 0.0 collective-permute-done.5.near
  16.8 0.7 %finish.1 = f32[192,128]{1,0:T(8,128)} custom-call(f32[192,128]{1,0:T(8,128)S(1)} %sum.1.total, f32[192,128]{1,0:T(8,128)S(1)} %collective-permute-done.5.near), custom_call_target="tpu_custom_call" | custom-call | tf_op jit(solution)/shard_map/finish/pallas_call | solution.py:162
  (17 shorter events, 0.0 us)
Async XLA Ops:
  0.0 4.7 %copy-start.4 = (s32[4]{0:T(128)S(1)}, s32[4]{0:T(128)}, u32[]{:S(2)}) copy-start(s32[4]{0:T(128)} %wall_counts.3) | copy-start | bytes 52
  0.0 4.7 %copy-start.6 = (f32[32]{0:T(128)S(1)}, f32[32]{0:T(128)}, u32[]{:S(2)}) copy-start(f32[32]{0:T(128)} %z_second.1) | copy-start | bytes 388
  0.0 4.7 %copy-start.5 = (f32[32]{0:T(128)S(1)}, f32[32]{0:T(128)}, u32[]{:S(2)}) copy-start(f32[32]{0:T(128)} %z_first.1) | copy-start | bytes 388
  0.0 8.3 %collective-permute-start.2 = (f32[192,128]{1,0:T(8,128)}, f32[192,128]{1,0:T(8,128)S(1)}, u32[]{:S(2)}, u32[]{:S(2)}) collective-permute-start(f32[192,128]{1,0:T(8,128)} %bitcast.6), channel_id=1, source_target_pairs={{0,3},{1,2},{2,1},{3,0},{4,7},{5,6},{6,5},{7,4},{8,11},{9,10},{10,... | collective-permute-start | bytes 294920 | tf_op jit(solution)/shard_map/ppermute | solution.py:196
  4.0 5.4 %collective-permute-start.1 = (f32[192,128]{1,0:T(8,128)}, f32[192,128]{1,0:T(8,128)S(1)}, u32[]{:S(2)}, u32[]{:S(2)}) collective-permute-start(f32[192,128]{1,0:T(8,128)} %bitcast.7), channel_id=1, source_target_pairs={{0,2},{1,3},{2,0},{3,1},{4,6},{5,7},{6,4},{7,5},{8,10},{9,11},{10,... | collective-permute-start | bytes 294920 | tf_op jit(solution)/shard_map/ppermute | solution.py:196
  4.5 4.9 %collective-permute-start = (f32[192,128]{1,0:T(8,128)}, f32[192,128]{1,0:T(8,128)S(1)}, u32[]{:S(2)}, u32[]{:S(2)}) collective-permute-start(f32[192,128]{1,0:T(8,128)} %bitcast.8), channel_id=1, source_target_pairs={{0,1},{1,0},{2,3},{3,2},{4,5},{5,4},{6,7},{7,6},{8,9},{9,8},{10,11... | collective-permute-start | bytes 294920 | tf_op jit(solution)/shard_map/ppermute | solution.py:196
  4.7 0.9 %copy-start = (f32[3,16,4,128]{3,2,1,0:T(4,128)S(1)}, f32[3,16,4,128]{3,2,1,0:T(4,128)}, u32[]{:S(2)}) copy-start(f32[3,16,4,128]{3,2,1,0:T(4,128)} %param.10) | copy-start | bytes 294916
  5.6 3.8 %copy-start.1 = (f32[3,16,4,128]{3,2,1,0:T(4,128)S(1)}, f32[3,16,4,128]{3,2,1,0:T(4,128)}, u32[]{:S(2)}) copy-start(f32[3,16,4,128]{3,2,1,0:T(4,128)} %param.10) | copy-start | bytes 294916
  6.3 8.8 %collective-permute-start.3 = (f32[192,128]{1,0:T(8,128)S(1)}, f32[192,128]{1,0:T(8,128)S(1)}, u32[]{:S(2)}, u32[]{:S(2)}) collective-permute-start(f32[192,128]{1,0:T(8,128)S(1)} %get-tuple-element.15), channel_id=1, source_target_pairs={{0,16},{8,24},{16,0},{24,8},{1,17},{9,25},{17,1},{25,9},{2,18},{10... | collective-permute-start | bytes 294920 | tf_op jit(solution)/shard_map/ppermute | solution.py:199
  9.8 7.0 %collective-permute-start.4 = (f32[192,128]{1,0:T(8,128)S(1)}, f32[192,128]{1,0:T(8,128)S(1)}, u32[]{:S(2)}, u32[]{:S(2)}) collective-permute-start(f32[192,128]{1,0:T(8,128)S(1)} %get-tuple-element.17), channel_id=1, source_target_pairs={{0,4},{1,5},{2,6},{3,7},{4,0},{5,1},{6,2},{7,3},{8,12},{9,13},{10,... | collective-permute-start | bytes 294920 | tf_op jit(solution)/shard_map/ppermute | solution.py:196
  12.5 0.7 %copy-start.7 = (f32[128]{0:T(128)S(1)}, f32[128]{0:T(128)}, u32[]{:S(2)}) copy-start(f32[128]{0:T(128)} %param.12) | copy-start | bytes 1540
  12.5 0.7 %copy-start.8 = (f32[128]{0:T(128)S(1)}, f32[128]{0:T(128)}, u32[]{:S(2)}) copy-start(f32[128]{0:T(128)} %param.13) | copy-start | bytes 1540
  13.1 0.7 %copy-start.2 = (f32[32,32]{1,0:T(8,128)S(1)}, f32[32,32]{1,0:T(8,128)}, u32[]{:S(2)}) copy-start(f32[32,32]{1,0:T(8,128)} %y_first.1) | copy-start | bytes 12292
  13.1 0.7 %copy-start.3 = (f32[32,32]{1,0:T(8,128)S(1)}, f32[32,32]{1,0:T(8,128)}, u32[]{:S(2)}) copy-start(f32[32,32]{1,0:T(8,128)} %y_second.1) | copy-start | bytes 12292
  13.5 0.7 %copy-start.9 = (f32[64]{0:T(128)S(1)}, f32[64]{0:T(128)}, u32[]{:S(2)}) copy-start(f32[64]{0:T(128)} %param.18) | copy-start | bytes 772
  13.5 0.7 %copy-start.10 = (s32[32]{0:T(128)S(1)}, s32[32]{0:T(128)}, u32[]{:S(2)}) copy-start(s32[32]{0:T(128)} %param.19) | copy-start | bytes 388
  15.5 1.4 %collective-permute-start.5 = (f32[192,128]{1,0:T(8,128)S(1)}, f32[192,128]{1,0:T(8,128)S(1)}, u32[]{:S(2)}, u32[]{:S(2)}) collective-permute-start(f32[192,128]{1,0:T(8,128)S(1)} %get-tuple-element.18), channel_id=1, source_target_pairs={{0,8},{8,0},{16,24},{24,16},{1,9},{9,1},{17,25},{25,17},{2,10},{10... | collective-permute-start | bytes 294920 | tf_op jit(solution)/shard_map/ppermute | solution.py:199

commit v21 on v20

--- a/solution.py
+++ b/solution.py
@@ -26,24 +26,42 @@
     mul = functools.partial(lax.dot_general, dimension_numbers=dims, preferred_element_type=jnp.float32)
     lh, ll = halves(left)
     rh, rl = halves(right)
-    return mul(lh, rh) + (mul(lh, rl) + mul(ll, rh))
-
-
-def span_kernel(comps, across, pieces, matrix, *refs):
-    fields, parts = refs[:quad], refs[quad:]
+    both = mul(jnp.concatenate([lh, ll], axis=0), rh)
+    count = left.shape[0]
+    return both[:count] + (mul(lh, rl) + both[count:])
+
+
+def quad_sums(comps, matrix, fields, chosen):
     depth, length = fields[0].shape[0] // comps, fields[0].shape[1]
-    group = matrix.shape[0] // across
+    half = matrix.shape[1] // 2
+    group = half // quad
+    left = jnp.concatenate(
+        [matrix[:, start + s * group : start + (s + 1) * group] for start in (0, half) for s in chosen], axis=1
+    )
     right = []
     for comp in range(comps):
         for at in range(0, depth, group):
             stack = [field[comp * depth + at : comp * depth + at + group] for field in fields]
             stack += [value * field[2 * depth + at : 2 * depth + at + group] for value, field in zip(stack, fields)]
             right.append(jnp.concatenate(stack, axis=0))
-    result = dot_split(matrix[...], jnp.concatenate(right, axis=1))
-    for part, (t, low, high) in zip(parts, pieces):
-        for at in range(low, high, group):
-            i = at // group
-            part[at - low : at - low + group] = result[t * group : (t + 1) * group, i * length : (i + 1) * length]
+    return dot_split(left, jnp.concatenate(right, axis=1))
+
+
+def early_kernel(comps, chosen, matrix, *refs):
+    refs[-1][...] = quad_sums(comps, matrix, refs[:-1], chosen)
+
+
+def span_kernel(comps, chosen, matrix, early, *refs):
+    fields, parts = refs[: len(chosen)], refs[len(chosen) :]
+    result = early[...] + quad_sums(comps, matrix, fields, chosen)
+    rows, length = parts[0].shape
+    count = len(parts)
+    group = result.shape[0] // count
+    for t in range(count):
+        for i in range(rows // group):
+            parts[t][i * group : (i + 1) * group] = result[
+                t * group : (t + 1) * group, i * length : (i + 1) * length
+            ]
 
 
 def circulant_rows(row, length):
@@ -140,16 +158,12 @@
         away[at] = result[depth:]
 
 
-def sum_kernel(comps, pieces, mask, total, *refs):
+def sum_kernel(comps, mask, *refs):
     parts, out = refs[:-1], refs[-1]
     depth = mask.shape[0]
     for comp in range(comps):
         at = slice(comp * depth, (comp + 1) * depth)
-        value = total[at]
-        for part, (_, low, high) in zip(parts, pieces):
-            if low <= at.start and at.stop <= high:
-                value += part[at.start - low : at.stop - low]
-        out[at] = jnp.where(mask[...] > 0, value, 0.0)
+        out[at] = jnp.where(mask[...] > 0, sum(part[at] for part in parts[1:]) + parts[0][at], 0.0)
 
 
 def finish_kernel(total, near, out):
@@ -190,7 +204,6 @@
     field = velocity.reshape(comps * depth, length)
     group = min(depth, 32)
     wide = cols // quad
-    pieces = [(t, 0, comps * depth) for t in range(wide)]
 
     def along(value, step):
         return lax.ppermute(value, "col", [(i, i ^ step) for i in range(cols)])
@@ -207,14 +220,21 @@
         "span_matrix",
     )
     far = [across(held, step) for step in range(2, rows, 2)]
+    (early,) = call(
+        functools.partial(early_kernel, comps, (0, quad - 1)),
+        [z_matrix, field, gathered[-1]],
+        [VMEM] * 3,
+        [(wide * group, comps * (depth // group) * length)],
+        "early",
+    )
     parts = call(
-        functools.partial(span_kernel, comps, wide, pieces),
-        [z_matrix, field] + gathered,
-        [VMEM] * (1 + quad),
-        [(high - low, length) for _, low, high in pieces],
+        functools.partial(span_kernel, comps, tuple(range(1, quad - 1))),
+        [z_matrix, early] + gathered[:-1],
+        [VMEM] * quad,
+        [field.shape] * wide,
         "span",
     )
-    returned = [along(part, quad * t) for part, (t, _, _) in zip(parts[1:], pieces[1:])]
+    returned = [along(parts[t], quad * t) for t in range(1, wide)]
     (x_part,) = call(
         functools.partial(stream_kernel, comps),
         [field, x_first.reshape(1, length), x_second.reshape(1, length), parts[0]],
@@ -238,7 +258,7 @@
     )
     near = across(away, 1)
     (summed,) = call(
-        functools.partial(sum_kernel, comps, pieces[1:]),
+        functools.partial(sum_kernel, comps),
         [mask, total] + returned,
         [VMEM] * (2 + len(returned)),
         [field.shape],

time: 17.7 us -> 17.7 us (level)
  waiting for transfers between devices: 2.4 us -> 2.11 us
  Pallas kernels: 3.4 us -> 3.59 us
    ppermute x4, waiting for transfers between devices: 2.36 us -> 2.08 us  [along(): return lax.ppermute(value, 'col', [(i, i ^ step) for i in range(cols)])]
    pallas_call x7 -> x8, Pallas kernels: 3.4 us -> 3.59 us  [call(): pl.pallas_call(kernel, out_shape=results, in_specs=[pl.BlockSpec(memory_s...]
  transfers between devices with their start and end apart: 6 -> 6, of which waited for: 2 -> 2; matrix products, arithmetic and copies ran while one was open for 0% -> 0% of each run, Pallas kernels for 16% -> 17%
where the time goes in v21:
time: 17.7 us; the launch traced here: 17.4 us
  starting transfers between devices  9.38 us (53%)
  Pallas kernels  3.59 us (20%)
  local copies, waits for them, and re-layouts  2.26 us (13%)
  waiting for transfers between devices  2.11 us (12%)
    ppermute x4, starting transfers between devices, along(): return lax.ppermute(value, 'col', [(i, i ^ step) for i in range(cols)])  7.38 us
    pallas_call x8, Pallas kernels, call(): pl.pallas_call(kernel, out_shape=results, in_specs=[pl.BlockSpec(memory_s...  3.59 us
    unnamed x22, local copies, waits for them, and re-layouts  2.26 us
    ppermute x4, waiting for transfers between devices, along(): return lax.ppermute(value, 'col', [(i, i ^ step) for i in range(cols)])  2.08 us
    ppermute x2, starting transfers between devices, across(): return lax.ppermute(value, 'row', [(i, i ^ step) for i in range(rows)])  2 us
  transfers between devices with their start and end apart: 6, of which 2 were waited for; matrix products, arithmetic and copies ran while one was open for 0% of the time, Pallas kernels for 17%

profile of v21, /device:TPU:0, one launch (start us, length us, event | category | flops | bytes accessed | tf_op | source)
XLA Modules:
  0.0 17.4 jit_solution(621753924177137582)
XLA Ops:
  0.0 4.0 %collective-permute-start = (f32[192,128]{1,0:T(8,128)}, f32[192,128]{1,0:T(8,128)S(1)}, u32[]{:S(2)}, u32[]{:S(2)}) collective-permute-start(f32[192,128]{1,0:T(8,128)} %bitcast.6), channel_id=1, source_target_pairs={{0,3},{1,2},{2,1},{3,0},{4,7},{5,6},{6,5},{7,4},{8,11},{9,10},{10,... | collective-permute-start | bytes 294920 | tf_op jit(solution)/shard_map/ppermute | solution.py:209
  4.0 0.4 %collective-permute-start.2 = (f32[192,128]{1,0:T(8,128)}, f32[192,128]{1,0:T(8,128)S(1)}, u32[]{:S(2)}, u32[]{:S(2)}) collective-permute-start(f32[192,128]{1,0:T(8,128)} %bitcast.7), channel_id=1, source_target_pairs={{0,2},{1,3},{2,0},{3,1},{4,6},{5,7},{6,4},{7,5},{8,10},{9,11},{10,... | collective-permute-start | bytes 294920 | tf_op jit(solution)/shard_map/ppermute | solution.py:209
  4.5 0.2 %collective-permute-start.1 = (f32[192,128]{1,0:T(8,128)}, f32[192,128]{1,0:T(8,128)S(1)}, u32[]{:S(2)}, u32[]{:S(2)}) collective-permute-start(f32[192,128]{1,0:T(8,128)} %bitcast.8), channel_id=1, source_target_pairs={{0,1},{1,0},{2,3},{3,2},{4,5},{5,4},{6,7},{7,6},{8,9},{9,8},{10,11... | collective-permute-start | bytes 294920 | tf_op jit(solution)/shard_map/ppermute | solution.py:209
  4.7 0.9 %copy-done = f32[3,16,4,128]{3,2,1,0:T(4,128)S(1)} copy-done((f32[3,16,4,128]{3,2,1,0:T(4,128)S(1)}, f32[3,16,4,128]{3,2,1,0:T(4,128)}, u32[]{:S(2)}) %copy-start) | copy-done | bytes 98328
  5.6 0.7 %span_matrix.1 = (f32[64,256]{1,0:T(8,128)S(1)}, f32[64,128]{1,0:T(8,128)S(1)}, f32[192,128]{1,0:T(8,128)S(1)}) custom-call(s32[4]{0:T(128)S(1)} %copy-done.4, f32[32]{0:T(128)S(1)} %copy-done.5, f32[32]{0:T(128)S(1)} %copy-done.6, f32[192,128]{1,0:T(8,128)S(1)} %bitcast.9), custom_call_target="tpu_custom_call" | custom-call | tf_op jit(solution)/shard_map/span_matrix/pallas_call | solution.py:176
  6.3 1.9 %collective-permute-start.3 = (f32[192,128]{1,0:T(8,128)S(1)}, f32[192,128]{1,0:T(8,128)S(1)}, u32[]{:S(2)}, u32[]{:S(2)}) collective-permute-start(f32[192,128]{1,0:T(8,128)S(1)} %get-tuple-element.15), channel_id=1, source_target_pairs={{0,16},{8,24},{16,0},{24,8},{1,17},{9,25},{17,1},{25,9},{2,18},{10... | collective-permute-start | bytes 294920 | tf_op jit(solution)/shard_map/ppermute | solution.py:212
  8.3 0.3 %early.1 = f32[64,768]{1,0:T(8,128)S(1)} custom-call(f32[64,256]{1,0:T(8,128)S(1)} %get-tuple-element.13.matrix, f32[192,128]{1,0:T(8,128)S(1)} %bitcast.10, f32[192,128]{1,0:T(8,128)S(1)} %collective-permute-done.refs_1_), custom_call_target="tpu_custom_call" | custom-call | tf_op jit(solution)/shard_map/early/pallas_call | solution.py:176
  8.6 0.8 %collective-permute-done.2.refs_1_ = f32[192,128]{1,0:T(8,128)S(1)} collective-permute-done((f32[192,128]{1,0:T(8,128)}, f32[192,128]{1,0:T(8,128)S(1)}, u32[]{:S(2)}, u32[]{:S(2)}) %collective-permute-start.2) | collective-permute-done | bytes 98336 | tf_op jit(solution)/shard_map/ppermute | solution.py:209
  9.4 0.3 %span.1 = (f32[192,128]{1,0:T(8,128)S(1)}, f32[192,128]{1,0:T(8,128)S(1)}) custom-call(f32[64,256]{1,0:T(8,128)S(1)} %get-tuple-element.13.matrix, f32[64,768]{1,0:T(8,128)S(1)} %early.1, f32[192,128]{1,0:T(8,128)S(1)} %collective-permute-done.1.refs_0_, f32[192,128]{1,0:T(8,128)S(1)} %collective-permute-done.2.refs_1_), custom_call_target="tpu_custom_call" | custom-call | tf_op jit(solution)/shard_map/span/pallas_call | solution.py:176
  9.7 2.7 %collective-permute-start.4 = (f32[192,128]{1,0:T(8,128)S(1)}, f32[192,128]{1,0:T(8,128)S(1)}, u32[]{:S(2)}, u32[]{:S(2)}) collective-permute-start(f32[192,128]{1,0:T(8,128)S(1)} %get-tuple-element.17), channel_id=1, source_target_pairs={{0,4},{1,5},{2,6},{3,7},{4,0},{5,1},{6,2},{7,3},{8,12},{9,13},{10,... | collective-permute-start | bytes 294920 | tf_op jit(solution)/shard_map/ppermute | solution.py:209
  12.4 0.7 %copy-done.7 = f32[128]{0:T(128)S(1)} copy-done((f32[128]{0:T(128)S(1)}, f32[128]{0:T(128)}, u32[]{:S(2)}) %copy-start.7) | copy-done | bytes 536
  13.1 0.0 copy-done.8
  13.1 0.3 %stream.1.x_part = f32[192,128]{1,0:T(8,128)S(1)} custom-call(f32[192,128]{1,0:T(8,128)S(1)} %bitcast.11, f32[1,128]{1,0:T(1,128)S(1)} %bitcast.13, f32[1,128]{1,0:T(1,128)S(1)} %bitcast.14, f32[192,128]{1,0:T(8,128)S(1)} %get-tuple-element.14.after.z_part), custom_call_target="tpu_custom_call" | custom-call | tf_op jit(solution)/shard_map/stream/pallas_call | solution.py:176
  13.4 0.0 copy-start.10
  13.4 0.4 %copy-done.2 = f32[32,32]{1,0:T(8,128)S(1)} copy-done((f32[32,32]{1,0:T(8,128)S(1)}, f32[32,32]{1,0:T(8,128)}, u32[]{:S(2)}) %copy-start.2) | copy-done | bytes 4120
  13.8 0.0 copy-done.3
  13.8 0.2 %copy-done.9 = f32[64]{0:T(128)S(1)} copy-done((f32[64]{0:T(128)S(1)}, f32[64]{0:T(128)}, u32[]{:S(2)}) %copy-start.9) | copy-done | bytes 280
  14.0 0.0 copy-done.10
  14.1 1.0 %wall_matrix.1.matrix = f32[128,256]{1,0:T(8,128)S(1)} custom-call(s32[4]{0:T(128)S(1)} %copy-done.4, f32[1,64]{1,0:T(1,128)S(1)} %bitcast.15, s32[1,32]{1,0:T(1,128)S(1)} %bitcast.16, f32[32,32]{1,0:T(8,128)S(1)} %copy-done.2, f32[32,32]{1,0:T(8,128)S(1)} %copy-done.3, f32[192,128]{1,0:T(8,128)S(1)} %get-tuple-element.14.after.z_part), custom_call_target="tpu_custom_call" | custom-call | tf_op jit(solution)/shard_map/wall_matrix/pallas_call | solution.py:176
  15.1 0.3 %wall.1 = (f32[192,128]{1,0:T(8,128)S(1)}, f32[192,128]{1,0:T(8,128)S(1)}) custom-call(f32[128,256]{1,0:T(8,128)S(1)} %wall_matrix.1.matrix, f32[192,128]{1,0:T(8,128)S(1)} %stream.1.x_part, f32[192,128]{1,0:T(8,128)S(1)} %get-tuple-element.14.after.z_part, f32[192,128]{1,0:T(8,128)S(1)} %bitcast.12, f32[192,128]{1,0:T(8,128)S(1)} %collective-permute-done.3.refs_1_), custom_call_target="tpu_custom_call" | custom-call | tf_op jit(solution)/shard_map/wall/pallas_call | solution.py:176
  15.4 0.1 collective-permute-start.5
  15.5 1.2 %collective-permute-done.4.refs_1_ = f32[192,128]{1,0:T(8,128)S(1)} collective-permute-done((f32[192,128]{1,0:T(8,128)S(1)}, f32[192,128]{1,0:T(8,128)S(1)}, u32[]{:S(2)}, u32[]{:S(2)}) %collective-permute-start.4) | collective-permute-done | bytes 98336 | tf_op jit(solution)/shard_map/ppermute | solution.py:209
  16.7 0.0 collective-permute-done.5.near
  16.8 0.7 %finish.1 = f32[192,128]{1,0:T(8,128)} custom-call(f32[192,128]{1,0:T(8,128)S(1)} %sum.1.total, f32[192,128]{1,0:T(8,128)S(1)} %collective-permute-done.5.near), custom_call_target="tpu_custom_call" | custom-call | tf_op jit(solution)/shard_map/finish/pallas_call | solution.py:176
  (18 shorter events, 0.0 us)
Async XLA Ops:
  0.0 4.7 %copy-start.4 = (s32[4]{0:T(128)S(1)}, s32[4]{0:T(128)}, u32[]{:S(2)}) copy-start(s32[4]{0:T(128)} %wall_counts.3) | copy-start | bytes 52
  0.0 4.7 %copy-start.6 = (f32[32]{0:T(128)S(1)}, f32[32]{0:T(128)}, u32[]{:S(2)}) copy-start(f32[32]{0:T(128)} %z_second.1) | copy-start | bytes 388
  0.0 4.7 %copy-start.5 = (f32[32]{0:T(128)S(1)}, f32[32]{0:T(128)}, u32[]{:S(2)}) copy-start(f32[32]{0:T(128)} %z_first.1) | copy-start | bytes 388
  0.0 8.3 %collective-permute-start = (f32[192,128]{1,0:T(8,128)}, f32[192,128]{1,0:T(8,128)S(1)}, u32[]{:S(2)}, u32[]{:S(2)}) collective-permute-start(f32[192,128]{1,0:T(8,128)} %bitcast.6), channel_id=1, source_target_pairs={{0,3},{1,2},{2,1},{3,0},{4,7},{5,6},{6,5},{7,4},{8,11},{9,10},{10,... | collective-permute-start | bytes 294920 | tf_op jit(solution)/shard_map/ppermute | solution.py:209
  4.0 5.4 %collective-permute-start.2 = (f32[192,128]{1,0:T(8,128)}, f32[192,128]{1,0:T(8,128)S(1)}, u32[]{:S(2)}, u32[]{:S(2)}) collective-permute-start(f32[192,128]{1,0:T(8,128)} %bitcast.7), channel_id=1, source_target_pairs={{0,2},{1,3},{2,0},{3,1},{4,6},{5,7},{6,4},{7,5},{8,10},{9,11},{10,... | collective-permute-start | bytes 294920 | tf_op jit(solution)/shard_map/ppermute | solution.py:209
  4.5 4.9 %collective-permute-start.1 = (f32[192,128]{1,0:T(8,128)}, f32[192,128]{1,0:T(8,128)S(1)}, u32[]{:S(2)}, u32[]{:S(2)}) collective-permute-start(f32[192,128]{1,0:T(8,128)} %bitcast.8), channel_id=1, source_target_pairs={{0,1},{1,0},{2,3},{3,2},{4,5},{5,4},{6,7},{7,6},{8,9},{9,8},{10,11... | collective-permute-start | bytes 294920 | tf_op jit(solution)/shard_map/ppermute | solution.py:209
  4.7 0.9 %copy-start = (f32[3,16,4,128]{3,2,1,0:T(4,128)S(1)}, f32[3,16,4,128]{3,2,1,0:T(4,128)}, u32[]{:S(2)}) copy-start(f32[3,16,4,128]{3,2,1,0:T(4,128)} %param.10) | copy-start | bytes 294916
  5.6 2.7 %copy-start.1 = (f32[3,16,4,128]{3,2,1,0:T(4,128)S(1)}, f32[3,16,4,128]{3,2,1,0:T(4,128)}, u32[]{:S(2)}) copy-start(f32[3,16,4,128]{3,2,1,0:T(4,128)} %param.10) | copy-start | bytes 294916
  6.3 8.8 %collective-permute-start.3 = (f32[192,128]{1,0:T(8,128)S(1)}, f32[192,128]{1,0:T(8,128)S(1)}, u32[]{:S(2)}, u32[]{:S(2)}) collective-permute-start(f32[192,128]{1,0:T(8,128)S(1)} %get-tuple-element.15), channel_id=1, source_target_pairs={{0,16},{8,24},{16,0},{24,8},{1,17},{9,25},{17,1},{25,9},{2,18},{10... | collective-permute-start | bytes 294920 | tf_op jit(solution)/shard_map/ppermute | solution.py:212
  9.7 7.1 %collective-permute-start.4 = (f32[192,128]{1,0:T(8,128)S(1)}, f32[192,128]{1,0:T(8,128)S(1)}, u32[]{:S(2)}, u32[]{:S(2)}) collective-permute-start(f32[192,128]{1,0:T(8,128)S(1)} %get-tuple-element.17), channel_id=1, source_target_pairs={{0,4},{1,5},{2,6},{3,7},{4,0},{5,1},{6,2},{7,3},{8,12},{9,13},{10,... | collective-permute-start | bytes 294920 | tf_op jit(solution)/shard_map/ppermute | solution.py:209
  12.4 0.7 %copy-start.7 = (f32[128]{0:T(128)S(1)}, f32[128]{0:T(128)}, u32[]{:S(2)}) copy-start(f32[128]{0:T(128)} %param.12) | copy-start | bytes 1540
  12.4 0.7 %copy-start.8 = (f32[128]{0:T(128)S(1)}, f32[128]{0:T(128)}, u32[]{:S(2)}) copy-start(f32[128]{0:T(128)} %param.13) | copy-start | bytes 1540
  13.1 0.7 %copy-start.2 = (f32[32,32]{1,0:T(8,128)S(1)}, f32[32,32]{1,0:T(8,128)}, u32[]{:S(2)}) copy-start(f32[32,32]{1,0:T(8,128)} %y_first.1) | copy-start | bytes 12292
  13.1 0.7 %copy-start.3 = (f32[32,32]{1,0:T(8,128)S(1)}, f32[32,32]{1,0:T(8,128)}, u32[]{:S(2)}) copy-start(f32[32,32]{1,0:T(8,128)} %y_second.1) | copy-start | bytes 12292
  13.4 0.7 %copy-start.9 = (f32[64]{0:T(128)S(1)}, f32[64]{0:T(128)}, u32[]{:S(2)}) copy-start(f32[64]{0:T(128)} %param.18) | copy-start | bytes 772
  13.4 0.7 %copy-start.10 = (s32[32]{0:T(128)S(1)}, s32[32]{0:T(128)}, u32[]{:S(2)}) copy-start(s32[32]{0:T(128)} %param.19) | copy-start | bytes 388
  15.4 1.4 %collective-permute-start.5 = (f32[192,128]{1,0:T(8,128)S(1)}, f32[192,128]{1,0:T(8,128)S(1)}, u32[]{:S(2)}, u32[]{:S(2)}) collective-permute-start(f32[192,128]{1,0:T(8,128)S(1)} %get-tuple-element.18), channel_id=1, source_target_pairs={{0,8},{8,0},{16,24},{24,16},{1,9},{9,1},{17,25},{25,17},{2,10},{10... | collective-permute-start | bytes 294920 | tf_op jit(solution)/shard_map/ppermute | solution.py:212

commit v22 on v21

--- a/solution.py
+++ b/solution.py
@@ -228,8 +228,8 @@
         "early",
     )
     parts = call(
-        functools.partial(span_kernel, comps, tuple(range(1, quad - 1))),
-        [z_matrix, early] + gathered[:-1],
+        functools.partial(span_kernel, comps, tuple(range(quad - 2, 0, -1))),
+        [z_matrix, early] + gathered[-2::-1],
         [VMEM] * quad,
         [field.shape] * wide,
         "span",

time: 17.7 us -> 18.1 us (1.023)
  waiting for transfers between devices: 2.11 us -> 2.62 us
    ppermute x4, waiting for transfers between devices: 2.08 us -> 2.62 us  [along(): return lax.ppermute(value, 'col', [(i, i ^ step) for i in range(cols)])]
  transfers between devices with their start and end apart: 6 -> 6, of which waited for: 2 -> 3; matrix products, arithmetic and copies ran while one was open for 0% -> 0% of each run, Pallas kernels for 17% -> 16%
where the time goes in v22:
time: 18.1 us; the launch traced here: 17.9 us
  starting transfers between devices  9.32 us (51%)
  Pallas kernels  3.6 us (20%)
  waiting for transfers between devices  2.62 us (14%)
  local copies, waits for them, and re-layouts  2.26 us (12%)
    ppermute x4, starting transfers between devices, along(): return lax.ppermute(value, 'col', [(i, i ^ step) for i in range(cols)])  7.32 us
    pallas_call x8, Pallas kernels, call(): pl.pallas_call(kernel, out_shape=results, in_specs=[pl.BlockSpec(memory_s...  3.6 us
    ppermute x4, waiting for transfers between devices, along(): return lax.ppermute(value, 'col', [(i, i ^ step) for i in range(cols)])  2.62 us
    unnamed x22, local copies, waits for them, and re-layouts  2.26 us
    ppermute x2, starting transfers between devices, across(): return lax.ppermute(value, 'row', [(i, i ^ step) for i in range(rows)])  2 us
  transfers between devices with their start and end apart: 6, of which 3 were waited for; matrix products, arithmetic and copies ran while one was open for 0% of the time, Pallas kernels for 16%

profile of v22, /device:TPU:0, one launch (start us, length us, event | category | flops | bytes accessed | tf_op | source)
XLA Modules:
  0.0 17.9 jit_solution(12967967150432268412)
XLA Ops:
  0.0 4.0 %collective-permute-start = (f32[192,128]{1,0:T(8,128)}, f32[192,128]{1,0:T(8,128)S(1)}, u32[]{:S(2)}, u32[]{:S(2)}) collective-permute-start(f32[192,128]{1,0:T(8,128)} %bitcast.6), channel_id=1, source_target_pairs={{0,3},{1,2},{2,1},{3,0},{4,7},{5,6},{6,5},{7,4},{8,11},{9,10},{10,... | collective-permute-start | bytes 294920 | tf_op jit(solution)/shard_map/ppermute | solution.py:209
  4.0 0.5 %collective-permute-start.2 = (f32[192,128]{1,0:T(8,128)}, f32[192,128]{1,0:T(8,128)S(1)}, u32[]{:S(2)}, u32[]{:S(2)}) collective-permute-start(f32[192,128]{1,0:T(8,128)} %bitcast.7), channel_id=1, source_target_pairs={{0,1},{1,0},{2,3},{3,2},{4,5},{5,4},{6,7},{7,6},{8,9},{9,8},{10,11... | collective-permute-start | bytes 294920 | tf_op jit(solution)/shard_map/ppermute | solution.py:209
  4.6 0.1 collective-permute-start.1
  4.7 0.9 %copy-done = f32[3,16,4,128]{3,2,1,0:T(4,128)S(1)} copy-done((f32[3,16,4,128]{3,2,1,0:T(4,128)S(1)}, f32[3,16,4,128]{3,2,1,0:T(4,128)}, u32[]{:S(2)}) %copy-start) | copy-done | bytes 98328
  5.6 0.7 %span_matrix.1 = (f32[64,256]{1,0:T(8,128)S(1)}, f32[64,128]{1,0:T(8,128)S(1)}, f32[192,128]{1,0:T(8,128)S(1)}) custom-call(s32[4]{0:T(128)S(1)} %copy-done.4, f32[32]{0:T(128)S(1)} %copy-done.5, f32[32]{0:T(128)S(1)} %copy-done.6, f32[192,128]{1,0:T(8,128)S(1)} %bitcast.9), custom_call_target="tpu_custom_call" | custom-call | tf_op jit(solution)/shard_map/span_matrix/pallas_call | solution.py:176
  6.3 1.9 %collective-permute-start.3 = (f32[192,128]{1,0:T(8,128)S(1)}, f32[192,128]{1,0:T(8,128)S(1)}, u32[]{:S(2)}, u32[]{:S(2)}) collective-permute-start(f32[192,128]{1,0:T(8,128)S(1)} %get-tuple-element.15), channel_id=1, source_target_pairs={{0,16},{8,24},{16,0},{24,8},{1,17},{9,25},{17,1},{25,9},{2,18},{10... | collective-permute-start | bytes 294920 | tf_op jit(solution)/shard_map/ppermute | solution.py:212
  8.3 0.3 %early.1 = f32[64,768]{1,0:T(8,128)S(1)} custom-call(f32[64,256]{1,0:T(8,128)S(1)} %get-tuple-element.13.matrix, f32[192,128]{1,0:T(8,128)S(1)} %bitcast.10, f32[192,128]{1,0:T(8,128)S(1)} %collective-permute-done.refs_1_), custom_call_target="tpu_custom_call" | custom-call | tf_op jit(solution)/shard_map/early/pallas_call | solution.py:176
  8.6 0.6 %collective-permute-done.2.refs_1_ = f32[192,128]{1,0:T(8,128)S(1)} collective-permute-done((f32[192,128]{1,0:T(8,128)}, f32[192,128]{1,0:T(8,128)S(1)}, u32[]{:S(2)}, u32[]{:S(2)}) %collective-permute-start.2) | collective-permute-done | bytes 98336 | tf_op jit(solution)/shard_map/ppermute | solution.py:209
  9.1 0.3 %collective-permute-done.1.refs_0_ = f32[192,128]{1,0:T(8,128)S(1)} collective-permute-done((f32[192,128]{1,0:T(8,128)}, f32[192,128]{1,0:T(8,128)S(1)}, u32[]{:S(2)}, u32[]{:S(2)}) %collective-permute-start.1) | collective-permute-done | bytes 98336 | tf_op jit(solution)/shard_map/ppermute | solution.py:209
  9.4 0.3 %span.1 = (f32[192,128]{1,0:T(8,128)S(1)}, f32[192,128]{1,0:T(8,128)S(1)}) custom-call(f32[64,256]{1,0:T(8,128)S(1)} %get-tuple-element.13.matrix, f32[64,768]{1,0:T(8,128)S(1)} %early.1, f32[192,128]{1,0:T(8,128)S(1)} %collective-permute-done.1.refs_0_, f32[192,128]{1,0:T(8,128)S(1)} %collective-permute-done.2.refs_1_), custom_call_target="tpu_custom_call" | custom-call | tf_op jit(solution)/shard_map/span/pallas_call | solution.py:176
  9.7 2.7 %collective-permute-start.4 = (f32[192,128]{1,0:T(8,128)S(1)}, f32[192,128]{1,0:T(8,128)S(1)}, u32[]{:S(2)}, u32[]{:S(2)}) collective-permute-start(f32[192,128]{1,0:T(8,128)S(1)} %get-tuple-element.17), channel_id=1, source_target_pairs={{0,4},{1,5},{2,6},{3,7},{4,0},{5,1},{6,2},{7,3},{8,12},{9,13},{10,... | collective-permute-start | bytes 294920 | tf_op jit(solution)/shard_map/ppermute | solution.py:209
  12.3 0.7 %copy-done.7 = f32[128]{0:T(128)S(1)} copy-done((f32[128]{0:T(128)S(1)}, f32[128]{0:T(128)}, u32[]{:S(2)}) %copy-start.7) | copy-done | bytes 536
  13.0 0.0 copy-done.8
  13.0 0.3 %stream.1.x_part = f32[192,128]{1,0:T(8,128)S(1)} custom-call(f32[192,128]{1,0:T(8,128)S(1)} %bitcast.11, f32[1,128]{1,0:T(1,128)S(1)} %bitcast.13, f32[1,128]{1,0:T(1,128)S(1)} %bitcast.14, f32[192,128]{1,0:T(8,128)S(1)} %get-tuple-element.14.after.z_part), custom_call_target="tpu_custom_call" | custom-call | tf_op jit(solution)/shard_map/stream/pallas_call | solution.py:176
  13.3 0.0 copy-start.10
  13.4 0.4 %copy-done.2 = f32[32,32]{1,0:T(8,128)S(1)} copy-done((f32[32,32]{1,0:T(8,128)S(1)}, f32[32,32]{1,0:T(8,128)}, u32[]{:S(2)}) %copy-start.2) | copy-done | bytes 4120
  13.7 0.0 copy-done.3
  13.8 0.2 %copy-done.9 = f32[64]{0:T(128)S(1)} copy-done((f32[64]{0:T(128)S(1)}, f32[64]{0:T(128)}, u32[]{:S(2)}) %copy-start.9) | copy-done | bytes 280
  14.0 0.0 copy-done.10
  14.0 1.0 %wall_matrix.1.matrix = f32[128,256]{1,0:T(8,128)S(1)} custom-call(s32[4]{0:T(128)S(1)} %copy-done.4, f32[1,64]{1,0:T(1,128)S(1)} %bitcast.15, s32[1,32]{1,0:T(1,128)S(1)} %bitcast.16, f32[32,32]{1,0:T(8,128)S(1)} %copy-done.2, f32[32,32]{1,0:T(8,128)S(1)} %copy-done.3, f32[192,128]{1,0:T(8,128)S(1)} %get-tuple-element.14.after.z_part), custom_call_target="tpu_custom_call" | custom-call | tf_op jit(solution)/shard_map/wall_matrix/pallas_call | solution.py:176
  15.0 0.3 %wall.1 = (f32[192,128]{1,0:T(8,128)S(1)}, f32[192,128]{1,0:T(8,128)S(1)}) custom-call(f32[128,256]{1,0:T(8,128)S(1)} %wall_matrix.1.matrix, f32[192,128]{1,0:T(8,128)S(1)} %stream.1.x_part, f32[192,128]{1,0:T(8,128)S(1)} %get-tuple-element.14.after.z_part, f32[192,128]{1,0:T(8,128)S(1)} %bitcast.12, f32[192,128]{1,0:T(8,128)S(1)} %collective-permute-done.3.refs_1_), custom_call_target="tpu_custom_call" | custom-call | tf_op jit(solution)/shard_map/wall/pallas_call | solution.py:176
  15.4 0.1 collective-permute-start.5
  15.4 1.8 %collective-permute-done.4.refs_1_ = f32[192,128]{1,0:T(8,128)S(1)} collective-permute-done((f32[192,128]{1,0:T(8,128)S(1)}, f32[192,128]{1,0:T(8,128)S(1)}, u32[]{:S(2)}, u32[]{:S(2)}) %collective-permute-start.4) | collective-permute-done | bytes 98336 | tf_op jit(solution)/shard_map/ppermute | solution.py:209
  17.2 0.7 %finish.1 = f32[192,128]{1,0:T(8,128)} custom-call(f32[192,128]{1,0:T(8,128)S(1)} %sum.1.total, f32[192,128]{1,0:T(8,128)S(1)} %collective-permute-done.5.near), custom_call_target="tpu_custom_call" | custom-call | tf_op jit(solution)/shard_map/finish/pallas_call | solution.py:176
  (18 shorter events, 0.0 us)
Async XLA Ops:
  0.0 4.7 %copy-start.4 = (s32[4]{0:T(128)S(1)}, s32[4]{0:T(128)}, u32[]{:S(2)}) copy-start(s32[4]{0:T(128)} %wall_counts.3) | copy-start | bytes 52
  0.0 4.7 %copy-start.6 = (f32[32]{0:T(128)S(1)}, f32[32]{0:T(128)}, u32[]{:S(2)}) copy-start(f32[32]{0:T(128)} %z_second.1) | copy-start | bytes 388
  0.0 4.7 %copy-start.5 = (f32[32]{0:T(128)S(1)}, f32[32]{0:T(128)}, u32[]{:S(2)}) copy-start(f32[32]{0:T(128)} %z_first.1) | copy-start | bytes 388
  0.0 8.3 %collective-permute-start = (f32[192,128]{1,0:T(8,128)}, f32[192,128]{1,0:T(8,128)S(1)}, u32[]{:S(2)}, u32[]{:S(2)}) collective-permute-start(f32[192,128]{1,0:T(8,128)} %bitcast.6), channel_id=1, source_target_pairs={{0,3},{1,2},{2,1},{3,0},{4,7},{5,6},{6,5},{7,4},{8,11},{9,10},{10,... | collective-permute-start | bytes 294920 | tf_op jit(solution)/shard_map/ppermute | solution.py:209
  4.0 5.1 %collective-permute-start.2 = (f32[192,128]{1,0:T(8,128)}, f32[192,128]{1,0:T(8,128)S(1)}, u32[]{:S(2)}, u32[]{:S(2)}) collective-permute-start(f32[192,128]{1,0:T(8,128)} %bitcast.7), channel_id=1, source_target_pairs={{0,1},{1,0},{2,3},{3,2},{4,5},{5,4},{6,7},{7,6},{8,9},{9,8},{10,11... | collective-permute-start | bytes 294920 | tf_op jit(solution)/shard_map/ppermute | solution.py:209
  4.6 4.8 %collective-permute-start.1 = (f32[192,128]{1,0:T(8,128)}, f32[192,128]{1,0:T(8,128)S(1)}, u32[]{:S(2)}, u32[]{:S(2)}) collective-permute-start(f32[192,128]{1,0:T(8,128)} %bitcast.8), channel_id=1, source_target_pairs={{0,2},{1,3},{2,0},{3,1},{4,6},{5,7},{6,4},{7,5},{8,10},{9,11},{10,... | collective-permute-start | bytes 294920 | tf_op jit(solution)/shard_map/ppermute | solution.py:209
  4.7 0.9 %copy-start = (f32[3,16,4,128]{3,2,1,0:T(4,128)S(1)}, f32[3,16,4,128]{3,2,1,0:T(4,128)}, u32[]{:S(2)}) copy-start(f32[3,16,4,128]{3,2,1,0:T(4,128)} %param.10) | copy-start | bytes 294916
  5.6 2.7 %copy-start.1 = (f32[3,16,4,128]{3,2,1,0:T(4,128)S(1)}, f32[3,16,4,128]{3,2,1,0:T(4,128)}, u32[]{:S(2)}) copy-start(f32[3,16,4,128]{3,2,1,0:T(4,128)} %param.10) | copy-start | bytes 294916
  6.3 8.7 %collective-permute-start.3 = (f32[192,128]{1,0:T(8,128)S(1)}, f32[192,128]{1,0:T(8,128)S(1)}, u32[]{:S(2)}, u32[]{:S(2)}) collective-permute-start(f32[192,128]{1,0:T(8,128)S(1)} %get-tuple-element.15), channel_id=1, source_target_pairs={{0,16},{8,24},{16,0},{24,8},{1,17},{9,25},{17,1},{25,9},{2,18},{10... | collective-permute-start | bytes 294920 | tf_op jit(solution)/shard_map/ppermute | solution.py:212
  9.7 7.5 %collective-permute-start.4 = (f32[192,128]{1,0:T(8,128)S(1)}, f32[192,128]{1,0:T(8,128)S(1)}, u32[]{:S(2)}, u32[]{:S(2)}) collective-permute-start(f32[192,128]{1,0:T(8,128)S(1)} %get-tuple-element.17), channel_id=1, source_target_pairs={{0,4},{1,5},{2,6},{3,7},{4,0},{5,1},{6,2},{7,3},{8,12},{9,13},{10,... | collective-permute-start | bytes 294920 | tf_op jit(solution)/shard_map/ppermute | solution.py:209
  12.3 0.7 %copy-start.7 = (f32[128]{0:T(128)S(1)}, f32[128]{0:T(128)}, u32[]{:S(2)}) copy-start(f32[128]{0:T(128)} %param.12) | copy-start | bytes 1540
  12.3 0.7 %copy-start.8 = (f32[128]{0:T(128)S(1)}, f32[128]{0:T(128)}, u32[]{:S(2)}) copy-start(f32[128]{0:T(128)} %param.13) | copy-start | bytes 1540
  13.0 0.7 %copy-start.2 = (f32[32,32]{1,0:T(8,128)S(1)}, f32[32,32]{1,0:T(8,128)}, u32[]{:S(2)}) copy-start(f32[32,32]{1,0:T(8,128)} %y_first.1) | copy-start | bytes 12292
  13.0 0.7 %copy-start.3 = (f32[32,32]{1,0:T(8,128)S(1)}, f32[32,32]{1,0:T(8,128)}, u32[]{:S(2)}) copy-start(f32[32,32]{1,0:T(8,128)} %y_second.1) | copy-start | bytes 12292
  13.3 0.7 %copy-start.9 = (f32[64]{0:T(128)S(1)}, f32[64]{0:T(128)}, u32[]{:S(2)}) copy-start(f32[64]{0:T(128)} %param.18) | copy-start | bytes 772
  13.3 0.7 %copy-start.10 = (s32[32]{0:T(128)S(1)}, s32[32]{0:T(128)}, u32[]{:S(2)}) copy-start(s32[32]{0:T(128)} %param.19) | copy-start | bytes 388
  15.4 1.9 %collective-permute-start.5 = (f32[192,128]{1,0:T(8,128)S(1)}, f32[192,128]{1,0:T(8,128)S(1)}, u32[]{:S(2)}, u32[]{:S(2)}) collective-permute-start(f32[192,128]{1,0:T(8,128)S(1)} %get-tuple-element.18), channel_id=1, source_target_pairs={{0,8},{8,0},{16,24},{24,16},{1,9},{9,1},{17,25},{25,17},{2,10},{10... | collective-permute-start | bytes 294920 | tf_op jit(solution)/shard_map/ppermute | solution.py:212

commit v23 on v21

--- a/solution.py
+++ b/solution.py
@@ -29,6 +29,10 @@
     both = mul(jnp.concatenate([lh, ll], axis=0), rh)
     count = left.shape[0]
     return both[:count] + (mul(lh, rl) + both[count:])
+
+
+def over(t):
+    return quad * t + 2 * (t != 0)
 
 
 def quad_sums(comps, matrix, fields, chosen):
@@ -81,7 +85,7 @@
     r = lax.broadcasted_iota(jnp.int32, shape, 0)
     q = lax.broadcasted_iota(jnp.int32, shape, 1)
     q = jnp.where(q < half, q, q - half)
-    out_cell = ((quad * (r // group)) ^ mine) * zloc + r % zloc
+    out_cell = (over(r // group) ^ mine) * zloc + r % zloc
     in_cell = ((q // group) ^ mine) * zloc + q % zloc
     same = (r % group) // zloc == (q % group) // zloc
     gap = jnp.where(same, (in_cell - out_cell + cells_z) % cells_z, -1)
@@ -234,7 +238,7 @@
         [field.shape] * wide,
         "span",
     )
-    returned = [along(parts[t], quad * t) for t in range(1, wide)]
+    returned = [along(parts[t], over(t)) for t in range(1, wide)]
     (x_part,) = call(
         functools.partial(stream_kernel, comps),
         [field, x_first.reshape(1, length), x_second.reshape(1, length), parts[0]],

time: 17.7 us -> 18.8 us (1.062)
  starting transfers between devices: 9.38 us -> 10.5 us
    ppermute x4, waiting for transfers between devices: 2.08 us -> 0.83 us  [along(): return lax.ppermute(value, 'col', [(i, i ^ step) for i in range(cols)])]
    ppermute x2, waiting for transfers between devices: 0.03 us -> 1.26 us  [across(): return lax.ppermute(value, 'row', [(i, i ^ step) for i in range(rows)])]
    ppermute x4, starting transfers between devices: 7.38 us -> 8.48 us  [along(): return lax.ppermute(value, 'col', [(i, i ^ step) for i in range(cols)])]
  transfers between devices with their start and end apart: 6 -> 6, of which waited for: 2 -> 2; matrix products, arithmetic and copies ran while one was open for 0% -> 0% of each run, Pallas kernels for 17% -> 16%
where the time goes in v23:
time: 18.8 us; the launch traced here: 18.5 us
  starting transfers between devices  10.5 us (56%)
  Pallas kernels  3.6 us (19%)
  local copies, waits for them, and re-layouts  2.26 us (12%)
  waiting for transfers between devices  2.09 us (11%)
    ppermute x4, starting transfers between devices, along(): return lax.ppermute(value, 'col', [(i, i ^ step) for i in range(cols)])  8.48 us
    pallas_call x8, Pallas kernels, call(): pl.pallas_call(kernel, out_shape=results, in_specs=[pl.BlockSpec(memory_s...  3.6 us
    unnamed x22, local copies, waits for them, and re-layouts  2.26 us
    ppermute x2, starting transfers between devices, across(): return lax.ppermute(value, 'row', [(i, i ^ step) for i in range(rows)])  2 us
    ppermute x2, waiting for transfers between devices, across(): return lax.ppermute(value, 'row', [(i, i ^ step) for i in range(rows)])  1.26 us
    ppermute x4, waiting for transfers between devices, along(): return lax.ppermute(value, 'col', [(i, i ^ step) for i in range(cols)])  0.83 us
  transfers between devices with their start and end apart: 6, of which 2 were waited for; matrix products, arithmetic and copies ran while one was open for 0% of the time, Pallas kernels for 16%

profile of v23, /device:TPU:0, one launch (start us, length us, event | category | flops | bytes accessed | tf_op | source)
XLA Modules:
  0.0 18.5 jit_solution(7570688785862675903)
XLA Ops:
  0.0 4.0 %collective-permute-start = (f32[192,128]{1,0:T(8,128)}, f32[192,128]{1,0:T(8,128)S(1)}, u32[]{:S(2)}, u32[]{:S(2)}) collective-permute-start(f32[192,128]{1,0:T(8,128)} %bitcast.6), channel_id=1, source_target_pairs={{0,3},{1,2},{2,1},{3,0},{4,7},{5,6},{6,5},{7,4},{8,11},{9,10},{10,... | collective-permute-start | bytes 294920 | tf_op jit(solution)/shard_map/ppermute | solution.py:213
  4.0 0.4 %collective-permute-start.2 = (f32[192,128]{1,0:T(8,128)}, f32[192,128]{1,0:T(8,128)S(1)}, u32[]{:S(2)}, u32[]{:S(2)}) collective-permute-start(f32[192,128]{1,0:T(8,128)} %bitcast.7), channel_id=1, source_target_pairs={{0,2},{1,3},{2,0},{3,1},{4,6},{5,7},{6,4},{7,5},{8,10},{9,11},{10,... | collective-permute-start | bytes 294920 | tf_op jit(solution)/shard_map/ppermute | solution.py:213
  4.5 0.2 %collective-permute-start.1 = (f32[192,128]{1,0:T(8,128)}, f32[192,128]{1,0:T(8,128)S(1)}, u32[]{:S(2)}, u32[]{:S(2)}) collective-permute-start(f32[192,128]{1,0:T(8,128)} %bitcast.8), channel_id=1, source_target_pairs={{0,1},{1,0},{2,3},{3,2},{4,5},{5,4},{6,7},{7,6},{8,9},{9,8},{10,11... | collective-permute-start | bytes 294920 | tf_op jit(solution)/shard_map/ppermute | solution.py:213
  4.7 0.9 %copy-done = f32[3,16,4,128]{3,2,1,0:T(4,128)S(1)} copy-done((f32[3,16,4,128]{3,2,1,0:T(4,128)S(1)}, f32[3,16,4,128]{3,2,1,0:T(4,128)}, u32[]{:S(2)}) %copy-start) | copy-done | bytes 98328
  5.6 0.7 %span_matrix.1 = (f32[64,256]{1,0:T(8,128)S(1)}, f32[64,128]{1,0:T(8,128)S(1)}, f32[192,128]{1,0:T(8,128)S(1)}) custom-call(s32[4]{0:T(128)S(1)} %copy-done.4, f32[32]{0:T(128)S(1)} %copy-done.5, f32[32]{0:T(128)S(1)} %copy-done.6, f32[192,128]{1,0:T(8,128)S(1)} %bitcast.9), custom_call_target="tpu_custom_call" | custom-call | tf_op jit(solution)/shard_map/span_matrix/pallas_call | solution.py:180
  6.3 1.9 %collective-permute-start.3 = (f32[192,128]{1,0:T(8,128)S(1)}, f32[192,128]{1,0:T(8,128)S(1)}, u32[]{:S(2)}, u32[]{:S(2)}) collective-permute-start(f32[192,128]{1,0:T(8,128)S(1)} %get-tuple-element.15), channel_id=1, source_target_pairs={{0,16},{8,24},{16,0},{24,8},{1,17},{9,25},{17,1},{25,9},{2,18},{10... | collective-permute-start | bytes 294920 | tf_op jit(solution)/shard_map/ppermute | solution.py:216
  8.3 0.3 %early.1 = f32[64,768]{1,0:T(8,128)S(1)} custom-call(f32[64,256]{1,0:T(8,128)S(1)} %get-tuple-element.13.matrix, f32[192,128]{1,0:T(8,128)S(1)} %bitcast.10, f32[192,128]{1,0:T(8,128)S(1)} %collective-permute-done.refs_1_), custom_call_target="tpu_custom_call" | custom-call | tf_op jit(solution)/shard_map/early/pallas_call | solution.py:180
  8.6 0.8 %collective-permute-done.2.refs_1_ = f32[192,128]{1,0:T(8,128)S(1)} collective-permute-done((f32[192,128]{1,0:T(8,128)}, f32[192,128]{1,0:T(8,128)S(1)}, u32[]{:S(2)}, u32[]{:S(2)}) %collective-permute-start.2) | collective-permute-done | bytes 98336 | tf_op jit(solution)/shard_map/ppermute | solution.py:213
  9.4 0.3 %span.1 = (f32[192,128]{1,0:T(8,128)S(1)}, f32[192,128]{1,0:T(8,128)S(1)}) custom-call(f32[64,256]{1,0:T(8,128)S(1)} %get-tuple-element.13.matrix, f32[64,768]{1,0:T(8,128)S(1)} %early.1, f32[192,128]{1,0:T(8,128)S(1)} %collective-permute-done.1.refs_0_, f32[192,128]{1,0:T(8,128)S(1)} %collective-permute-done.2.refs_1_), custom_call_target="tpu_custom_call" | custom-call | tf_op jit(solution)/shard_map/span/pallas_call | solution.py:180
  9.7 3.8 %collective-permute-start.4 = (f32[192,128]{1,0:T(8,128)S(1)}, f32[192,128]{1,0:T(8,128)S(1)}, u32[]{:S(2)}, u32[]{:S(2)}) collective-permute-start(f32[192,128]{1,0:T(8,128)S(1)} %get-tuple-element.17), channel_id=1, source_target_pairs={{0,6},{1,7},{2,4},{3,5},{4,2},{5,3},{6,0},{7,1},{8,14},{9,15},{10,... | collective-permute-start | bytes 294920 | tf_op jit(solution)/shard_map/ppermute | solution.py:213
  13.5 0.7 %copy-done.7 = f32[128]{0:T(128)S(1)} copy-done((f32[128]{0:T(128)S(1)}, f32[128]{0:T(128)}, u32[]{:S(2)}) %copy-start.7) | copy-done | bytes 536
  14.2 0.0 copy-done.8
  14.2 0.3 %stream.1.x_part = f32[192,128]{1,0:T(8,128)S(1)} custom-call(f32[192,128]{1,0:T(8,128)S(1)} %bitcast.11, f32[1,128]{1,0:T(1,128)S(1)} %bitcast.13, f32[1,128]{1,0:T(1,128)S(1)} %bitcast.14, f32[192,128]{1,0:T(8,128)S(1)} %get-tuple-element.14.after.z_part), custom_call_target="tpu_custom_call" | custom-call | tf_op jit(solution)/shard_map/stream/pallas_call | solution.py:180
  14.5 0.0 copy-start.9
  14.5 0.0 copy-start.10
  14.5 0.4 %copy-done.2 = f32[32,32]{1,0:T(8,128)S(1)} copy-done((f32[32,32]{1,0:T(8,128)S(1)}, f32[32,32]{1,0:T(8,128)}, u32[]{:S(2)}) %copy-start.2) | copy-done | bytes 4120
  14.9 0.0 copy-done.3
  14.9 0.2 %copy-done.9 = f32[64]{0:T(128)S(1)} copy-done((f32[64]{0:T(128)S(1)}, f32[64]{0:T(128)}, u32[]{:S(2)}) %copy-start.9) | copy-done | bytes 280
  15.1 0.0 copy-done.10
  15.2 1.0 %wall_matrix.1.matrix = f32[128,256]{1,0:T(8,128)S(1)} custom-call(s32[4]{0:T(128)S(1)} %copy-done.4, f32[1,64]{1,0:T(1,128)S(1)} %bitcast.15, s32[1,32]{1,0:T(1,128)S(1)} %bitcast.16, f32[32,32]{1,0:T(8,128)S(1)} %copy-done.2, f32[32,32]{1,0:T(8,128)S(1)} %copy-done.3, f32[192,128]{1,0:T(8,128)S(1)} %get-tuple-element.14.after.z_part), custom_call_target="tpu_custom_call" | custom-call | tf_op jit(solution)/shard_map/wall_matrix/pallas_call | solution.py:180
  16.2 0.3 %wall.1 = (f32[192,128]{1,0:T(8,128)S(1)}, f32[192,128]{1,0:T(8,128)S(1)}) custom-call(f32[128,256]{1,0:T(8,128)S(1)} %wall_matrix.1.matrix, f32[192,128]{1,0:T(8,128)S(1)} %stream.1.x_part, f32[192,128]{1,0:T(8,128)S(1)} %get-tuple-element.14.after.z_part, f32[192,128]{1,0:T(8,128)S(1)} %bitcast.12, f32[192,128]{1,0:T(8,128)S(1)} %collective-permute-done.3.refs_1_), custom_call_target="tpu_custom_call" | custom-call | tf_op jit(solution)/shard_map/wall/pallas_call | solution.py:180
  16.5 0.1 collective-permute-start.5
  16.6 1.3 %collective-permute-done.5.near = f32[192,128]{1,0:T(8,128)S(1)} collective-permute-done((f32[192,128]{1,0:T(8,128)S(1)}, f32[192,128]{1,0:T(8,128)S(1)}, u32[]{:S(2)}, u32[]{:S(2)}) %collective-permute-start.5) | collective-permute-done | bytes 98336 | tf_op jit(solution)/shard_map/ppermute | solution.py:216
  17.9 0.7 %finish.1 = f32[192,128]{1,0:T(8,128)} custom-call(f32[192,128]{1,0:T(8,128)S(1)} %sum.1.total, f32[192,128]{1,0:T(8,128)S(1)} %collective-permute-done.5.near), custom_call_target="tpu_custom_call" | custom-call | tf_op jit(solution)/shard_map/finish/pallas_call | solution.py:180
  (18 shorter events, 0.0 us)
Async XLA Ops:
  0.0 4.7 %copy-start.4 = (s32[4]{0:T(128)S(1)}, s32[4]{0:T(128)}, u32[]{:S(2)}) copy-start(s32[4]{0:T(128)} %wall_counts.3) | copy-start | bytes 52
  0.0 4.7 %copy-start.6 = (f32[32]{0:T(128)S(1)}, f32[32]{0:T(128)}, u32[]{:S(2)}) copy-start(f32[32]{0:T(128)} %z_second.1) | copy-start | bytes 388
  0.0 4.7 %copy-start.5 = (f32[32]{0:T(128)S(1)}, f32[32]{0:T(128)}, u32[]{:S(2)}) copy-start(f32[32]{0:T(128)} %z_first.1) | copy-start | bytes 388
  0.0 8.3 %collective-permute-start = (f32[192,128]{1,0:T(8,128)}, f32[192,128]{1,0:T(8,128)S(1)}, u32[]{:S(2)}, u32[]{:S(2)}) collective-permute-start(f32[192,128]{1,0:T(8,128)} %bitcast.6), channel_id=1, source_target_pairs={{0,3},{1,2},{2,1},{3,0},{4,7},{5,6},{6,5},{7,4},{8,11},{9,10},{10,... | collective-permute-start | bytes 294920 | tf_op jit(solution)/shard_map/ppermute | solution.py:213
  4.0 5.4 %collective-permute-start.2 = (f32[192,128]{1,0:T(8,128)}, f32[192,128]{1,0:T(8,128)S(1)}, u32[]{:S(2)}, u32[]{:S(2)}) collective-permute-start(f32[192,128]{1,0:T(8,128)} %bitcast.7), channel_id=1, source_target_pairs={{0,2},{1,3},{2,0},{3,1},{4,6},{5,7},{6,4},{7,5},{8,10},{9,11},{10,... | collective-permute-start | bytes 294920 | tf_op jit(solution)/shard_map/ppermute | solution.py:213
  4.5 4.9 %collective-permute-start.1 = (f32[192,128]{1,0:T(8,128)}, f32[192,128]{1,0:T(8,128)S(1)}, u32[]{:S(2)}, u32[]{:S(2)}) collective-permute-start(f32[192,128]{1,0:T(8,128)} %bitcast.8), channel_id=1, source_target_pairs={{0,1},{1,0},{2,3},{3,2},{4,5},{5,4},{6,7},{7,6},{8,9},{9,8},{10,11... | collective-permute-start | bytes 294920 | tf_op jit(solution)/shard_map/ppermute | solution.py:213
  4.7 0.9 %copy-start = (f32[3,16,4,128]{3,2,1,0:T(4,128)S(1)}, f32[3,16,4,128]{3,2,1,0:T(4,128)}, u32[]{:S(2)}) copy-start(f32[3,16,4,128]{3,2,1,0:T(4,128)} %param.10) | copy-start | bytes 294916
  5.6 2.7 %copy-start.1 = (f32[3,16,4,128]{3,2,1,0:T(4,128)S(1)}, f32[3,16,4,128]{3,2,1,0:T(4,128)}, u32[]{:S(2)}) copy-start(f32[3,16,4,128]{3,2,1,0:T(4,128)} %param.10) | copy-start | bytes 294916
  6.3 9.9 %collective-permute-start.3 = (f32[192,128]{1,0:T(8,128)S(1)}, f32[192,128]{1,0:T(8,128)S(1)}, u32[]{:S(2)}, u32[]{:S(2)}) collective-permute-start(f32[192,128]{1,0:T(8,128)S(1)} %get-tuple-element.15), channel_id=1, source_target_pairs={{0,16},{8,24},{16,0},{24,8},{1,17},{9,25},{17,1},{25,9},{2,18},{10... | collective-permute-start | bytes 294920 | tf_op jit(solution)/shard_map/ppermute | solution.py:216
  9.7 6.9 %collective-permute-start.4 = (f32[192,128]{1,0:T(8,128)S(1)}, f32[192,128]{1,0:T(8,128)S(1)}, u32[]{:S(2)}, u32[]{:S(2)}) collective-permute-start(f32[192,128]{1,0:T(8,128)S(1)} %get-tuple-element.17), channel_id=1, source_target_pairs={{0,6},{1,7},{2,4},{3,5},{4,2},{5,3},{6,0},{7,1},{8,14},{9,15},{10,... | collective-permute-start | bytes 294920 | tf_op jit(solution)/shard_map/ppermute | solution.py:213
  13.5 0.7 %copy-start.7 = (f32[128]{0:T(128)S(1)}, f32[128]{0:T(128)}, u32[]{:S(2)}) copy-start(f32[128]{0:T(128)} %param.12) | copy-start | bytes 1540
  13.5 0.7 %copy-start.8 = (f32[128]{0:T(128)S(1)}, f32[128]{0:T(128)}, u32[]{:S(2)}) copy-start(f32[128]{0:T(128)} %param.13) | copy-start | bytes 1540
  14.2 0.7 %copy-start.2 = (f32[32,32]{1,0:T(8,128)S(1)}, f32[32,32]{1,0:T(8,128)}, u32[]{:S(2)}) copy-start(f32[32,32]{1,0:T(8,128)} %y_first.1) | copy-start | bytes 12292
  14.2 0.7 %copy-start.3 = (f32[32,32]{1,0:T(8,128)S(1)}, f32[32,32]{1,0:T(8,128)}, u32[]{:S(2)}) copy-start(f32[32,32]{1,0:T(8,128)} %y_second.1) | copy-start | bytes 12292
  14.5 0.7 %copy-start.9 = (f32[64]{0:T(128)S(1)}, f32[64]{0:T(128)}, u32[]{:S(2)}) copy-start(f32[64]{0:T(128)} %param.18) | copy-start | bytes 772
  14.5 0.7 %copy-start.10 = (s32[32]{0:T(128)S(1)}, s32[32]{0:T(128)}, u32[]{:S(2)}) copy-start(s32[32]{0:T(128)} %param.19) | copy-start | bytes 388
  16.5 1.4 %collective-permute-start.5 = (f32[192,128]{1,0:T(8,128)S(1)}, f32[192,128]{1,0:T(8,128)S(1)}, u32[]{:S(2)}, u32[]{:S(2)}) collective-permute-start(f32[192,128]{1,0:T(8,128)S(1)} %get-tuple-element.18), channel_id=1, source_target_pairs={{0,8},{8,0},{16,24},{24,16},{1,9},{9,1},{17,25},{25,17},{2,10},{10... | collective-permute-start | bytes 294920 | tf_op jit(solution)/shard_map/ppermute | solution.py:216

commit v24 on v23

--- a/solution.py
+++ b/solution.py
@@ -130,16 +130,21 @@
         return ((plane < wall_counts[index]) & (plane + start == cell)).astype(jnp.float32)
 
     levels = metric_table.shape[1]
-    entry = (lax.broadcasted_iota(jnp.int32, (levels, cells), 0) == metric_index[...]).astype(jnp.float32)
-    table = jnp.broadcast_to(metric_table[...], (8, levels))
-    metric = plain(table, entry, precision=lax.Precision.HIGHEST)[:1]
+    entry = (lax.broadcasted_iota(jnp.int32, (levels, cells), 0) == metric_index[...]).astype(jnp.bfloat16)
+    high, low = halves(metric_table[...])
+    rest = (metric_table[...] - high.astype(jnp.float32) - low.astype(jnp.float32)).astype(jnp.bfloat16)
+    table = jnp.concatenate([jnp.broadcast_to(part, (16, levels)) for part in (high, low, rest)], axis=0)
+    metric = plain(table, entry)
+    metric = metric[:1] + metric[16:17] + metric[32:33]
     ends = jnp.concatenate([spots(me), spots(me ^ 1)], axis=0)
     scale = jnp.sum(ends * metric, axis=1, keepdims=True)
-    pick = ends.astype(jnp.bfloat16)
-    second = sum(plain(pick, part) for part in halves(viscosity * y_second[...]))
-    first = -scale * sum(plain(pick, part) for part in halves(y_first[...]))
+    both = halves(jnp.concatenate([viscosity * y_second[...], y_first[...]], axis=1))
+    picked = plain(ends.astype(jnp.bfloat16), jnp.concatenate(both, axis=1))
+    picked = picked[:, : 2 * cells] + picked[:, 2 * cells :]
+    second, first = picked[:, :cells], -scale * picked[:, cells:]
     other = jnp.concatenate([spots(me ^ step) for step in range(0, rows, 2)], axis=0).astype(jnp.bfloat16)
-    wide = sum(turned(part, other) for part in halves(jnp.concatenate([second, first], axis=0)))
+    wide = turned(jnp.concatenate(halves(jnp.concatenate([second, first], axis=0)), axis=0), other)
+    wide = wide[: 4 * depth] + wide[4 * depth :]
     match = lax.broadcasted_iota(jnp.int32, wide.shape, 0) % zloc == lax.broadcasted_iota(jnp.int32, wide.shape, 1) % zloc
     wide = jnp.where(match, wide, 0.0)
     for b in range(rows // 2):
@@ -149,16 +154,16 @@
             ]
 
 
-def wall_kernel(comps, matrix, x_part, z_part, *refs):
+def wall_kernel(comps, matrix, z_part, *refs):
     fields, (total, away) = refs[:-2], refs[-2:]
-    depth = x_part.shape[0] // comps
+    depth = z_part.shape[0] // comps
     for comp in range(comps):
         at = slice(comp * depth, (comp + 1) * depth)
         stack = []
         for field in fields:
             stack += [field[at], field[depth : 2 * depth] * field[at]]
         result = dot_split(matrix[...], jnp.concatenate(stack, axis=0))
-        total[at] = x_part[at] + z_part[at] + result[:depth]
+        total[at] = z_part[at] + result[:depth]
         away[at] = result[depth:]
 
 
@@ -239,13 +244,6 @@
         "span",
     )
     returned = [along(parts[t], over(t)) for t in range(1, wide)]
-    (x_part,) = call(
-        functools.partial(stream_kernel, comps),
-        [field, x_first.reshape(1, length), x_second.reshape(1, length), parts[0]],
-        [VMEM] * 3 + [pl.ANY],
-        [field.shape],
-        "stream",
-    )
     (y_matrix,) = call(
         functools.partial(wall_matrix_kernel, rows, zloc),
         [wall_counts, metric_table.reshape(1, -1), metric_index.reshape(1, -1), y_first, y_second, parts[0]],
@@ -255,16 +253,23 @@
     )
     total, away = call(
         functools.partial(wall_kernel, comps),
-        [y_matrix, x_part, parts[0], field] + far,
-        [VMEM] * (4 + len(far)),
+        [y_matrix, parts[0], field] + far,
+        [VMEM] * (3 + len(far)),
         [field.shape] * 2,
         "wall",
     )
     near = across(away, 1)
+    (x_part,) = call(
+        functools.partial(stream_kernel, comps),
+        [field, x_first.reshape(1, length), x_second.reshape(1, length), away],
+        [VMEM] * 3 + [pl.ANY],
+        [field.shape],
+        "stream",
+    )
     (summed,) = call(
         functools.partial(sum_kernel, comps),
-        [mask, total] + returned,
-        [VMEM] * (2 + len(returned)),
+        [mask, total, x_part] + returned,
+        [VMEM] * (3 + len(returned)),
         [field.shape],
         "sum",
         cost=pl.CostEstimate(flops=1 << 30, bytes_accessed=1 << 22, transcendentals=0),

time: 18.8 us -> 17.9 us (0.952)
  waiting for transfers between devices: 2.09 us -> 1.1 us
    ppermute x2, waiting for transfers between devices: 1.26 us -> 0.27 us  [across(): return lax.ppermute(value, 'row', [(i, i ^ step) for i in range(rows)])]
  transfers between devices with their start and end apart: 6 -> 6, of which waited for: 2 -> 2; matrix products, arithmetic and copies ran while one was open for 0% -> 0% of each run, Pallas kernels for 16% -> 18%
where the time goes in v24:
time: 17.9 us; the launch traced here: 17.7 us
  starting transfers between devices  10.5 us (59%)
  Pallas kernels  3.78 us (21%)
  local copies, waits for them, and re-layouts  2.26 us (13%)
  waiting for transfers between devices  1.1 us (6%)
    ppermute x4, starting transfers between devices, along(): return lax.ppermute(value, 'col', [(i, i ^ step) for i in range(cols)])  8.48 us
    pallas_call x8, Pallas kernels, call(): pl.pallas_call(kernel, out_shape=results, in_specs=[pl.BlockSpec(memory_s...  3.78 us
    unnamed x22, local copies, waits for them, and re-layouts  2.26 us
    ppermute x2, starting transfers between devices, across(): return lax.ppermute(value, 'row', [(i, i ^ step) for i in range(rows)])  2 us
    ppermute x4, waiting for transfers between devices, along(): return lax.ppermute(value, 'col', [(i, i ^ step) for i in range(cols)])  0.83 us
  transfers between devices with their start and end apart: 6, of which 2 were waited for; matrix products, arithmetic and copies ran while one was open for 0% of the time, Pallas kernels for 18%

profile of v24, /device:TPU:0, one launch (start us, length us, event | category | flops | bytes accessed | tf_op | source)
XLA Modules:
  0.0 17.7 jit_solution(7310892467074892263)
XLA Ops:
  0.0 4.0 %collective-permute-start = (f32[192,128]{1,0:T(8,128)}, f32[192,128]{1,0:T(8,128)S(1)}, u32[]{:S(2)}, u32[]{:S(2)}) collective-permute-start(f32[192,128]{1,0:T(8,128)} %bitcast.6), channel_id=1, source_target_pairs={{0,3},{1,2},{2,1},{3,0},{4,7},{5,6},{6,5},{7,4},{8,11},{9,10},{10,... | collective-permute-start | bytes 294920 | tf_op jit(solution)/shard_map/ppermute | solution.py:218
  4.0 0.4 %collective-permute-start.2 = (f32[192,128]{1,0:T(8,128)}, f32[192,128]{1,0:T(8,128)S(1)}, u32[]{:S(2)}, u32[]{:S(2)}) collective-permute-start(f32[192,128]{1,0:T(8,128)} %bitcast.7), channel_id=1, source_target_pairs={{0,2},{1,3},{2,0},{3,1},{4,6},{5,7},{6,4},{7,5},{8,10},{9,11},{10,... | collective-permute-start | bytes 294920 | tf_op jit(solution)/shard_map/ppermute | solution.py:218
  4.5 0.2 %collective-permute-start.1 = (f32[192,128]{1,0:T(8,128)}, f32[192,128]{1,0:T(8,128)S(1)}, u32[]{:S(2)}, u32[]{:S(2)}) collective-permute-start(f32[192,128]{1,0:T(8,128)} %bitcast.8), channel_id=1, source_target_pairs={{0,1},{1,0},{2,3},{3,2},{4,5},{5,4},{6,7},{7,6},{8,9},{9,8},{10,11... | collective-permute-start | bytes 294920 | tf_op jit(solution)/shard_map/ppermute | solution.py:218
  4.7 0.9 %copy-done = f32[3,16,4,128]{3,2,1,0:T(4,128)S(1)} copy-done((f32[3,16,4,128]{3,2,1,0:T(4,128)S(1)}, f32[3,16,4,128]{3,2,1,0:T(4,128)}, u32[]{:S(2)}) %copy-start) | copy-done | bytes 98328
  5.6 0.7 %span_matrix.1 = (f32[64,256]{1,0:T(8,128)S(1)}, f32[64,128]{1,0:T(8,128)S(1)}, f32[192,128]{1,0:T(8,128)S(1)}) custom-call(s32[4]{0:T(128)S(1)} %copy-done.4, f32[32]{0:T(128)S(1)} %copy-done.5, f32[32]{0:T(128)S(1)} %copy-done.6, f32[192,128]{1,0:T(8,128)S(1)} %bitcast.9), custom_call_target="tpu_custom_call" | custom-call | tf_op jit(solution)/shard_map/span_matrix/pallas_call | solution.py:185
  6.3 1.9 %collective-permute-start.3 = (f32[192,128]{1,0:T(8,128)S(1)}, f32[192,128]{1,0:T(8,128)S(1)}, u32[]{:S(2)}, u32[]{:S(2)}) collective-permute-start(f32[192,128]{1,0:T(8,128)S(1)} %get-tuple-element.15), channel_id=1, source_target_pairs={{0,16},{8,24},{16,0},{24,8},{1,17},{9,25},{17,1},{25,9},{2,18},{10... | collective-permute-start | bytes 294920 | tf_op jit(solution)/shard_map/ppermute | solution.py:221
  8.3 0.3 %early.1 = f32[64,768]{1,0:T(8,128)S(1)} custom-call(f32[64,256]{1,0:T(8,128)S(1)} %get-tuple-element.13.matrix, f32[192,128]{1,0:T(8,128)S(1)} %bitcast.10, f32[192,128]{1,0:T(8,128)S(1)} %collective-permute-done.refs_1_), custom_call_target="tpu_custom_call" | custom-call | tf_op jit(solution)/shard_map/early/pallas_call | solution.py:185
  8.6 0.8 %collective-permute-done.2.refs_1_ = f32[192,128]{1,0:T(8,128)S(1)} collective-permute-done((f32[192,128]{1,0:T(8,128)}, f32[192,128]{1,0:T(8,128)S(1)}, u32[]{:S(2)}, u32[]{:S(2)}) %collective-permute-start.2) | collective-permute-done | bytes 98336 | tf_op jit(solution)/shard_map/ppermute | solution.py:218
  9.4 0.0 collective-permute-done.1.refs_0_
  9.4 0.3 %span.1 = (f32[192,128]{1,0:T(8,128)S(1)}, f32[192,128]{1,0:T(8,128)S(1)}) custom-call(f32[64,256]{1,0:T(8,128)S(1)} %get-tuple-element.13.matrix, f32[64,768]{1,0:T(8,128)S(1)} %early.1, f32[192,128]{1,0:T(8,128)S(1)} %collective-permute-done.1.refs_0_, f32[192,128]{1,0:T(8,128)S(1)} %collective-permute-done.2.refs_1_), custom_call_target="tpu_custom_call" | custom-call | tf_op jit(solution)/shard_map/span/pallas_call | solution.py:185
  9.7 3.8 %collective-permute-start.4 = (f32[192,128]{1,0:T(8,128)S(1)}, f32[192,128]{1,0:T(8,128)S(1)}, u32[]{:S(2)}, u32[]{:S(2)}) collective-permute-start(f32[192,128]{1,0:T(8,128)S(1)} %get-tuple-element.18), channel_id=1, source_target_pairs={{0,6},{1,7},{2,4},{3,5},{4,2},{5,3},{6,0},{7,1},{8,14},{9,15},{10,... | collective-permute-start | bytes 294920 | tf_op jit(solution)/shard_map/ppermute | solution.py:218
  13.5 0.6 %copy-done.7 = f32[64]{0:T(128)S(1)} copy-done((f32[64]{0:T(128)S(1)}, f32[64]{0:T(128)}, u32[]{:S(2)}) %copy-start.7) | copy-done | bytes 280
  14.2 0.0 copy-done.8
  14.2 1.2 %wall_matrix.1.matrix = f32[128,256]{1,0:T(8,128)S(1)} custom-call(s32[4]{0:T(128)S(1)} %copy-done.4, f32[1,64]{1,0:T(1,128)S(1)} %bitcast.13, s32[1,32]{1,0:T(1,128)S(1)} %bitcast.14, f32[32,32]{1,0:T(8,128)S(1)} %copy-done.2, f32[32,32]{1,0:T(8,128)S(1)} %copy-done.3, f32[192,128]{1,0:T(8,128)S(1)} %get-tuple-element.14.after.z_part), custom_call_target="tpu_custom_call" | custom-call | tf_op jit(solution)/shard_map/wall_matrix/pallas_call | solution.py:185
  15.4 0.0 collective-permute-done.3.refs_1_
  15.4 0.3 %wall.1 = (f32[192,128]{1,0:T(8,128)S(1)}, f32[192,128]{1,0:T(8,128)S(1)}) custom-call(f32[128,256]{1,0:T(8,128)S(1)} %wall_matrix.1.matrix, f32[192,128]{1,0:T(8,128)S(1)} %get-tuple-element.14.after.z_part, f32[192,128]{1,0:T(8,128)S(1)} %bitcast.11, f32[192,128]{1,0:T(8,128)S(1)} %collective-permute-done.3.refs_1_), custom_call_target="tpu_custom_call" | custom-call | tf_op jit(solution)/shard_map/wall/pallas_call | solution.py:185
  15.7 0.1 collective-permute-start.5
  15.8 0.0 copy-start.9
  15.8 0.0 copy-start.10
  15.8 0.6 %copy-done.9 = f32[128]{0:T(128)S(1)} copy-done((f32[128]{0:T(128)S(1)}, f32[128]{0:T(128)}, u32[]{:S(2)}) %copy-start.9) | copy-done | bytes 536
  16.4 0.0 copy-done.10
  16.5 0.3 %stream.1.refs_1_ = f32[192,128]{1,0:T(8,128)S(1)} custom-call(f32[192,128]{1,0:T(8,128)S(1)} %bitcast.12, f32[1,128]{1,0:T(1,128)S(1)} %bitcast.15, f32[1,128]{1,0:T(1,128)S(1)} %bitcast.16, f32[192,128]{1,0:T(8,128)S(1)} %get-tuple-element.17.after), custom_call_target="tpu_custom_call" | custom-call | tf_op jit(solution)/shard_map/stream/pallas_call | solution.py:185
  16.8 0.3 %collective-permute-done.5.near = f32[192,128]{1,0:T(8,128)S(1)} collective-permute-done((f32[192,128]{1,0:T(8,128)S(1)}, f32[192,128]{1,0:T(8,128)S(1)}, u32[]{:S(2)}, u32[]{:S(2)}) %collective-permute-start.5) | collective-permute-done | bytes 98336 | tf_op jit(solution)/shard_map/ppermute | solution.py:221
  17.1 0.7 %finish.1 = f32[192,128]{1,0:T(8,128)} custom-call(f32[192,128]{1,0:T(8,128)S(1)} %sum.1.total, f32[192,128]{1,0:T(8,128)S(1)} %collective-permute-done.5.near), custom_call_target="tpu_custom_call" | custom-call | tf_op jit(solution)/shard_map/finish/pallas_call | solution.py:185
  (18 shorter events, 0.1 us)
Async XLA Ops:
  0.0 4.7 %copy-start.4 = (s32[4]{0:T(128)S(1)}, s32[4]{0:T(128)}, u32[]{:S(2)}) copy-start(s32[4]{0:T(128)} %wall_counts.3) | copy-start | bytes 52
  0.0 4.7 %copy-start.6 = (f32[32]{0:T(128)S(1)}, f32[32]{0:T(128)}, u32[]{:S(2)}) copy-start(f32[32]{0:T(128)} %z_second.1) | copy-start | bytes 388
  0.0 4.7 %copy-start.5 = (f32[32]{0:T(128)S(1)}, f32[32]{0:T(128)}, u32[]{:S(2)}) copy-start(f32[32]{0:T(128)} %z_first.1) | copy-start | bytes 388
  0.0 8.3 %collective-permute-start = (f32[192,128]{1,0:T(8,128)}, f32[192,128]{1,0:T(8,128)S(1)}, u32[]{:S(2)}, u32[]{:S(2)}) collective-permute-start(f32[192,128]{1,0:T(8,128)} %bitcast.6), channel_id=1, source_target_pairs={{0,3},{1,2},{2,1},{3,0},{4,7},{5,6},{6,5},{7,4},{8,11},{9,10},{10,... | collective-permute-start | bytes 294920 | tf_op jit(solution)/shard_map/ppermute | solution.py:218
  4.0 5.4 %collective-permute-start.2 = (f32[192,128]{1,0:T(8,128)}, f32[192,128]{1,0:T(8,128)S(1)}, u32[]{:S(2)}, u32[]{:S(2)}) collective-permute-start(f32[192,128]{1,0:T(8,128)} %bitcast.7), channel_id=1, source_target_pairs={{0,2},{1,3},{2,0},{3,1},{4,6},{5,7},{6,4},{7,5},{8,10},{9,11},{10,... | collective-permute-start | bytes 294920 | tf_op jit(solution)/shard_map/ppermute | solution.py:218
  4.5 4.9 %collective-permute-start.1 = (f32[192,128]{1,0:T(8,128)}, f32[192,128]{1,0:T(8,128)S(1)}, u32[]{:S(2)}, u32[]{:S(2)}) collective-permute-start(f32[192,128]{1,0:T(8,128)} %bitcast.8), channel_id=1, source_target_pairs={{0,1},{1,0},{2,3},{3,2},{4,5},{5,4},{6,7},{7,6},{8,9},{9,8},{10,11... | collective-permute-start | bytes 294920 | tf_op jit(solution)/shard_map/ppermute | solution.py:218
  4.7 0.9 %copy-start = (f32[3,16,4,128]{3,2,1,0:T(4,128)S(1)}, f32[3,16,4,128]{3,2,1,0:T(4,128)}, u32[]{:S(2)}) copy-start(f32[3,16,4,128]{3,2,1,0:T(4,128)} %param.10) | copy-start | bytes 294916
  5.6 2.7 %copy-start.1 = (f32[3,16,4,128]{3,2,1,0:T(4,128)S(1)}, f32[3,16,4,128]{3,2,1,0:T(4,128)}, u32[]{:S(2)}) copy-start(f32[3,16,4,128]{3,2,1,0:T(4,128)} %param.10) | copy-start | bytes 294916
  6.3 9.0 %collective-permute-start.3 = (f32[192,128]{1,0:T(8,128)S(1)}, f32[192,128]{1,0:T(8,128)S(1)}, u32[]{:S(2)}, u32[]{:S(2)}) collective-permute-start(f32[192,128]{1,0:T(8,128)S(1)} %get-tuple-element.15), channel_id=1, source_target_pairs={{0,16},{8,24},{16,0},{24,8},{1,17},{9,25},{17,1},{25,9},{2,18},{10... | collective-permute-start | bytes 294920 | tf_op jit(solution)/shard_map/ppermute | solution.py:221
  9.4 4.1 %copy-start.2 = (f32[32,32]{1,0:T(8,128)S(1)}, f32[32,32]{1,0:T(8,128)}, u32[]{:S(2)}) copy-start(f32[32,32]{1,0:T(8,128)} %y_first.1) | copy-start | bytes 12292
  9.4 4.1 %copy-start.3 = (f32[32,32]{1,0:T(8,128)S(1)}, f32[32,32]{1,0:T(8,128)}, u32[]{:S(2)}) copy-start(f32[32,32]{1,0:T(8,128)} %y_second.1) | copy-start | bytes 12292
  9.7 7.1 %collective-permute-start.4 = (f32[192,128]{1,0:T(8,128)S(1)}, f32[192,128]{1,0:T(8,128)S(1)}, u32[]{:S(2)}, u32[]{:S(2)}) collective-permute-start(f32[192,128]{1,0:T(8,128)S(1)} %get-tuple-element.18), channel_id=1, source_target_pairs={{0,6},{1,7},{2,4},{3,5},{4,2},{5,3},{6,0},{7,1},{8,14},{9,15},{10,... | collective-permute-start | bytes 294920 | tf_op jit(solution)/shard_map/ppermute | solution.py:218
  13.5 0.7 %copy-start.7 = (f32[64]{0:T(128)S(1)}, f32[64]{0:T(128)}, u32[]{:S(2)}) copy-start(f32[64]{0:T(128)} %param.18) | copy-start | bytes 772
  13.5 0.7 %copy-start.8 = (s32[32]{0:T(128)S(1)}, s32[32]{0:T(128)}, u32[]{:S(2)}) copy-start(s32[32]{0:T(128)} %param.19) | copy-start | bytes 388
  15.7 1.4 %collective-permute-start.5 = (f32[192,128]{1,0:T(8,128)S(1)}, f32[192,128]{1,0:T(8,128)S(1)}, u32[]{:S(2)}, u32[]{:S(2)}) collective-permute-start(f32[192,128]{1,0:T(8,128)S(1)} %get-tuple-element.17.after), channel_id=1, source_target_pairs={{0,8},{8,0},{16,24},{24,16},{1,9},{9,1},{17,25},{25,17},{2,10},{10... | collective-permute-start | bytes 294920 | tf_op jit(solution)/shard_map/ppermute | solution.py:221
  15.8 0.7 %copy-start.9 = (f32[128]{0:T(128)S(1)}, f32[128]{0:T(128)}, u32[]{:S(2)}) copy-start(f32[128]{0:T(128)} %param.12) | copy-start | bytes 1540
  15.8 0.7 %copy-start.10 = (f32[128]{0:T(128)S(1)}, f32[128]{0:T(128)}, u32[]{:S(2)}) copy-start(f32[128]{0:T(128)} %param.13) | copy-start | bytes 1540

commit v25 on v24

--- a/solution.py
+++ b/solution.py
@@ -72,10 +72,24 @@
     return pltpu.roll(jnp.broadcast_to(row, (length, length)), 0, 1, stride=1, stride_axis=0)
 
 
-def span_matrix_kernel(cols, zloc, wall_counts, z_first, z_second, field, z_matrix, mask, held):
+def span_matrix_kernel(
+    rows, cols, zloc, wall_counts, z_first, z_second, field, z_matrix, mask, held, ends, others
+):
     held[...] = field[...]
-    count = wall_counts[lax.axis_index("row")]
-    mask[...] = (lax.broadcasted_iota(jnp.int32, mask.shape, 0) // zloc < count).astype(jnp.float32)
+    me = lax.axis_index("row")
+    mask[...] = (lax.broadcasted_iota(jnp.int32, mask.shape, 0) // zloc < wall_counts[me]).astype(jnp.float32)
+    depth = mask.shape[0]
+    plane = lax.broadcasted_iota(jnp.int32, (depth, ends.shape[1]), 0) // zloc
+    cell = lax.broadcasted_iota(jnp.int32, (depth, ends.shape[1]), 1)
+
+    def spots(index):
+        start = lax.fori_loop(0, rows, lambda i, acc: acc + jnp.where(i < index, wall_counts[i], 0), 0, unroll=True)
+        return ((plane < wall_counts[index]) & (plane + start == cell)).astype(jnp.float32)
+
+    for i in range(2):
+        ends[i * depth : (i + 1) * depth] = spots(me ^ i)
+    for i in range(rows // 2):
+        others[i * depth : (i + 1) * depth] = spots(me ^ (2 * i))
 
     cells_z = cols * zloc
     shape = z_matrix.shape
@@ -112,42 +126,28 @@
     x_part[...] = dot_split(left, right, transposed=True)
 
 
-def wall_matrix_kernel(rows, zloc, wall_counts, metric_table, metric_index, y_first, y_second, after, matrix):
+def wall_matrix_kernel(zloc, ends, others, metric_table, metric_index, y_first, y_second, after, matrix):
     cells = y_first.shape[0]
     depth = matrix.shape[0] // 2
-    me = lax.axis_index("row")
     plain = functools.partial(
         lax.dot_general, dimension_numbers=(((1,), (0,)), ((), ())), preferred_element_type=jnp.float32
     )
     turned = functools.partial(
         lax.dot_general, dimension_numbers=(((1,), (1,)), ((), ())), preferred_element_type=jnp.float32
     )
-
-    def spots(index):
-        start = lax.fori_loop(0, rows, lambda i, acc: acc + jnp.where(i < index, wall_counts[i], 0), 0, unroll=True)
-        plane = lax.broadcasted_iota(jnp.int32, (depth, cells), 0) // zloc
-        cell = lax.broadcasted_iota(jnp.int32, (depth, cells), 1)
-        return ((plane < wall_counts[index]) & (plane + start == cell)).astype(jnp.float32)
-
     levels = metric_table.shape[1]
-    entry = (lax.broadcasted_iota(jnp.int32, (levels, cells), 0) == metric_index[...]).astype(jnp.bfloat16)
-    high, low = halves(metric_table[...])
-    rest = (metric_table[...] - high.astype(jnp.float32) - low.astype(jnp.float32)).astype(jnp.bfloat16)
-    table = jnp.concatenate([jnp.broadcast_to(part, (16, levels)) for part in (high, low, rest)], axis=0)
-    metric = plain(table, entry)
-    metric = metric[:1] + metric[16:17] + metric[32:33]
-    ends = jnp.concatenate([spots(me), spots(me ^ 1)], axis=0)
-    scale = jnp.sum(ends * metric, axis=1, keepdims=True)
-    both = halves(jnp.concatenate([viscosity * y_second[...], y_first[...]], axis=1))
-    picked = plain(ends.astype(jnp.bfloat16), jnp.concatenate(both, axis=1))
-    picked = picked[:, : 2 * cells] + picked[:, 2 * cells :]
-    second, first = picked[:, :cells], -scale * picked[:, cells:]
-    other = jnp.concatenate([spots(me ^ step) for step in range(0, rows, 2)], axis=0).astype(jnp.bfloat16)
-    wide = turned(jnp.concatenate(halves(jnp.concatenate([second, first], axis=0)), axis=0), other)
-    wide = wide[: 4 * depth] + wide[4 * depth :]
+    entry = (lax.broadcasted_iota(jnp.int32, (levels, cells), 0) == metric_index[...]).astype(jnp.float32)
+    table = jnp.broadcast_to(metric_table[...], (8, levels))
+    metric = plain(table, entry, precision=lax.Precision.HIGHEST)[:1]
+    scale = jnp.sum(ends[...] * metric, axis=1, keepdims=True)
+    pick = ends[...].astype(jnp.bfloat16)
+    second = sum(plain(pick, part) for part in halves(viscosity * y_second[...]))
+    first = -scale * sum(plain(pick, part) for part in halves(y_first[...]))
+    other = others[...].astype(jnp.bfloat16)
+    wide = sum(turned(part, other) for part in halves(jnp.concatenate([second, first], axis=0)))
     match = lax.broadcasted_iota(jnp.int32, wide.shape, 0) % zloc == lax.broadcasted_iota(jnp.int32, wide.shape, 1) % zloc
     wide = jnp.where(match, wide, 0.0)
-    for b in range(rows // 2):
+    for b in range(others.shape[0] // depth):
         for k in range(2):
             matrix[:, (2 * b + k) * depth : (2 * b + k + 1) * depth] = wide[
                 2 * k * depth : 2 * (k + 1) * depth, b * depth : (b + 1) * depth
@@ -221,11 +221,18 @@
         return lax.ppermute(value, "row", [(i, i ^ step) for i in range(rows)])
 
     gathered = [along(field, t) for t in range(1, quad)]
-    z_matrix, mask, held = call(
-        functools.partial(span_matrix_kernel, cols, zloc),
+    cells = metric_index.shape[0]
+    z_matrix, mask, held, ends, others = call(
+        functools.partial(span_matrix_kernel, rows, cols, zloc),
         [wall_counts, z_first, z_second, field],
         [SMEM] * 3 + [VMEM],
-        [(wide * group, 2 * quad * group), (depth, length), field.shape],
+        [
+            (wide * group, 2 * quad * group),
+            (depth, length),
+            field.shape,
+            (2 * depth, cells),
+            (rows // 2 * depth, cells),
+        ],
         "span_matrix",
     )
     far = [across(held, step) for step in range(2, rows, 2)]
@@ -245,9 +252,9 @@
     )
     returned = [along(parts[t], over(t)) for t in range(1, wide)]
     (y_matrix,) = call(
-        functools.partial(wall_matrix_kernel, rows, zloc),
-        [wall_counts, metric_table.reshape(1, -1), metric_index.reshape(1, -1), y_first, y_second, parts[0]],
-        [SMEM] + [VMEM] * 4 + [pl.ANY],
+        functools.partial(wall_matrix_kernel, zloc),
+        [ends, others, metric_table.reshape(1, -1), metric_index.reshape(1, -1), y_first, y_second, parts[0]],
+        [VMEM] * 6 + [pl.ANY],
         [(2 * depth, rows * depth)],
         "wall_matrix",
     )

time: 17.9 us -> 17.2 us (0.961)
  Pallas kernels: 3.78 us -> 3.08 us
    pallas_call x8, Pallas kernels: 3.78 us -> 3.08 us  [call(): pl.pallas_call(kernel, out_shape=results, in_specs=[pl.BlockSpec(memory_s...]
  transfers between devices with their start and end apart: 6 -> 6, of which waited for: 2 -> 3; matrix products, arithmetic and copies ran while one was open for 0% -> 0% of each run, Pallas kernels for 18% -> 14%
where the time goes in v25:
time: 17.2 us; the launch traced here: 17 us
  starting transfers between devices  10.5 us (61%)
  Pallas kernels  3.08 us (18%)
  local copies, waits for them, and re-layouts  2.26 us (13%)
  waiting for transfers between devices  1.1 us (6%)
    ppermute x4, starting transfers between devices, along(): return lax.ppermute(value, 'col', [(i, i ^ step) for i in range(cols)])  8.48 us
    pallas_call x8, Pallas kernels, call(): pl.pallas_call(kernel, out_shape=results, in_specs=[pl.BlockSpec(memory_s...  3.08 us
    unnamed x22, local copies, waits for them, and re-layouts  2.26 us
    ppermute x2, starting transfers between devices, across(): return lax.ppermute(value, 'row', [(i, i ^ step) for i in range(rows)])  2 us
    ppermute x4, waiting for transfers between devices, along(): return lax.ppermute(value, 'col', [(i, i ^ step) for i in range(cols)])  0.99 us
  transfers between devices with their start and end apart: 6, of which 3 were waited for; matrix products, arithmetic and copies ran while one was open for 0% of the time, Pallas kernels for 14%

profile of v25, /device:TPU:0, one launch (start us, length us, event | category | flops | bytes accessed | tf_op | source)
XLA Modules:
  0.0 17.0 jit_solution(3172672204132652421)
XLA Ops:
  0.0 4.0 %collective-permute-start = (f32[192,128]{1,0:T(8,128)}, f32[192,128]{1,0:T(8,128)S(1)}, u32[]{:S(2)}, u32[]{:S(2)}) collective-permute-start(f32[192,128]{1,0:T(8,128)} %bitcast.6), channel_id=1, source_target_pairs={{0,3},{1,2},{2,1},{3,0},{4,7},{5,6},{6,5},{7,4},{8,11},{9,10},{10,... | collective-permute-start | bytes 294920 | tf_op jit(solution)/shard_map/ppermute | solution.py:218
  4.0 0.4 %collective-permute-start.2 = (f32[192,128]{1,0:T(8,128)}, f32[192,128]{1,0:T(8,128)S(1)}, u32[]{:S(2)}, u32[]{:S(2)}) collective-permute-start(f32[192,128]{1,0:T(8,128)} %bitcast.7), channel_id=1, source_target_pairs={{0,2},{1,3},{2,0},{3,1},{4,6},{5,7},{6,4},{7,5},{8,10},{9,11},{10,... | collective-permute-start | bytes 294920 | tf_op jit(solution)/shard_map/ppermute | solution.py:218
  4.5 0.2 %collective-permute-start.1 = (f32[192,128]{1,0:T(8,128)}, f32[192,128]{1,0:T(8,128)S(1)}, u32[]{:S(2)}, u32[]{:S(2)}) collective-permute-start(f32[192,128]{1,0:T(8,128)} %bitcast.8), channel_id=1, source_target_pairs={{0,1},{1,0},{2,3},{3,2},{4,5},{5,4},{6,7},{7,6},{8,9},{9,8},{10,11... | collective-permute-start | bytes 294920 | tf_op jit(solution)/shard_map/ppermute | solution.py:218
  4.7 0.9 %copy-done = f32[3,16,4,128]{3,2,1,0:T(4,128)S(1)} copy-done((f32[3,16,4,128]{3,2,1,0:T(4,128)S(1)}, f32[3,16,4,128]{3,2,1,0:T(4,128)}, u32[]{:S(2)}) %copy-start) | copy-done | bytes 98328
  5.6 0.7 %span_matrix.1 = (f32[64,256]{1,0:T(8,128)S(1)}, f32[64,128]{1,0:T(8,128)S(1)}, f32[192,128]{1,0:T(8,128)S(1)}, f32[128,32]{1,0:T(8,128)S(1)}, f32[128,32]{1,0:T(8,128)S(1)}) custom-call(s32[4]{0:T(128)S(1)} %copy-done.4, f32[32]{0:T(128)S(1)} %copy-done.5, f32[32]{0:T(128)S(1)} %copy-done.6, f32[192,128]{1,0:T(8,128)S(1)} %bitcast.9), custom_call_target="tpu_custom_call" | custom-call | tf_op jit(solution)/shard_map/span_matrix/pallas_call | solution.py:185
  6.3 1.9 %collective-permute-start.3 = (f32[192,128]{1,0:T(8,128)S(1)}, f32[192,128]{1,0:T(8,128)S(1)}, u32[]{:S(2)}, u32[]{:S(2)}) collective-permute-start(f32[192,128]{1,0:T(8,128)S(1)} %get-tuple-element.19), channel_id=1, source_target_pairs={{0,16},{8,24},{16,0},{24,8},{1,17},{9,25},{17,1},{25,9},{2,18},{10... | collective-permute-start | bytes 294920 | tf_op jit(solution)/shard_map/ppermute | solution.py:221
  8.3 0.0 collective-permute-done.refs_1_
  8.3 0.3 %early.1 = f32[64,768]{1,0:T(8,128)S(1)} custom-call(f32[64,256]{1,0:T(8,128)S(1)} %get-tuple-element.17.matrix, f32[192,128]{1,0:T(8,128)S(1)} %bitcast.10, f32[192,128]{1,0:T(8,128)S(1)} %collective-permute-done.refs_1_), custom_call_target="tpu_custom_call" | custom-call | tf_op jit(solution)/shard_map/early/pallas_call | solution.py:185
  8.6 0.8 %collective-permute-done.2.refs_1_ = f32[192,128]{1,0:T(8,128)S(1)} collective-permute-done((f32[192,128]{1,0:T(8,128)}, f32[192,128]{1,0:T(8,128)S(1)}, u32[]{:S(2)}, u32[]{:S(2)}) %collective-permute-start.2) | collective-permute-done | bytes 98336 | tf_op jit(solution)/shard_map/ppermute | solution.py:218
  9.4 0.3 %span.1 = (f32[192,128]{1,0:T(8,128)S(1)}, f32[192,128]{1,0:T(8,128)S(1)}) custom-call(f32[64,256]{1,0:T(8,128)S(1)} %get-tuple-element.17.matrix, f32[64,768]{1,0:T(8,128)S(1)} %early.1, f32[192,128]{1,0:T(8,128)S(1)} %collective-permute-done.1.refs_0_, f32[192,128]{1,0:T(8,128)S(1)} %collective-permute-done.2.refs_1_), custom_call_target="tpu_custom_call" | custom-call | tf_op jit(solution)/shard_map/span/pallas_call | solution.py:185
  9.7 3.8 %collective-permute-start.4 = (f32[192,128]{1,0:T(8,128)S(1)}, f32[192,128]{1,0:T(8,128)S(1)}, u32[]{:S(2)}, u32[]{:S(2)}) collective-permute-start(f32[192,128]{1,0:T(8,128)S(1)} %get-tuple-element.22), channel_id=1, source_target_pairs={{0,6},{1,7},{2,4},{3,5},{4,2},{5,3},{6,0},{7,1},{8,14},{9,15},{10,... | collective-permute-start | bytes 294920 | tf_op jit(solution)/shard_map/ppermute | solution.py:218
  13.5 0.6 %copy-done.7 = f32[64]{0:T(128)S(1)} copy-done((f32[64]{0:T(128)S(1)}, f32[64]{0:T(128)}, u32[]{:S(2)}) %copy-start.7) | copy-done | bytes 280
  14.2 0.0 copy-done.8
  14.2 0.5 %wall_matrix.1.matrix = f32[128,256]{1,0:T(8,128)S(1)} custom-call(f32[128,32]{1,0:T(8,128)S(1)} %get-tuple-element.15.ends, f32[128,32]{1,0:T(8,128)S(1)} %get-tuple-element.16.others, f32[1,64]{1,0:T(1,128)S(1)} %bitcast.13, s32[1,32]{1,0:T(1,128)S(1)} %bitcast.14, f32[32,32]{1,0:T(8,128)S(1)} %copy-done.2, f32[32,32]{1,0:T(8,128)S(1)} %copy-done.3, ...), custom_call_target="tpu_custom_call" | custom-call | tf_op jit(solution)/shard_map/wall_matrix/pallas_call | solution.py:185
  14.7 0.3 %wall.1 = (f32[192,128]{1,0:T(8,128)S(1)}, f32[192,128]{1,0:T(8,128)S(1)}) custom-call(f32[128,256]{1,0:T(8,128)S(1)} %wall_matrix.1.matrix, f32[192,128]{1,0:T(8,128)S(1)} %get-tuple-element.18.after.z_part, f32[192,128]{1,0:T(8,128)S(1)} %bitcast.11, f32[192,128]{1,0:T(8,128)S(1)} %collective-permute-done.3.refs_1_), custom_call_target="tpu_custom_call" | custom-call | tf_op jit(solution)/shard_map/wall/pallas_call | solution.py:185
  15.0 0.1 collective-permute-start.5
  15.1 0.0 copy-start.9
  15.1 0.0 copy-start.10
  15.1 0.6 %copy-done.9 = f32[128]{0:T(128)S(1)} copy-done((f32[128]{0:T(128)S(1)}, f32[128]{0:T(128)}, u32[]{:S(2)}) %copy-start.9) | copy-done | bytes 536
  15.7 0.0 copy-done.10
  15.7 0.3 %stream.1.refs_1_ = f32[192,128]{1,0:T(8,128)S(1)} custom-call(f32[192,128]{1,0:T(8,128)S(1)} %bitcast.12, f32[1,128]{1,0:T(1,128)S(1)} %bitcast.15, f32[1,128]{1,0:T(1,128)S(1)} %bitcast.16, f32[192,128]{1,0:T(8,128)S(1)} %get-tuple-element.21.after), custom_call_target="tpu_custom_call" | custom-call | tf_op jit(solution)/shard_map/stream/pallas_call | solution.py:185
  16.0 0.2 %collective-permute-done.4.refs_2_ = f32[192,128]{1,0:T(8,128)S(1)} collective-permute-done((f32[192,128]{1,0:T(8,128)S(1)}, f32[192,128]{1,0:T(8,128)S(1)}, u32[]{:S(2)}, u32[]{:S(2)}) %collective-permute-start.4) | collective-permute-done | bytes 98336 | tf_op jit(solution)/shard_map/ppermute | solution.py:218
  16.2 0.1 collective-permute-done.5.near
  16.4 0.7 %finish.1 = f32[192,128]{1,0:T(8,128)} custom-call(f32[192,128]{1,0:T(8,128)S(1)} %sum.1.total, f32[192,128]{1,0:T(8,128)S(1)} %collective-permute-done.5.near), custom_call_target="tpu_custom_call" | custom-call | tf_op jit(solution)/shard_map/finish/pallas_call | solution.py:185
  (18 shorter events, 0.1 us)
Async XLA Ops:
  0.0 4.7 %copy-start.6 = (f32[32]{0:T(128)S(1)}, f32[32]{0:T(128)}, u32[]{:S(2)}) copy-start(f32[32]{0:T(128)} %z_second.1) | copy-start | bytes 388
  0.0 4.7 %copy-start.5 = (f32[32]{0:T(128)S(1)}, f32[32]{0:T(128)}, u32[]{:S(2)}) copy-start(f32[32]{0:T(128)} %z_first.1) | copy-start | bytes 388
  0.0 4.7 %copy-start.4 = (s32[4]{0:T(128)S(1)}, s32[4]{0:T(128)}, u32[]{:S(2)}) copy-start(s32[4]{0:T(128)} %wall_counts.1) | copy-start | bytes 52
  0.0 8.3 %collective-permute-start = (f32[192,128]{1,0:T(8,128)}, f32[192,128]{1,0:T(8,128)S(1)}, u32[]{:S(2)}, u32[]{:S(2)}) collective-permute-start(f32[192,128]{1,0:T(8,128)} %bitcast.6), channel_id=1, source_target_pairs={{0,3},{1,2},{2,1},{3,0},{4,7},{5,6},{6,5},{7,4},{8,11},{9,10},{10,... | collective-permute-start | bytes 294920 | tf_op jit(solution)/shard_map/ppermute | solution.py:218
  4.0 5.4 %collective-permute-start.2 = (f32[192,128]{1,0:T(8,128)}, f32[192,128]{1,0:T(8,128)S(1)}, u32[]{:S(2)}, u32[]{:S(2)}) collective-permute-start(f32[192,128]{1,0:T(8,128)} %bitcast.7), channel_id=1, source_target_pairs={{0,2},{1,3},{2,0},{3,1},{4,6},{5,7},{6,4},{7,5},{8,10},{9,11},{10,... | collective-permute-start | bytes 294920 | tf_op jit(solution)/shard_map/ppermute | solution.py:218
  4.5 4.9 %collective-permute-start.1 = (f32[192,128]{1,0:T(8,128)}, f32[192,128]{1,0:T(8,128)S(1)}, u32[]{:S(2)}, u32[]{:S(2)}) collective-permute-start(f32[192,128]{1,0:T(8,128)} %bitcast.8), channel_id=1, source_target_pairs={{0,1},{1,0},{2,3},{3,2},{4,5},{5,4},{6,7},{7,6},{8,9},{9,8},{10,11... | collective-permute-start | bytes 294920 | tf_op jit(solution)/shard_map/ppermute | solution.py:218
  4.7 0.9 %copy-start = (f32[3,16,4,128]{3,2,1,0:T(4,128)S(1)}, f32[3,16,4,128]{3,2,1,0:T(4,128)}, u32[]{:S(2)}) copy-start(f32[3,16,4,128]{3,2,1,0:T(4,128)} %param.10) | copy-start | bytes 294916
  5.6 2.7 %copy-start.1 = (f32[3,16,4,128]{3,2,1,0:T(4,128)S(1)}, f32[3,16,4,128]{3,2,1,0:T(4,128)}, u32[]{:S(2)}) copy-start(f32[3,16,4,128]{3,2,1,0:T(4,128)} %param.10) | copy-start | bytes 294916
  6.3 8.3 %collective-permute-start.3 = (f32[192,128]{1,0:T(8,128)S(1)}, f32[192,128]{1,0:T(8,128)S(1)}, u32[]{:S(2)}, u32[]{:S(2)}) collective-permute-start(f32[192,128]{1,0:T(8,128)S(1)} %get-tuple-element.19), channel_id=1, source_target_pairs={{0,16},{8,24},{16,0},{24,8},{1,17},{9,25},{17,1},{25,9},{2,18},{10... | collective-permute-start | bytes 294920 | tf_op jit(solution)/shard_map/ppermute | solution.py:221
  9.4 4.1 %copy-start.2 = (f32[32,32]{1,0:T(8,128)S(1)}, f32[32,32]{1,0:T(8,128)}, u32[]{:S(2)}) copy-start(f32[32,32]{1,0:T(8,128)} %y_first.1) | copy-start | bytes 12292
  9.4 4.1 %copy-start.3 = (f32[32,32]{1,0:T(8,128)S(1)}, f32[32,32]{1,0:T(8,128)}, u32[]{:S(2)}) copy-start(f32[32,32]{1,0:T(8,128)} %y_second.1) | copy-start | bytes 12292
  9.7 6.5 %collective-permute-start.4 = (f32[192,128]{1,0:T(8,128)S(1)}, f32[192,128]{1,0:T(8,128)S(1)}, u32[]{:S(2)}, u32[]{:S(2)}) collective-permute-start(f32[192,128]{1,0:T(8,128)S(1)} %get-tuple-element.22), channel_id=1, source_target_pairs={{0,6},{1,7},{2,4},{3,5},{4,2},{5,3},{6,0},{7,1},{8,14},{9,15},{10,... | collective-permute-start | bytes 294920 | tf_op jit(solution)/shard_map/ppermute | solution.py:218
  13.5 0.7 %copy-start.7 = (f32[64]{0:T(128)S(1)}, f32[64]{0:T(128)}, u32[]{:S(2)}) copy-start(f32[64]{0:T(128)} %param.18) | copy-start | bytes 772
  13.5 0.7 %copy-start.8 = (s32[32]{0:T(128)S(1)}, s32[32]{0:T(128)}, u32[]{:S(2)}) copy-start(s32[32]{0:T(128)} %param.19) | copy-start | bytes 388
  15.0 1.4 %collective-permute-start.5 = (f32[192,128]{1,0:T(8,128)S(1)}, f32[192,128]{1,0:T(8,128)S(1)}, u32[]{:S(2)}, u32[]{:S(2)}) collective-permute-start(f32[192,128]{1,0:T(8,128)S(1)} %get-tuple-element.21.after), channel_id=1, source_target_pairs={{0,8},{8,0},{16,24},{24,16},{1,9},{9,1},{17,25},{25,17},{2,10},{10... | collective-permute-start | bytes 294920 | tf_op jit(solution)/shard_map/ppermute | solution.py:221
  15.1 0.7 %copy-start.9 = (f32[128]{0:T(128)S(1)}, f32[128]{0:T(128)}, u32[]{:S(2)}) copy-start(f32[128]{0:T(128)} %param.12) | copy-start | bytes 1540
  15.1 0.7 %copy-start.10 = (f32[128]{0:T(128)S(1)}, f32[128]{0:T(128)}, u32[]{:S(2)}) copy-start(f32[128]{0:T(128)} %param.13) | copy-start | bytes 1540

commit v26 on v25

--- a/solution.py
+++ b/solution.py
@@ -236,17 +236,18 @@
         "span_matrix",
     )
     far = [across(held, step) for step in range(2, rows, 2)]
+    first, last = 2, (1, 3)
     (early,) = call(
-        functools.partial(early_kernel, comps, (0, quad - 1)),
-        [z_matrix, field, gathered[-1]],
+        functools.partial(early_kernel, comps, (0, first)),
+        [z_matrix, field, gathered[first - 1]],
         [VMEM] * 3,
         [(wide * group, comps * (depth // group) * length)],
         "early",
     )
     parts = call(
-        functools.partial(span_kernel, comps, tuple(range(1, quad - 1))),
-        [z_matrix, early] + gathered[:-1],
-        [VMEM] * quad,
+        functools.partial(span_kernel, comps, last),
+        [z_matrix, early] + [gathered[s - 1] for s in last],
+        [VMEM] * (2 + len(last)),
         [field.shape] * wide,
         "span",
     )

time: 17.2 us -> 18.4 us (1.070)
  waiting for transfers between devices: 1.1 us -> 2.64 us
  starting transfers between devices: 10.5 us -> 10.2 us
    ppermute x4, waiting for transfers between devices: 0.99 us -> 2.63 us  [along(): return lax.ppermute(value, 'col', [(i, i ^ step) for i in range(cols)])]
    ppermute x4, starting transfers between devices: 8.48 us -> 8.14 us  [along(): return lax.ppermute(value, 'col', [(i, i ^ step) for i in range(cols)])]
  transfers between devices with their start and end apart: 6 -> 6, of which waited for: 3 -> 3; matrix products, arithmetic and copies ran while one was open for 0% -> 0% of each run, Pallas kernels for 14% -> 13%
where the time goes in v26:
time: 18.4 us; the launch traced here: 18.2 us
  starting transfers between devices  10.2 us (55%)
  Pallas kernels  3.09 us (17%)
  waiting for transfers between devices  2.64 us (14%)
  local copies, waits for them, and re-layouts  2.26 us (12%)
    ppermute x4, starting transfers between devices, along(): return lax.ppermute(value, 'col', [(i, i ^ step) for i in range(cols)])  8.14 us
    pallas_call x8, Pallas kernels, call(): pl.pallas_call(kernel, out_shape=results, in_specs=[pl.BlockSpec(memory_s...  3.09 us
    ppermute x4, waiting for transfers between devices, along(): return lax.ppermute(value, 'col', [(i, i ^ step) for i in range(cols)])  2.63 us
    unnamed x22, local copies, waits for them, and re-layouts  2.26 us
    ppermute x2, starting transfers between devices, across(): return lax.ppermute(value, 'row', [(i, i ^ step) for i in range(rows)])  2.03 us
  transfers between devices with their start and end apart: 6, of which 3 were waited for; matrix products, arithmetic and copies ran while one was open for 0% of the time, Pallas kernels for 13%

profile of v26, /device:TPU:0, one launch (start us, length us, event | category | flops | bytes accessed | tf_op | source)
XLA Modules:
  0.0 18.2 jit_solution(17065693253812303272)
XLA Ops:
  0.0 3.1 %collective-permute-start = (f32[192,128]{1,0:T(8,128)}, f32[192,128]{1,0:T(8,128)S(1)}, u32[]{:S(2)}, u32[]{:S(2)}) collective-permute-start(f32[192,128]{1,0:T(8,128)} %bitcast.6), channel_id=1, source_target_pairs={{0,2},{1,3},{2,0},{3,1},{4,6},{5,7},{6,4},{7,5},{8,10},{9,11},{10,... | collective-permute-start | bytes 294920 | tf_op jit(solution)/shard_map/ppermute | solution.py:218
  3.1 1.4 %collective-permute-start.2 = (f32[192,128]{1,0:T(8,128)}, f32[192,128]{1,0:T(8,128)S(1)}, u32[]{:S(2)}, u32[]{:S(2)}) collective-permute-start(f32[192,128]{1,0:T(8,128)} %bitcast.7), channel_id=1, source_target_pairs={{0,3},{1,2},{2,1},{3,0},{4,7},{5,6},{6,5},{7,4},{8,11},{9,10},{10,... | collective-permute-start | bytes 294920 | tf_op jit(solution)/shard_map/ppermute | solution.py:218
  4.5 0.2 collective-permute-start.1
  4.7 0.9 %copy-done = f32[3,16,4,128]{3,2,1,0:T(4,128)S(1)} copy-done((f32[3,16,4,128]{3,2,1,0:T(4,128)S(1)}, f32[3,16,4,128]{3,2,1,0:T(4,128)}, u32[]{:S(2)}) %copy-start) | copy-done | bytes 98328
  5.6 0.7 %span_matrix.1 = (f32[64,256]{1,0:T(8,128)S(1)}, f32[64,128]{1,0:T(8,128)S(1)}, f32[192,128]{1,0:T(8,128)S(1)}, f32[128,32]{1,0:T(8,128)S(1)}, f32[128,32]{1,0:T(8,128)S(1)}) custom-call(s32[4]{0:T(128)S(1)} %copy-done.4, f32[32]{0:T(128)S(1)} %copy-done.5, f32[32]{0:T(128)S(1)} %copy-done.6, f32[192,128]{1,0:T(8,128)S(1)} %bitcast.9), custom_call_target="tpu_custom_call" | custom-call | tf_op jit(solution)/shard_map/span_matrix/pallas_call | solution.py:185
  6.3 2.0 %collective-permute-start.3 = (f32[192,128]{1,0:T(8,128)S(1)}, f32[192,128]{1,0:T(8,128)S(1)}, u32[]{:S(2)}, u32[]{:S(2)}) collective-permute-start(f32[192,128]{1,0:T(8,128)S(1)} %get-tuple-element.19), channel_id=1, source_target_pairs={{0,16},{8,24},{16,0},{24,8},{1,17},{9,25},{17,1},{25,9},{2,18},{10... | collective-permute-start | bytes 294920 | tf_op jit(solution)/shard_map/ppermute | solution.py:221
  8.3 0.0 collective-permute-done.refs_1_
  8.3 0.3 %early.1 = f32[64,768]{1,0:T(8,128)S(1)} custom-call(f32[64,256]{1,0:T(8,128)S(1)} %get-tuple-element.17.matrix, f32[192,128]{1,0:T(8,128)S(1)} %bitcast.10, f32[192,128]{1,0:T(8,128)S(1)} %collective-permute-done.refs_1_), custom_call_target="tpu_custom_call" | custom-call | tf_op jit(solution)/shard_map/early/pallas_call | solution.py:185
  8.6 0.9 %collective-permute-done.2.refs_1_ = f32[192,128]{1,0:T(8,128)S(1)} collective-permute-done((f32[192,128]{1,0:T(8,128)}, f32[192,128]{1,0:T(8,128)S(1)}, u32[]{:S(2)}, u32[]{:S(2)}) %collective-permute-start.2) | collective-permute-done | bytes 98336 | tf_op jit(solution)/shard_map/ppermute | solution.py:218
  9.5 1.2 %collective-permute-done.1.refs_0_ = f32[192,128]{1,0:T(8,128)S(1)} collective-permute-done((f32[192,128]{1,0:T(8,128)}, f32[192,128]{1,0:T(8,128)S(1)}, u32[]{:S(2)}, u32[]{:S(2)}) %collective-permute-start.1) | collective-permute-done | bytes 98336 | tf_op jit(solution)/shard_map/ppermute | solution.py:218
  10.7 0.3 %span.1 = (f32[192,128]{1,0:T(8,128)S(1)}, f32[192,128]{1,0:T(8,128)S(1)}) custom-call(f32[64,256]{1,0:T(8,128)S(1)} %get-tuple-element.17.matrix, f32[64,768]{1,0:T(8,128)S(1)} %early.1, f32[192,128]{1,0:T(8,128)S(1)} %collective-permute-done.1.refs_0_, f32[192,128]{1,0:T(8,128)S(1)} %collective-permute-done.2.refs_1_), custom_call_target="tpu_custom_call" | custom-call | tf_op jit(solution)/shard_map/span/pallas_call | solution.py:185
  11.0 3.5 %collective-permute-start.4 = (f32[192,128]{1,0:T(8,128)S(1)}, f32[192,128]{1,0:T(8,128)S(1)}, u32[]{:S(2)}, u32[]{:S(2)}) collective-permute-start(f32[192,128]{1,0:T(8,128)S(1)} %get-tuple-element.22), channel_id=1, source_target_pairs={{0,6},{1,7},{2,4},{3,5},{4,2},{5,3},{6,0},{7,1},{8,14},{9,15},{10,... | collective-permute-start | bytes 294920 | tf_op jit(solution)/shard_map/ppermute | solution.py:218
  14.5 0.6 %copy-done.7 = f32[64]{0:T(128)S(1)} copy-done((f32[64]{0:T(128)S(1)}, f32[64]{0:T(128)}, u32[]{:S(2)}) %copy-start.7) | copy-done | bytes 280
  15.1 0.0 copy-done.8
  15.2 0.5 %wall_matrix.1.matrix = f32[128,256]{1,0:T(8,128)S(1)} custom-call(f32[128,32]{1,0:T(8,128)S(1)} %get-tuple-element.15.ends, f32[128,32]{1,0:T(8,128)S(1)} %get-tuple-element.16.others, f32[1,64]{1,0:T(1,128)S(1)} %bitcast.13, s32[1,32]{1,0:T(1,128)S(1)} %bitcast.14, f32[32,32]{1,0:T(8,128)S(1)} %copy-done.2, f32[32,32]{1,0:T(8,128)S(1)} %copy-done.3, ...), custom_call_target="tpu_custom_call" | custom-call | tf_op jit(solution)/shard_map/wall_matrix/pallas_call | solution.py:185
  15.6 0.3 %wall.1 = (f32[192,128]{1,0:T(8,128)S(1)}, f32[192,128]{1,0:T(8,128)S(1)}) custom-call(f32[128,256]{1,0:T(8,128)S(1)} %wall_matrix.1.matrix, f32[192,128]{1,0:T(8,128)S(1)} %get-tuple-element.18.after.z_part, f32[192,128]{1,0:T(8,128)S(1)} %bitcast.11, f32[192,128]{1,0:T(8,128)S(1)} %collective-permute-done.3.refs_1_), custom_call_target="tpu_custom_call" | custom-call | tf_op jit(solution)/shard_map/wall/pallas_call | solution.py:185
  16.0 0.1 collective-permute-start.5
  16.0 0.0 copy-start.9
  16.1 0.0 copy-start.10
  16.1 0.6 %copy-done.9 = f32[128]{0:T(128)S(1)} copy-done((f32[128]{0:T(128)S(1)}, f32[128]{0:T(128)}, u32[]{:S(2)}) %copy-start.9) | copy-done | bytes 536
  16.7 0.0 copy-done.10
  16.7 0.3 %stream.1.refs_1_ = f32[192,128]{1,0:T(8,128)S(1)} custom-call(f32[192,128]{1,0:T(8,128)S(1)} %bitcast.12, f32[1,128]{1,0:T(1,128)S(1)} %bitcast.15, f32[1,128]{1,0:T(1,128)S(1)} %bitcast.16, f32[192,128]{1,0:T(8,128)S(1)} %get-tuple-element.21.after), custom_call_target="tpu_custom_call" | custom-call | tf_op jit(solution)/shard_map/stream/pallas_call | solution.py:185
  17.0 0.5 %collective-permute-done.4.refs_2_ = f32[192,128]{1,0:T(8,128)S(1)} collective-permute-done((f32[192,128]{1,0:T(8,128)S(1)}, f32[192,128]{1,0:T(8,128)S(1)}, u32[]{:S(2)}, u32[]{:S(2)}) %collective-permute-start.4) | collective-permute-done | bytes 98336 | tf_op jit(solution)/shard_map/ppermute | solution.py:218
  17.6 0.7 %finish.1 = f32[192,128]{1,0:T(8,128)} custom-call(f32[192,128]{1,0:T(8,128)S(1)} %sum.1.total, f32[192,128]{1,0:T(8,128)S(1)} %collective-permute-done.5.near), custom_call_target="tpu_custom_call" | custom-call | tf_op jit(solution)/shard_map/finish/pallas_call | solution.py:185
  (18 shorter events, 0.1 us)
Async XLA Ops:
  0.0 4.6 %copy-start.6 = (f32[32]{0:T(128)S(1)}, f32[32]{0:T(128)}, u32[]{:S(2)}) copy-start(f32[32]{0:T(128)} %z_second.1) | copy-start | bytes 388
  0.0 4.6 %copy-start.5 = (f32[32]{0:T(128)S(1)}, f32[32]{0:T(128)}, u32[]{:S(2)}) copy-start(f32[32]{0:T(128)} %z_first.1) | copy-start | bytes 388
  0.0 4.6 %copy-start.4 = (s32[4]{0:T(128)S(1)}, s32[4]{0:T(128)}, u32[]{:S(2)}) copy-start(s32[4]{0:T(128)} %wall_counts.1) | copy-start | bytes 52
  0.0 8.3 %collective-permute-start = (f32[192,128]{1,0:T(8,128)}, f32[192,128]{1,0:T(8,128)S(1)}, u32[]{:S(2)}, u32[]{:S(2)}) collective-permute-start(f32[192,128]{1,0:T(8,128)} %bitcast.6), channel_id=1, source_target_pairs={{0,2},{1,3},{2,0},{3,1},{4,6},{5,7},{6,4},{7,5},{8,10},{9,11},{10,... | collective-permute-start | bytes 294920 | tf_op jit(solution)/shard_map/ppermute | solution.py:218
  3.1 6.4 %collective-permute-start.2 = (f32[192,128]{1,0:T(8,128)}, f32[192,128]{1,0:T(8,128)S(1)}, u32[]{:S(2)}, u32[]{:S(2)}) collective-permute-start(f32[192,128]{1,0:T(8,128)} %bitcast.7), channel_id=1, source_target_pairs={{0,3},{1,2},{2,1},{3,0},{4,7},{5,6},{6,5},{7,4},{8,11},{9,10},{10,... | collective-permute-start | bytes 294920 | tf_op jit(solution)/shard_map/ppermute | solution.py:218
  4.5 6.2 %collective-permute-start.1 = (f32[192,128]{1,0:T(8,128)}, f32[192,128]{1,0:T(8,128)S(1)}, u32[]{:S(2)}, u32[]{:S(2)}) collective-permute-start(f32[192,128]{1,0:T(8,128)} %bitcast.8), channel_id=1, source_target_pairs={{0,1},{1,0},{2,3},{3,2},{4,5},{5,4},{6,7},{7,6},{8,9},{9,8},{10,11... | collective-permute-start | bytes 294920 | tf_op jit(solution)/shard_map/ppermute | solution.py:218
  4.6 0.9 %copy-start = (f32[3,16,4,128]{3,2,1,0:T(4,128)S(1)}, f32[3,16,4,128]{3,2,1,0:T(4,128)}, u32[]{:S(2)}) copy-start(f32[3,16,4,128]{3,2,1,0:T(4,128)} %param.10) | copy-start | bytes 294916
  5.6 2.7 %copy-start.1 = (f32[3,16,4,128]{3,2,1,0:T(4,128)S(1)}, f32[3,16,4,128]{3,2,1,0:T(4,128)}, u32[]{:S(2)}) copy-start(f32[3,16,4,128]{3,2,1,0:T(4,128)} %param.10) | copy-start | bytes 294916
  6.3 9.3 %collective-permute-start.3 = (f32[192,128]{1,0:T(8,128)S(1)}, f32[192,128]{1,0:T(8,128)S(1)}, u32[]{:S(2)}, u32[]{:S(2)}) collective-permute-start(f32[192,128]{1,0:T(8,128)S(1)} %get-tuple-element.19), channel_id=1, source_target_pairs={{0,16},{8,24},{16,0},{24,8},{1,17},{9,25},{17,1},{25,9},{2,18},{10... | collective-permute-start | bytes 294920 | tf_op jit(solution)/shard_map/ppermute | solution.py:221
  10.7 3.8 %copy-start.2 = (f32[32,32]{1,0:T(8,128)S(1)}, f32[32,32]{1,0:T(8,128)}, u32[]{:S(2)}) copy-start(f32[32,32]{1,0:T(8,128)} %y_first.1) | copy-start | bytes 12292
  10.7 3.8 %copy-start.3 = (f32[32,32]{1,0:T(8,128)S(1)}, f32[32,32]{1,0:T(8,128)}, u32[]{:S(2)}) copy-start(f32[32,32]{1,0:T(8,128)} %y_second.1) | copy-start | bytes 12292
  11.0 6.6 %collective-permute-start.4 = (f32[192,128]{1,0:T(8,128)S(1)}, f32[192,128]{1,0:T(8,128)S(1)}, u32[]{:S(2)}, u32[]{:S(2)}) collective-permute-start(f32[192,128]{1,0:T(8,128)S(1)} %get-tuple-element.22), channel_id=1, source_target_pairs={{0,6},{1,7},{2,4},{3,5},{4,2},{5,3},{6,0},{7,1},{8,14},{9,15},{10,... | collective-permute-start | bytes 294920 | tf_op jit(solution)/shard_map/ppermute | solution.py:218
  14.5 0.7 %copy-start.7 = (f32[64]{0:T(128)S(1)}, f32[64]{0:T(128)}, u32[]{:S(2)}) copy-start(f32[64]{0:T(128)} %param.18) | copy-start | bytes 772
  14.5 0.7 %copy-start.8 = (s32[32]{0:T(128)S(1)}, s32[32]{0:T(128)}, u32[]{:S(2)}) copy-start(s32[32]{0:T(128)} %param.19) | copy-start | bytes 388
  16.0 1.6 %collective-permute-start.5 = (f32[192,128]{1,0:T(8,128)S(1)}, f32[192,128]{1,0:T(8,128)S(1)}, u32[]{:S(2)}, u32[]{:S(2)}) collective-permute-start(f32[192,128]{1,0:T(8,128)S(1)} %get-tuple-element.21.after), channel_id=1, source_target_pairs={{0,8},{8,0},{16,24},{24,16},{1,9},{9,1},{17,25},{25,17},{2,10},{10... | collective-permute-start | bytes 294920 | tf_op jit(solution)/shard_map/ppermute | solution.py:221
  16.0 0.7 %copy-start.9 = (f32[128]{0:T(128)S(1)}, f32[128]{0:T(128)}, u32[]{:S(2)}) copy-start(f32[128]{0:T(128)} %param.12) | copy-start | bytes 1540
  16.1 0.7 %copy-start.10 = (f32[128]{0:T(128)S(1)}, f32[128]{0:T(128)}, u32[]{:S(2)}) copy-start(f32[128]{0:T(128)} %param.13) | copy-start | bytes 1540

commit v27 on v25

--- a/solution.py
+++ b/solution.py
@@ -35,34 +35,19 @@
     return quad * t + 2 * (t != 0)
 
 
-def quad_sums(comps, matrix, fields, chosen):
+def span_kernel(comps, sources, matrix, *refs):
+    fields, parts = refs[:sources], refs[sources:]
     depth, length = fields[0].shape[0] // comps, fields[0].shape[1]
-    half = matrix.shape[1] // 2
-    group = half // quad
-    left = jnp.concatenate(
-        [matrix[:, start + s * group : start + (s + 1) * group] for start in (0, half) for s in chosen], axis=1
-    )
+    group = matrix.shape[0] // quad
     right = []
     for comp in range(comps):
         for at in range(0, depth, group):
             stack = [field[comp * depth + at : comp * depth + at + group] for field in fields]
             stack += [value * field[2 * depth + at : 2 * depth + at + group] for value, field in zip(stack, fields)]
             right.append(jnp.concatenate(stack, axis=0))
-    return dot_split(left, jnp.concatenate(right, axis=1))
-
-
-def early_kernel(comps, chosen, matrix, *refs):
-    refs[-1][...] = quad_sums(comps, matrix, refs[:-1], chosen)
-
-
-def span_kernel(comps, chosen, matrix, early, *refs):
-    fields, parts = refs[: len(chosen)], refs[len(chosen) :]
-    result = early[...] + quad_sums(comps, matrix, fields, chosen)
-    rows, length = parts[0].shape
-    count = len(parts)
-    group = result.shape[0] // count
-    for t in range(count):
-        for i in range(rows // group):
+    result = dot_split(matrix[...], jnp.concatenate(right, axis=1))
+    for t in range(quad):
+        for i in range(len(right)):
             parts[t][i * group : (i + 1) * group] = result[
                 t * group : (t + 1) * group, i * length : (i + 1) * length
             ]
@@ -94,13 +79,13 @@
     cells_z = cols * zloc
     shape = z_matrix.shape
     half = shape[1] // 2
-    group = half // quad
+    group = shape[0] // quad
     mine = lax.axis_index("col")
     r = lax.broadcasted_iota(jnp.int32, shape, 0)
     q = lax.broadcasted_iota(jnp.int32, shape, 1)
     q = jnp.where(q < half, q, q - half)
-    out_cell = (over(r // group) ^ mine) * zloc + r % zloc
-    in_cell = ((q // group) ^ mine) * zloc + q % zloc
+    out_cell = ((r // group) ^ mine) * zloc + r % zloc
+    in_cell = (over(q // group) ^ mine) * zloc + q % zloc
     same = (r % group) // zloc == (q % group) // zloc
     gap = jnp.where(same, (in_cell - out_cell + cells_z) % cells_z, -1)
     kind = lax.broadcasted_iota(jnp.int32, (1, shape[1]), 1) < half
@@ -220,14 +205,14 @@
     def across(value, step):
         return lax.ppermute(value, "row", [(i, i ^ step) for i in range(rows)])
 
-    gathered = [along(field, t) for t in range(1, quad)]
+    gathered = [along(field, over(t)) for t in range(1, wide)]
     cells = metric_index.shape[0]
     z_matrix, mask, held, ends, others = call(
         functools.partial(span_matrix_kernel, rows, cols, zloc),
         [wall_counts, z_first, z_second, field],
         [SMEM] * 3 + [VMEM],
         [
-            (wide * group, 2 * quad * group),
+            (quad * group, 2 * wide * group),
             (depth, length),
             field.shape,
             (2 * depth, cells),
@@ -236,21 +221,14 @@
         "span_matrix",
     )
     far = [across(held, step) for step in range(2, rows, 2)]
-    (early,) = call(
-        functools.partial(early_kernel, comps, (0, quad - 1)),
-        [z_matrix, field, gathered[-1]],
-        [VMEM] * 3,
-        [(wide * group, comps * (depth // group) * length)],
-        "early",
-    )
     parts = call(
-        functools.partial(span_kernel, comps, tuple(range(1, quad - 1))),
-        [z_matrix, early] + gathered[:-1],
-        [VMEM] * quad,
-        [field.shape] * wide,
+        functools.partial(span_kernel, comps, wide),
+        [z_matrix, field] + gathered,
+        [VMEM] * (1 + wide),
+        [field.shape] * quad,
         "span",
     )
-    returned = [along(parts[t], over(t)) for t in range(1, wide)]
+    returned = [along(parts[t], t) for t in reversed(range(1, quad))]
     (y_matrix,) = call(
         functools.partial(wall_matrix_kernel, zloc),
         [ends, others, metric_table.reshape(1, -1), metric_index.reshape(1, -1), y_first, y_second, parts[0]],

time: 17.2 us -> 17.3 us (level)
  waiting for transfers between devices: 1.1 us -> 1.54 us
  starting transfers between devices: 10.5 us -> 10.3 us
  Pallas kernels: 3.08 us -> 2.9 us
    ppermute x4, waiting for transfers between devices: 0.99 us -> 1.53 us  [along(): return lax.ppermute(value, 'col', [(i, i ^ step) for i in range(cols)])]
    ppermute x2, starting transfers between devices: 2 us -> 1.66 us  [across(): return lax.ppermute(value, 'row', [(i, i ^ step) for i in range(rows)])]
    ppermute x4, starting transfers between devices: 8.48 us -> 8.67 us  [along(): return lax.ppermute(value, 'col', [(i, i ^ step) for i in range(cols)])]
    pallas_call x8 -> x7, Pallas kernels: 3.08 us -> 2.9 us  [call(): pl.pallas_call(kernel, out_shape=results, in_specs=[pl.BlockSpec(memory_s...]
  transfers between devices with their start and end apart: 6 -> 6, of which waited for: 3 -> 2; matrix products, arithmetic and copies ran while one was open for 0% -> 0% of each run, Pallas kernels for 14% -> 13%
where the time goes in v27:
time: 17.3 us; the launch traced here: 17.1 us
  starting transfers between devices  10.3 us (60%)
  Pallas kernels  2.9 us (17%)
  local copies, waits for them, and re-layouts  2.26 us (13%)
  waiting for transfers between devices  1.54 us (9%)
    ppermute x4, starting transfers between devices, along(): return lax.ppermute(value, 'col', [(i, i ^ step) for i in range(cols)])  8.67 us
    pallas_call x7, Pallas kernels, call(): pl.pallas_call(kernel, out_shape=results, in_specs=[pl.BlockSpec(memory_s...  2.9 us
    unnamed x22, local copies, waits for them, and re-layouts  2.26 us
    ppermute x2, starting transfers between devices, across(): return lax.ppermute(value, 'row', [(i, i ^ step) for i in range(rows)])  1.66 us
    ppermute x4, waiting for transfers between devices, along(): return lax.ppermute(value, 'col', [(i, i ^ step) for i in range(cols)])  1.53 us
  transfers between devices with their start and end apart: 6, of which 2 were waited for; matrix products, arithmetic and copies ran while one was open for 0% of the time, Pallas kernels for 13%

profile of v27, /device:TPU:0, one launch (start us, length us, event | category | flops | bytes accessed | tf_op | source)
XLA Modules:
  0.0 17.1 jit_solution(18297869914859512508)
XLA Ops:
  0.0 5.1 %collective-permute-start = (f32[192,128]{1,0:T(8,128)}, f32[192,128]{1,0:T(8,128)S(1)}, u32[]{:S(2)}, u32[]{:S(2)}) collective-permute-start(f32[192,128]{1,0:T(8,128)} %bitcast.6), channel_id=1, source_target_pairs={{0,6},{1,7},{2,4},{3,5},{4,2},{5,3},{6,0},{7,1},{8,14},{9,15},{10,... | collective-permute-start | bytes 294920 | tf_op jit(solution)/shard_map/ppermute | solution.py:203
  5.1 0.9 %copy-done = f32[3,16,4,128]{3,2,1,0:T(4,128)S(1)} copy-done((f32[3,16,4,128]{3,2,1,0:T(4,128)S(1)}, f32[3,16,4,128]{3,2,1,0:T(4,128)}, u32[]{:S(2)}) %copy-start) | copy-done | bytes 98328
  6.1 0.8 %span_matrix.1 = (f32[128,128]{1,0:T(8,128)S(1)}, f32[64,128]{1,0:T(8,128)S(1)}, f32[192,128]{1,0:T(8,128)S(1)}, f32[128,32]{1,0:T(8,128)S(1)}, f32[128,32]{1,0:T(8,128)S(1)}) custom-call(s32[4]{0:T(128)S(1)} %copy-done.4, f32[32]{0:T(128)S(1)} %copy-done.5, f32[32]{0:T(128)S(1)} %copy-done.6, f32[192,128]{1,0:T(8,128)S(1)} %bitcast.7), custom_call_target="tpu_custom_call" | custom-call | tf_op jit(solution)/shard_map/span_matrix/pallas_call | solution.py:170
  6.9 1.6 %collective-permute-start.1 = (f32[192,128]{1,0:T(8,128)S(1)}, f32[192,128]{1,0:T(8,128)S(1)}, u32[]{:S(2)}, u32[]{:S(2)}) collective-permute-start(f32[192,128]{1,0:T(8,128)S(1)} %get-tuple-element.21), channel_id=1, source_target_pairs={{0,16},{8,24},{16,0},{24,8},{1,17},{9,25},{17,1},{25,9},{2,18},{10... | collective-permute-start | bytes 294920 | tf_op jit(solution)/shard_map/ppermute | solution.py:206
  8.5 0.0 collective-permute-done.refs_1_
  8.5 0.3 %span.1 = (f32[192,128]{1,0:T(8,128)S(1)}, f32[192,128]{1,0:T(8,128)S(1)}, f32[192,128]{1,0:T(8,128)S(1)}, f32[192,128]{1,0:T(8,128)S(1)}) custom-call(f32[128,128]{1,0:T(8,128)S(1)} %get-tuple-element.19.matrix, f32[192,128]{1,0:T(8,128)S(1)} %bitcast.8, f32[192,128]{1,0:T(8,128)S(1)} %collective-permute-done.refs_1_), custom_call_target="tpu_custom_call" | custom-call | tf_op jit(solution)/shard_map/span/pallas_call | solution.py:170
  8.8 2.5 %collective-permute-start.2 = (f32[192,128]{1,0:T(8,128)S(1)}, f32[192,128]{1,0:T(8,128)S(1)}, u32[]{:S(2)}, u32[]{:S(2)}) collective-permute-start(f32[192,128]{1,0:T(8,128)S(1)} %get-tuple-element.24), channel_id=1, source_target_pairs={{0,3},{1,2},{2,1},{3,0},{4,7},{5,6},{6,5},{7,4},{8,11},{9,10},{10,... | collective-permute-start | bytes 294920 | tf_op jit(solution)/shard_map/ppermute | solution.py:203
  11.3 0.5 %collective-permute-start.3 = (f32[192,128]{1,0:T(8,128)S(1)}, f32[192,128]{1,0:T(8,128)S(1)}, u32[]{:S(2)}, u32[]{:S(2)}) collective-permute-start(f32[192,128]{1,0:T(8,128)S(1)} %get-tuple-element.25), channel_id=1, source_target_pairs={{0,2},{1,3},{2,0},{3,1},{4,6},{5,7},{6,4},{7,5},{8,10},{9,11},{10,... | collective-permute-start | bytes 294920 | tf_op jit(solution)/shard_map/ppermute | solution.py:203
  11.8 0.5 %collective-permute-start.4 = (f32[192,128]{1,0:T(8,128)S(1)}, f32[192,128]{1,0:T(8,128)S(1)}, u32[]{:S(2)}, u32[]{:S(2)}) collective-permute-start(f32[192,128]{1,0:T(8,128)S(1)} %get-tuple-element.26), channel_id=1, source_target_pairs={{0,1},{1,0},{2,3},{3,2},{4,5},{5,4},{6,7},{7,6},{8,9},{9,8},{10,11... | collective-permute-start | bytes 294920 | tf_op jit(solution)/shard_map/ppermute | solution.py:203
  12.3 0.6 %copy-done.7 = f32[64]{0:T(128)S(1)} copy-done((f32[64]{0:T(128)S(1)}, f32[64]{0:T(128)}, u32[]{:S(2)}) %copy-start.7) | copy-done | bytes 280
  13.0 0.0 copy-done.8
  13.0 0.5 %wall_matrix.1.matrix = f32[128,256]{1,0:T(8,128)S(1)} custom-call(f32[128,32]{1,0:T(8,128)S(1)} %get-tuple-element.17.ends, f32[128,32]{1,0:T(8,128)S(1)} %get-tuple-element.18.others, f32[1,64]{1,0:T(1,128)S(1)} %bitcast.11, s32[1,32]{1,0:T(1,128)S(1)} %bitcast.12, f32[32,32]{1,0:T(8,128)S(1)} %copy-done.2, f32[32,32]{1,0:T(8,128)S(1)} %copy-done.3, ...), custom_call_target="tpu_custom_call" | custom-call | tf_op jit(solution)/shard_map/wall_matrix/pallas_call | solution.py:170
  13.5 0.0 collective-permute-done.1.refs_1_
  13.5 0.3 %wall.1 = (f32[192,128]{1,0:T(8,128)S(1)}, f32[192,128]{1,0:T(8,128)S(1)}) custom-call(f32[128,256]{1,0:T(8,128)S(1)} %wall_matrix.1.matrix, f32[192,128]{1,0:T(8,128)S(1)} %get-tuple-element.20.after.z_part, f32[192,128]{1,0:T(8,128)S(1)} %bitcast.9, f32[192,128]{1,0:T(8,128)S(1)} %collective-permute-done.1.refs_1_), custom_call_target="tpu_custom_call" | custom-call | tf_op jit(solution)/shard_map/wall/pallas_call | solution.py:170
  13.8 0.1 collective-permute-start.5
  13.9 0.0 copy-start.9
  13.9 0.0 copy-start.10
  13.9 0.6 %copy-done.9 = f32[128]{0:T(128)S(1)} copy-done((f32[128]{0:T(128)S(1)}, f32[128]{0:T(128)}, u32[]{:S(2)}) %copy-start.9) | copy-done | bytes 536
  14.5 0.0 copy-done.10
  14.6 0.3 %stream.1.refs_1_ = f32[192,128]{1,0:T(8,128)S(1)} custom-call(f32[192,128]{1,0:T(8,128)S(1)} %bitcast.10, f32[1,128]{1,0:T(1,128)S(1)} %bitcast.13, f32[1,128]{1,0:T(1,128)S(1)} %bitcast.14, f32[192,128]{1,0:T(8,128)S(1)} %get-tuple-element.23.after), custom_call_target="tpu_custom_call" | custom-call | tf_op jit(solution)/shard_map/stream/pallas_call | solution.py:170
  14.9 1.0 %collective-permute-done.3.refs_3_ = f32[192,128]{1,0:T(8,128)S(1)} collective-permute-done((f32[192,128]{1,0:T(8,128)S(1)}, f32[192,128]{1,0:T(8,128)S(1)}, u32[]{:S(2)}, u32[]{:S(2)}) %collective-permute-start.3) | collective-permute-done | bytes 98336 | tf_op jit(solution)/shard_map/ppermute | solution.py:203
  15.9 0.5 %collective-permute-done.4.refs_4_ = f32[192,128]{1,0:T(8,128)S(1)} collective-permute-done((f32[192,128]{1,0:T(8,128)S(1)}, f32[192,128]{1,0:T(8,128)S(1)}, u32[]{:S(2)}, u32[]{:S(2)}) %collective-permute-start.4) | collective-permute-done | bytes 98336 | tf_op jit(solution)/shard_map/ppermute | solution.py:203
  16.4 0.0 collective-permute-done.5.near
  16.5 0.7 %finish.1 = f32[192,128]{1,0:T(8,128)} custom-call(f32[192,128]{1,0:T(8,128)S(1)} %sum.1.total, f32[192,128]{1,0:T(8,128)S(1)} %collective-permute-done.5.near), custom_call_target="tpu_custom_call" | custom-call | tf_op jit(solution)/shard_map/finish/pallas_call | solution.py:170
  (17 shorter events, 0.1 us)
Async XLA Ops:
  0.0 5.1 %copy-start.6 = (f32[32]{0:T(128)S(1)}, f32[32]{0:T(128)}, u32[]{:S(2)}) copy-start(f32[32]{0:T(128)} %z_second.1) | copy-start | bytes 388
  0.0 5.1 %copy-start.5 = (f32[32]{0:T(128)S(1)}, f32[32]{0:T(128)}, u32[]{:S(2)}) copy-start(f32[32]{0:T(128)} %z_first.1) | copy-start | bytes 388
  0.0 5.1 %copy-start.4 = (s32[4]{0:T(128)S(1)}, s32[4]{0:T(128)}, u32[]{:S(2)}) copy-start(s32[4]{0:T(128)} %wall_counts.1) | copy-start | bytes 52
  0.0 8.5 %collective-permute-start = (f32[192,128]{1,0:T(8,128)}, f32[192,128]{1,0:T(8,128)S(1)}, u32[]{:S(2)}, u32[]{:S(2)}) collective-permute-start(f32[192,128]{1,0:T(8,128)} %bitcast.6), channel_id=1, source_target_pairs={{0,6},{1,7},{2,4},{3,5},{4,2},{5,3},{6,0},{7,1},{8,14},{9,15},{10,... | collective-permute-start | bytes 294920 | tf_op jit(solution)/shard_map/ppermute | solution.py:203
  5.1 0.9 %copy-start = (f32[3,16,4,128]{3,2,1,0:T(4,128)S(1)}, f32[3,16,4,128]{3,2,1,0:T(4,128)}, u32[]{:S(2)}) copy-start(f32[3,16,4,128]{3,2,1,0:T(4,128)} %param.10) | copy-start | bytes 294916
  6.1 2.4 %copy-start.1 = (f32[3,16,4,128]{3,2,1,0:T(4,128)S(1)}, f32[3,16,4,128]{3,2,1,0:T(4,128)}, u32[]{:S(2)}) copy-start(f32[3,16,4,128]{3,2,1,0:T(4,128)} %param.10) | copy-start | bytes 294916
  6.9 6.6 %collective-permute-start.1 = (f32[192,128]{1,0:T(8,128)S(1)}, f32[192,128]{1,0:T(8,128)S(1)}, u32[]{:S(2)}, u32[]{:S(2)}) collective-permute-start(f32[192,128]{1,0:T(8,128)S(1)} %get-tuple-element.21), channel_id=1, source_target_pairs={{0,16},{8,24},{16,0},{24,8},{1,17},{9,25},{17,1},{25,9},{2,18},{10... | collective-permute-start | bytes 294920 | tf_op jit(solution)/shard_map/ppermute | solution.py:206
  8.5 3.9 %copy-start.2 = (f32[32,32]{1,0:T(8,128)S(1)}, f32[32,32]{1,0:T(8,128)}, u32[]{:S(2)}) copy-start(f32[32,32]{1,0:T(8,128)} %y_first.1) | copy-start | bytes 12292
  8.5 3.9 %copy-start.3 = (f32[32,32]{1,0:T(8,128)S(1)}, f32[32,32]{1,0:T(8,128)}, u32[]{:S(2)}) copy-start(f32[32,32]{1,0:T(8,128)} %y_second.1) | copy-start | bytes 12292
  8.8 6.1 %collective-permute-start.2 = (f32[192,128]{1,0:T(8,128)S(1)}, f32[192,128]{1,0:T(8,128)S(1)}, u32[]{:S(2)}, u32[]{:S(2)}) collective-permute-start(f32[192,128]{1,0:T(8,128)S(1)} %get-tuple-element.24), channel_id=1, source_target_pairs={{0,3},{1,2},{2,1},{3,0},{4,7},{5,6},{6,5},{7,4},{8,11},{9,10},{10,... | collective-permute-start | bytes 294920 | tf_op jit(solution)/shard_map/ppermute | solution.py:203
  11.3 4.6 %collective-permute-start.3 = (f32[192,128]{1,0:T(8,128)S(1)}, f32[192,128]{1,0:T(8,128)S(1)}, u32[]{:S(2)}, u32[]{:S(2)}) collective-permute-start(f32[192,128]{1,0:T(8,128)S(1)} %get-tuple-element.25), channel_id=1, source_target_pairs={{0,2},{1,3},{2,0},{3,1},{4,6},{5,7},{6,4},{7,5},{8,10},{9,11},{10,... | collective-permute-start | bytes 294920 | tf_op jit(solution)/shard_map/ppermute | solution.py:203
  11.8 4.6 %collective-permute-start.4 = (f32[192,128]{1,0:T(8,128)S(1)}, f32[192,128]{1,0:T(8,128)S(1)}, u32[]{:S(2)}, u32[]{:S(2)}) collective-permute-start(f32[192,128]{1,0:T(8,128)S(1)} %get-tuple-element.26), channel_id=1, source_target_pairs={{0,1},{1,0},{2,3},{3,2},{4,5},{5,4},{6,7},{7,6},{8,9},{9,8},{10,11... | collective-permute-start | bytes 294920 | tf_op jit(solution)/shard_map/ppermute | solution.py:203
  12.3 0.7 %copy-start.7 = (f32[64]{0:T(128)S(1)}, f32[64]{0:T(128)}, u32[]{:S(2)}) copy-start(f32[64]{0:T(128)} %param.18) | copy-start | bytes 772
  12.3 0.7 %copy-start.8 = (s32[32]{0:T(128)S(1)}, s32[32]{0:T(128)}, u32[]{:S(2)}) copy-start(s32[32]{0:T(128)} %param.19) | copy-start | bytes 388
  13.8 2.6 %collective-permute-start.5 = (f32[192,128]{1,0:T(8,128)S(1)}, f32[192,128]{1,0:T(8,128)S(1)}, u32[]{:S(2)}, u32[]{:S(2)}) collective-permute-start(f32[192,128]{1,0:T(8,128)S(1)} %get-tuple-element.23.after), channel_id=1, source_target_pairs={{0,8},{8,0},{16,24},{24,16},{1,9},{9,1},{17,25},{25,17},{2,10},{10... | collective-permute-start | bytes 294920 | tf_op jit(solution)/shard_map/ppermute | solution.py:206
  13.9 0.7 %copy-start.9 = (f32[128]{0:T(128)S(1)}, f32[128]{0:T(128)}, u32[]{:S(2)}) copy-start(f32[128]{0:T(128)} %param.12) | copy-start | bytes 1540
  13.9 0.7 %copy-start.10 = (f32[128]{0:T(128)S(1)}, f32[128]{0:T(128)}, u32[]{:S(2)}) copy-start(f32[128]{0:T(128)} %param.13) | copy-start | bytes 1540

commit v28 on v27

--- a/solution.py
+++ b/solution.py
@@ -32,7 +32,7 @@
 
 
 def over(t):
-    return quad * t + 2 * (t != 0)
+    return quad * t + 3 * (t != 0)
 
 
 def span_kernel(comps, sources, matrix, *refs):

time: 17.3 us -> 17.9 us (1.035)
  starting transfers between devices: 10.3 us -> 11.3 us
  waiting for transfers between devices: 1.54 us -> 1.21 us
    ppermute x4, starting transfers between devices: 8.67 us -> 9.6 us  [along(): return lax.ppermute(value, 'col', [(i, i ^ step) for i in range(cols)])]
    ppermute x4, waiting for transfers between devices: 1.53 us -> 1.21 us  [along(): return lax.ppermute(value, 'col', [(i, i ^ step) for i in range(cols)])]
where the time goes in v28:
time: 17.9 us; the launch traced here: 17.7 us
  starting transfers between devices  11.3 us (63%)
  Pallas kernels  2.9 us (16%)
  local copies, waits for them, and re-layouts  2.26 us (13%)
  waiting for transfers between devices  1.21 us (7%)
    ppermute x4, starting transfers between devices, along(): return lax.ppermute(value, 'col', [(i, i ^ step) for i in range(cols)])  9.6 us
    pallas_call x7, Pallas kernels, call(): pl.pallas_call(kernel, out_shape=results, in_specs=[pl.BlockSpec(memory_s...  2.9 us
    unnamed x22, local copies, waits for them, and re-layouts  2.26 us
    ppermute x2, starting transfers between devices, across(): return lax.ppermute(value, 'row', [(i, i ^ step) for i in range(rows)])  1.66 us
    ppermute x4, waiting for transfers between devices, along(): return lax.ppermute(value, 'col', [(i, i ^ step) for i in range(cols)])  1.21 us
  transfers between devices with their start and end apart: 6, of which 2 were waited for; matrix products, arithmetic and copies ran while one was open for 0% of the time, Pallas kernels for 13%

profile of v28, /device:TPU:0, one launch (start us, length us, event | category | flops | bytes accessed | tf_op | source)
XLA Modules:
  0.0 17.7 jit_solution(11726603343076888351)
XLA Ops:
  0.0 6.0 %collective-permute-start = (f32[192,128]{1,0:T(8,128)}, f32[192,128]{1,0:T(8,128)S(1)}, u32[]{:S(2)}, u32[]{:S(2)}) collective-permute-start(f32[192,128]{1,0:T(8,128)} %bitcast.6), channel_id=1, source_target_pairs={{0,7},{1,6},{2,5},{3,4},{4,3},{5,2},{6,1},{7,0},{8,15},{9,14},{10,... | collective-permute-start | bytes 294920 | tf_op jit(solution)/shard_map/ppermute | solution.py:203
  6.1 0.9 %copy-done = f32[3,16,4,128]{3,2,1,0:T(4,128)S(1)} copy-done((f32[3,16,4,128]{3,2,1,0:T(4,128)S(1)}, f32[3,16,4,128]{3,2,1,0:T(4,128)}, u32[]{:S(2)}) %copy-start) | copy-done | bytes 98328
  7.0 0.8 %span_matrix.1 = (f32[128,128]{1,0:T(8,128)S(1)}, f32[64,128]{1,0:T(8,128)S(1)}, f32[192,128]{1,0:T(8,128)S(1)}, f32[128,32]{1,0:T(8,128)S(1)}, f32[128,32]{1,0:T(8,128)S(1)}) custom-call(s32[4]{0:T(128)S(1)} %copy-done.4, f32[32]{0:T(128)S(1)} %copy-done.5, f32[32]{0:T(128)S(1)} %copy-done.6, f32[192,128]{1,0:T(8,128)S(1)} %bitcast.7), custom_call_target="tpu_custom_call" | custom-call | tf_op jit(solution)/shard_map/span_matrix/pallas_call | solution.py:170
  7.8 1.6 %collective-permute-start.1 = (f32[192,128]{1,0:T(8,128)S(1)}, f32[192,128]{1,0:T(8,128)S(1)}, u32[]{:S(2)}, u32[]{:S(2)}) collective-permute-start(f32[192,128]{1,0:T(8,128)S(1)} %get-tuple-element.21), channel_id=1, source_target_pairs={{0,16},{8,24},{16,0},{24,8},{1,17},{9,25},{17,1},{25,9},{2,18},{10... | collective-permute-start | bytes 294920 | tf_op jit(solution)/shard_map/ppermute | solution.py:206
  9.4 0.0 collective-permute-done.refs_1_
  9.4 0.3 %span.1 = (f32[192,128]{1,0:T(8,128)S(1)}, f32[192,128]{1,0:T(8,128)S(1)}, f32[192,128]{1,0:T(8,128)S(1)}, f32[192,128]{1,0:T(8,128)S(1)}) custom-call(f32[128,128]{1,0:T(8,128)S(1)} %get-tuple-element.19.matrix, f32[192,128]{1,0:T(8,128)S(1)} %bitcast.8, f32[192,128]{1,0:T(8,128)S(1)} %collective-permute-done.refs_1_), custom_call_target="tpu_custom_call" | custom-call | tf_op jit(solution)/shard_map/span/pallas_call | solution.py:170
  9.7 2.4 %collective-permute-start.2 = (f32[192,128]{1,0:T(8,128)S(1)}, f32[192,128]{1,0:T(8,128)S(1)}, u32[]{:S(2)}, u32[]{:S(2)}) collective-permute-start(f32[192,128]{1,0:T(8,128)S(1)} %get-tuple-element.24), channel_id=1, source_target_pairs={{0,3},{1,2},{2,1},{3,0},{4,7},{5,6},{6,5},{7,4},{8,11},{9,10},{10,... | collective-permute-start | bytes 294920 | tf_op jit(solution)/shard_map/ppermute | solution.py:203
  12.2 0.2 %collective-permute-start.3 = (f32[192,128]{1,0:T(8,128)S(1)}, f32[192,128]{1,0:T(8,128)S(1)}, u32[]{:S(2)}, u32[]{:S(2)}) collective-permute-start(f32[192,128]{1,0:T(8,128)S(1)} %get-tuple-element.25), channel_id=1, source_target_pairs={{0,2},{1,3},{2,0},{3,1},{4,6},{5,7},{6,4},{7,5},{8,10},{9,11},{10,... | collective-permute-start | bytes 294920 | tf_op jit(solution)/shard_map/ppermute | solution.py:203
  12.4 0.9 %collective-permute-start.4 = (f32[192,128]{1,0:T(8,128)S(1)}, f32[192,128]{1,0:T(8,128)S(1)}, u32[]{:S(2)}, u32[]{:S(2)}) collective-permute-start(f32[192,128]{1,0:T(8,128)S(1)} %get-tuple-element.26), channel_id=1, source_target_pairs={{0,1},{1,0},{2,3},{3,2},{4,5},{5,4},{6,7},{7,6},{8,9},{9,8},{10,11... | collective-permute-start | bytes 294920 | tf_op jit(solution)/shard_map/ppermute | solution.py:203
  13.3 0.6 %copy-done.7 = f32[64]{0:T(128)S(1)} copy-done((f32[64]{0:T(128)S(1)}, f32[64]{0:T(128)}, u32[]{:S(2)}) %copy-start.7) | copy-done | bytes 280
  13.9 0.0 copy-done.8
  13.9 0.5 %wall_matrix.1.matrix = f32[128,256]{1,0:T(8,128)S(1)} custom-call(f32[128,32]{1,0:T(8,128)S(1)} %get-tuple-element.17.ends, f32[128,32]{1,0:T(8,128)S(1)} %get-tuple-element.18.others, f32[1,64]{1,0:T(1,128)S(1)} %bitcast.11, s32[1,32]{1,0:T(1,128)S(1)} %bitcast.12, f32[32,32]{1,0:T(8,128)S(1)} %copy-done.2, f32[32,32]{1,0:T(8,128)S(1)} %copy-done.3, ...), custom_call_target="tpu_custom_call" | custom-call | tf_op jit(solution)/shard_map/wall_matrix/pallas_call | solution.py:170
  14.4 0.0 collective-permute-done.1.refs_1_
  14.4 0.3 %wall.1 = (f32[192,128]{1,0:T(8,128)S(1)}, f32[192,128]{1,0:T(8,128)S(1)}) custom-call(f32[128,256]{1,0:T(8,128)S(1)} %wall_matrix.1.matrix, f32[192,128]{1,0:T(8,128)S(1)} %get-tuple-element.20.after.z_part, f32[192,128]{1,0:T(8,128)S(1)} %bitcast.9, f32[192,128]{1,0:T(8,128)S(1)} %collective-permute-done.1.refs_1_), custom_call_target="tpu_custom_call" | custom-call | tf_op jit(solution)/shard_map/wall/pallas_call | solution.py:170
  14.7 0.1 collective-permute-start.5
  14.8 0.0 copy-start.9
  14.8 0.0 copy-start.10
  14.8 0.6 %copy-done.9 = f32[128]{0:T(128)S(1)} copy-done((f32[128]{0:T(128)S(1)}, f32[128]{0:T(128)}, u32[]{:S(2)}) %copy-start.9) | copy-done | bytes 536
  15.5 0.0 copy-done.10
  15.5 0.3 %stream.1.refs_1_ = f32[192,128]{1,0:T(8,128)S(1)} custom-call(f32[192,128]{1,0:T(8,128)S(1)} %bitcast.10, f32[1,128]{1,0:T(1,128)S(1)} %bitcast.13, f32[1,128]{1,0:T(1,128)S(1)} %bitcast.14, f32[192,128]{1,0:T(8,128)S(1)} %get-tuple-element.23.after), custom_call_target="tpu_custom_call" | custom-call | tf_op jit(solution)/shard_map/stream/pallas_call | solution.py:170
  15.8 0.0 collective-permute-done.2.refs_2_
  15.8 1.0 %collective-permute-done.3.refs_3_ = f32[192,128]{1,0:T(8,128)S(1)} collective-permute-done((f32[192,128]{1,0:T(8,128)S(1)}, f32[192,128]{1,0:T(8,128)S(1)}, u32[]{:S(2)}, u32[]{:S(2)}) %collective-permute-start.3) | collective-permute-done | bytes 98336 | tf_op jit(solution)/shard_map/ppermute | solution.py:203
  16.8 0.2 %collective-permute-done.4.refs_4_ = f32[192,128]{1,0:T(8,128)S(1)} collective-permute-done((f32[192,128]{1,0:T(8,128)S(1)}, f32[192,128]{1,0:T(8,128)S(1)}, u32[]{:S(2)}, u32[]{:S(2)}) %collective-permute-start.4) | collective-permute-done | bytes 98336 | tf_op jit(solution)/shard_map/ppermute | solution.py:203
  17.1 0.7 %finish.1 = f32[192,128]{1,0:T(8,128)} custom-call(f32[192,128]{1,0:T(8,128)S(1)} %sum.1.total, f32[192,128]{1,0:T(8,128)S(1)} %collective-permute-done.5.near), custom_call_target="tpu_custom_call" | custom-call | tf_op jit(solution)/shard_map/finish/pallas_call | solution.py:170
  (17 shorter events, 0.1 us)
Async XLA Ops:
  0.0 6.1 %copy-start.6 = (f32[32]{0:T(128)S(1)}, f32[32]{0:T(128)}, u32[]{:S(2)}) copy-start(f32[32]{0:T(128)} %z_second.1) | copy-start | bytes 388
  0.0 6.1 %copy-start.5 = (f32[32]{0:T(128)S(1)}, f32[32]{0:T(128)}, u32[]{:S(2)}) copy-start(f32[32]{0:T(128)} %z_first.1) | copy-start | bytes 388
  0.0 6.1 %copy-start.4 = (s32[4]{0:T(128)S(1)}, s32[4]{0:T(128)}, u32[]{:S(2)}) copy-start(s32[4]{0:T(128)} %wall_counts.1) | copy-start | bytes 52
  0.0 9.4 %collective-permute-start = (f32[192,128]{1,0:T(8,128)}, f32[192,128]{1,0:T(8,128)S(1)}, u32[]{:S(2)}, u32[]{:S(2)}) collective-permute-start(f32[192,128]{1,0:T(8,128)} %bitcast.6), channel_id=1, source_target_pairs={{0,7},{1,6},{2,5},{3,4},{4,3},{5,2},{6,1},{7,0},{8,15},{9,14},{10,... | collective-permute-start | bytes 294920 | tf_op jit(solution)/shard_map/ppermute | solution.py:203
  6.1 0.9 %copy-start = (f32[3,16,4,128]{3,2,1,0:T(4,128)S(1)}, f32[3,16,4,128]{3,2,1,0:T(4,128)}, u32[]{:S(2)}) copy-start(f32[3,16,4,128]{3,2,1,0:T(4,128)} %param.10) | copy-start | bytes 294916
  7.0 2.4 %copy-start.1 = (f32[3,16,4,128]{3,2,1,0:T(4,128)S(1)}, f32[3,16,4,128]{3,2,1,0:T(4,128)}, u32[]{:S(2)}) copy-start(f32[3,16,4,128]{3,2,1,0:T(4,128)} %param.10) | copy-start | bytes 294916
  7.8 6.6 %collective-permute-start.1 = (f32[192,128]{1,0:T(8,128)S(1)}, f32[192,128]{1,0:T(8,128)S(1)}, u32[]{:S(2)}, u32[]{:S(2)}) collective-permute-start(f32[192,128]{1,0:T(8,128)S(1)} %get-tuple-element.21), channel_id=1, source_target_pairs={{0,16},{8,24},{16,0},{24,8},{1,17},{9,25},{17,1},{25,9},{2,18},{10... | collective-permute-start | bytes 294920 | tf_op jit(solution)/shard_map/ppermute | solution.py:206
  9.4 3.9 %copy-start.2 = (f32[32,32]{1,0:T(8,128)S(1)}, f32[32,32]{1,0:T(8,128)}, u32[]{:S(2)}) copy-start(f32[32,32]{1,0:T(8,128)} %y_first.1) | copy-start | bytes 12292
  9.4 3.9 %copy-start.3 = (f32[32,32]{1,0:T(8,128)S(1)}, f32[32,32]{1,0:T(8,128)}, u32[]{:S(2)}) copy-start(f32[32,32]{1,0:T(8,128)} %y_second.1) | copy-start | bytes 12292
  9.7 6.1 %collective-permute-start.2 = (f32[192,128]{1,0:T(8,128)S(1)}, f32[192,128]{1,0:T(8,128)S(1)}, u32[]{:S(2)}, u32[]{:S(2)}) collective-permute-start(f32[192,128]{1,0:T(8,128)S(1)} %get-tuple-element.24), channel_id=1, source_target_pairs={{0,3},{1,2},{2,1},{3,0},{4,7},{5,6},{6,5},{7,4},{8,11},{9,10},{10,... | collective-permute-start | bytes 294920 | tf_op jit(solution)/shard_map/ppermute | solution.py:203
  12.2 4.7 %collective-permute-start.3 = (f32[192,128]{1,0:T(8,128)S(1)}, f32[192,128]{1,0:T(8,128)S(1)}, u32[]{:S(2)}, u32[]{:S(2)}) collective-permute-start(f32[192,128]{1,0:T(8,128)S(1)} %get-tuple-element.25), channel_id=1, source_target_pairs={{0,2},{1,3},{2,0},{3,1},{4,6},{5,7},{6,4},{7,5},{8,10},{9,11},{10,... | collective-permute-start | bytes 294920 | tf_op jit(solution)/shard_map/ppermute | solution.py:203
  12.4 4.6 %collective-permute-start.4 = (f32[192,128]{1,0:T(8,128)S(1)}, f32[192,128]{1,0:T(8,128)S(1)}, u32[]{:S(2)}, u32[]{:S(2)}) collective-permute-start(f32[192,128]{1,0:T(8,128)S(1)} %get-tuple-element.26), channel_id=1, source_target_pairs={{0,1},{1,0},{2,3},{3,2},{4,5},{5,4},{6,7},{7,6},{8,9},{9,8},{10,11... | collective-permute-start | bytes 294920 | tf_op jit(solution)/shard_map/ppermute | solution.py:203
  13.3 0.7 %copy-start.7 = (f32[64]{0:T(128)S(1)}, f32[64]{0:T(128)}, u32[]{:S(2)}) copy-start(f32[64]{0:T(128)} %param.18) | copy-start | bytes 772
  13.3 0.7 %copy-start.8 = (s32[32]{0:T(128)S(1)}, s32[32]{0:T(128)}, u32[]{:S(2)}) copy-start(s32[32]{0:T(128)} %param.19) | copy-start | bytes 388
  14.7 2.3 %collective-permute-start.5 = (f32[192,128]{1,0:T(8,128)S(1)}, f32[192,128]{1,0:T(8,128)S(1)}, u32[]{:S(2)}, u32[]{:S(2)}) collective-permute-start(f32[192,128]{1,0:T(8,128)S(1)} %get-tuple-element.23.after), channel_id=1, source_target_pairs={{0,8},{8,0},{16,24},{24,16},{1,9},{9,1},{17,25},{25,17},{2,10},{10... | collective-permute-start | bytes 294920 | tf_op jit(solution)/shard_map/ppermute | solution.py:206
  14.8 0.7 %copy-start.9 = (f32[128]{0:T(128)S(1)}, f32[128]{0:T(128)}, u32[]{:S(2)}) copy-start(f32[128]{0:T(128)} %param.12) | copy-start | bytes 1540
  14.8 0.7 %copy-start.10 = (f32[128]{0:T(128)S(1)}, f32[128]{0:T(128)}, u32[]{:S(2)}) copy-start(f32[128]{0:T(128)} %param.13) | copy-start | bytes 1540

commit v29 on v25

--- a/solution.py
+++ b/solution.py
@@ -51,8 +51,10 @@
     return dot_split(left, jnp.concatenate(right, axis=1))
 
 
-def early_kernel(comps, chosen, matrix, *refs):
-    refs[-1][...] = quad_sums(comps, matrix, refs[:-1], chosen)
+def early_kernel(comps, chosen, count, matrix, *refs):
+    fields, before, out = refs[:count], refs[count:-1], refs[-1]
+    value = quad_sums(comps, matrix, fields, chosen)
+    out[...] = value + before[0][...] if before else value
 
 
 def span_kernel(comps, chosen, matrix, early, *refs):
@@ -236,17 +238,21 @@
         "span_matrix",
     )
     far = [across(held, step) for step in range(2, rows, 2)]
-    (early,) = call(
-        functools.partial(early_kernel, comps, (0, quad - 1)),
-        [z_matrix, field, gathered[-1]],
+    early_shape = (wide * group, comps * (depth // group) * length)
+    early = []
+    for chosen in ((0, 3), (2,)):
+        fields = [field if s == 0 else gathered[s - 1] for s in chosen]
+        early = list(call(
+            functools.partial(early_kernel, comps, chosen, len(chosen)),
+            [z_matrix] + fields + early,
+            [VMEM] * (1 + len(chosen) + len(early)),
+            [early_shape],
+            "early",
+        ))
+    parts = call(
+        functools.partial(span_kernel, comps, (1,)),
+        [z_matrix] + early + [gathered[0]],
         [VMEM] * 3,
-        [(wide * group, comps * (depth // group) * length)],
-        "early",
-    )
-    parts = call(
-        functools.partial(span_kernel, comps, tuple(range(1, quad - 1))),
-        [z_matrix, early] + gathered[:-1],
-        [VMEM] * quad,
         [field.shape] * wide,
         "span",
     )

time: 17.2 us -> 17.4 us (1.012)
  starting transfers between devices: 10.5 us -> 10.2 us
  Pallas kernels: 3.08 us -> 3.36 us
  waiting for transfers between devices: 1.1 us -> 1.29 us
    ppermute x4, waiting for transfers between devices: 0.99 us -> 1.28 us  [along(): return lax.ppermute(value, 'col', [(i, i ^ step) for i in range(cols)])]
    pallas_call x8 -> x9, Pallas kernels: 3.08 us -> 3.36 us  [call(): pl.pallas_call(kernel, out_shape=results, in_specs=[pl.BlockSpec(memory_s...]
    ppermute x4, starting transfers between devices: 8.48 us -> 8.24 us  [along(): return lax.ppermute(value, 'col', [(i, i ^ step) for i in range(cols)])]
  transfers between devices with their start and end apart: 6 -> 6, of which waited for: 3 -> 2; matrix products, arithmetic and copies ran while one was open for 0% -> 0% of each run, Pallas kernels for 14% -> 16%
where the time goes in v29:
time: 17.4 us; the launch traced here: 17.3 us
  starting transfers between devices  10.2 us (59%)
  Pallas kernels  3.36 us (19%)
  local copies, waits for them, and re-layouts  2.26 us (13%)
  waiting for transfers between devices  1.29 us (7%)
    ppermute x4, starting transfers between devices, along(): return lax.ppermute(value, 'col', [(i, i ^ step) for i in range(cols)])  8.24 us
    pallas_call x9, Pallas kernels, call(): pl.pallas_call(kernel, out_shape=results, in_specs=[pl.BlockSpec(memory_s...  3.36 us
    unnamed x22, local copies, waits for them, and re-layouts  2.26 us
    ppermute x2, starting transfers between devices, across(): return lax.ppermute(value, 'row', [(i, i ^ step) for i in range(rows)])  2 us
    ppermute x4, waiting for transfers between devices, along(): return lax.ppermute(value, 'col', [(i, i ^ step) for i in range(cols)])  1.28 us
  transfers between devices with their start and end apart: 6, of which 2 were waited for; matrix products, arithmetic and copies ran while one was open for 0% of the time, Pallas kernels for 16%

profile of v29, /device:TPU:0, one launch (start us, length us, event | category | flops | bytes accessed | tf_op | source)
XLA Modules:
  0.0 17.3 jit_solution(13333092101562913740)
XLA Ops:
  0.0 4.0 %collective-permute-start.1 = (f32[192,128]{1,0:T(8,128)}, f32[192,128]{1,0:T(8,128)S(1)}, u32[]{:S(2)}, u32[]{:S(2)}) collective-permute-start(f32[192,128]{1,0:T(8,128)} %bitcast.6), channel_id=1, source_target_pairs={{0,3},{1,2},{2,1},{3,0},{4,7},{5,6},{6,5},{7,4},{8,11},{9,10},{10,... | collective-permute-start | bytes 294920 | tf_op jit(solution)/shard_map/ppermute | solution.py:220
  4.0 0.4 %collective-permute-start = (f32[192,128]{1,0:T(8,128)}, f32[192,128]{1,0:T(8,128)S(1)}, u32[]{:S(2)}, u32[]{:S(2)}) collective-permute-start(f32[192,128]{1,0:T(8,128)} %bitcast.7), channel_id=1, source_target_pairs={{0,2},{1,3},{2,0},{3,1},{4,6},{5,7},{6,4},{7,5},{8,10},{9,11},{10,... | collective-permute-start | bytes 294920 | tf_op jit(solution)/shard_map/ppermute | solution.py:220
  4.5 0.2 %collective-permute-start.2 = (f32[192,128]{1,0:T(8,128)}, f32[192,128]{1,0:T(8,128)S(1)}, u32[]{:S(2)}, u32[]{:S(2)}) collective-permute-start(f32[192,128]{1,0:T(8,128)} %bitcast.8), channel_id=1, source_target_pairs={{0,1},{1,0},{2,3},{3,2},{4,5},{5,4},{6,7},{7,6},{8,9},{9,8},{10,11... | collective-permute-start | bytes 294920 | tf_op jit(solution)/shard_map/ppermute | solution.py:220
  4.7 0.9 %copy-done = f32[3,16,4,128]{3,2,1,0:T(4,128)S(1)} copy-done((f32[3,16,4,128]{3,2,1,0:T(4,128)S(1)}, f32[3,16,4,128]{3,2,1,0:T(4,128)}, u32[]{:S(2)}) %copy-start) | copy-done | bytes 98328
  5.6 0.7 %span_matrix.1 = (f32[64,256]{1,0:T(8,128)S(1)}, f32[64,128]{1,0:T(8,128)S(1)}, f32[192,128]{1,0:T(8,128)S(1)}, f32[128,32]{1,0:T(8,128)S(1)}, f32[128,32]{1,0:T(8,128)S(1)}) custom-call(s32[4]{0:T(128)S(1)} %copy-done.4, f32[32]{0:T(128)S(1)} %copy-done.5, f32[32]{0:T(128)S(1)} %copy-done.6, f32[192,128]{1,0:T(8,128)S(1)} %bitcast.9), custom_call_target="tpu_custom_call" | custom-call | tf_op jit(solution)/shard_map/span_matrix/pallas_call | solution.py:187
  6.3 1.9 %collective-permute-start.3 = (f32[192,128]{1,0:T(8,128)S(1)}, f32[192,128]{1,0:T(8,128)S(1)}, u32[]{:S(2)}, u32[]{:S(2)}) collective-permute-start(f32[192,128]{1,0:T(8,128)S(1)} %get-tuple-element.19), channel_id=1, source_target_pairs={{0,16},{8,24},{16,0},{24,8},{1,17},{9,25},{17,1},{25,9},{2,18},{10... | collective-permute-start | bytes 294920 | tf_op jit(solution)/shard_map/ppermute | solution.py:223
  8.3 0.3 %early.2.refs_1_ = f32[64,768]{1,0:T(8,128)S(1)} custom-call(f32[64,256]{1,0:T(8,128)S(1)} %get-tuple-element.17.matrix, f32[192,128]{1,0:T(8,128)S(1)} %bitcast.10, f32[192,128]{1,0:T(8,128)S(1)} %collective-permute-done.1.refs_1_), custom_call_target="tpu_custom_call" | custom-call | tf_op jit(solution)/shard_map/early/pallas_call | solution.py:187
  8.6 0.8 %collective-permute-done.refs_0_ = f32[192,128]{1,0:T(8,128)S(1)} collective-permute-done((f32[192,128]{1,0:T(8,128)}, f32[192,128]{1,0:T(8,128)S(1)}, u32[]{:S(2)}, u32[]{:S(2)}) %collective-permute-start) | collective-permute-done | bytes 98336 | tf_op jit(solution)/shard_map/ppermute | solution.py:220
  9.4 0.3 %early.3 = f32[64,768]{1,0:T(8,128)S(1)} custom-call(f32[64,256]{1,0:T(8,128)S(1)} %get-tuple-element.17.matrix, f32[192,128]{1,0:T(8,128)S(1)} %collective-permute-done.refs_0_, f32[64,768]{1,0:T(8,128)S(1)} %early.2.refs_1_), custom_call_target="tpu_custom_call" | custom-call | tf_op jit(solution)/shard_map/early/pallas_call | solution.py:187
  9.7 0.0 copy-start.2
  9.7 0.0 copy-start.3
  9.7 0.3 %span.1 = (f32[192,128]{1,0:T(8,128)S(1)}, f32[192,128]{1,0:T(8,128)S(1)}) custom-call(f32[64,256]{1,0:T(8,128)S(1)} %get-tuple-element.17.matrix, f32[64,768]{1,0:T(8,128)S(1)} %early.3, f32[192,128]{1,0:T(8,128)S(1)} %collective-permute-done.2.refs_0_), custom_call_target="tpu_custom_call" | custom-call | tf_op jit(solution)/shard_map/span/pallas_call | solution.py:187
  10.0 3.6 %collective-permute-start.4 = (f32[192,128]{1,0:T(8,128)S(1)}, f32[192,128]{1,0:T(8,128)S(1)}, u32[]{:S(2)}, u32[]{:S(2)}) collective-permute-start(f32[192,128]{1,0:T(8,128)S(1)} %get-tuple-element.22), channel_id=1, source_target_pairs={{0,6},{1,7},{2,4},{3,5},{4,2},{5,3},{6,0},{7,1},{8,14},{9,15},{10,... | collective-permute-start | bytes 294920 | tf_op jit(solution)/shard_map/ppermute | solution.py:220
  13.6 0.6 %copy-done.7 = f32[64]{0:T(128)S(1)} copy-done((f32[64]{0:T(128)S(1)}, f32[64]{0:T(128)}, u32[]{:S(2)}) %copy-start.7) | copy-done | bytes 280
  14.2 0.0 copy-done.8
  14.2 0.5 %wall_matrix.1.matrix = f32[128,256]{1,0:T(8,128)S(1)} custom-call(f32[128,32]{1,0:T(8,128)S(1)} %get-tuple-element.15.ends, f32[128,32]{1,0:T(8,128)S(1)} %get-tuple-element.16.others, f32[1,64]{1,0:T(1,128)S(1)} %bitcast.13, s32[1,32]{1,0:T(1,128)S(1)} %bitcast.14, f32[32,32]{1,0:T(8,128)S(1)} %copy-done.2, f32[32,32]{1,0:T(8,128)S(1)} %copy-done.3, ...), custom_call_target="tpu_custom_call" | custom-call | tf_op jit(solution)/shard_map/wall_matrix/pallas_call | solution.py:187
  14.7 0.3 %wall.1 = (f32[192,128]{1,0:T(8,128)S(1)}, f32[192,128]{1,0:T(8,128)S(1)}) custom-call(f32[128,256]{1,0:T(8,128)S(1)} %wall_matrix.1.matrix, f32[192,128]{1,0:T(8,128)S(1)} %get-tuple-element.18.after.z_part, f32[192,128]{1,0:T(8,128)S(1)} %bitcast.11, f32[192,128]{1,0:T(8,128)S(1)} %collective-permute-done.3.refs_1_), custom_call_target="tpu_custom_call" | custom-call | tf_op jit(solution)/shard_map/wall/pallas_call | solution.py:187
  15.1 0.1 collective-permute-start.5
  15.1 0.0 copy-start.9
  15.2 0.6 %copy-done.9 = f32[128]{0:T(128)S(1)} copy-done((f32[128]{0:T(128)S(1)}, f32[128]{0:T(128)}, u32[]{:S(2)}) %copy-start.9) | copy-done | bytes 536
  15.8 0.0 copy-done.10
  15.8 0.3 %stream.1.refs_1_ = f32[192,128]{1,0:T(8,128)S(1)} custom-call(f32[192,128]{1,0:T(8,128)S(1)} %bitcast.12, f32[1,128]{1,0:T(1,128)S(1)} %bitcast.15, f32[1,128]{1,0:T(1,128)S(1)} %bitcast.16, f32[192,128]{1,0:T(8,128)S(1)} %get-tuple-element.21.after), custom_call_target="tpu_custom_call" | custom-call | tf_op jit(solution)/shard_map/stream/pallas_call | solution.py:187
  16.1 0.5 %collective-permute-done.4.refs_2_ = f32[192,128]{1,0:T(8,128)S(1)} collective-permute-done((f32[192,128]{1,0:T(8,128)S(1)}, f32[192,128]{1,0:T(8,128)S(1)}, u32[]{:S(2)}, u32[]{:S(2)}) %collective-permute-start.4) | collective-permute-done | bytes 98336 | tf_op jit(solution)/shard_map/ppermute | solution.py:220
  16.6 0.7 %finish.1 = f32[192,128]{1,0:T(8,128)} custom-call(f32[192,128]{1,0:T(8,128)S(1)} %sum.1.total, f32[192,128]{1,0:T(8,128)S(1)} %collective-permute-done.5.near), custom_call_target="tpu_custom_call" | custom-call | tf_op jit(solution)/shard_map/finish/pallas_call | solution.py:187
  (19 shorter events, 0.1 us)
Async XLA Ops:
  0.0 4.7 %copy-start.4 = (s32[4]{0:T(128)S(1)}, s32[4]{0:T(128)}, u32[]{:S(2)}) copy-start(s32[4]{0:T(128)} %wall_counts.1) | copy-start | bytes 52
  0.0 4.7 %copy-start.5 = (f32[32]{0:T(128)S(1)}, f32[32]{0:T(128)}, u32[]{:S(2)}) copy-start(f32[32]{0:T(128)} %z_first.1) | copy-start | bytes 388
  0.0 4.7 %copy-start.6 = (f32[32]{0:T(128)S(1)}, f32[32]{0:T(128)}, u32[]{:S(2)}) copy-start(f32[32]{0:T(128)} %z_second.1) | copy-start | bytes 388
  0.0 8.3 %collective-permute-start.1 = (f32[192,128]{1,0:T(8,128)}, f32[192,128]{1,0:T(8,128)S(1)}, u32[]{:S(2)}, u32[]{:S(2)}) collective-permute-start(f32[192,128]{1,0:T(8,128)} %bitcast.6), channel_id=1, source_target_pairs={{0,3},{1,2},{2,1},{3,0},{4,7},{5,6},{6,5},{7,4},{8,11},{9,10},{10,... | collective-permute-start | bytes 294920 | tf_op jit(solution)/shard_map/ppermute | solution.py:220
  4.0 5.4 %collective-permute-start = (f32[192,128]{1,0:T(8,128)}, f32[192,128]{1,0:T(8,128)S(1)}, u32[]{:S(2)}, u32[]{:S(2)}) collective-permute-start(f32[192,128]{1,0:T(8,128)} %bitcast.7), channel_id=1, source_target_pairs={{0,2},{1,3},{2,0},{3,1},{4,6},{5,7},{6,4},{7,5},{8,10},{9,11},{10,... | collective-permute-start | bytes 294920 | tf_op jit(solution)/shard_map/ppermute | solution.py:220
  4.5 5.2 %collective-permute-start.2 = (f32[192,128]{1,0:T(8,128)}, f32[192,128]{1,0:T(8,128)S(1)}, u32[]{:S(2)}, u32[]{:S(2)}) collective-permute-start(f32[192,128]{1,0:T(8,128)} %bitcast.8), channel_id=1, source_target_pairs={{0,1},{1,0},{2,3},{3,2},{4,5},{5,4},{6,7},{7,6},{8,9},{9,8},{10,11... | collective-permute-start | bytes 294920 | tf_op jit(solution)/shard_map/ppermute | solution.py:220
  4.7 0.9 %copy-start = (f32[3,16,4,128]{3,2,1,0:T(4,128)S(1)}, f32[3,16,4,128]{3,2,1,0:T(4,128)}, u32[]{:S(2)}) copy-start(f32[3,16,4,128]{3,2,1,0:T(4,128)} %param.10) | copy-start | bytes 294916
  5.6 2.7 %copy-start.1 = (f32[3,16,4,128]{3,2,1,0:T(4,128)S(1)}, f32[3,16,4,128]{3,2,1,0:T(4,128)}, u32[]{:S(2)}) copy-start(f32[3,16,4,128]{3,2,1,0:T(4,128)} %param.10) | copy-start | bytes 294916
  6.3 8.4 %collective-permute-start.3 = (f32[192,128]{1,0:T(8,128)S(1)}, f32[192,128]{1,0:T(8,128)S(1)}, u32[]{:S(2)}, u32[]{:S(2)}) collective-permute-start(f32[192,128]{1,0:T(8,128)S(1)} %get-tuple-element.19), channel_id=1, source_target_pairs={{0,16},{8,24},{16,0},{24,8},{1,17},{9,25},{17,1},{25,9},{2,18},{10... | collective-permute-start | bytes 294920 | tf_op jit(solution)/shard_map/ppermute | solution.py:223
  9.7 3.9 %copy-start.2 = (f32[32,32]{1,0:T(8,128)S(1)}, f32[32,32]{1,0:T(8,128)}, u32[]{:S(2)}) copy-start(f32[32,32]{1,0:T(8,128)} %y_first.1) | copy-start | bytes 12292
  9.7 3.9 %copy-start.3 = (f32[32,32]{1,0:T(8,128)S(1)}, f32[32,32]{1,0:T(8,128)}, u32[]{:S(2)}) copy-start(f32[32,32]{1,0:T(8,128)} %y_second.1) | copy-start | bytes 12292
  10.0 6.6 %collective-permute-start.4 = (f32[192,128]{1,0:T(8,128)S(1)}, f32[192,128]{1,0:T(8,128)S(1)}, u32[]{:S(2)}, u32[]{:S(2)}) collective-permute-start(f32[192,128]{1,0:T(8,128)S(1)} %get-tuple-element.22), channel_id=1, source_target_pairs={{0,6},{1,7},{2,4},{3,5},{4,2},{5,3},{6,0},{7,1},{8,14},{9,15},{10,... | collective-permute-start | bytes 294920 | tf_op jit(solution)/shard_map/ppermute | solution.py:220
  13.6 0.7 %copy-start.7 = (f32[64]{0:T(128)S(1)}, f32[64]{0:T(128)}, u32[]{:S(2)}) copy-start(f32[64]{0:T(128)} %param.18) | copy-start | bytes 772
  13.6 0.7 %copy-start.8 = (s32[32]{0:T(128)S(1)}, s32[32]{0:T(128)}, u32[]{:S(2)}) copy-start(s32[32]{0:T(128)} %param.19) | copy-start | bytes 388
  15.1 1.6 %collective-permute-start.5 = (f32[192,128]{1,0:T(8,128)S(1)}, f32[192,128]{1,0:T(8,128)S(1)}, u32[]{:S(2)}, u32[]{:S(2)}) collective-permute-start(f32[192,128]{1,0:T(8,128)S(1)} %get-tuple-element.21.after), channel_id=1, source_target_pairs={{0,8},{8,0},{16,24},{24,16},{1,9},{9,1},{17,25},{25,17},{2,10},{10... | collective-permute-start | bytes 294920 | tf_op jit(solution)/shard_map/ppermute | solution.py:223
  15.1 0.7 %copy-start.9 = (f32[128]{0:T(128)S(1)}, f32[128]{0:T(128)}, u32[]{:S(2)}) copy-start(f32[128]{0:T(128)} %param.12) | copy-start | bytes 1540
  15.1 0.7 %copy-start.10 = (f32[128]{0:T(128)S(1)}, f32[128]{0:T(128)}, u32[]{:S(2)}) copy-start(f32[128]{0:T(128)} %param.13) | copy-start | bytes 1540

commit v30 on v27

--- a/solution.py
+++ b/solution.py
@@ -228,7 +228,7 @@
         [field.shape] * quad,
         "span",
     )
-    returned = [along(parts[t], t) for t in reversed(range(1, quad))]
+    returned = [along(parts[t], t) for t in (3, 1, 2)]
     (y_matrix,) = call(
         functools.partial(wall_matrix_kernel, zloc),
         [ends, others, metric_table.reshape(1, -1), metric_index.reshape(1, -1), y_first, y_second, parts[0]],

time: 17.3 us -> 17.3 us (level)
  no operation moved by 1% of the time
where the time goes in v30:
time: 17.3 us; the launch traced here: 17.1 us
  starting transfers between devices  10.3 us (60%)
  Pallas kernels  2.9 us (17%)
  local copies, waits for them, and re-layouts  2.26 us (13%)
  waiting for transfers between devices  1.53 us (9%)
    ppermute x4, starting transfers between devices, along(): return lax.ppermute(value, 'col', [(i, i ^ step) for i in range(cols)])  8.67 us
    pallas_call x7, Pallas kernels, call(): pl.pallas_call(kernel, out_shape=results, in_specs=[pl.BlockSpec(memory_s...  2.9 us
    unnamed x22, local copies, waits for them, and re-layouts  2.26 us
    ppermute x2, starting transfers between devices, across(): return lax.ppermute(value, 'row', [(i, i ^ step) for i in range(rows)])  1.66 us
    ppermute x4, waiting for transfers between devices, along(): return lax.ppermute(value, 'col', [(i, i ^ step) for i in range(cols)])  1.53 us
  transfers between devices with their start and end apart: 6, of which 2 were waited for; matrix products, arithmetic and copies ran while one was open for 0% of the time, Pallas kernels for 13%

profile of v30, /device:TPU:0, one launch (start us, length us, event | category | flops | bytes accessed | tf_op | source)
XLA Modules:
  0.0 17.1 jit_solution(3818229892084159174)
XLA Ops:
  0.0 5.1 %collective-permute-start = (f32[192,128]{1,0:T(8,128)}, f32[192,128]{1,0:T(8,128)S(1)}, u32[]{:S(2)}, u32[]{:S(2)}) collective-permute-start(f32[192,128]{1,0:T(8,128)} %bitcast.6), channel_id=1, source_target_pairs={{0,6},{1,7},{2,4},{3,5},{4,2},{5,3},{6,0},{7,1},{8,14},{9,15},{10,... | collective-permute-start | bytes 294920 | tf_op jit(solution)/shard_map/ppermute | solution.py:203
  5.1 0.9 %copy-done = f32[3,16,4,128]{3,2,1,0:T(4,128)S(1)} copy-done((f32[3,16,4,128]{3,2,1,0:T(4,128)S(1)}, f32[3,16,4,128]{3,2,1,0:T(4,128)}, u32[]{:S(2)}) %copy-start) | copy-done | bytes 98328
  6.1 0.8 %span_matrix.1 = (f32[128,128]{1,0:T(8,128)S(1)}, f32[64,128]{1,0:T(8,128)S(1)}, f32[192,128]{1,0:T(8,128)S(1)}, f32[128,32]{1,0:T(8,128)S(1)}, f32[128,32]{1,0:T(8,128)S(1)}) custom-call(s32[4]{0:T(128)S(1)} %copy-done.4, f32[32]{0:T(128)S(1)} %copy-done.5, f32[32]{0:T(128)S(1)} %copy-done.6, f32[192,128]{1,0:T(8,128)S(1)} %bitcast.7), custom_call_target="tpu_custom_call" | custom-call | tf_op jit(solution)/shard_map/span_matrix/pallas_call | solution.py:170
  6.9 1.6 %collective-permute-start.1 = (f32[192,128]{1,0:T(8,128)S(1)}, f32[192,128]{1,0:T(8,128)S(1)}, u32[]{:S(2)}, u32[]{:S(2)}) collective-permute-start(f32[192,128]{1,0:T(8,128)S(1)} %get-tuple-element.21), channel_id=1, source_target_pairs={{0,16},{8,24},{16,0},{24,8},{1,17},{9,25},{17,1},{25,9},{2,18},{10... | collective-permute-start | bytes 294920 | tf_op jit(solution)/shard_map/ppermute | solution.py:206
  8.5 0.0 collective-permute-done.refs_1_
  8.5 0.3 %span.1 = (f32[192,128]{1,0:T(8,128)S(1)}, f32[192,128]{1,0:T(8,128)S(1)}, f32[192,128]{1,0:T(8,128)S(1)}, f32[192,128]{1,0:T(8,128)S(1)}) custom-call(f32[128,128]{1,0:T(8,128)S(1)} %get-tuple-element.19.matrix, f32[192,128]{1,0:T(8,128)S(1)} %bitcast.8, f32[192,128]{1,0:T(8,128)S(1)} %collective-permute-done.refs_1_), custom_call_target="tpu_custom_call" | custom-call | tf_op jit(solution)/shard_map/span/pallas_call | solution.py:170
  8.8 2.5 %collective-permute-start.2 = (f32[192,128]{1,0:T(8,128)S(1)}, f32[192,128]{1,0:T(8,128)S(1)}, u32[]{:S(2)}, u32[]{:S(2)}) collective-permute-start(f32[192,128]{1,0:T(8,128)S(1)} %get-tuple-element.24), channel_id=1, source_target_pairs={{0,3},{1,2},{2,1},{3,0},{4,7},{5,6},{6,5},{7,4},{8,11},{9,10},{10,... | collective-permute-start | bytes 294920 | tf_op jit(solution)/shard_map/ppermute | solution.py:203
  11.3 0.5 %collective-permute-start.3 = (f32[192,128]{1,0:T(8,128)S(1)}, f32[192,128]{1,0:T(8,128)S(1)}, u32[]{:S(2)}, u32[]{:S(2)}) collective-permute-start(f32[192,128]{1,0:T(8,128)S(1)} %get-tuple-element.25), channel_id=1, source_target_pairs={{0,1},{1,0},{2,3},{3,2},{4,5},{5,4},{6,7},{7,6},{8,9},{9,8},{10,11... | collective-permute-start | bytes 294920 | tf_op jit(solution)/shard_map/ppermute | solution.py:203
  11.8 0.5 %collective-permute-start.4 = (f32[192,128]{1,0:T(8,128)S(1)}, f32[192,128]{1,0:T(8,128)S(1)}, u32[]{:S(2)}, u32[]{:S(2)}) collective-permute-start(f32[192,128]{1,0:T(8,128)S(1)} %get-tuple-element.26), channel_id=1, source_target_pairs={{0,2},{1,3},{2,0},{3,1},{4,6},{5,7},{6,4},{7,5},{8,10},{9,11},{10,... | collective-permute-start | bytes 294920 | tf_op jit(solution)/shard_map/ppermute | solution.py:203
  12.3 0.6 %copy-done.7 = f32[64]{0:T(128)S(1)} copy-done((f32[64]{0:T(128)S(1)}, f32[64]{0:T(128)}, u32[]{:S(2)}) %copy-start.7) | copy-done | bytes 280
  13.0 0.0 copy-done.8
  13.0 0.5 %wall_matrix.1.matrix = f32[128,256]{1,0:T(8,128)S(1)} custom-call(f32[128,32]{1,0:T(8,128)S(1)} %get-tuple-element.17.ends, f32[128,32]{1,0:T(8,128)S(1)} %get-tuple-element.18.others, f32[1,64]{1,0:T(1,128)S(1)} %bitcast.11, s32[1,32]{1,0:T(1,128)S(1)} %bitcast.12, f32[32,32]{1,0:T(8,128)S(1)} %copy-done.2, f32[32,32]{1,0:T(8,128)S(1)} %copy-done.3, ...), custom_call_target="tpu_custom_call" | custom-call | tf_op jit(solution)/shard_map/wall_matrix/pallas_call | solution.py:170
  13.5 0.0 collective-permute-done.1.refs_1_
  13.5 0.3 %wall.1 = (f32[192,128]{1,0:T(8,128)S(1)}, f32[192,128]{1,0:T(8,128)S(1)}) custom-call(f32[128,256]{1,0:T(8,128)S(1)} %wall_matrix.1.matrix, f32[192,128]{1,0:T(8,128)S(1)} %get-tuple-element.20.after.z_part, f32[192,128]{1,0:T(8,128)S(1)} %bitcast.9, f32[192,128]{1,0:T(8,128)S(1)} %collective-permute-done.1.refs_1_), custom_call_target="tpu_custom_call" | custom-call | tf_op jit(solution)/shard_map/wall/pallas_call | solution.py:170
  13.8 0.1 collective-permute-start.5
  13.9 0.0 copy-start.9
  13.9 0.0 copy-start.10
  13.9 0.6 %copy-done.9 = f32[128]{0:T(128)S(1)} copy-done((f32[128]{0:T(128)S(1)}, f32[128]{0:T(128)}, u32[]{:S(2)}) %copy-start.9) | copy-done | bytes 536
  14.5 0.0 copy-done.10
  14.6 0.3 %stream.1.refs_1_ = f32[192,128]{1,0:T(8,128)S(1)} custom-call(f32[192,128]{1,0:T(8,128)S(1)} %bitcast.10, f32[1,128]{1,0:T(1,128)S(1)} %bitcast.13, f32[1,128]{1,0:T(1,128)S(1)} %bitcast.14, f32[192,128]{1,0:T(8,128)S(1)} %get-tuple-element.23.after), custom_call_target="tpu_custom_call" | custom-call | tf_op jit(solution)/shard_map/stream/pallas_call | solution.py:170
  14.9 1.0 %collective-permute-done.3.refs_3_ = f32[192,128]{1,0:T(8,128)S(1)} collective-permute-done((f32[192,128]{1,0:T(8,128)S(1)}, f32[192,128]{1,0:T(8,128)S(1)}, u32[]{:S(2)}, u32[]{:S(2)}) %collective-permute-start.3) | collective-permute-done | bytes 98336 | tf_op jit(solution)/shard_map/ppermute | solution.py:203
  15.9 0.5 %collective-permute-done.4.refs_4_ = f32[192,128]{1,0:T(8,128)S(1)} collective-permute-done((f32[192,128]{1,0:T(8,128)S(1)}, f32[192,128]{1,0:T(8,128)S(1)}, u32[]{:S(2)}, u32[]{:S(2)}) %collective-permute-start.4) | collective-permute-done | bytes 98336 | tf_op jit(solution)/shard_map/ppermute | solution.py:203
  16.4 0.0 collective-permute-done.5.near
  16.5 0.7 %finish.1 = f32[192,128]{1,0:T(8,128)} custom-call(f32[192,128]{1,0:T(8,128)S(1)} %sum.1.total, f32[192,128]{1,0:T(8,128)S(1)} %collective-permute-done.5.near), custom_call_target="tpu_custom_call" | custom-call | tf_op jit(solution)/shard_map/finish/pallas_call | solution.py:170
  (17 shorter events, 0.1 us)
Async XLA Ops:
  0.0 5.1 %copy-start.6 = (f32[32]{0:T(128)S(1)}, f32[32]{0:T(128)}, u32[]{:S(2)}) copy-start(f32[32]{0:T(128)} %z_second.1) | copy-start | bytes 388
  0.0 5.1 %copy-start.5 = (f32[32]{0:T(128)S(1)}, f32[32]{0:T(128)}, u32[]{:S(2)}) copy-start(f32[32]{0:T(128)} %z_first.1) | copy-start | bytes 388
  0.0 5.1 %copy-start.4 = (s32[4]{0:T(128)S(1)}, s32[4]{0:T(128)}, u32[]{:S(2)}) copy-start(s32[4]{0:T(128)} %wall_counts.1) | copy-start | bytes 52
  0.0 8.5 %collective-permute-start = (f32[192,128]{1,0:T(8,128)}, f32[192,128]{1,0:T(8,128)S(1)}, u32[]{:S(2)}, u32[]{:S(2)}) collective-permute-start(f32[192,128]{1,0:T(8,128)} %bitcast.6), channel_id=1, source_target_pairs={{0,6},{1,7},{2,4},{3,5},{4,2},{5,3},{6,0},{7,1},{8,14},{9,15},{10,... | collective-permute-start | bytes 294920 | tf_op jit(solution)/shard_map/ppermute | solution.py:203
  5.1 0.9 %copy-start = (f32[3,16,4,128]{3,2,1,0:T(4,128)S(1)}, f32[3,16,4,128]{3,2,1,0:T(4,128)}, u32[]{:S(2)}) copy-start(f32[3,16,4,128]{3,2,1,0:T(4,128)} %param.10) | copy-start | bytes 294916
  6.1 2.4 %copy-start.1 = (f32[3,16,4,128]{3,2,1,0:T(4,128)S(1)}, f32[3,16,4,128]{3,2,1,0:T(4,128)}, u32[]{:S(2)}) copy-start(f32[3,16,4,128]{3,2,1,0:T(4,128)} %param.10) | copy-start | bytes 294916
  6.9 6.6 %collective-permute-start.1 = (f32[192,128]{1,0:T(8,128)S(1)}, f32[192,128]{1,0:T(8,128)S(1)}, u32[]{:S(2)}, u32[]{:S(2)}) collective-permute-start(f32[192,128]{1,0:T(8,128)S(1)} %get-tuple-element.21), channel_id=1, source_target_pairs={{0,16},{8,24},{16,0},{24,8},{1,17},{9,25},{17,1},{25,9},{2,18},{10... | collective-permute-start | bytes 294920 | tf_op jit(solution)/shard_map/ppermute | solution.py:206
  8.5 3.9 %copy-start.2 = (f32[32,32]{1,0:T(8,128)S(1)}, f32[32,32]{1,0:T(8,128)}, u32[]{:S(2)}) copy-start(f32[32,32]{1,0:T(8,128)} %y_first.1) | copy-start | bytes 12292
  8.5 3.9 %copy-start.3 = (f32[32,32]{1,0:T(8,128)S(1)}, f32[32,32]{1,0:T(8,128)}, u32[]{:S(2)}) copy-start(f32[32,32]{1,0:T(8,128)} %y_second.1) | copy-start | bytes 12292
  8.8 6.1 %collective-permute-start.2 = (f32[192,128]{1,0:T(8,128)S(1)}, f32[192,128]{1,0:T(8,128)S(1)}, u32[]{:S(2)}, u32[]{:S(2)}) collective-permute-start(f32[192,128]{1,0:T(8,128)S(1)} %get-tuple-element.24), channel_id=1, source_target_pairs={{0,3},{1,2},{2,1},{3,0},{4,7},{5,6},{6,5},{7,4},{8,11},{9,10},{10,... | collective-permute-start | bytes 294920 | tf_op jit(solution)/shard_map/ppermute | solution.py:203
  11.3 4.6 %collective-permute-start.3 = (f32[192,128]{1,0:T(8,128)S(1)}, f32[192,128]{1,0:T(8,128)S(1)}, u32[]{:S(2)}, u32[]{:S(2)}) collective-permute-start(f32[192,128]{1,0:T(8,128)S(1)} %get-tuple-element.25), channel_id=1, source_target_pairs={{0,1},{1,0},{2,3},{3,2},{4,5},{5,4},{6,7},{7,6},{8,9},{9,8},{10,11... | collective-permute-start | bytes 294920 | tf_op jit(solution)/shard_map/ppermute | solution.py:203
  11.8 4.6 %collective-permute-start.4 = (f32[192,128]{1,0:T(8,128)S(1)}, f32[192,128]{1,0:T(8,128)S(1)}, u32[]{:S(2)}, u32[]{:S(2)}) collective-permute-start(f32[192,128]{1,0:T(8,128)S(1)} %get-tuple-element.26), channel_id=1, source_target_pairs={{0,2},{1,3},{2,0},{3,1},{4,6},{5,7},{6,4},{7,5},{8,10},{9,11},{10,... | collective-permute-start | bytes 294920 | tf_op jit(solution)/shard_map/ppermute | solution.py:203
  12.3 0.7 %copy-start.7 = (f32[64]{0:T(128)S(1)}, f32[64]{0:T(128)}, u32[]{:S(2)}) copy-start(f32[64]{0:T(128)} %param.18) | copy-start | bytes 772
  12.3 0.7 %copy-start.8 = (s32[32]{0:T(128)S(1)}, s32[32]{0:T(128)}, u32[]{:S(2)}) copy-start(s32[32]{0:T(128)} %param.19) | copy-start | bytes 388
  13.8 2.6 %collective-permute-start.5 = (f32[192,128]{1,0:T(8,128)S(1)}, f32[192,128]{1,0:T(8,128)S(1)}, u32[]{:S(2)}, u32[]{:S(2)}) collective-permute-start(f32[192,128]{1,0:T(8,128)S(1)} %get-tuple-element.23.after), channel_id=1, source_target_pairs={{0,8},{8,0},{16,24},{24,16},{1,9},{9,1},{17,25},{25,17},{2,10},{10... | collective-permute-start | bytes 294920 | tf_op jit(solution)/shard_map/ppermute | solution.py:206
  13.9 0.7 %copy-start.9 = (f32[128]{0:T(128)S(1)}, f32[128]{0:T(128)}, u32[]{:S(2)}) copy-start(f32[128]{0:T(128)} %param.12) | copy-start | bytes 1540
  13.9 0.7 %copy-start.10 = (f32[128]{0:T(128)S(1)}, f32[128]{0:T(128)}, u32[]{:S(2)}) copy-start(f32[128]{0:T(128)} %param.13) | copy-start | bytes 1540

commit v31 on v30

--- a/solution.py
+++ b/solution.py
@@ -33,6 +33,10 @@
 
 def over(t):
     return quad * t + 2 * (t != 0)
+
+
+def reach(t, odd):
+    return t if odd else (t + 1) % 3 + 1 if t else 0
 
 
 def span_kernel(comps, sources, matrix, *refs):
@@ -84,7 +88,11 @@
     r = lax.broadcasted_iota(jnp.int32, shape, 0)
     q = lax.broadcasted_iota(jnp.int32, shape, 1)
     q = jnp.where(q < half, q, q - half)
-    out_cell = ((r // group) ^ mine) * zloc + r % zloc
+    odd = lax.axis_index("row") % 2
+    distance = jnp.zeros(shape, jnp.int32)
+    for t in range(1, quad):
+        distance = jnp.where(r // group == t, jnp.where(odd == 1, reach(t, 1), reach(t, 0)), distance)
+    out_cell = (distance ^ mine) * zloc + r % zloc
     in_cell = (over(q // group) ^ mine) * zloc + q % zloc
     same = (r % group) // zloc == (q % group) // zloc
     gap = jnp.where(same, (in_cell - out_cell + cells_z) % cells_z, -1)
@@ -228,7 +236,14 @@
         [field.shape] * quad,
         "span",
     )
-    returned = [along(parts[t], t) for t in (3, 1, 2)]
+    returned = [
+        lax.ppermute(
+            parts[t],
+            ("row", "col"),
+            [(i * cols + j, i * cols + (j ^ reach(t, i % 2))) for i in range(rows) for j in range(cols)],
+        )
+        for t in range(1, quad)
+    ]
     (y_matrix,) = call(
         functools.partial(wall_matrix_kernel, zloc),
         [ends, others, metric_table.reshape(1, -1), metric_index.reshape(1, -1), y_first, y_second, parts[0]],

time: 17.3 us -> 17.3 us (level)
    ppermute x0 -> x3, starting transfers between devices: none -> 3.55 us  [local(): lax.ppermute(parts[t], ('row', 'col'), [(i * cols + j, i * cols + (j ^ re...]
    ppermute x4 -> x1, starting transfers between devices: 8.67 us -> 5.12 us  [along(): return lax.ppermute(value, 'col', [(i, i ^ step) for i in range(cols)])]
    ppermute x0 -> x3, waiting for transfers between devices: none -> 1.59 us  [local(): lax.ppermute(parts[t], ('row', 'col'), [(i * cols + j, i * cols + (j ^ re...]
    ppermute x4 -> x1, waiting for transfers between devices: 1.53 us -> 0.01 us  [along(): return lax.ppermute(value, 'col', [(i, i ^ step) for i in range(cols)])]
  transfers between devices with their start and end apart: 6 -> 6, of which waited for: 2 -> 1; matrix products, arithmetic and copies ran while one was open for 0% -> 0% of each run, Pallas kernels for 13% -> 13%
where the time goes in v31:
time: 17.3 us; the launch traced here: 17.2 us
  starting transfers between devices  10.3 us (60%)
  Pallas kernels  2.89 us (17%)
  local copies, waits for them, and re-layouts  2.26 us (13%)
  waiting for transfers between devices  1.6 us (9%)
    ppermute x1, starting transfers between devices, along(): return lax.ppermute(value, 'col', [(i, i ^ step) for i in range(cols)])  5.12 us
    ppermute x3, starting transfers between devices, local(): lax.ppermute(parts[t], ('row', 'col'), [(i * cols + j, i * cols + (j ^ re...  3.55 us
    pallas_call x7, Pallas kernels, call(): pl.pallas_call(kernel, out_shape=results, in_specs=[pl.BlockSpec(memory_s...  2.89 us
    unnamed x22, local copies, waits for them, and re-layouts  2.26 us
    ppermute x2, starting transfers between devices, across(): return lax.ppermute(value, 'row', [(i, i ^ step) for i in range(rows)])  1.66 us
    ppermute x3, waiting for transfers between devices, local(): lax.ppermute(parts[t], ('row', 'col'), [(i * cols + j, i * cols + (j ^ re...  1.59 us
  transfers between devices with their start and end apart: 6, of which 1 were waited for; matrix products, arithmetic and copies ran while one was open for 0% of the time, Pallas kernels for 13%

profile of v31, /device:TPU:0, one launch (start us, length us, event | category | flops | bytes accessed | tf_op | source)
XLA Modules:
  0.0 17.2 jit_solution(13955197108925186915)
XLA Ops:
  0.0 5.1 %collective-permute-start = (f32[192,128]{1,0:T(8,128)}, f32[192,128]{1,0:T(8,128)S(1)}, u32[]{:S(2)}, u32[]{:S(2)}) collective-permute-start(f32[192,128]{1,0:T(8,128)} %bitcast.6), channel_id=1, source_target_pairs={{0,6},{1,7},{2,4},{3,5},{4,2},{5,3},{6,0},{7,1},{8,14},{9,15},{10,... | collective-permute-start | bytes 294920 | tf_op jit(solution)/shard_map/ppermute | solution.py:211
  5.1 0.9 %copy-done = f32[3,16,4,128]{3,2,1,0:T(4,128)S(1)} copy-done((f32[3,16,4,128]{3,2,1,0:T(4,128)S(1)}, f32[3,16,4,128]{3,2,1,0:T(4,128)}, u32[]{:S(2)}) %copy-start) | copy-done | bytes 98328
  6.1 0.8 %span_matrix.1 = (f32[128,128]{1,0:T(8,128)S(1)}, f32[64,128]{1,0:T(8,128)S(1)}, f32[192,128]{1,0:T(8,128)S(1)}, f32[128,32]{1,0:T(8,128)S(1)}, f32[128,32]{1,0:T(8,128)S(1)}) custom-call(s32[4]{0:T(128)S(1)} %copy-done.4, f32[32]{0:T(128)S(1)} %copy-done.5, f32[32]{0:T(128)S(1)} %copy-done.6, f32[192,128]{1,0:T(8,128)S(1)} %bitcast.7), custom_call_target="tpu_custom_call" | custom-call | tf_op jit(solution)/shard_map/span_matrix/pallas_call | solution.py:178
  6.9 1.6 %collective-permute-start.1 = (f32[192,128]{1,0:T(8,128)S(1)}, f32[192,128]{1,0:T(8,128)S(1)}, u32[]{:S(2)}, u32[]{:S(2)}) collective-permute-start(f32[192,128]{1,0:T(8,128)S(1)} %get-tuple-element.21), channel_id=1, source_target_pairs={{0,16},{8,24},{16,0},{24,8},{1,17},{9,25},{17,1},{25,9},{2,18},{10... | collective-permute-start | bytes 294920 | tf_op jit(solution)/shard_map/ppermute | solution.py:214
  8.5 0.0 collective-permute-done.refs_1_
  8.5 0.3 %span.1 = (f32[192,128]{1,0:T(8,128)S(1)}, f32[192,128]{1,0:T(8,128)S(1)}, f32[192,128]{1,0:T(8,128)S(1)}, f32[192,128]{1,0:T(8,128)S(1)}) custom-call(f32[128,128]{1,0:T(8,128)S(1)} %get-tuple-element.19.matrix, f32[192,128]{1,0:T(8,128)S(1)} %bitcast.8, f32[192,128]{1,0:T(8,128)S(1)} %collective-permute-done.refs_1_), custom_call_target="tpu_custom_call" | custom-call | tf_op jit(solution)/shard_map/span/pallas_call | solution.py:178
  8.8 2.5 %collective-permute-start.2 = (f32[192,128]{1,0:T(8,128)S(1)}, f32[192,128]{1,0:T(8,128)S(1)}, u32[]{:S(2)}, u32[]{:S(2)}) collective-permute-start(f32[192,128]{1,0:T(8,128)S(1)} %get-tuple-element.24), channel_id=1, source_target_pairs={{0,3},{1,2},{2,1},{3,0},{4,7},{5,6},{6,5},{7,4},{8,9},{9,8},{10,11... | collective-permute-start | bytes 294920 | tf_op jit(solution)/shard_map/ppermute | solution.py:240
  11.3 0.5 %collective-permute-start.3 = (f32[192,128]{1,0:T(8,128)S(1)}, f32[192,128]{1,0:T(8,128)S(1)}, u32[]{:S(2)}, u32[]{:S(2)}) collective-permute-start(f32[192,128]{1,0:T(8,128)S(1)} %get-tuple-element.25), channel_id=1, source_target_pairs={{0,1},{1,0},{2,3},{3,2},{4,5},{5,4},{6,7},{7,6},{8,10},{9,11},{10,... | collective-permute-start | bytes 294920 | tf_op jit(solution)/shard_map/ppermute | solution.py:240
  11.8 0.5 %collective-permute-start.4 = (f32[192,128]{1,0:T(8,128)S(1)}, f32[192,128]{1,0:T(8,128)S(1)}, u32[]{:S(2)}, u32[]{:S(2)}) collective-permute-start(f32[192,128]{1,0:T(8,128)S(1)} %get-tuple-element.26), channel_id=1, source_target_pairs={{0,2},{1,3},{2,0},{3,1},{4,6},{5,7},{6,4},{7,5},{8,11},{9,10},{10,... | collective-permute-start | bytes 294920 | tf_op jit(solution)/shard_map/ppermute | solution.py:240
  12.3 0.6 %copy-done.7 = f32[64]{0:T(128)S(1)} copy-done((f32[64]{0:T(128)S(1)}, f32[64]{0:T(128)}, u32[]{:S(2)}) %copy-start.7) | copy-done | bytes 280
  13.0 0.0 copy-done.8
  13.0 0.5 %wall_matrix.1.matrix = f32[128,256]{1,0:T(8,128)S(1)} custom-call(f32[128,32]{1,0:T(8,128)S(1)} %get-tuple-element.17.ends, f32[128,32]{1,0:T(8,128)S(1)} %get-tuple-element.18.others, f32[1,64]{1,0:T(1,128)S(1)} %bitcast.11, s32[1,32]{1,0:T(1,128)S(1)} %bitcast.12, f32[32,32]{1,0:T(8,128)S(1)} %copy-done.2, f32[32,32]{1,0:T(8,128)S(1)} %copy-done.3, ...), custom_call_target="tpu_custom_call" | custom-call | tf_op jit(solution)/shard_map/wall_matrix/pallas_call | solution.py:178
  13.5 0.0 collective-permute-done.1.refs_1_
  13.5 0.3 %wall.1 = (f32[192,128]{1,0:T(8,128)S(1)}, f32[192,128]{1,0:T(8,128)S(1)}) custom-call(f32[128,256]{1,0:T(8,128)S(1)} %wall_matrix.1.matrix, f32[192,128]{1,0:T(8,128)S(1)} %get-tuple-element.20.after.z_part, f32[192,128]{1,0:T(8,128)S(1)} %bitcast.9, f32[192,128]{1,0:T(8,128)S(1)} %collective-permute-done.1.refs_1_), custom_call_target="tpu_custom_call" | custom-call | tf_op jit(solution)/shard_map/wall/pallas_call | solution.py:178
  13.8 0.1 collective-permute-start.5
  13.9 0.0 copy-start.9
  13.9 0.0 copy-start.10
  13.9 0.6 %copy-done.9 = f32[128]{0:T(128)S(1)} copy-done((f32[128]{0:T(128)S(1)}, f32[128]{0:T(128)}, u32[]{:S(2)}) %copy-start.9) | copy-done | bytes 536
  14.5 0.0 copy-done.10
  14.6 0.3 %stream.1.refs_1_ = f32[192,128]{1,0:T(8,128)S(1)} custom-call(f32[192,128]{1,0:T(8,128)S(1)} %bitcast.10, f32[1,128]{1,0:T(1,128)S(1)} %bitcast.13, f32[1,128]{1,0:T(1,128)S(1)} %bitcast.14, f32[192,128]{1,0:T(8,128)S(1)} %get-tuple-element.23.after), custom_call_target="tpu_custom_call" | custom-call | tf_op jit(solution)/shard_map/stream/pallas_call | solution.py:178
  14.9 1.6 %collective-permute-done.3.refs_3_ = f32[192,128]{1,0:T(8,128)S(1)} collective-permute-done((f32[192,128]{1,0:T(8,128)S(1)}, f32[192,128]{1,0:T(8,128)S(1)}, u32[]{:S(2)}, u32[]{:S(2)}) %collective-permute-start.3) | collective-permute-done | bytes 98336 | tf_op jit(solution)/shard_map/ppermute | solution.py:240
  16.5 0.0 collective-permute-done.4.refs_4_
  16.5 0.0 collective-permute-done.5.near
  16.5 0.7 %finish.1 = f32[192,128]{1,0:T(8,128)} custom-call(f32[192,128]{1,0:T(8,128)S(1)} %sum.1.total, f32[192,128]{1,0:T(8,128)S(1)} %collective-permute-done.5.near), custom_call_target="tpu_custom_call" | custom-call | tf_op jit(solution)/shard_map/finish/pallas_call | solution.py:178
  (17 shorter events, 0.1 us)
Async XLA Ops:
  0.0 5.1 %copy-start.6 = (f32[32]{0:T(128)S(1)}, f32[32]{0:T(128)}, u32[]{:S(2)}) copy-start(f32[32]{0:T(128)} %z_second.1) | copy-start | bytes 388
  0.0 5.1 %copy-start.5 = (f32[32]{0:T(128)S(1)}, f32[32]{0:T(128)}, u32[]{:S(2)}) copy-start(f32[32]{0:T(128)} %z_first.1) | copy-start | bytes 388
  0.0 5.1 %copy-start.4 = (s32[4]{0:T(128)S(1)}, s32[4]{0:T(128)}, u32[]{:S(2)}) copy-start(s32[4]{0:T(128)} %wall_counts.1) | copy-start | bytes 52
  0.0 8.5 %collective-permute-start = (f32[192,128]{1,0:T(8,128)}, f32[192,128]{1,0:T(8,128)S(1)}, u32[]{:S(2)}, u32[]{:S(2)}) collective-permute-start(f32[192,128]{1,0:T(8,128)} %bitcast.6), channel_id=1, source_target_pairs={{0,6},{1,7},{2,4},{3,5},{4,2},{5,3},{6,0},{7,1},{8,14},{9,15},{10,... | collective-permute-start | bytes 294920 | tf_op jit(solution)/shard_map/ppermute | solution.py:211
  5.1 0.9 %copy-start = (f32[3,16,4,128]{3,2,1,0:T(4,128)S(1)}, f32[3,16,4,128]{3,2,1,0:T(4,128)}, u32[]{:S(2)}) copy-start(f32[3,16,4,128]{3,2,1,0:T(4,128)} %param.10) | copy-start | bytes 294916
  6.1 2.4 %copy-start.1 = (f32[3,16,4,128]{3,2,1,0:T(4,128)S(1)}, f32[3,16,4,128]{3,2,1,0:T(4,128)}, u32[]{:S(2)}) copy-start(f32[3,16,4,128]{3,2,1,0:T(4,128)} %param.10) | copy-start | bytes 294916
  6.9 6.6 %collective-permute-start.1 = (f32[192,128]{1,0:T(8,128)S(1)}, f32[192,128]{1,0:T(8,128)S(1)}, u32[]{:S(2)}, u32[]{:S(2)}) collective-permute-start(f32[192,128]{1,0:T(8,128)S(1)} %get-tuple-element.21), channel_id=1, source_target_pairs={{0,16},{8,24},{16,0},{24,8},{1,17},{9,25},{17,1},{25,9},{2,18},{10... | collective-permute-start | bytes 294920 | tf_op jit(solution)/shard_map/ppermute | solution.py:214
  8.5 3.9 %copy-start.2 = (f32[32,32]{1,0:T(8,128)S(1)}, f32[32,32]{1,0:T(8,128)}, u32[]{:S(2)}) copy-start(f32[32,32]{1,0:T(8,128)} %y_first.1) | copy-start | bytes 12292
  8.5 3.9 %copy-start.3 = (f32[32,32]{1,0:T(8,128)S(1)}, f32[32,32]{1,0:T(8,128)}, u32[]{:S(2)}) copy-start(f32[32,32]{1,0:T(8,128)} %y_second.1) | copy-start | bytes 12292
  8.8 6.1 %collective-permute-start.2 = (f32[192,128]{1,0:T(8,128)S(1)}, f32[192,128]{1,0:T(8,128)S(1)}, u32[]{:S(2)}, u32[]{:S(2)}) collective-permute-start(f32[192,128]{1,0:T(8,128)S(1)} %get-tuple-element.24), channel_id=1, source_target_pairs={{0,3},{1,2},{2,1},{3,0},{4,7},{5,6},{6,5},{7,4},{8,9},{9,8},{10,11... | collective-permute-start | bytes 294920 | tf_op jit(solution)/shard_map/ppermute | solution.py:240
  11.3 5.2 %collective-permute-start.3 = (f32[192,128]{1,0:T(8,128)S(1)}, f32[192,128]{1,0:T(8,128)S(1)}, u32[]{:S(2)}, u32[]{:S(2)}) collective-permute-start(f32[192,128]{1,0:T(8,128)S(1)} %get-tuple-element.25), channel_id=1, source_target_pairs={{0,1},{1,0},{2,3},{3,2},{4,5},{5,4},{6,7},{7,6},{8,10},{9,11},{10,... | collective-permute-start | bytes 294920 | tf_op jit(solution)/shard_map/ppermute | solution.py:240
  11.8 4.7 %collective-permute-start.4 = (f32[192,128]{1,0:T(8,128)S(1)}, f32[192,128]{1,0:T(8,128)S(1)}, u32[]{:S(2)}, u32[]{:S(2)}) collective-permute-start(f32[192,128]{1,0:T(8,128)S(1)} %get-tuple-element.26), channel_id=1, source_target_pairs={{0,2},{1,3},{2,0},{3,1},{4,6},{5,7},{6,4},{7,5},{8,11},{9,10},{10,... | collective-permute-start | bytes 294920 | tf_op jit(solution)/shard_map/ppermute | solution.py:240
  12.3 0.7 %copy-start.7 = (f32[64]{0:T(128)S(1)}, f32[64]{0:T(128)}, u32[]{:S(2)}) copy-start(f32[64]{0:T(128)} %param.18) | copy-start | bytes 772
  12.3 0.7 %copy-start.8 = (s32[32]{0:T(128)S(1)}, s32[32]{0:T(128)}, u32[]{:S(2)}) copy-start(s32[32]{0:T(128)} %param.19) | copy-start | bytes 388
  13.8 2.7 %collective-permute-start.5 = (f32[192,128]{1,0:T(8,128)S(1)}, f32[192,128]{1,0:T(8,128)S(1)}, u32[]{:S(2)}, u32[]{:S(2)}) collective-permute-start(f32[192,128]{1,0:T(8,128)S(1)} %get-tuple-element.23.after), channel_id=1, source_target_pairs={{0,8},{8,0},{16,24},{24,16},{1,9},{9,1},{17,25},{25,17},{2,10},{10... | collective-permute-start | bytes 294920 | tf_op jit(solution)/shard_map/ppermute | solution.py:214
  13.9 0.7 %copy-start.9 = (f32[128]{0:T(128)S(1)}, f32[128]{0:T(128)}, u32[]{:S(2)}) copy-start(f32[128]{0:T(128)} %param.12) | copy-start | bytes 1540
  13.9 0.7 %copy-start.10 = (f32[128]{0:T(128)S(1)}, f32[128]{0:T(128)}, u32[]{:S(2)}) copy-start(f32[128]{0:T(128)} %param.13) | copy-start | bytes 1540

commit v32 on v25

--- a/solution.py
+++ b/solution.py
@@ -33,6 +33,10 @@
 
 def over(t):
     return quad * t + 2 * (t != 0)
+
+
+def quad_step(s, odd):
+    return (quad - s) % quad if odd else s
 
 
 def quad_sums(comps, matrix, fields, chosen):
@@ -100,7 +104,8 @@
     q = lax.broadcasted_iota(jnp.int32, shape, 1)
     q = jnp.where(q < half, q, q - half)
     out_cell = (over(r // group) ^ mine) * zloc + r % zloc
-    in_cell = ((q // group) ^ mine) * zloc + q % zloc
+    odd = lax.axis_index("row") % 2
+    in_cell = (jnp.where(odd == 1, quad_step(q // group, 1), q // group) ^ mine) * zloc + q % zloc
     same = (r % group) // zloc == (q % group) // zloc
     gap = jnp.where(same, (in_cell - out_cell + cells_z) % cells_z, -1)
     kind = lax.broadcasted_iota(jnp.int32, (1, shape[1]), 1) < half
@@ -220,7 +225,14 @@
     def across(value, step):
         return lax.ppermute(value, "row", [(i, i ^ step) for i in range(rows)])
 
-    gathered = [along(field, t) for t in range(1, quad)]
+    gathered = [
+        lax.ppermute(
+            field,
+            ("row", "col"),
+            [(i * cols + j, i * cols + (j ^ quad_step(s, i % 2))) for i in range(rows) for j in range(cols)],
+        )
+        for s in range(1, quad)
+    ]
     cells = metric_index.shape[0]
     z_matrix, mask, held, ends, others = call(
         functools.partial(span_matrix_kernel, rows, cols, zloc),

time: 17.2 us -> 17.6 us (1.023)
  waiting for transfers between devices: 1.1 us -> 2 us
  starting transfers between devices: 10.5 us -> 10 us
    ppermute x4 -> x1, starting transfers between devices: 8.48 us -> 3.34 us  [along(): return lax.ppermute(value, 'col', [(i, i ^ step) for i in range(cols)])]
    ppermute x0 -> x3, starting transfers between devices: none -> 4.66 us  [local(): lax.ppermute(field, ('row', 'col'), [(i * cols + j, i * cols + (j ^ quad_...]
    ppermute x0 -> x3, waiting for transfers between devices: none -> 1.34 us  [local(): lax.ppermute(field, ('row', 'col'), [(i * cols + j, i * cols + (j ^ quad_...]
    ppermute x4 -> x1, waiting for transfers between devices: 0.99 us -> 0.65 us  [along(): return lax.ppermute(value, 'col', [(i, i ^ step) for i in range(cols)])]
where the time goes in v32:
time: 17.6 us; the launch traced here: 17.4 us
  starting transfers between devices  10 us (57%)
  Pallas kernels  3.09 us (18%)
  local copies, waits for them, and re-layouts  2.26 us (13%)
  waiting for transfers between devices  2 us (11%)
    ppermute x3, starting transfers between devices, local(): lax.ppermute(field, ('row', 'col'), [(i * cols + j, i * cols + (j ^ quad_...  4.66 us
    ppermute x1, starting transfers between devices, along(): return lax.ppermute(value, 'col', [(i, i ^ step) for i in range(cols)])  3.34 us
    pallas_call x8, Pallas kernels, call(): pl.pallas_call(kernel, out_shape=results, in_specs=[pl.BlockSpec(memory_s...  3.09 us
    unnamed x22, local copies, waits for them, and re-layouts  2.26 us
    ppermute x2, starting transfers between devices, across(): return lax.ppermute(value, 'row', [(i, i ^ step) for i in range(rows)])  2 us
    ppermute x3, waiting for transfers between devices, local(): lax.ppermute(field, ('row', 'col'), [(i * cols + j, i * cols + (j ^ quad_...  1.34 us
    ppermute x1, waiting for transfers between devices, along(): return lax.ppermute(value, 'col', [(i, i ^ step) for i in range(cols)])  0.65 us
  transfers between devices with their start and end apart: 6, of which 3 were waited for; matrix products, arithmetic and copies ran while one was open for 0% of the time, Pallas kernels for 14%

profile of v32, /device:TPU:0, one launch (start us, length us, event | category | flops | bytes accessed | tf_op | source)
XLA Modules:
  0.0 17.4 jit_solution(11250377844987893211)
XLA Ops:
  0.0 4.0 %collective-permute-start = (f32[192,128]{1,0:T(8,128)}, f32[192,128]{1,0:T(8,128)S(1)}, u32[]{:S(2)}, u32[]{:S(2)}) collective-permute-start(f32[192,128]{1,0:T(8,128)} %bitcast.6), channel_id=1, source_target_pairs={{0,3},{1,2},{2,1},{3,0},{4,7},{5,6},{6,5},{7,4},{8,9},{9,8},{10,11... | collective-permute-start | bytes 294920 | tf_op jit(solution)/shard_map/ppermute | solution.py:229
  4.0 0.4 %collective-permute-start.2 = (f32[192,128]{1,0:T(8,128)}, f32[192,128]{1,0:T(8,128)S(1)}, u32[]{:S(2)}, u32[]{:S(2)}) collective-permute-start(f32[192,128]{1,0:T(8,128)} %bitcast.7), channel_id=1, source_target_pairs={{0,2},{1,3},{2,0},{3,1},{4,6},{5,7},{6,4},{7,5},{8,10},{9,11},{10,... | collective-permute-start | bytes 294920 | tf_op jit(solution)/shard_map/ppermute | solution.py:229
  4.5 0.2 %collective-permute-start.1 = (f32[192,128]{1,0:T(8,128)}, f32[192,128]{1,0:T(8,128)S(1)}, u32[]{:S(2)}, u32[]{:S(2)}) collective-permute-start(f32[192,128]{1,0:T(8,128)} %bitcast.8), channel_id=1, source_target_pairs={{0,1},{1,0},{2,3},{3,2},{4,5},{5,4},{6,7},{7,6},{8,11},{9,10},{10,... | collective-permute-start | bytes 294920 | tf_op jit(solution)/shard_map/ppermute | solution.py:229
  4.7 0.9 %copy-done = f32[3,16,4,128]{3,2,1,0:T(4,128)S(1)} copy-done((f32[3,16,4,128]{3,2,1,0:T(4,128)S(1)}, f32[3,16,4,128]{3,2,1,0:T(4,128)}, u32[]{:S(2)}) %copy-start) | copy-done | bytes 98328
  5.6 0.7 %span_matrix.1 = (f32[64,256]{1,0:T(8,128)S(1)}, f32[64,128]{1,0:T(8,128)S(1)}, f32[192,128]{1,0:T(8,128)S(1)}, f32[128,32]{1,0:T(8,128)S(1)}, f32[128,32]{1,0:T(8,128)S(1)}) custom-call(s32[4]{0:T(128)S(1)} %copy-done.4, f32[32]{0:T(128)S(1)} %copy-done.5, f32[32]{0:T(128)S(1)} %copy-done.6, f32[192,128]{1,0:T(8,128)S(1)} %bitcast.9), custom_call_target="tpu_custom_call" | custom-call | tf_op jit(solution)/shard_map/span_matrix/pallas_call | solution.py:190
  6.3 1.9 %collective-permute-start.3 = (f32[192,128]{1,0:T(8,128)S(1)}, f32[192,128]{1,0:T(8,128)S(1)}, u32[]{:S(2)}, u32[]{:S(2)}) collective-permute-start(f32[192,128]{1,0:T(8,128)S(1)} %get-tuple-element.19), channel_id=1, source_target_pairs={{0,16},{8,24},{16,0},{24,8},{1,17},{9,25},{17,1},{25,9},{2,18},{10... | collective-permute-start | bytes 294920 | tf_op jit(solution)/shard_map/ppermute | solution.py:226
  8.3 0.0 collective-permute-done.refs_1_
  8.3 0.3 %early.1 = f32[64,768]{1,0:T(8,128)S(1)} custom-call(f32[64,256]{1,0:T(8,128)S(1)} %get-tuple-element.17.matrix, f32[192,128]{1,0:T(8,128)S(1)} %bitcast.10, f32[192,128]{1,0:T(8,128)S(1)} %collective-permute-done.refs_1_), custom_call_target="tpu_custom_call" | custom-call | tf_op jit(solution)/shard_map/early/pallas_call | solution.py:190
  8.6 1.0 %collective-permute-done.2.refs_1_ = f32[192,128]{1,0:T(8,128)S(1)} collective-permute-done((f32[192,128]{1,0:T(8,128)}, f32[192,128]{1,0:T(8,128)S(1)}, u32[]{:S(2)}, u32[]{:S(2)}) %collective-permute-start.2) | collective-permute-done | bytes 98336 | tf_op jit(solution)/shard_map/ppermute | solution.py:229
  9.6 0.3 %collective-permute-done.1.refs_0_ = f32[192,128]{1,0:T(8,128)S(1)} collective-permute-done((f32[192,128]{1,0:T(8,128)}, f32[192,128]{1,0:T(8,128)S(1)}, u32[]{:S(2)}, u32[]{:S(2)}) %collective-permute-start.1) | collective-permute-done | bytes 98336 | tf_op jit(solution)/shard_map/ppermute | solution.py:229
  9.9 0.3 %span.1 = (f32[192,128]{1,0:T(8,128)S(1)}, f32[192,128]{1,0:T(8,128)S(1)}) custom-call(f32[64,256]{1,0:T(8,128)S(1)} %get-tuple-element.17.matrix, f32[64,768]{1,0:T(8,128)S(1)} %early.1, f32[192,128]{1,0:T(8,128)S(1)} %collective-permute-done.1.refs_0_, f32[192,128]{1,0:T(8,128)S(1)} %collective-permute-done.2.refs_1_), custom_call_target="tpu_custom_call" | custom-call | tf_op jit(solution)/shard_map/span/pallas_call | solution.py:190
  10.2 3.3 %collective-permute-start.4 = (f32[192,128]{1,0:T(8,128)S(1)}, f32[192,128]{1,0:T(8,128)S(1)}, u32[]{:S(2)}, u32[]{:S(2)}) collective-permute-start(f32[192,128]{1,0:T(8,128)S(1)} %get-tuple-element.22), channel_id=1, source_target_pairs={{0,6},{1,7},{2,4},{3,5},{4,2},{5,3},{6,0},{7,1},{8,14},{9,15},{10,... | collective-permute-start | bytes 294920 | tf_op jit(solution)/shard_map/ppermute | solution.py:223
  13.6 0.6 %copy-done.7 = f32[64]{0:T(128)S(1)} copy-done((f32[64]{0:T(128)S(1)}, f32[64]{0:T(128)}, u32[]{:S(2)}) %copy-start.7) | copy-done | bytes 280
  14.2 0.0 copy-done.8
  14.2 0.5 %wall_matrix.1.matrix = f32[128,256]{1,0:T(8,128)S(1)} custom-call(f32[128,32]{1,0:T(8,128)S(1)} %get-tuple-element.15.ends, f32[128,32]{1,0:T(8,128)S(1)} %get-tuple-element.16.others, f32[1,64]{1,0:T(1,128)S(1)} %bitcast.13, s32[1,32]{1,0:T(1,128)S(1)} %bitcast.14, f32[32,32]{1,0:T(8,128)S(1)} %copy-done.2, f32[32,32]{1,0:T(8,128)S(1)} %copy-done.3, ...), custom_call_target="tpu_custom_call" | custom-call | tf_op jit(solution)/shard_map/wall_matrix/pallas_call | solution.py:190
  14.7 0.3 %wall.1 = (f32[192,128]{1,0:T(8,128)S(1)}, f32[192,128]{1,0:T(8,128)S(1)}) custom-call(f32[128,256]{1,0:T(8,128)S(1)} %wall_matrix.1.matrix, f32[192,128]{1,0:T(8,128)S(1)} %get-tuple-element.18.after.z_part, f32[192,128]{1,0:T(8,128)S(1)} %bitcast.11, f32[192,128]{1,0:T(8,128)S(1)} %collective-permute-done.3.refs_1_), custom_call_target="tpu_custom_call" | custom-call | tf_op jit(solution)/shard_map/wall/pallas_call | solution.py:190
  15.0 0.1 collective-permute-start.5
  15.1 0.0 copy-start.9
  15.1 0.0 copy-start.10
  15.1 0.6 %copy-done.9 = f32[128]{0:T(128)S(1)} copy-done((f32[128]{0:T(128)S(1)}, f32[128]{0:T(128)}, u32[]{:S(2)}) %copy-start.9) | copy-done | bytes 536
  15.8 0.0 copy-done.10
  15.8 0.3 %stream.1.refs_1_ = f32[192,128]{1,0:T(8,128)S(1)} custom-call(f32[192,128]{1,0:T(8,128)S(1)} %bitcast.12, f32[1,128]{1,0:T(1,128)S(1)} %bitcast.15, f32[1,128]{1,0:T(1,128)S(1)} %bitcast.16, f32[192,128]{1,0:T(8,128)S(1)} %get-tuple-element.21.after), custom_call_target="tpu_custom_call" | custom-call | tf_op jit(solution)/shard_map/stream/pallas_call | solution.py:190
  16.1 0.7 %collective-permute-done.4.refs_2_ = f32[192,128]{1,0:T(8,128)S(1)} collective-permute-done((f32[192,128]{1,0:T(8,128)S(1)}, f32[192,128]{1,0:T(8,128)S(1)}, u32[]{:S(2)}, u32[]{:S(2)}) %collective-permute-start.4) | collective-permute-done | bytes 98336 | tf_op jit(solution)/shard_map/ppermute | solution.py:223
  16.8 0.7 %finish.1 = f32[192,128]{1,0:T(8,128)} custom-call(f32[192,128]{1,0:T(8,128)S(1)} %sum.1.total, f32[192,128]{1,0:T(8,128)S(1)} %collective-permute-done.5.near), custom_call_target="tpu_custom_call" | custom-call | tf_op jit(solution)/shard_map/finish/pallas_call | solution.py:190
  (18 shorter events, 0.1 us)
Async XLA Ops:
  0.0 4.7 %copy-start.6 = (f32[32]{0:T(128)S(1)}, f32[32]{0:T(128)}, u32[]{:S(2)}) copy-start(f32[32]{0:T(128)} %z_second.1) | copy-start | bytes 388
  0.0 4.7 %copy-start.5 = (f32[32]{0:T(128)S(1)}, f32[32]{0:T(128)}, u32[]{:S(2)}) copy-start(f32[32]{0:T(128)} %z_first.1) | copy-start | bytes 388
  0.0 4.7 %copy-start.4 = (s32[4]{0:T(128)S(1)}, s32[4]{0:T(128)}, u32[]{:S(2)}) copy-start(s32[4]{0:T(128)} %wall_counts.1) | copy-start | bytes 52
  0.0 8.3 %collective-permute-start = (f32[192,128]{1,0:T(8,128)}, f32[192,128]{1,0:T(8,128)S(1)}, u32[]{:S(2)}, u32[]{:S(2)}) collective-permute-start(f32[192,128]{1,0:T(8,128)} %bitcast.6), channel_id=1, source_target_pairs={{0,3},{1,2},{2,1},{3,0},{4,7},{5,6},{6,5},{7,4},{8,9},{9,8},{10,11... | collective-permute-start | bytes 294920 | tf_op jit(solution)/shard_map/ppermute | solution.py:229
  4.0 5.6 %collective-permute-start.2 = (f32[192,128]{1,0:T(8,128)}, f32[192,128]{1,0:T(8,128)S(1)}, u32[]{:S(2)}, u32[]{:S(2)}) collective-permute-start(f32[192,128]{1,0:T(8,128)} %bitcast.7), channel_id=1, source_target_pairs={{0,2},{1,3},{2,0},{3,1},{4,6},{5,7},{6,4},{7,5},{8,10},{9,11},{10,... | collective-permute-start | bytes 294920 | tf_op jit(solution)/shard_map/ppermute | solution.py:229
  4.5 5.4 %collective-permute-start.1 = (f32[192,128]{1,0:T(8,128)}, f32[192,128]{1,0:T(8,128)S(1)}, u32[]{:S(2)}, u32[]{:S(2)}) collective-permute-start(f32[192,128]{1,0:T(8,128)} %bitcast.8), channel_id=1, source_target_pairs={{0,1},{1,0},{2,3},{3,2},{4,5},{5,4},{6,7},{7,6},{8,11},{9,10},{10,... | collective-permute-start | bytes 294920 | tf_op jit(solution)/shard_map/ppermute | solution.py:229
  4.7 0.9 %copy-start = (f32[3,16,4,128]{3,2,1,0:T(4,128)S(1)}, f32[3,16,4,128]{3,2,1,0:T(4,128)}, u32[]{:S(2)}) copy-start(f32[3,16,4,128]{3,2,1,0:T(4,128)} %param.10) | copy-start | bytes 294916
  5.6 2.7 %copy-start.1 = (f32[3,16,4,128]{3,2,1,0:T(4,128)S(1)}, f32[3,16,4,128]{3,2,1,0:T(4,128)}, u32[]{:S(2)}) copy-start(f32[3,16,4,128]{3,2,1,0:T(4,128)} %param.10) | copy-start | bytes 294916
  6.3 8.4 %collective-permute-start.3 = (f32[192,128]{1,0:T(8,128)S(1)}, f32[192,128]{1,0:T(8,128)S(1)}, u32[]{:S(2)}, u32[]{:S(2)}) collective-permute-start(f32[192,128]{1,0:T(8,128)S(1)} %get-tuple-element.19), channel_id=1, source_target_pairs={{0,16},{8,24},{16,0},{24,8},{1,17},{9,25},{17,1},{25,9},{2,18},{10... | collective-permute-start | bytes 294920 | tf_op jit(solution)/shard_map/ppermute | solution.py:226
  9.9 3.6 %copy-start.2 = (f32[32,32]{1,0:T(8,128)S(1)}, f32[32,32]{1,0:T(8,128)}, u32[]{:S(2)}) copy-start(f32[32,32]{1,0:T(8,128)} %y_first.1) | copy-start | bytes 12292
  9.9 3.6 %copy-start.3 = (f32[32,32]{1,0:T(8,128)S(1)}, f32[32,32]{1,0:T(8,128)}, u32[]{:S(2)}) copy-start(f32[32,32]{1,0:T(8,128)} %y_second.1) | copy-start | bytes 12292
  10.2 6.5 %collective-permute-start.4 = (f32[192,128]{1,0:T(8,128)S(1)}, f32[192,128]{1,0:T(8,128)S(1)}, u32[]{:S(2)}, u32[]{:S(2)}) collective-permute-start(f32[192,128]{1,0:T(8,128)S(1)} %get-tuple-element.22), channel_id=1, source_target_pairs={{0,6},{1,7},{2,4},{3,5},{4,2},{5,3},{6,0},{7,1},{8,14},{9,15},{10,... | collective-permute-start | bytes 294920 | tf_op jit(solution)/shard_map/ppermute | solution.py:223
  13.6 0.7 %copy-start.7 = (f32[64]{0:T(128)S(1)}, f32[64]{0:T(128)}, u32[]{:S(2)}) copy-start(f32[64]{0:T(128)} %param.18) | copy-start | bytes 772
  13.6 0.7 %copy-start.8 = (s32[32]{0:T(128)S(1)}, s32[32]{0:T(128)}, u32[]{:S(2)}) copy-start(s32[32]{0:T(128)} %param.19) | copy-start | bytes 388
  15.0 1.7 %collective-permute-start.5 = (f32[192,128]{1,0:T(8,128)S(1)}, f32[192,128]{1,0:T(8,128)S(1)}, u32[]{:S(2)}, u32[]{:S(2)}) collective-permute-start(f32[192,128]{1,0:T(8,128)S(1)} %get-tuple-element.21.after), channel_id=1, source_target_pairs={{0,8},{8,0},{16,24},{24,16},{1,9},{9,1},{17,25},{25,17},{2,10},{10... | collective-permute-start | bytes 294920 | tf_op jit(solution)/shard_map/ppermute | solution.py:226
  15.1 0.7 %copy-start.9 = (f32[128]{0:T(128)S(1)}, f32[128]{0:T(128)}, u32[]{:S(2)}) copy-start(f32[128]{0:T(128)} %param.12) | copy-start | bytes 1540
  15.1 0.7 %copy-start.10 = (f32[128]{0:T(128)S(1)}, f32[128]{0:T(128)}, u32[]{:S(2)}) copy-start(f32[128]{0:T(128)} %param.13) | copy-start | bytes 1540

commit v33 on v25

--- a/solution.py
+++ b/solution.py
@@ -31,8 +31,8 @@
     return both[:count] + (mul(lh, rl) + both[count:])
 
 
-def over(t):
-    return quad * t + 2 * (t != 0)
+def over(t, odd):
+    return quad * t + (0 if odd else 2 * (t != 0))
 
 
 def quad_sums(comps, matrix, fields, chosen):
@@ -99,7 +99,8 @@
     r = lax.broadcasted_iota(jnp.int32, shape, 0)
     q = lax.broadcasted_iota(jnp.int32, shape, 1)
     q = jnp.where(q < half, q, q - half)
-    out_cell = (over(r // group) ^ mine) * zloc + r % zloc
+    odd = lax.axis_index("row") % 2
+    out_cell = (jnp.where(odd == 1, over(r // group, 1), over(r // group, 0)) ^ mine) * zloc + r % zloc
     in_cell = ((q // group) ^ mine) * zloc + q % zloc
     same = (r % group) // zloc == (q % group) // zloc
     gap = jnp.where(same, (in_cell - out_cell + cells_z) % cells_z, -1)
@@ -250,7 +251,14 @@
         [field.shape] * wide,
         "span",
     )
-    returned = [along(parts[t], over(t)) for t in range(1, wide)]
+    returned = [
+        lax.ppermute(
+            parts[t],
+            ("row", "col"),
+            [(i * cols + j, i * cols + (j ^ over(t, i % 2))) for i in range(rows) for j in range(cols)],
+        )
+        for t in range(1, wide)
+    ]
     (y_matrix,) = call(
         functools.partial(wall_matrix_kernel, zloc),
         [ends, others, metric_table.reshape(1, -1), metric_index.reshape(1, -1), y_first, y_second, parts[0]],

time: 17.2 us -> 17.2 us (level)
    ppermute x0 -> x1, starting transfers between devices: none -> 3.82 us  [local(): lax.ppermute(parts[t], ('row', 'col'), [(i * cols + j, i * cols + (j ^ ov...]
    ppermute x4 -> x3, starting transfers between devices: 8.48 us -> 4.66 us  [along(): return lax.ppermute(value, 'col', [(i, i ^ step) for i in range(cols)])]
    ppermute x0 -> x1, waiting for transfers between devices: none -> 0.23 us  [local(): lax.ppermute(parts[t], ('row', 'col'), [(i * cols + j, i * cols + (j ^ ov...]
    ppermute x4 -> x3, waiting for transfers between devices: 0.99 us -> 0.81 us  [along(): return lax.ppermute(value, 'col', [(i, i ^ step) for i in range(cols)])]
where the time goes in v33:
time: 17.2 us; the launch traced here: 17 us
  starting transfers between devices  10.5 us (61%)
  Pallas kernels  3.08 us (18%)
  local copies, waits for them, and re-layouts  2.26 us (13%)
  waiting for transfers between devices  1.1 us (6%)
    ppermute x3, starting transfers between devices, along(): return lax.ppermute(value, 'col', [(i, i ^ step) for i in range(cols)])  4.66 us
    ppermute x1, starting transfers between devices, local(): lax.ppermute(parts[t], ('row', 'col'), [(i * cols + j, i * cols + (j ^ ov...  3.82 us
    pallas_call x8, Pallas kernels, call(): pl.pallas_call(kernel, out_shape=results, in_specs=[pl.BlockSpec(memory_s...  3.08 us
    unnamed x22, local copies, waits for them, and re-layouts  2.26 us
    ppermute x2, starting transfers between devices, across(): return lax.ppermute(value, 'row', [(i, i ^ step) for i in range(rows)])  2 us
    ppermute x3, waiting for transfers between devices, along(): return lax.ppermute(value, 'col', [(i, i ^ step) for i in range(cols)])  0.81 us
  transfers between devices with their start and end apart: 6, of which 3 were waited for; matrix products, arithmetic and copies ran while one was open for 0% of the time, Pallas kernels for 14%

profile of v33, /device:TPU:0, one launch (start us, length us, event | category | flops | bytes accessed | tf_op | source)
XLA Modules:
  0.0 17.0 jit_solution(4686189059585380526)
XLA Ops:
  0.0 4.0 %collective-permute-start = (f32[192,128]{1,0:T(8,128)}, f32[192,128]{1,0:T(8,128)S(1)}, u32[]{:S(2)}, u32[]{:S(2)}) collective-permute-start(f32[192,128]{1,0:T(8,128)} %bitcast.6), channel_id=1, source_target_pairs={{0,3},{1,2},{2,1},{3,0},{4,7},{5,6},{6,5},{7,4},{8,11},{9,10},{10,... | collective-permute-start | bytes 294920 | tf_op jit(solution)/shard_map/ppermute | solution.py:219
  4.0 0.4 %collective-permute-start.2 = (f32[192,128]{1,0:T(8,128)}, f32[192,128]{1,0:T(8,128)S(1)}, u32[]{:S(2)}, u32[]{:S(2)}) collective-permute-start(f32[192,128]{1,0:T(8,128)} %bitcast.7), channel_id=1, source_target_pairs={{0,2},{1,3},{2,0},{3,1},{4,6},{5,7},{6,4},{7,5},{8,10},{9,11},{10,... | collective-permute-start | bytes 294920 | tf_op jit(solution)/shard_map/ppermute | solution.py:219
  4.5 0.2 %collective-permute-start.1 = (f32[192,128]{1,0:T(8,128)}, f32[192,128]{1,0:T(8,128)S(1)}, u32[]{:S(2)}, u32[]{:S(2)}) collective-permute-start(f32[192,128]{1,0:T(8,128)} %bitcast.8), channel_id=1, source_target_pairs={{0,1},{1,0},{2,3},{3,2},{4,5},{5,4},{6,7},{7,6},{8,9},{9,8},{10,11... | collective-permute-start | bytes 294920 | tf_op jit(solution)/shard_map/ppermute | solution.py:219
  4.7 0.9 %copy-done = f32[3,16,4,128]{3,2,1,0:T(4,128)S(1)} copy-done((f32[3,16,4,128]{3,2,1,0:T(4,128)S(1)}, f32[3,16,4,128]{3,2,1,0:T(4,128)}, u32[]{:S(2)}) %copy-start) | copy-done | bytes 98328
  5.6 0.7 %span_matrix.1 = (f32[64,256]{1,0:T(8,128)S(1)}, f32[64,128]{1,0:T(8,128)S(1)}, f32[192,128]{1,0:T(8,128)S(1)}, f32[128,32]{1,0:T(8,128)S(1)}, f32[128,32]{1,0:T(8,128)S(1)}) custom-call(s32[4]{0:T(128)S(1)} %copy-done.4, f32[32]{0:T(128)S(1)} %copy-done.5, f32[32]{0:T(128)S(1)} %copy-done.6, f32[192,128]{1,0:T(8,128)S(1)} %bitcast.9), custom_call_target="tpu_custom_call" | custom-call | tf_op jit(solution)/shard_map/span_matrix/pallas_call | solution.py:186
  6.3 1.9 %collective-permute-start.3 = (f32[192,128]{1,0:T(8,128)S(1)}, f32[192,128]{1,0:T(8,128)S(1)}, u32[]{:S(2)}, u32[]{:S(2)}) collective-permute-start(f32[192,128]{1,0:T(8,128)S(1)} %get-tuple-element.19), channel_id=1, source_target_pairs={{0,16},{8,24},{16,0},{24,8},{1,17},{9,25},{17,1},{25,9},{2,18},{10... | collective-permute-start | bytes 294920 | tf_op jit(solution)/shard_map/ppermute | solution.py:222
  8.3 0.0 collective-permute-done.refs_1_
  8.3 0.3 %early.1 = f32[64,768]{1,0:T(8,128)S(1)} custom-call(f32[64,256]{1,0:T(8,128)S(1)} %get-tuple-element.17.matrix, f32[192,128]{1,0:T(8,128)S(1)} %bitcast.10, f32[192,128]{1,0:T(8,128)S(1)} %collective-permute-done.refs_1_), custom_call_target="tpu_custom_call" | custom-call | tf_op jit(solution)/shard_map/early/pallas_call | solution.py:186
  8.6 0.8 %collective-permute-done.2.refs_1_ = f32[192,128]{1,0:T(8,128)S(1)} collective-permute-done((f32[192,128]{1,0:T(8,128)}, f32[192,128]{1,0:T(8,128)S(1)}, u32[]{:S(2)}, u32[]{:S(2)}) %collective-permute-start.2) | collective-permute-done | bytes 98336 | tf_op jit(solution)/shard_map/ppermute | solution.py:219
  9.4 0.3 %span.1 = (f32[192,128]{1,0:T(8,128)S(1)}, f32[192,128]{1,0:T(8,128)S(1)}) custom-call(f32[64,256]{1,0:T(8,128)S(1)} %get-tuple-element.17.matrix, f32[64,768]{1,0:T(8,128)S(1)} %early.1, f32[192,128]{1,0:T(8,128)S(1)} %collective-permute-done.1.refs_0_, f32[192,128]{1,0:T(8,128)S(1)} %collective-permute-done.2.refs_1_), custom_call_target="tpu_custom_call" | custom-call | tf_op jit(solution)/shard_map/span/pallas_call | solution.py:186
  9.7 3.8 %collective-permute-start.4 = (f32[192,128]{1,0:T(8,128)S(1)}, f32[192,128]{1,0:T(8,128)S(1)}, u32[]{:S(2)}, u32[]{:S(2)}) collective-permute-start(f32[192,128]{1,0:T(8,128)S(1)} %get-tuple-element.22), channel_id=1, source_target_pairs={{0,6},{1,7},{2,4},{3,5},{4,2},{5,3},{6,0},{7,1},{8,12},{9,13},{10,... | collective-permute-start | bytes 294920 | tf_op jit(solution)/shard_map/ppermute | solution.py:255
  13.5 0.6 %copy-done.7 = f32[64]{0:T(128)S(1)} copy-done((f32[64]{0:T(128)S(1)}, f32[64]{0:T(128)}, u32[]{:S(2)}) %copy-start.7) | copy-done | bytes 280
  14.2 0.0 copy-done.8
  14.2 0.5 %wall_matrix.1.matrix = f32[128,256]{1,0:T(8,128)S(1)} custom-call(f32[128,32]{1,0:T(8,128)S(1)} %get-tuple-element.15.ends, f32[128,32]{1,0:T(8,128)S(1)} %get-tuple-element.16.others, f32[1,64]{1,0:T(1,128)S(1)} %bitcast.13, s32[1,32]{1,0:T(1,128)S(1)} %bitcast.14, f32[32,32]{1,0:T(8,128)S(1)} %copy-done.2, f32[32,32]{1,0:T(8,128)S(1)} %copy-done.3, ...), custom_call_target="tpu_custom_call" | custom-call | tf_op jit(solution)/shard_map/wall_matrix/pallas_call | solution.py:186
  14.7 0.3 %wall.1 = (f32[192,128]{1,0:T(8,128)S(1)}, f32[192,128]{1,0:T(8,128)S(1)}) custom-call(f32[128,256]{1,0:T(8,128)S(1)} %wall_matrix.1.matrix, f32[192,128]{1,0:T(8,128)S(1)} %get-tuple-element.18.after.z_part, f32[192,128]{1,0:T(8,128)S(1)} %bitcast.11, f32[192,128]{1,0:T(8,128)S(1)} %collective-permute-done.3.refs_1_), custom_call_target="tpu_custom_call" | custom-call | tf_op jit(solution)/shard_map/wall/pallas_call | solution.py:186
  15.0 0.1 collective-permute-start.5
  15.1 0.0 copy-start.9
  15.1 0.0 copy-start.10
  15.1 0.6 %copy-done.9 = f32[128]{0:T(128)S(1)} copy-done((f32[128]{0:T(128)S(1)}, f32[128]{0:T(128)}, u32[]{:S(2)}) %copy-start.9) | copy-done | bytes 536
  15.7 0.0 copy-done.10
  15.7 0.3 %stream.1.refs_1_ = f32[192,128]{1,0:T(8,128)S(1)} custom-call(f32[192,128]{1,0:T(8,128)S(1)} %bitcast.12, f32[1,128]{1,0:T(1,128)S(1)} %bitcast.15, f32[1,128]{1,0:T(1,128)S(1)} %bitcast.16, f32[192,128]{1,0:T(8,128)S(1)} %get-tuple-element.21.after), custom_call_target="tpu_custom_call" | custom-call | tf_op jit(solution)/shard_map/stream/pallas_call | solution.py:186
  16.0 0.2 %collective-permute-done.4.refs_2_ = f32[192,128]{1,0:T(8,128)S(1)} collective-permute-done((f32[192,128]{1,0:T(8,128)S(1)}, f32[192,128]{1,0:T(8,128)S(1)}, u32[]{:S(2)}, u32[]{:S(2)}) %collective-permute-start.4) | collective-permute-done | bytes 98336 | tf_op jit(solution)/shard_map/ppermute | solution.py:255
  16.3 0.1 collective-permute-done.5.near
  16.4 0.7 %finish.1 = f32[192,128]{1,0:T(8,128)} custom-call(f32[192,128]{1,0:T(8,128)S(1)} %sum.1.total, f32[192,128]{1,0:T(8,128)S(1)} %collective-permute-done.5.near), custom_call_target="tpu_custom_call" | custom-call | tf_op jit(solution)/shard_map/finish/pallas_call | solution.py:186
  (18 shorter events, 0.1 us)
Async XLA Ops:
  0.0 4.7 %copy-start.6 = (f32[32]{0:T(128)S(1)}, f32[32]{0:T(128)}, u32[]{:S(2)}) copy-start(f32[32]{0:T(128)} %z_second.1) | copy-start | bytes 388
  0.0 4.7 %copy-start.5 = (f32[32]{0:T(128)S(1)}, f32[32]{0:T(128)}, u32[]{:S(2)}) copy-start(f32[32]{0:T(128)} %z_first.1) | copy-start | bytes 388
  0.0 4.7 %copy-start.4 = (s32[4]{0:T(128)S(1)}, s32[4]{0:T(128)}, u32[]{:S(2)}) copy-start(s32[4]{0:T(128)} %wall_counts.1) | copy-start | bytes 52
  0.0 8.3 %collective-permute-start = (f32[192,128]{1,0:T(8,128)}, f32[192,128]{1,0:T(8,128)S(1)}, u32[]{:S(2)}, u32[]{:S(2)}) collective-permute-start(f32[192,128]{1,0:T(8,128)} %bitcast.6), channel_id=1, source_target_pairs={{0,3},{1,2},{2,1},{3,0},{4,7},{5,6},{6,5},{7,4},{8,11},{9,10},{10,... | collective-permute-start | bytes 294920 | tf_op jit(solution)/shard_map/ppermute | solution.py:219
  4.0 5.4 %collective-permute-start.2 = (f32[192,128]{1,0:T(8,128)}, f32[192,128]{1,0:T(8,128)S(1)}, u32[]{:S(2)}, u32[]{:S(2)}) collective-permute-start(f32[192,128]{1,0:T(8,128)} %bitcast.7), channel_id=1, source_target_pairs={{0,2},{1,3},{2,0},{3,1},{4,6},{5,7},{6,4},{7,5},{8,10},{9,11},{10,... | collective-permute-start | bytes 294920 | tf_op jit(solution)/shard_map/ppermute | solution.py:219
  4.5 4.9 %collective-permute-start.1 = (f32[192,128]{1,0:T(8,128)}, f32[192,128]{1,0:T(8,128)S(1)}, u32[]{:S(2)}, u32[]{:S(2)}) collective-permute-start(f32[192,128]{1,0:T(8,128)} %bitcast.8), channel_id=1, source_target_pairs={{0,1},{1,0},{2,3},{3,2},{4,5},{5,4},{6,7},{7,6},{8,9},{9,8},{10,11... | collective-permute-start | bytes 294920 | tf_op jit(solution)/shard_map/ppermute | solution.py:219
  4.7 0.9 %copy-start = (f32[3,16,4,128]{3,2,1,0:T(4,128)S(1)}, f32[3,16,4,128]{3,2,1,0:T(4,128)}, u32[]{:S(2)}) copy-start(f32[3,16,4,128]{3,2,1,0:T(4,128)} %param.10) | copy-start | bytes 294916
  5.6 2.7 %copy-start.1 = (f32[3,16,4,128]{3,2,1,0:T(4,128)S(1)}, f32[3,16,4,128]{3,2,1,0:T(4,128)}, u32[]{:S(2)}) copy-start(f32[3,16,4,128]{3,2,1,0:T(4,128)} %param.10) | copy-start | bytes 294916
  6.3 8.3 %collective-permute-start.3 = (f32[192,128]{1,0:T(8,128)S(1)}, f32[192,128]{1,0:T(8,128)S(1)}, u32[]{:S(2)}, u32[]{:S(2)}) collective-permute-start(f32[192,128]{1,0:T(8,128)S(1)} %get-tuple-element.19), channel_id=1, source_target_pairs={{0,16},{8,24},{16,0},{24,8},{1,17},{9,25},{17,1},{25,9},{2,18},{10... | collective-permute-start | bytes 294920 | tf_op jit(solution)/shard_map/ppermute | solution.py:222
  9.4 4.1 %copy-start.2 = (f32[32,32]{1,0:T(8,128)S(1)}, f32[32,32]{1,0:T(8,128)}, u32[]{:S(2)}) copy-start(f32[32,32]{1,0:T(8,128)} %y_first.1) | copy-start | bytes 12292
  9.4 4.1 %copy-start.3 = (f32[32,32]{1,0:T(8,128)S(1)}, f32[32,32]{1,0:T(8,128)}, u32[]{:S(2)}) copy-start(f32[32,32]{1,0:T(8,128)} %y_second.1) | copy-start | bytes 12292
  9.7 6.6 %collective-permute-start.4 = (f32[192,128]{1,0:T(8,128)S(1)}, f32[192,128]{1,0:T(8,128)S(1)}, u32[]{:S(2)}, u32[]{:S(2)}) collective-permute-start(f32[192,128]{1,0:T(8,128)S(1)} %get-tuple-element.22), channel_id=1, source_target_pairs={{0,6},{1,7},{2,4},{3,5},{4,2},{5,3},{6,0},{7,1},{8,12},{9,13},{10,... | collective-permute-start | bytes 294920 | tf_op jit(solution)/shard_map/ppermute | solution.py:255
  13.5 0.7 %copy-start.7 = (f32[64]{0:T(128)S(1)}, f32[64]{0:T(128)}, u32[]{:S(2)}) copy-start(f32[64]{0:T(128)} %param.18) | copy-start | bytes 772
  13.5 0.7 %copy-start.8 = (s32[32]{0:T(128)S(1)}, s32[32]{0:T(128)}, u32[]{:S(2)}) copy-start(s32[32]{0:T(128)} %param.19) | copy-start | bytes 388
  15.0 1.4 %collective-permute-start.5 = (f32[192,128]{1,0:T(8,128)S(1)}, f32[192,128]{1,0:T(8,128)S(1)}, u32[]{:S(2)}, u32[]{:S(2)}) collective-permute-start(f32[192,128]{1,0:T(8,128)S(1)} %get-tuple-element.21.after), channel_id=1, source_target_pairs={{0,8},{8,0},{16,24},{24,16},{1,9},{9,1},{17,25},{25,17},{2,10},{10... | collective-permute-start | bytes 294920 | tf_op jit(solution)/shard_map/ppermute | solution.py:222
  15.1 0.7 %copy-start.9 = (f32[128]{0:T(128)S(1)}, f32[128]{0:T(128)}, u32[]{:S(2)}) copy-start(f32[128]{0:T(128)} %param.12) | copy-start | bytes 1540
  15.1 0.7 %copy-start.10 = (f32[128]{0:T(128)S(1)}, f32[128]{0:T(128)}, u32[]{:S(2)}) copy-start(f32[128]{0:T(128)} %param.13) | copy-start | bytes 1540

commit v34 on v33

--- a/solution.py
+++ b/solution.py
@@ -212,7 +212,7 @@
     comps, slots, zloc, length = velocity.shape
     depth = slots * zloc
     field = velocity.reshape(comps * depth, length)
-    group = min(depth, 32)
+    group = min(depth, 16)
     wide = cols // quad
 
     def along(value, step):

time: 17.2 us -> 17.2 us (level)
  no operation moved by 1% of the time
where the time goes in v34:
time: 17.2 us; the launch traced here: 17 us
  starting transfers between devices  10.5 us (61%)
  Pallas kernels  2.99 us (17%)
  local copies, waits for them, and re-layouts  2.26 us (13%)
  waiting for transfers between devices  1.18 us (7%)
    ppermute x3, starting transfers between devices, along(): return lax.ppermute(value, 'col', [(i, i ^ step) for i in range(cols)])  4.66 us
    ppermute x1, starting transfers between devices, local(): lax.ppermute(parts[t], ('row', 'col'), [(i * cols + j, i * cols + (j ^ ov...  3.82 us
    pallas_call x8, Pallas kernels, call(): pl.pallas_call(kernel, out_shape=results, in_specs=[pl.BlockSpec(memory_s...  2.99 us
    unnamed x22, local copies, waits for them, and re-layouts  2.26 us
    ppermute x2, starting transfers between devices, across(): return lax.ppermute(value, 'row', [(i, i ^ step) for i in range(rows)])  2 us
    ppermute x3, waiting for transfers between devices, along(): return lax.ppermute(value, 'col', [(i, i ^ step) for i in range(cols)])  0.9 us
  transfers between devices with their start and end apart: 6, of which 3 were waited for; matrix products, arithmetic and copies ran while one was open for 0% of the time, Pallas kernels for 14%

profile of v34, /device:TPU:0, one launch (start us, length us, event | category | flops | bytes accessed | tf_op | source)
XLA Modules:
  0.0 17.0 jit_solution(15739883070914056486)
XLA Ops:
  0.0 4.0 %collective-permute-start = (f32[192,128]{1,0:T(8,128)}, f32[192,128]{1,0:T(8,128)S(1)}, u32[]{:S(2)}, u32[]{:S(2)}) collective-permute-start(f32[192,128]{1,0:T(8,128)} %bitcast.6), channel_id=1, source_target_pairs={{0,3},{1,2},{2,1},{3,0},{4,7},{5,6},{6,5},{7,4},{8,11},{9,10},{10,... | collective-permute-start | bytes 294920 | tf_op jit(solution)/shard_map/ppermute | solution.py:219
  4.0 0.4 %collective-permute-start.2 = (f32[192,128]{1,0:T(8,128)}, f32[192,128]{1,0:T(8,128)S(1)}, u32[]{:S(2)}, u32[]{:S(2)}) collective-permute-start(f32[192,128]{1,0:T(8,128)} %bitcast.7), channel_id=1, source_target_pairs={{0,2},{1,3},{2,0},{3,1},{4,6},{5,7},{6,4},{7,5},{8,10},{9,11},{10,... | collective-permute-start | bytes 294920 | tf_op jit(solution)/shard_map/ppermute | solution.py:219
  4.5 0.2 %collective-permute-start.1 = (f32[192,128]{1,0:T(8,128)}, f32[192,128]{1,0:T(8,128)S(1)}, u32[]{:S(2)}, u32[]{:S(2)}) collective-permute-start(f32[192,128]{1,0:T(8,128)} %bitcast.8), channel_id=1, source_target_pairs={{0,1},{1,0},{2,3},{3,2},{4,5},{5,4},{6,7},{7,6},{8,9},{9,8},{10,11... | collective-permute-start | bytes 294920 | tf_op jit(solution)/shard_map/ppermute | solution.py:219
  4.7 0.9 %copy-done = f32[3,16,4,128]{3,2,1,0:T(4,128)S(1)} copy-done((f32[3,16,4,128]{3,2,1,0:T(4,128)S(1)}, f32[3,16,4,128]{3,2,1,0:T(4,128)}, u32[]{:S(2)}) %copy-start) | copy-done | bytes 98328
  5.6 0.7 %span_matrix.1 = (f32[32,128]{1,0:T(8,128)S(1)}, f32[64,128]{1,0:T(8,128)S(1)}, f32[192,128]{1,0:T(8,128)S(1)}, f32[128,32]{1,0:T(8,128)S(1)}, f32[128,32]{1,0:T(8,128)S(1)}) custom-call(s32[4]{0:T(128)S(1)} %copy-done.4, f32[32]{0:T(128)S(1)} %copy-done.5, f32[32]{0:T(128)S(1)} %copy-done.6, f32[192,128]{1,0:T(8,128)S(1)} %bitcast.9), custom_call_target="tpu_custom_call" | custom-call | tf_op jit(solution)/shard_map/span_matrix/pallas_call | solution.py:186
  6.3 1.9 %collective-permute-start.3 = (f32[192,128]{1,0:T(8,128)S(1)}, f32[192,128]{1,0:T(8,128)S(1)}, u32[]{:S(2)}, u32[]{:S(2)}) collective-permute-start(f32[192,128]{1,0:T(8,128)S(1)} %get-tuple-element.19), channel_id=1, source_target_pairs={{0,16},{8,24},{16,0},{24,8},{1,17},{9,25},{17,1},{25,9},{2,18},{10... | collective-permute-start | bytes 294920 | tf_op jit(solution)/shard_map/ppermute | solution.py:222
  8.2 0.3 %early.1 = f32[32,1536]{1,0:T(8,128)S(1)} custom-call(f32[32,128]{1,0:T(8,128)S(1)} %get-tuple-element.17.matrix, f32[192,128]{1,0:T(8,128)S(1)} %bitcast.10, f32[192,128]{1,0:T(8,128)S(1)} %collective-permute-done.refs_1_), custom_call_target="tpu_custom_call" | custom-call | tf_op jit(solution)/shard_map/early/pallas_call | solution.py:186
  8.5 0.9 %collective-permute-done.2.refs_1_ = f32[192,128]{1,0:T(8,128)S(1)} collective-permute-done((f32[192,128]{1,0:T(8,128)}, f32[192,128]{1,0:T(8,128)S(1)}, u32[]{:S(2)}, u32[]{:S(2)}) %collective-permute-start.2) | collective-permute-done | bytes 98336 | tf_op jit(solution)/shard_map/ppermute | solution.py:219
  9.4 0.3 %span.1 = (f32[192,128]{1,0:T(8,128)S(1)}, f32[192,128]{1,0:T(8,128)S(1)}) custom-call(f32[32,128]{1,0:T(8,128)S(1)} %get-tuple-element.17.matrix, f32[32,1536]{1,0:T(8,128)S(1)} %early.1, f32[192,128]{1,0:T(8,128)S(1)} %collective-permute-done.1.refs_0_, f32[192,128]{1,0:T(8,128)S(1)} %collective-permute-done.2.refs_1_), custom_call_target="tpu_custom_call" | custom-call | tf_op jit(solution)/shard_map/span/pallas_call | solution.py:186
  9.7 3.8 %collective-permute-start.4 = (f32[192,128]{1,0:T(8,128)S(1)}, f32[192,128]{1,0:T(8,128)S(1)}, u32[]{:S(2)}, u32[]{:S(2)}) collective-permute-start(f32[192,128]{1,0:T(8,128)S(1)} %get-tuple-element.22), channel_id=1, source_target_pairs={{0,6},{1,7},{2,4},{3,5},{4,2},{5,3},{6,0},{7,1},{8,12},{9,13},{10,... | collective-permute-start | bytes 294920 | tf_op jit(solution)/shard_map/ppermute | solution.py:255
  13.5 0.6 %copy-done.7 = f32[64]{0:T(128)S(1)} copy-done((f32[64]{0:T(128)S(1)}, f32[64]{0:T(128)}, u32[]{:S(2)}) %copy-start.7) | copy-done | bytes 280
  14.2 0.0 copy-done.8
  14.2 0.5 %wall_matrix.1.matrix = f32[128,256]{1,0:T(8,128)S(1)} custom-call(f32[128,32]{1,0:T(8,128)S(1)} %get-tuple-element.15.ends, f32[128,32]{1,0:T(8,128)S(1)} %get-tuple-element.16.others, f32[1,64]{1,0:T(1,128)S(1)} %bitcast.13, s32[1,32]{1,0:T(1,128)S(1)} %bitcast.14, f32[32,32]{1,0:T(8,128)S(1)} %copy-done.2, f32[32,32]{1,0:T(8,128)S(1)} %copy-done.3, ...), custom_call_target="tpu_custom_call" | custom-call | tf_op jit(solution)/shard_map/wall_matrix/pallas_call | solution.py:186
  14.7 0.0 collective-permute-done.3.refs_1_
  14.7 0.3 %wall.1 = (f32[192,128]{1,0:T(8,128)S(1)}, f32[192,128]{1,0:T(8,128)S(1)}) custom-call(f32[128,256]{1,0:T(8,128)S(1)} %wall_matrix.1.matrix, f32[192,128]{1,0:T(8,128)S(1)} %get-tuple-element.18.after.z_part, f32[192,128]{1,0:T(8,128)S(1)} %bitcast.11, f32[192,128]{1,0:T(8,128)S(1)} %collective-permute-done.3.refs_1_), custom_call_target="tpu_custom_call" | custom-call | tf_op jit(solution)/shard_map/wall/pallas_call | solution.py:186
  15.0 0.1 collective-permute-start.5
  15.1 0.0 copy-start.9
  15.1 0.0 copy-start.10
  15.1 0.6 %copy-done.9 = f32[128]{0:T(128)S(1)} copy-done((f32[128]{0:T(128)S(1)}, f32[128]{0:T(128)}, u32[]{:S(2)}) %copy-start.9) | copy-done | bytes 536
  15.7 0.0 copy-done.10
  15.7 0.3 %stream.1.refs_1_ = f32[192,128]{1,0:T(8,128)S(1)} custom-call(f32[192,128]{1,0:T(8,128)S(1)} %bitcast.12, f32[1,128]{1,0:T(1,128)S(1)} %bitcast.15, f32[1,128]{1,0:T(1,128)S(1)} %bitcast.16, f32[192,128]{1,0:T(8,128)S(1)} %get-tuple-element.21.after), custom_call_target="tpu_custom_call" | custom-call | tf_op jit(solution)/shard_map/stream/pallas_call | solution.py:186
  16.0 0.2 %collective-permute-done.4.refs_2_ = f32[192,128]{1,0:T(8,128)S(1)} collective-permute-done((f32[192,128]{1,0:T(8,128)S(1)}, f32[192,128]{1,0:T(8,128)S(1)}, u32[]{:S(2)}, u32[]{:S(2)}) %collective-permute-start.4) | collective-permute-done | bytes 98336 | tf_op jit(solution)/shard_map/ppermute | solution.py:255
  16.3 0.1 collective-permute-done.5.near
  16.3 0.7 %finish.1 = f32[192,128]{1,0:T(8,128)} custom-call(f32[192,128]{1,0:T(8,128)S(1)} %sum.1.total, f32[192,128]{1,0:T(8,128)S(1)} %collective-permute-done.5.near), custom_call_target="tpu_custom_call" | custom-call | tf_op jit(solution)/shard_map/finish/pallas_call | solution.py:186
  (18 shorter events, 0.1 us)
Async XLA Ops:
  0.0 4.7 %copy-start.6 = (f32[32]{0:T(128)S(1)}, f32[32]{0:T(128)}, u32[]{:S(2)}) copy-start(f32[32]{0:T(128)} %z_second.1) | copy-start | bytes 388
  0.0 4.7 %copy-start.5 = (f32[32]{0:T(128)S(1)}, f32[32]{0:T(128)}, u32[]{:S(2)}) copy-start(f32[32]{0:T(128)} %z_first.1) | copy-start | bytes 388
  0.0 4.7 %copy-start.4 = (s32[4]{0:T(128)S(1)}, s32[4]{0:T(128)}, u32[]{:S(2)}) copy-start(s32[4]{0:T(128)} %wall_counts.1) | copy-start | bytes 52
  0.0 8.2 %collective-permute-start = (f32[192,128]{1,0:T(8,128)}, f32[192,128]{1,0:T(8,128)S(1)}, u32[]{:S(2)}, u32[]{:S(2)}) collective-permute-start(f32[192,128]{1,0:T(8,128)} %bitcast.6), channel_id=1, source_target_pairs={{0,3},{1,2},{2,1},{3,0},{4,7},{5,6},{6,5},{7,4},{8,11},{9,10},{10,... | collective-permute-start | bytes 294920 | tf_op jit(solution)/shard_map/ppermute | solution.py:219
  4.0 5.4 %collective-permute-start.2 = (f32[192,128]{1,0:T(8,128)}, f32[192,128]{1,0:T(8,128)S(1)}, u32[]{:S(2)}, u32[]{:S(2)}) collective-permute-start(f32[192,128]{1,0:T(8,128)} %bitcast.7), channel_id=1, source_target_pairs={{0,2},{1,3},{2,0},{3,1},{4,6},{5,7},{6,4},{7,5},{8,10},{9,11},{10,... | collective-permute-start | bytes 294920 | tf_op jit(solution)/shard_map/ppermute | solution.py:219
  4.5 4.9 %collective-permute-start.1 = (f32[192,128]{1,0:T(8,128)}, f32[192,128]{1,0:T(8,128)S(1)}, u32[]{:S(2)}, u32[]{:S(2)}) collective-permute-start(f32[192,128]{1,0:T(8,128)} %bitcast.8), channel_id=1, source_target_pairs={{0,1},{1,0},{2,3},{3,2},{4,5},{5,4},{6,7},{7,6},{8,9},{9,8},{10,11... | collective-permute-start | bytes 294920 | tf_op jit(solution)/shard_map/ppermute | solution.py:219
  4.7 0.9 %copy-start = (f32[3,16,4,128]{3,2,1,0:T(4,128)S(1)}, f32[3,16,4,128]{3,2,1,0:T(4,128)}, u32[]{:S(2)}) copy-start(f32[3,16,4,128]{3,2,1,0:T(4,128)} %param.10) | copy-start | bytes 294916
  5.6 2.6 %copy-start.1 = (f32[3,16,4,128]{3,2,1,0:T(4,128)S(1)}, f32[3,16,4,128]{3,2,1,0:T(4,128)}, u32[]{:S(2)}) copy-start(f32[3,16,4,128]{3,2,1,0:T(4,128)} %param.10) | copy-start | bytes 294916
  6.3 8.4 %collective-permute-start.3 = (f32[192,128]{1,0:T(8,128)S(1)}, f32[192,128]{1,0:T(8,128)S(1)}, u32[]{:S(2)}, u32[]{:S(2)}) collective-permute-start(f32[192,128]{1,0:T(8,128)S(1)} %get-tuple-element.19), channel_id=1, source_target_pairs={{0,16},{8,24},{16,0},{24,8},{1,17},{9,25},{17,1},{25,9},{2,18},{10... | collective-permute-start | bytes 294920 | tf_op jit(solution)/shard_map/ppermute | solution.py:222
  9.4 4.1 %copy-start.2 = (f32[32,32]{1,0:T(8,128)S(1)}, f32[32,32]{1,0:T(8,128)}, u32[]{:S(2)}) copy-start(f32[32,32]{1,0:T(8,128)} %y_first.1) | copy-start | bytes 12292
  9.4 4.1 %copy-start.3 = (f32[32,32]{1,0:T(8,128)S(1)}, f32[32,32]{1,0:T(8,128)}, u32[]{:S(2)}) copy-start(f32[32,32]{1,0:T(8,128)} %y_second.1) | copy-start | bytes 12292
  9.7 6.6 %collective-permute-start.4 = (f32[192,128]{1,0:T(8,128)S(1)}, f32[192,128]{1,0:T(8,128)S(1)}, u32[]{:S(2)}, u32[]{:S(2)}) collective-permute-start(f32[192,128]{1,0:T(8,128)S(1)} %get-tuple-element.22), channel_id=1, source_target_pairs={{0,6},{1,7},{2,4},{3,5},{4,2},{5,3},{6,0},{7,1},{8,12},{9,13},{10,... | collective-permute-start | bytes 294920 | tf_op jit(solution)/shard_map/ppermute | solution.py:255
  13.5 0.7 %copy-start.7 = (f32[64]{0:T(128)S(1)}, f32[64]{0:T(128)}, u32[]{:S(2)}) copy-start(f32[64]{0:T(128)} %param.18) | copy-start | bytes 772
  13.5 0.7 %copy-start.8 = (s32[32]{0:T(128)S(1)}, s32[32]{0:T(128)}, u32[]{:S(2)}) copy-start(s32[32]{0:T(128)} %param.19) | copy-start | bytes 388
  15.0 1.4 %collective-permute-start.5 = (f32[192,128]{1,0:T(8,128)S(1)}, f32[192,128]{1,0:T(8,128)S(1)}, u32[]{:S(2)}, u32[]{:S(2)}) collective-permute-start(f32[192,128]{1,0:T(8,128)S(1)} %get-tuple-element.21.after), channel_id=1, source_target_pairs={{0,8},{8,0},{16,24},{24,16},{1,9},{9,1},{17,25},{25,17},{2,10},{10... | collective-permute-start | bytes 294920 | tf_op jit(solution)/shard_map/ppermute | solution.py:222
  15.1 0.7 %copy-start.9 = (f32[128]{0:T(128)S(1)}, f32[128]{0:T(128)}, u32[]{:S(2)}) copy-start(f32[128]{0:T(128)} %param.12) | copy-start | bytes 1540
  15.1 0.7 %copy-start.10 = (f32[128]{0:T(128)S(1)}, f32[128]{0:T(128)}, u32[]{:S(2)}) copy-start(f32[128]{0:T(128)} %param.13) | copy-start | bytes 1540

commit v35 on v34

--- a/solution.py
+++ b/solution.py
@@ -212,7 +212,7 @@
     comps, slots, zloc, length = velocity.shape
     depth = slots * zloc
     field = velocity.reshape(comps * depth, length)
-    group = min(depth, 16)
+    group = min(depth, 8)
     wide = cols // quad
 
     def along(value, step):

time: 17.2 us -> 17.2 us (level)
  no operation moved by 1% of the time
where the time goes in v35:
time: 17.2 us; the launch traced here: 17 us
  starting transfers between devices  10.5 us (61%)
  Pallas kernels  3.02 us (18%)
  local copies, waits for them, and re-layouts  2.26 us (13%)
  waiting for transfers between devices  1.18 us (7%)
    ppermute x3, starting transfers between devices, along(): return lax.ppermute(value, 'col', [(i, i ^ step) for i in range(cols)])  4.66 us
    ppermute x1, starting transfers between devices, local(): lax.ppermute(parts[t], ('row', 'col'), [(i * cols + j, i * cols + (j ^ ov...  3.82 us
    pallas_call x8, Pallas kernels, call(): pl.pallas_call(kernel, out_shape=results, in_specs=[pl.BlockSpec(memory_s...  3.02 us
    unnamed x22, local copies, waits for them, and re-layouts  2.26 us
    ppermute x2, starting transfers between devices, across(): return lax.ppermute(value, 'row', [(i, i ^ step) for i in range(rows)])  2 us
    ppermute x3, waiting for transfers between devices, along(): return lax.ppermute(value, 'col', [(i, i ^ step) for i in range(cols)])  0.9 us
  transfers between devices with their start and end apart: 6, of which 3 were waited for; matrix products, arithmetic and copies ran while one was open for 0% of the time, Pallas kernels for 14%

profile of v35, /device:TPU:0, one launch (start us, length us, event | category | flops | bytes accessed | tf_op | source)
XLA Modules:
  0.0 17.0 jit_solution(4733884423218736061)
XLA Ops:
  0.0 4.0 %collective-permute-start = (f32[192,128]{1,0:T(8,128)}, f32[192,128]{1,0:T(8,128)S(1)}, u32[]{:S(2)}, u32[]{:S(2)}) collective-permute-start(f32[192,128]{1,0:T(8,128)} %bitcast.6), channel_id=1, source_target_pairs={{0,3},{1,2},{2,1},{3,0},{4,7},{5,6},{6,5},{7,4},{8,11},{9,10},{10,... | collective-permute-start | bytes 294920 | tf_op jit(solution)/shard_map/ppermute | solution.py:219
  4.0 0.4 %collective-permute-start.2 = (f32[192,128]{1,0:T(8,128)}, f32[192,128]{1,0:T(8,128)S(1)}, u32[]{:S(2)}, u32[]{:S(2)}) collective-permute-start(f32[192,128]{1,0:T(8,128)} %bitcast.7), channel_id=1, source_target_pairs={{0,2},{1,3},{2,0},{3,1},{4,6},{5,7},{6,4},{7,5},{8,10},{9,11},{10,... | collective-permute-start | bytes 294920 | tf_op jit(solution)/shard_map/ppermute | solution.py:219
  4.5 0.2 %collective-permute-start.1 = (f32[192,128]{1,0:T(8,128)}, f32[192,128]{1,0:T(8,128)S(1)}, u32[]{:S(2)}, u32[]{:S(2)}) collective-permute-start(f32[192,128]{1,0:T(8,128)} %bitcast.8), channel_id=1, source_target_pairs={{0,1},{1,0},{2,3},{3,2},{4,5},{5,4},{6,7},{7,6},{8,9},{9,8},{10,11... | collective-permute-start | bytes 294920 | tf_op jit(solution)/shard_map/ppermute | solution.py:219
  4.7 0.9 %copy-done = f32[3,16,4,128]{3,2,1,0:T(4,128)S(1)} copy-done((f32[3,16,4,128]{3,2,1,0:T(4,128)S(1)}, f32[3,16,4,128]{3,2,1,0:T(4,128)}, u32[]{:S(2)}) %copy-start) | copy-done | bytes 98328
  5.6 0.7 %span_matrix.1 = (f32[16,64]{1,0:T(8,128)S(1)}, f32[64,128]{1,0:T(8,128)S(1)}, f32[192,128]{1,0:T(8,128)S(1)}, f32[128,32]{1,0:T(8,128)S(1)}, f32[128,32]{1,0:T(8,128)S(1)}) custom-call(s32[4]{0:T(128)S(1)} %copy-done.4, f32[32]{0:T(128)S(1)} %copy-done.5, f32[32]{0:T(128)S(1)} %copy-done.6, f32[192,128]{1,0:T(8,128)S(1)} %bitcast.9), custom_call_target="tpu_custom_call" | custom-call | tf_op jit(solution)/shard_map/span_matrix/pallas_call | solution.py:186
  6.3 1.9 %collective-permute-start.3 = (f32[192,128]{1,0:T(8,128)S(1)}, f32[192,128]{1,0:T(8,128)S(1)}, u32[]{:S(2)}, u32[]{:S(2)}) collective-permute-start(f32[192,128]{1,0:T(8,128)S(1)} %get-tuple-element.19), channel_id=1, source_target_pairs={{0,16},{8,24},{16,0},{24,8},{1,17},{9,25},{17,1},{25,9},{2,18},{10... | collective-permute-start | bytes 294920 | tf_op jit(solution)/shard_map/ppermute | solution.py:222
  8.2 0.3 %early.1 = f32[16,3072]{1,0:T(8,128)S(1)} custom-call(f32[16,64]{1,0:T(8,128)S(1)} %get-tuple-element.17.matrix, f32[192,128]{1,0:T(8,128)S(1)} %bitcast.10, f32[192,128]{1,0:T(8,128)S(1)} %collective-permute-done.refs_1_), custom_call_target="tpu_custom_call" | custom-call | tf_op jit(solution)/shard_map/early/pallas_call | solution.py:186
  8.5 0.9 %collective-permute-done.2.refs_1_ = f32[192,128]{1,0:T(8,128)S(1)} collective-permute-done((f32[192,128]{1,0:T(8,128)}, f32[192,128]{1,0:T(8,128)S(1)}, u32[]{:S(2)}, u32[]{:S(2)}) %collective-permute-start.2) | collective-permute-done | bytes 98336 | tf_op jit(solution)/shard_map/ppermute | solution.py:219
  9.4 0.0 collective-permute-done.1.refs_0_
  9.4 0.3 %span.1 = (f32[192,128]{1,0:T(8,128)S(1)}, f32[192,128]{1,0:T(8,128)S(1)}) custom-call(f32[16,64]{1,0:T(8,128)S(1)} %get-tuple-element.17.matrix, f32[16,3072]{1,0:T(8,128)S(1)} %early.1, f32[192,128]{1,0:T(8,128)S(1)} %collective-permute-done.1.refs_0_, f32[192,128]{1,0:T(8,128)S(1)} %collective-permute-done.2.refs_1_), custom_call_target="tpu_custom_call" | custom-call | tf_op jit(solution)/shard_map/span/pallas_call | solution.py:186
  9.7 3.8 %collective-permute-start.4 = (f32[192,128]{1,0:T(8,128)S(1)}, f32[192,128]{1,0:T(8,128)S(1)}, u32[]{:S(2)}, u32[]{:S(2)}) collective-permute-start(f32[192,128]{1,0:T(8,128)S(1)} %get-tuple-element.22), channel_id=1, source_target_pairs={{0,6},{1,7},{2,4},{3,5},{4,2},{5,3},{6,0},{7,1},{8,12},{9,13},{10,... | collective-permute-start | bytes 294920 | tf_op jit(solution)/shard_map/ppermute | solution.py:255
  13.5 0.6 %copy-done.7 = f32[64]{0:T(128)S(1)} copy-done((f32[64]{0:T(128)S(1)}, f32[64]{0:T(128)}, u32[]{:S(2)}) %copy-start.7) | copy-done | bytes 280
  14.2 0.0 copy-done.8
  14.2 0.5 %wall_matrix.1.matrix = f32[128,256]{1,0:T(8,128)S(1)} custom-call(f32[128,32]{1,0:T(8,128)S(1)} %get-tuple-element.15.ends, f32[128,32]{1,0:T(8,128)S(1)} %get-tuple-element.16.others, f32[1,64]{1,0:T(1,128)S(1)} %bitcast.13, s32[1,32]{1,0:T(1,128)S(1)} %bitcast.14, f32[32,32]{1,0:T(8,128)S(1)} %copy-done.2, f32[32,32]{1,0:T(8,128)S(1)} %copy-done.3, ...), custom_call_target="tpu_custom_call" | custom-call | tf_op jit(solution)/shard_map/wall_matrix/pallas_call | solution.py:186
  14.7 0.3 %wall.1 = (f32[192,128]{1,0:T(8,128)S(1)}, f32[192,128]{1,0:T(8,128)S(1)}) custom-call(f32[128,256]{1,0:T(8,128)S(1)} %wall_matrix.1.matrix, f32[192,128]{1,0:T(8,128)S(1)} %get-tuple-element.18.after.z_part, f32[192,128]{1,0:T(8,128)S(1)} %bitcast.11, f32[192,128]{1,0:T(8,128)S(1)} %collective-permute-done.3.refs_1_), custom_call_target="tpu_custom_call" | custom-call | tf_op jit(solution)/shard_map/wall/pallas_call | solution.py:186
  15.0 0.1 collective-permute-start.5
  15.1 0.0 copy-start.9
  15.1 0.0 copy-start.10
  15.1 0.6 %copy-done.9 = f32[128]{0:T(128)S(1)} copy-done((f32[128]{0:T(128)S(1)}, f32[128]{0:T(128)}, u32[]{:S(2)}) %copy-start.9) | copy-done | bytes 536
  15.7 0.0 copy-done.10
  15.7 0.3 %stream.1.refs_1_ = f32[192,128]{1,0:T(8,128)S(1)} custom-call(f32[192,128]{1,0:T(8,128)S(1)} %bitcast.12, f32[1,128]{1,0:T(1,128)S(1)} %bitcast.15, f32[1,128]{1,0:T(1,128)S(1)} %bitcast.16, f32[192,128]{1,0:T(8,128)S(1)} %get-tuple-element.21.after), custom_call_target="tpu_custom_call" | custom-call | tf_op jit(solution)/shard_map/stream/pallas_call | solution.py:186
  16.1 0.2 %collective-permute-done.4.refs_2_ = f32[192,128]{1,0:T(8,128)S(1)} collective-permute-done((f32[192,128]{1,0:T(8,128)S(1)}, f32[192,128]{1,0:T(8,128)S(1)}, u32[]{:S(2)}, u32[]{:S(2)}) %collective-permute-start.4) | collective-permute-done | bytes 98336 | tf_op jit(solution)/shard_map/ppermute | solution.py:255
  16.3 0.1 collective-permute-done.5.near
  16.4 0.7 %finish.1 = f32[192,128]{1,0:T(8,128)} custom-call(f32[192,128]{1,0:T(8,128)S(1)} %sum.1.total, f32[192,128]{1,0:T(8,128)S(1)} %collective-permute-done.5.near), custom_call_target="tpu_custom_call" | custom-call | tf_op jit(solution)/shard_map/finish/pallas_call | solution.py:186
  (18 shorter events, 0.1 us)
Async XLA Ops:
  0.0 4.7 %copy-start.6 = (f32[32]{0:T(128)S(1)}, f32[32]{0:T(128)}, u32[]{:S(2)}) copy-start(f32[32]{0:T(128)} %z_second.1) | copy-start | bytes 388
  0.0 4.7 %copy-start.5 = (f32[32]{0:T(128)S(1)}, f32[32]{0:T(128)}, u32[]{:S(2)}) copy-start(f32[32]{0:T(128)} %z_first.1) | copy-start | bytes 388
  0.0 4.7 %copy-start.4 = (s32[4]{0:T(128)S(1)}, s32[4]{0:T(128)}, u32[]{:S(2)}) copy-start(s32[4]{0:T(128)} %wall_counts.1) | copy-start | bytes 52
  0.0 8.2 %collective-permute-start = (f32[192,128]{1,0:T(8,128)}, f32[192,128]{1,0:T(8,128)S(1)}, u32[]{:S(2)}, u32[]{:S(2)}) collective-permute-start(f32[192,128]{1,0:T(8,128)} %bitcast.6), channel_id=1, source_target_pairs={{0,3},{1,2},{2,1},{3,0},{4,7},{5,6},{6,5},{7,4},{8,11},{9,10},{10,... | collective-permute-start | bytes 294920 | tf_op jit(solution)/shard_map/ppermute | solution.py:219
  4.0 5.4 %collective-permute-start.2 = (f32[192,128]{1,0:T(8,128)}, f32[192,128]{1,0:T(8,128)S(1)}, u32[]{:S(2)}, u32[]{:S(2)}) collective-permute-start(f32[192,128]{1,0:T(8,128)} %bitcast.7), channel_id=1, source_target_pairs={{0,2},{1,3},{2,0},{3,1},{4,6},{5,7},{6,4},{7,5},{8,10},{9,11},{10,... | collective-permute-start | bytes 294920 | tf_op jit(solution)/shard_map/ppermute | solution.py:219
  4.5 4.9 %collective-permute-start.1 = (f32[192,128]{1,0:T(8,128)}, f32[192,128]{1,0:T(8,128)S(1)}, u32[]{:S(2)}, u32[]{:S(2)}) collective-permute-start(f32[192,128]{1,0:T(8,128)} %bitcast.8), channel_id=1, source_target_pairs={{0,1},{1,0},{2,3},{3,2},{4,5},{5,4},{6,7},{7,6},{8,9},{9,8},{10,11... | collective-permute-start | bytes 294920 | tf_op jit(solution)/shard_map/ppermute | solution.py:219
  4.7 0.9 %copy-start = (f32[3,16,4,128]{3,2,1,0:T(4,128)S(1)}, f32[3,16,4,128]{3,2,1,0:T(4,128)}, u32[]{:S(2)}) copy-start(f32[3,16,4,128]{3,2,1,0:T(4,128)} %param.10) | copy-start | bytes 294916
  5.6 2.6 %copy-start.1 = (f32[3,16,4,128]{3,2,1,0:T(4,128)S(1)}, f32[3,16,4,128]{3,2,1,0:T(4,128)}, u32[]{:S(2)}) copy-start(f32[3,16,4,128]{3,2,1,0:T(4,128)} %param.10) | copy-start | bytes 294916
  6.3 8.4 %collective-permute-start.3 = (f32[192,128]{1,0:T(8,128)S(1)}, f32[192,128]{1,0:T(8,128)S(1)}, u32[]{:S(2)}, u32[]{:S(2)}) collective-permute-start(f32[192,128]{1,0:T(8,128)S(1)} %get-tuple-element.19), channel_id=1, source_target_pairs={{0,16},{8,24},{16,0},{24,8},{1,17},{9,25},{17,1},{25,9},{2,18},{10... | collective-permute-start | bytes 294920 | tf_op jit(solution)/shard_map/ppermute | solution.py:222
  9.4 4.1 %copy-start.2 = (f32[32,32]{1,0:T(8,128)S(1)}, f32[32,32]{1,0:T(8,128)}, u32[]{:S(2)}) copy-start(f32[32,32]{1,0:T(8,128)} %y_first.1) | copy-start | bytes 12292
  9.4 4.1 %copy-start.3 = (f32[32,32]{1,0:T(8,128)S(1)}, f32[32,32]{1,0:T(8,128)}, u32[]{:S(2)}) copy-start(f32[32,32]{1,0:T(8,128)} %y_second.1) | copy-start | bytes 12292
  9.7 6.6 %collective-permute-start.4 = (f32[192,128]{1,0:T(8,128)S(1)}, f32[192,128]{1,0:T(8,128)S(1)}, u32[]{:S(2)}, u32[]{:S(2)}) collective-permute-start(f32[192,128]{1,0:T(8,128)S(1)} %get-tuple-element.22), channel_id=1, source_target_pairs={{0,6},{1,7},{2,4},{3,5},{4,2},{5,3},{6,0},{7,1},{8,12},{9,13},{10,... | collective-permute-start | bytes 294920 | tf_op jit(solution)/shard_map/ppermute | solution.py:255
  13.5 0.7 %copy-start.7 = (f32[64]{0:T(128)S(1)}, f32[64]{0:T(128)}, u32[]{:S(2)}) copy-start(f32[64]{0:T(128)} %param.18) | copy-start | bytes 772
  13.5 0.7 %copy-start.8 = (s32[32]{0:T(128)S(1)}, s32[32]{0:T(128)}, u32[]{:S(2)}) copy-start(s32[32]{0:T(128)} %param.19) | copy-start | bytes 388
  15.0 1.4 %collective-permute-start.5 = (f32[192,128]{1,0:T(8,128)S(1)}, f32[192,128]{1,0:T(8,128)S(1)}, u32[]{:S(2)}, u32[]{:S(2)}) collective-permute-start(f32[192,128]{1,0:T(8,128)S(1)} %get-tuple-element.21.after), channel_id=1, source_target_pairs={{0,8},{8,0},{16,24},{24,16},{1,9},{9,1},{17,25},{25,17},{2,10},{10... | collective-permute-start | bytes 294920 | tf_op jit(solution)/shard_map/ppermute | solution.py:222
  15.1 0.7 %copy-start.9 = (f32[128]{0:T(128)S(1)}, f32[128]{0:T(128)}, u32[]{:S(2)}) copy-start(f32[128]{0:T(128)} %param.12) | copy-start | bytes 1540
  15.1 0.7 %copy-start.10 = (f32[128]{0:T(128)S(1)}, f32[128]{0:T(128)}, u32[]{:S(2)}) copy-start(f32[128]{0:T(128)} %param.13) | copy-start | bytes 1540
